TPU v7x, 32 devices: a whole 2x2x4 slice. The times are simulated.
32 devices in a mesh: seq: 4 (over y, core), shard: 4 (over z), replica: 2 (over x).
Axes of the slice: x: 2, y: 2, z: 4, core: 2. Of those that a mesh axis runs over, the one named last changes fastest.
Arguments:
- inputs: bfloat16 [8, 1024, 2048], P(('shard', 'replica'), 'seq'), may hold values from -6 to 6
- cotangent: bfloat16 [8, 1024, 2048], P(('shard', 'replica'), 'seq'), may hold values from -6 to 6
- norm1_gain: float32 [2048], P(('seq', 'shard')), may hold values from 0.5 to 1.5
- norm1_bias: float32 [2048], P(('seq', 'shard')), may hold values from -1.5 to 1.5
- w_qkv: float32 [2048, 6144], P(('seq', 'shard')), may hold values from -0.125 to 0.125
- query_bias: float32 [2048], P(('seq', 'shard')), may hold values from -1.5 to 1.5
- value_bias: float32 [2048], P(('seq', 'shard')), may hold values from -1.5 to 1.5
- w_attn_out: float32 [2048, 2048], P(('seq', 'shard')), may hold values from -0.5 to 0.5
- attn_out_bias: float32 [2048], P(('seq', 'shard')), may hold values from -1.5 to 1.5
- norm2_gain: float32 [2048], P(('seq', 'shard')), may hold values from 0.5 to 1.5
- norm2_bias: float32 [2048], P(('seq', 'shard')), may hold values from -1.5 to 1.5
- w_hidden: float32 [2048, 8192], P(('seq', 'shard')), may hold values from -0.125 to 0.125
- hidden_bias: float32 [8192], P(('seq', 'shard')), may hold values from -1.5 to 1.5
- w_output: float32 [8192, 2048], P(('seq', 'shard')), may hold values from -0.0625 to 0.0625
- output_bias: float32 [2048], P(('seq', 'shard')), may hold values from -1.5 to 1.5
Outputs:
- output: bfloat16 [8, 1024, 2048], P(('shard', 'replica'), 'seq')
- grad_inputs: float32 [8, 1024, 2048], P(('shard', 'replica'), 'seq')
- grad_norm1_gain: float32 [2048], P(('seq', 'shard'))
- grad_norm1_bias: float32 [2048], P(('seq', 'shard'))
- grad_w_qkv: float32 [2048, 6144], P(('seq', 'shard'))
- grad_query_bias: float32 [2048], P(('seq', 'shard'))
- grad_value_bias: float32 [2048], P(('seq', 'shard'))
- grad_w_attn_out: float32 [2048, 2048], P(('seq', 'shard'))
- grad_attn_out_bias: float32 [2048], P(('seq', 'shard'))
- grad_norm2_gain: float32 [2048], P(('seq', 'shard'))
- grad_norm2_bias: float32 [2048], P(('seq', 'shard'))
- grad_w_hidden: float32 [2048, 8192], P(('seq', 'shard'))
- grad_hidden_bias: float32 [8192], P(('seq', 'shard'))
- grad_w_output: float32 [8192, 2048], P(('seq', 'shard'))
- grad_output_bias: float32 [2048], P(('seq', 'shard'))
All inputs are finite; a program needn't handle non-finite values.
Results may differ from a plain program's by a relative error of at most 0.015.
Values may be sent and summed in bfloat16 or wider, within the bound.
No kernel may reach another device: no remote copies, remote signals or barrier semaphores. Data moves between devices by JAX's collectives and lax.ppermute only.
A program may use at most 512 MiB of HBM per device.

v0:
```python
import jax
import jax.numpy as jnp
from jax import lax
from jax.sharding import PartitionSpec as P

HEAD_DIM = 128


def normalize(values):
    mean_row = jnp.mean(values, axis=1, keepdims=True)
    centred = values - mean_row
    scale_row = lax.rsqrt(jnp.mean(centred * centred, axis=1, keepdims=True) + 1e-05)
    return (centred * scale_row, scale_row)


def norm_back(grad_normed, normed, scale_row):
    first_mean = jnp.mean(grad_normed, axis=1, keepdims=True)
    second_mean = jnp.mean(grad_normed * normed, axis=1, keepdims=True)
    return scale_row * (grad_normed - first_mean - normed * second_mean)


def gelu_slope(values):
    normal_cdf = 0.5 * (1.0 + lax.erf(values * 0.7071067811865476))
    return normal_cdf + values * jnp.exp(-0.5 * values * values) * 0.3989422804014327


def column_sums(values):
    return jnp.sum(values.astype(jnp.float32), axis=0)


def on_device(
    inputs,
    cotangent,
    norm1_gain,
    norm1_bias,
    w_qkv,
    query_bias,
    value_bias,
    w_attn_out,
    attn_out_bias,
    norm2_gain,
    norm2_bias,
    w_hidden,
    hidden_bias,
    w_output,
    output_bias,
):
    fp32 = jnp.float32
    bf16 = jnp.bfloat16
    seqs_here, block_len, model_width = inputs.shape
    total_rows = seqs_here * block_len
    head_count = model_width // HEAD_DIM
    scaling = HEAD_DIM ** (-0.5)
    masters = (
        norm1_gain,
        norm1_bias,
        w_qkv,
        query_bias,
        value_bias,
        w_attn_out,
        attn_out_bias,
        norm2_gain,
        norm2_bias,
        w_hidden,
        hidden_bias,
        w_output,
        output_bias,
    )
    halves = tuple((master.astype(bf16) for master in masters))
    attn_set = (
        lax.all_gather(halves[0], ("seq", "shard"), axis=0, tiled=True),
        lax.all_gather(halves[1], ("seq", "shard"), axis=0, tiled=True),
        lax.all_gather(halves[2], ("seq", "shard"), axis=0, tiled=True),
        lax.all_gather(halves[3], ("seq", "shard"), axis=0, tiled=True),
        lax.all_gather(halves[4], ("seq", "shard"), axis=0, tiled=True),
        lax.all_gather(halves[5], ("seq", "shard"), axis=0, tiled=True),
        lax.all_gather(halves[6], ("seq", "shard"), axis=0, tiled=True),
    )
    gain_first, shift_first, qkv_matrix, query_shift, value_shift, attn_matrix, attn_shift = (
        attn_set
    )
    flat_in = inputs.reshape(total_rows, model_width).astype(fp32)
    normed_one, inverse_one = normalize(flat_in)
    hidden_in = (normed_one * gain_first.astype(fp32) + shift_first.astype(fp32)).astype(bf16)
    bias_row = jnp.concatenate(
        [query_shift.astype(fp32), jnp.zeros((model_width,), fp32), value_shift.astype(fp32)]
    )
    qkv_rows = (jnp.dot(hidden_in, qkv_matrix, preferred_element_type=fp32) + bias_row).astype(bf16)
    queries = qkv_rows[:, :model_width].reshape(seqs_here, block_len, head_count, HEAD_DIM)
    keys_own = qkv_rows[:, model_width : 2 * model_width].reshape(seqs_here, block_len, model_width)
    values_own = qkv_rows[:, 2 * model_width :].reshape(seqs_here, block_len, model_width)
    keys_flat, values_flat = (
        lax.all_gather(keys_own, "seq", axis=1, tiled=True),
        lax.all_gather(values_own, "seq", axis=1, tiled=True),
    )
    full_len = keys_flat.shape[1]
    keys_all = keys_flat.reshape(seqs_here, full_len, head_count, HEAD_DIM)
    values_all = values_flat.reshape(seqs_here, full_len, head_count, HEAD_DIM)
    own_block = lax.axis_index("seq")
    allowed = jnp.arange(full_len) // block_len <= own_block

    def scores_of(query_part):
        raw_scores = (
            jnp.einsum("sqhd,skhd->shqk", query_part, keys_all, preferred_element_type=fp32)
            * scaling
        )
        return jnp.where(allowed, raw_scores, -1e30)

    scores = scores_of(queries)
    row_top = jnp.max(scores, axis=-1, keepdims=True)
    expons = jnp.exp(scores - row_top)
    totals = jnp.sum(expons, axis=-1, keepdims=True)
    soft_probs = expons / totals
    log_total = row_top + jnp.log(totals)
    probs_low = soft_probs.astype(bf16)
    attended = jnp.einsum("shqk,skhd->sqhd", probs_low, values_all, preferred_element_type=fp32)
    attended = attended.reshape(total_rows, model_width).astype(bf16)
    mid_rows = flat_in + (
        jnp.dot(attended, attn_matrix, preferred_element_type=fp32) + attn_shift.astype(fp32)
    )
    mlp_set = (
        lax.all_gather(halves[7], ("seq", "shard"), axis=0, tiled=True),
        lax.all_gather(halves[8], ("seq", "shard"), axis=0, tiled=True),
        lax.all_gather(halves[9], ("seq", "shard"), axis=0, tiled=True),
        lax.all_gather(halves[10], ("seq", "shard"), axis=0, tiled=True),
        lax.all_gather(halves[11], ("seq", "shard"), axis=0, tiled=True),
        lax.all_gather(halves[12], ("seq", "shard"), axis=0, tiled=True),
    )
    gain_second, shift_second, hidden_matrix, hidden_shift, output_matrix, output_shift = mlp_set
    normed_two, inverse_two = normalize(mid_rows)
    hidden_two = (normed_two * gain_second.astype(fp32) + shift_second.astype(fp32)).astype(bf16)
    preactive = jnp.dot(
        hidden_two, hidden_matrix, preferred_element_type=fp32
    ) + hidden_shift.astype(fp32)
    activated = jax.nn.gelu(preactive, approximate=False).astype(bf16)
    out_rows = mid_rows + (
        jnp.dot(activated, output_matrix, preferred_element_type=fp32) + output_shift.astype(fp32)
    )
    layer_out = out_rows.astype(bf16).reshape(seqs_here, block_len, model_width)
    mlp_back = (
        lax.all_gather(halves[7], ("seq", "shard"), axis=0, tiled=True),
        lax.all_gather(halves[8], ("seq", "shard"), axis=0, tiled=True),
        lax.all_gather(halves[9], ("seq", "shard"), axis=0, tiled=True),
        lax.all_gather(halves[10], ("seq", "shard"), axis=0, tiled=True),
        lax.all_gather(halves[11], ("seq", "shard"), axis=0, tiled=True),
        lax.all_gather(halves[12], ("seq", "shard"), axis=0, tiled=True),
    )
    gain_second_b = mlp_back[0].astype(fp32)
    hidden_matrix_b = mlp_back[2]
    output_matrix_b = mlp_back[4]
    grad_out = cotangent.reshape(total_rows, model_width).astype(fp32)
    grad_low = grad_out.astype(bf16)
    grad_output_matrix = jnp.einsum("rf,rd->fd", activated, grad_low, preferred_element_type=fp32)
    grad_output_shift = column_sums(grad_low)
    grad_activated = jnp.einsum("rd,fd->rf", grad_low, output_matrix_b, preferred_element_type=fp32)
    grad_pre = (grad_activated * gelu_slope(preactive)).astype(bf16)
    grad_hidden_matrix = jnp.einsum("rd,rf->df", hidden_two, grad_pre, preferred_element_type=fp32)
    grad_hidden_shift = column_sums(grad_pre)
    grad_hidden_two = jnp.einsum(
        "rf,df->rd", grad_pre, hidden_matrix_b, preferred_element_type=fp32
    )
    grad_gain_two = jnp.sum(grad_hidden_two * normed_two, axis=0)
    grad_shift_two = jnp.sum(grad_hidden_two, axis=0)
    grad_mid = grad_out + norm_back(grad_hidden_two * gain_second_b, normed_two, inverse_two)
    mlp_parts = (
        lax.psum_scatter(grad_gain_two, ("seq", "shard"), scatter_dimension=0, tiled=True),
        lax.psum_scatter(grad_shift_two, ("seq", "shard"), scatter_dimension=0, tiled=True),
        lax.psum_scatter(grad_hidden_matrix, ("seq", "shard"), scatter_dimension=0, tiled=True),
        lax.psum_scatter(grad_hidden_shift, ("seq", "shard"), scatter_dimension=0, tiled=True),
        lax.psum_scatter(grad_output_matrix, ("seq", "shard"), scatter_dimension=0, tiled=True),
        lax.psum_scatter(grad_output_shift, ("seq", "shard"), scatter_dimension=0, tiled=True),
    )
    attn_back = (
        lax.all_gather(halves[0], ("seq", "shard"), axis=0, tiled=True),
        lax.all_gather(halves[1], ("seq", "shard"), axis=0, tiled=True),
        lax.all_gather(halves[2], ("seq", "shard"), axis=0, tiled=True),
        lax.all_gather(halves[3], ("seq", "shard"), axis=0, tiled=True),
        lax.all_gather(halves[4], ("seq", "shard"), axis=0, tiled=True),
        lax.all_gather(halves[5], ("seq", "shard"), axis=0, tiled=True),
        lax.all_gather(halves[6], ("seq", "shard"), axis=0, tiled=True),
    )
    gain_first_b = attn_back[0].astype(fp32)
    qkv_matrix_b = attn_back[2]
    attn_matrix_b = attn_back[5]
    grad_mid_low = grad_mid.astype(bf16)
    grad_attn_matrix = jnp.einsum("rd,re->de", attended, grad_mid_low, preferred_element_type=fp32)
    grad_attn_shift = column_sums(grad_mid_low)
    grad_attended = jnp.einsum(
        "re,de->rd", grad_mid_low, attn_matrix_b, preferred_element_type=fp32
    )
    grad_attended = grad_attended.astype(bf16).reshape(seqs_here, block_len, head_count, HEAD_DIM)
    again_probs = jnp.exp(scores_of(queries) - log_total)
    again_low = again_probs.astype(bf16)
    grad_probs = jnp.einsum(
        "sqhd,skhd->shqk", grad_attended, values_all, preferred_element_type=fp32
    )
    grad_values_all = jnp.einsum(
        "shqk,sqhd->skhd", again_low, grad_attended, preferred_element_type=fp32
    )
    inner_sum = jnp.sum(again_probs * grad_probs, axis=-1, keepdims=True)
    grad_scores = (again_probs * (grad_probs - inner_sum)).astype(bf16)
    grad_queries = (
        jnp.einsum("shqk,skhd->sqhd", grad_scores, keys_all, preferred_element_type=fp32) * scaling
    )
    grad_keys_all = (
        jnp.einsum("shqk,sqhd->skhd", grad_scores, queries, preferred_element_type=fp32) * scaling
    )
    grad_keys, grad_values = (
        lax.psum_scatter(
            grad_keys_all.reshape(seqs_here, full_len, model_width).astype(jnp.bfloat16),
            "seq",
            scatter_dimension=1,
            tiled=True,
        ).astype(jnp.float32),
        lax.psum_scatter(
            grad_values_all.reshape(seqs_here, full_len, model_width).astype(jnp.bfloat16),
            "seq",
            scatter_dimension=1,
            tiled=True,
        ).astype(jnp.float32),
    )
    query_low = grad_queries.reshape(total_rows, model_width).astype(bf16)
    key_low = grad_keys.reshape(total_rows, model_width).astype(bf16)
    value_low = grad_values.reshape(total_rows, model_width).astype(bf16)
    grad_qkv = jnp.concatenate([query_low, key_low, value_low], axis=1)
    grad_qkv_matrix = jnp.einsum("rd,re->de", hidden_in, grad_qkv, preferred_element_type=fp32)
    grad_query_shift = column_sums(query_low)
    grad_value_shift = column_sums(value_low)
    grad_hidden_in = jnp.einsum("re,de->rd", grad_qkv, qkv_matrix_b, preferred_element_type=fp32)
    grad_gain_one = jnp.sum(grad_hidden_in * normed_one, axis=0)
    grad_shift_one = jnp.sum(grad_hidden_in, axis=0)
    grad_input_rows = grad_mid + norm_back(grad_hidden_in * gain_first_b, normed_one, inverse_one)
    grad_input_out = grad_input_rows.reshape(seqs_here, block_len, model_width)
    attn_parts = (
        lax.psum_scatter(grad_gain_one, ("seq", "shard"), scatter_dimension=0, tiled=True),
        lax.psum_scatter(grad_shift_one, ("seq", "shard"), scatter_dimension=0, tiled=True),
        lax.psum_scatter(grad_qkv_matrix, ("seq", "shard"), scatter_dimension=0, tiled=True),
        lax.psum_scatter(grad_query_shift, ("seq", "shard"), scatter_dimension=0, tiled=True),
        lax.psum_scatter(grad_value_shift, ("seq", "shard"), scatter_dimension=0, tiled=True),
        lax.psum_scatter(grad_attn_matrix, ("seq", "shard"), scatter_dimension=0, tiled=True),
        lax.psum_scatter(grad_attn_shift, ("seq", "shard"), scatter_dimension=0, tiled=True),
    )
    finals = (
        lax.psum(attn_parts[0].astype(jnp.bfloat16), "replica").astype(jnp.float32),
        lax.psum(attn_parts[1].astype(jnp.bfloat16), "replica").astype(jnp.float32),
        lax.psum(attn_parts[2].astype(jnp.bfloat16), "replica").astype(jnp.float32),
        lax.psum(attn_parts[3].astype(jnp.bfloat16), "replica").astype(jnp.float32),
        lax.psum(attn_parts[4].astype(jnp.bfloat16), "replica").astype(jnp.float32),
        lax.psum(attn_parts[5].astype(jnp.bfloat16), "replica").astype(jnp.float32),
        lax.psum(attn_parts[6].astype(jnp.bfloat16), "replica").astype(jnp.float32),
        lax.psum(mlp_parts[0].astype(jnp.bfloat16), "replica").astype(jnp.float32),
        lax.psum(mlp_parts[1].astype(jnp.bfloat16), "replica").astype(jnp.float32),
        lax.psum(mlp_parts[2].astype(jnp.bfloat16), "replica").astype(jnp.float32),
        lax.psum(mlp_parts[3].astype(jnp.bfloat16), "replica").astype(jnp.float32),
        lax.psum(mlp_parts[4].astype(jnp.bfloat16), "replica").astype(jnp.float32),
        lax.psum(mlp_parts[5].astype(jnp.bfloat16), "replica").astype(jnp.float32),
    )
    return (
        layer_out,
        grad_input_out,
        finals[0],
        finals[1],
        finals[2],
        finals[3],
        finals[4],
        finals[5],
        finals[6],
        finals[7],
        finals[8],
        finals[9],
        finals[10],
        finals[11],
        finals[12],
    )


def solution(mesh):
    in_specs = (
        P(("shard", "replica"), "seq", None),
        P(("shard", "replica"), "seq", None),
        P(("seq", "shard")),
        P(("seq", "shard")),
        P(("seq", "shard"), None),
        P(("seq", "shard")),
        P(("seq", "shard")),
        P(("seq", "shard"), None),
        P(("seq", "shard")),
        P(("seq", "shard")),
        P(("seq", "shard")),
        P(("seq", "shard"), None),
        P(("seq", "shard")),
        P(("seq", "shard"), None),
        P(("seq", "shard")),
    )
    out_specs = (
        P(("shard", "replica"), "seq", None),
        P(("shard", "replica"), "seq", None),
        P(("seq", "shard")),
        P(("seq", "shard")),
        P(("seq", "shard"), None),
        P(("seq", "shard")),
        P(("seq", "shard")),
        P(("seq", "shard"), None),
        P(("seq", "shard")),
        P(("seq", "shard")),
        P(("seq", "shard")),
        P(("seq", "shard"), None),
        P(("seq", "shard")),
        P(("seq", "shard"), None),
        P(("seq", "shard")),
    )
    return jax.shard_map(
        on_device, mesh=mesh, in_specs=in_specs, out_specs=out_specs, check_vma=False
    )
```

profile of v0, /device:TPU:0, one launch (start us, length us, event | category | flops | bytes accessed | tf_op | source)
XLA Modules:
  0.0 2931.8 jit_solution(11084785345381010854)
XLA Ops:
  7.2 3.3 convert_element_type.292
  11.3 33.7 %all-gather.5 = bf16[16,1,128]{2,1,0:T(2,128)(2,1)S(1)} all-gather(bf16[1,1,128]{2,1,0:T(2,128)(2,1)S(1)} %convert_bitcast_fusion.5), channel_id=1, replica_groups=mesh['seq'=4,'shard'=4,'replica'=2] {'seq','shard'}, dimensions={0}, use_global_device_ids=true | all-gather | bytes 4352 | tf_op jit(solution)/shard_map/all_gather | solution.py:75
  45.6 28.3 all-gather.4
  74.6 30.5 %all-gather.3 = bf16[16,1,128]{2,1,0:T(2,128)(2,1)S(1)} all-gather(bf16[1,1,128]{2,1,0:T(2,128)(2,1)S(1)} %convert_bitcast_fusion.7), channel_id=1, replica_groups=mesh['seq'=4,'shard'=4,'replica'=2] {'seq','shard'}, dimensions={0}, use_global_device_ids=true | all-gather | bytes 4352 | tf_op jit(solution)/shard_map/all_gather | solution.py:72
  105.8 28.3 all-gather.2
  134.2 1.5 convert_reduce_fusion.2
  135.7 1.7 fusion.49
  137.4 12.5 all-gather.18.cloned.1.call-done
  149.9 11.8 fusion.21
  161.7 1.5 fusion.72
  163.3 0.7 all-gather.26.cloned.1.call-update
  164.1 0.9 convert_element_type.303
  165.1 3.8 convert_element_type.311
  168.9 4.3 convert_element_type.315
  173.3 30.8 %all-gather.8 = bf16[16,1,128]{2,1,0:T(2,128)(2,1)S(1)} all-gather(bf16[1,1,128]{2,1,0:T(2,128)(2,1)S(1)} %convert_bitcast_fusion.2), channel_id=1, replica_groups=mesh['seq'=4,'shard'=4,'replica'=2] {'seq','shard'}, dimensions={0}, use_global_device_ids=true | all-gather | bytes 4352 | tf_op jit(solution)/shard_map/all_gather | solution.py:123
  204.2 28.3 all-gather.7
  232.5 30.7 %all-gather.6 = bf16[16,1,128]{2,1,0:T(2,128)(2,1)S(1)} all-gather(bf16[1,1,128]{2,1,0:T(2,128)(2,1)S(1)} %convert_bitcast_fusion.4), channel_id=1, replica_groups=mesh['seq'=4,'shard'=4,'replica'=2] {'seq','shard'}, dimensions={0}, use_global_device_ids=true | all-gather | bytes 4352 | tf_op jit(solution)/shard_map/all_gather | solution.py:77
  263.2 29.7 %all-gather.9 = bf16[16,1,512]{2,1,0:T(2,128)(2,1)S(1)} all-gather(bf16[1,1,512]{2,1,0:T(2,128)(2,1)S(1)} %reshape.253), channel_id=1, replica_groups=mesh['seq'=4,'shard'=4,'replica'=2] {'seq','shard'}, dimensions={0}, use_global_device_ids=true | all-gather | bytes 17408 | tf_op jit(solution)/shard_map/all_gather | solution.py:125
  293.5 6.6 copy.47
  300.1 4.8 fusion.73
  304.9 5.8 copy-done
  310.7 3.8 fusion
  314.6 11.1 fusion.50
  325.7 6.3 fusion.74
  332.5 158.1 %all-gather.22.cloned.1.call-done = bf16[2048,8192]{1,0:T(8,128)(2,1)} async-done(((bf16[128,8192]{1,0:T(8,128)(2,1)}), bf16[2048,8192]{1,0:T(8,128)(2,1)}) %all-gather.22.cloned.1.call-update) | async-done | bytes 33554448 | tf_op jit(solution)/shard_map/all_gather | solution.py:124
  490.6 17.8 convolution_add_fusion
  508.4 162.1 %all-gather.24.cloned.1.call-done = bf16[8192,2048]{1,0:T(8,128)(2,1)} async-done(((bf16[512,2048]{1,0:T(8,128)(2,1)}), bf16[8192,2048]{1,0:T(8,128)(2,1)}) %all-gather.24.cloned.1.call-update) | async-done | bytes 33554448 | tf_op jit(solution)/shard_map/all_gather | solution.py:126
  670.5 20.7 convert_reduce_fusion
  691.2 18.3 multiply_reduce_fusion.1
  709.6 3.6 convert_reduce_fusion.3
  713.2 1.3 copy-done.8
  714.5 5.7 convolution_convert_fusion
  720.8 8.7 fusion.27
  729.6 13.8 multiply_reduce_fusion
  743.4 12.5 multiply_convert_fusion
  756.0 3.5 multiply_convert_fusion.1
  759.5 1.3 copy-done.1
  760.9 9.4 fusion.64
  770.4 8.3 convert_reduce_fusion.5
  778.7 42.7 %reduce-scatter.7.cloned.1.call-done = bf16[1,256,2048]{1,2,0:T(8,128)(2,1)} async-done(((bf16[1,1024,2048]{1,2,0:T(8,128)(2,1)}), bf16[1,256,2048]{1,2,0:T(8,128)(2,1)}) %reduce-scatter.7.cloned.1.call-update) | async-done | bytes 1048592 | tf_op jit(solution)/shard_map/reduce_scatter | solution.py:209
  821.4 25.5 fusion.53
  847.0 1.3 copy-done.17
  848.3 34.7 %fusion.55 = f32[8192,2048]{1,0:T(8,128)} fusion(bf16[1,256,2048]{2,1,0:T(8,128)(2,1)S(1)} %copy-done.17, f32[256,8192]{1,0:T(8,128)} %convolution_add_fusion), kind=kOutput, calls=%fused_computation.90 | convolution fusion | flops 8726249472 | bytes 76546048 | tf_op jit(solution)/shard_map/rf,rd->fd/dot_general | solution.py:153
  883.2 1.6 copy-done.3
  884.7 26.6 fusion.69
  913.9 30.6 %all-gather.10 = bf16[16,1,128]{2,1,0:T(2,128)(2,1)S(1)} all-gather(bf16[1,1,128]{2,1,0:T(2,128)(2,1)S(1)} %convert_bitcast_fusion.1), channel_id=1, replica_groups=mesh['seq'=4,'shard'=4,'replica'=2] {'seq','shard'}, dimensions={0}, use_global_device_ids=true | all-gather | bytes 4352 | tf_op jit(solution)/shard_map/all_gather | solution.py:127
  944.4 59.6 %reduce-scatter.13.cloned.1.call-done = f32[128,2048]{1,0:T(8,128)} async-done(((f32[2048,2048]{1,0:T(8,128)}), f32[128,2048]{1,0:T(8,128)}) %reduce-scatter.13.cloned.1.call-update) | async-done | bytes 1048592 | tf_op jit(solution)/shard_map/reduce_scatter | solution.py:240
  1004.1 2.1 convert_element_type.351
  1006.2 468.8 %reduce-scatter.11.cloned.1.call-done = f32[128,6144]{1,0:T(8,128)} async-done(((f32[2048,6144]{1,0:T(8,128)}), f32[128,6144]{1,0:T(8,128)}) %reduce-scatter.11.cloned.1.call-update) | async-done | bytes 3145744 | tf_op jit(solution)/shard_map/reduce_scatter | solution.py:237
  1475.0 3.2 convert_element_type.343
  1478.2 636.8 %reduce-scatter.17.cloned.1.call-done = f32[512,2048]{1,0:T(8,128)} async-done(((f32[8192,2048]{1,0:T(8,128)}), f32[512,2048]{1,0:T(8,128)}) %reduce-scatter.17.cloned.1.call-update) | async-done | bytes 4194320 | tf_op jit(solution)/shard_map/reduce_scatter | solution.py:170
  2115.1 3.8 convert_element_type.365
  2118.9 636.2 %reduce-scatter.15.cloned.1.call-done = f32[128,8192]{1,0:T(8,128)} async-done(((f32[2048,8192]{1,0:T(8,128)}), f32[128,8192]{1,0:T(8,128)}) %reduce-scatter.15.cloned.1.call-update) | async-done | bytes 4194320 | tf_op jit(solution)/shard_map/reduce_scatter | solution.py:168
  2755.1 3.8 convert_element_type.360
  2759.0 31.5 %fusion.40 = bf16[1,256,2048]{2,1,0:T(8,128)(2,1)} fusion(f32[256,2048]{1,0:T(8,128)S(1)} %copy-done.3, bf16[8192,2048]{1,0:T(8,128)(2,1)} %all-gather.24.cloned.1.call-done, f32[2048]{0:T(1024)S(1)} %bitcast.174, f32[256,8192]{1,0:T(8,128)} %convolution_add_fusion), kind=kOutput, calls=%fused_computation.66 | convolution fusion | flops 8727822336 | bytes 45096960 | tf_op jit(solution)/shard_map/dot_general | solution.py:137
  2791.0 14.0 fusion.48
  2805.0 61.7 %all-reduce.9 = (bf16[2048]{0:T(1024)(128)(2,1)S(1)}, bf16[2048]{0:T(1024)(128)(2,1)S(1)}, bf16[2048]{0:T(1024)(128)(2,1)S(1)}, bf16[2048]{0:T(1024)(128)(2,1)S(...) all-reduce(f32[2048]{0:T(1024)S(1)} %get-tuple-element.17, ...), channel_id=6, replica_groups=mesh['seq'=4,'shard'=4,'replica'=2] {'seq','shard'}, use_global_device_ids=true, to_apply=%region_14.15.clone | all-reduce | flops 24576 | bytes 147456
  2867.4 5.1 all-reduce.10
  2877.2 3.7 fusion.47
  2880.9 31.7 %all-reduce.14.cloned.1.call-done = (bf16[128,6144]{1,0:T(8,128)(2,1)}, bf16[128,2048]{1,0:T(8,128)(2,1)}, bf16[128,8192]{1,0:T(8,128)(2,1)}, bf16[512,2048]{1,0:T(8,128)(2,1)}) async-done(((bf16[128,6144]{1,0:T(8,128)(2,1)}, bf16[128,2048]{1,0:T(8,128)(2,1)}, bf16[128,8192]{1,0:T(8,128)(2,1)}, bf16[512,2048]{1,0:T(8,128)(2,1)}), (bf16[128,6144]{1,0:T(8,128)(2,1)}, bf16[128,2048]{1,0:T(8,128)(2,1)}, ...) | async-done | bytes 6291472 | tf_op jit(solution)/shard_map/psum | solution.py:246
  2912.6 2.3 convert_element_type.352
  2914.9 3.4 convert_element_type.344
  2918.3 4.0 convert_element_type.361
  2922.3 2.5 convert_element_type.366
  (175 shorter events, 12.1 us)
Async XLA Ops:
  7.2 142.7 %copy-start.4 = (bf16[1,256,2048]{2,1,0:T(8,128)(2,1)S(1)}, bf16[1,256,2048]{2,1,0:T(8,128)(2,1)}, u32[]{:S(2)}) copy-start(bf16[1,256,2048]{2,1,0:T(8,128)(2,1)} %param.15) | copy-start | bytes 3145732
  7.2 142.7 %all-gather.18.cloned.1.call-start = ((), (), s32[]{:S(2)}) async-start(), calls=%async_computation.6 | async-start | bytes 26738688 | tf_op jit(solution)/shard_map/all_gather | solution.py:73
  10.6 282.9 %all-gather.28.cloned.1.call-start = ((), (), s32[]{:S(2)}) async-start(), calls=%async_computation.17 | async-start | bytes 5242880 | tf_op jit(solution)/shard_map/all_gather | solution.py:93
  105.2 44.7 %copy-start.21 = (f32[16,1,128]{2,1,0:T(1,128)}, f32[16,1,128]{2,1,0:T(1,128)S(1)}, u32[]{:S(2)}) copy-start(f32[16,1,128]{2,1,0:T(1,128)S(1)} %convert_element_type.370) | copy-start | bytes 24580
  134.2 15.7 copy-start.18
  135.7 14.2 copy-start.27
  137.3 12.5 copy-start.30
  161.7 2.4 copy-start.16
  163.3 151.3 %all-gather.26.cloned.1.call-start = ((), (), s32[]{:S(2)}) async-start(), calls=%async_computation.16 | async-start | bytes 5242880 | tf_op jit(solution)/shard_map/all_gather | solution.py:94
  164.0 161.7 %all-gather.20.cloned.1.call-start = ((), (), s32[]{:S(2)}) async-start(), calls=%async_computation.7 | async-start | bytes 8912896 | tf_op jit(solution)/shard_map/all_gather | solution.py:76
  165.0 8.3 copy-start.43
  165.0 8.3 copy-start.44
  165.0 39.1 %copy-start.45 = (f32[128]{0:T(128)S(1)}, f32[128]{0:T(128)}, u32[]{:S(2)}) copy-start(f32[128]{0:T(128)} %param.24) | copy-start | bytes 1540
  165.0 67.5 %copy-start.46 = (f32[128]{0:T(128)S(1)}, f32[128]{0:T(128)}, u32[]{:S(2)}) copy-start(f32[128]{0:T(128)} %param.23) | copy-start | bytes 1540
  165.0 325.6 %all-gather.22.cloned.1.call-start = ((), (), s32[]{:S(2)}) async-start(), calls=%async_computation.8 | async-start | bytes 35651584 | tf_op jit(solution)/shard_map/all_gather | solution.py:124
  168.8 501.7 %all-gather.24.cloned.1.call-start = ((), (), s32[]{:S(2)}) async-start(), calls=%async_computation.9 | async-start | bytes 35651584 | tf_op jit(solution)/shard_map/all_gather | solution.py:126
  173.2 605.5 %reduce-scatter.9.cloned.1.call-start = ((), (), s32[]{:S(2)}) async-start(), calls=%async_computation.11 | async-start | bytes 5242880 | tf_op jit(solution)/shard_map/reduce_scatter | solution.py:215
  204.1 286.5 %copy-start.25 = (f32[16,1,128]{2,1,0:T(1,128)}, f32[16,1,128]{2,1,0:T(1,128)S(1)}, u32[]{:S(2)}) copy-start(f32[16,1,128]{2,1,0:T(1,128)S(1)} %convert_element_type.375) | copy-start | bytes 24580
  232.5 477.1 %copy-start.23 = (f32[16,1,128]{2,1,0:T(1,128)}, f32[16,1,128]{2,1,0:T(1,128)S(1)}, u32[]{:S(2)}) copy-start(f32[16,1,128]{2,1,0:T(1,128)S(1)} %convert_element_type.374) | copy-start | bytes 24580
  293.5 11.4 copy-start.6
  304.9 5.8 copy-start
  332.1 377.5 %copy-start.2 = (f32[256,2048]{1,0:T(8,128)}, f32[256,2048]{1,0:T(8,128)S(1)}, u32[]{:S(2)}) copy-start(f32[256,2048]{1,0:T(8,128)S(1)} %get-tuple-element.54) | copy-start | bytes 6291460
  332.1 377.5 %copy-start.33 = (f32[256]{0:T(256)}, f32[256]{0:T(256)S(1)}, u32[]{:S(2)}) copy-start(f32[256]{0:T(256)S(1)} %broadcast_multiply_fusion.4) | copy-start | bytes 3076
  332.5 377.1 %copy-start.35 = (f32[256]{0:T(256)}, f32[256]{0:T(256)S(1)}, u32[]{:S(2)}) copy-start(f32[256]{0:T(256)S(1)} %add_rsqrt_fusion) | copy-start | bytes 3076
  713.2 1.3 copy-start.8
  729.6 91.8 %reduce-scatter.7.cloned.1.call-start = ((), (), s32[]{:S(2)}) async-start(), calls=%async_computation.10 | async-start | bytes 5242880 | tf_op jit(solution)/shard_map/reduce_scatter | solution.py:209
  743.4 12.6 copy-start.7
  756.0 4.8 copy-start.1
  756.0 4.9 copy-start.9
  760.8 243.3 %reduce-scatter.13.cloned.1.call-start = ((), (), s32[]{:S(2)}) async-start(), calls=%async_computation.13 | async-start | bytes 17825792 | tf_op jit(solution)/shard_map/reduce_scatter | solution.py:240
  770.3 51.1 %copy-start.19 = (f32[16,1,128]{2,1,0:T(1,128)S(1)}, f32[16,1,128]{2,1,0:T(1,128)}, u32[]{:S(2)}) copy-start(f32[16,1,128]{2,1,0:T(1,128)} %copy-done.18) | copy-start | bytes 24580
  770.3 51.1 %copy-start.22 = (f32[16,1,128]{2,1,0:T(1,128)S(1)}, f32[16,1,128]{2,1,0:T(1,128)}, u32[]{:S(2)}) copy-start(f32[16,1,128]{2,1,0:T(1,128)} %copy-done.21) | copy-start | bytes 24580
  770.3 51.1 %copy-start.28 = (f32[256]{0:T(256)S(1)}, f32[256]{0:T(256)}, u32[]{:S(2)}) copy-start(f32[256]{0:T(256)} %copy-done.27) | copy-start | bytes 3076
  770.3 51.1 %copy-start.31 = (f32[256]{0:T(256)S(1)}, f32[256]{0:T(256)}, u32[]{:S(2)}) copy-start(f32[256]{0:T(256)} %copy-done.30) | copy-start | bytes 3076
  770.3 704.7 %reduce-scatter.11.cloned.1.call-start = ((), (), s32[]{:S(2)}) async-start(), calls=%async_computation.12 | async-start | bytes 53477376 | tf_op jit(solution)/shard_map/reduce_scatter | solution.py:237
  778.7 68.2 %copy-start.11 = (bf16[16,128,256]{2,1,0:T(8,128)(2,1)}, bf16[16,128,256]{2,1,0:T(8,128)(2,1)S(1)}, u32[]{:S(2)}) copy-start(bf16[16,128,256]{2,1,0:T(8,128)(2,1)S(1)} %get-tuple-element.60) | copy-start | bytes 3145732
  846.9 1.4 copy-start.17
  846.9 1268.2 %reduce-scatter.17.cloned.1.call-start = ((), (), s32[]{:S(2)}) async-start(), calls=%async_computation.15 | async-start | bytes 71303168 | tf_op jit(solution)/shard_map/reduce_scatter | solution.py:170
  883.1 1.7 copy-start.3
  883.1 1.7 copy-start.24
  883.1 1.7 copy-start.26
  883.1 1.7 copy-start.34
  883.1 1.7 copy-start.36
  883.1 1872.0 %reduce-scatter.15.cloned.1.call-start = ((), (), s32[]{:S(2)}) async-start(), calls=%async_computation.14 | async-start | bytes 71303168 | tf_op jit(solution)/shard_map/reduce_scatter | solution.py:168
  911.3 0.7 copy-start.48
  911.3 2.5 copy-start.47
  911.3 2001.3 %all-reduce.14.cloned.1.call-start = ((), (), s32[]{:S(2)}) async-start(), calls=%async_computation.18 | async-start | bytes 12582912 | tf_op jit(solution)/shard_map/psum | solution.py:246
  2758.9 31.6 %copy-start.13 = (bf16[1,256,2048]{1,2,0:T(8,128)(2,1)S(1)}, bf16[1,256,2048]{1,2,0:T(8,128)(2,1)}, u32[]{:S(2)}) copy-start(bf16[1,256,2048]{1,2,0:T(8,128)(2,1)} %reduce-scatter.9.cloned.1.call-done) | copy-start | bytes 3145732
  2758.9 31.9 %copy-start.5 = (bf16[1,256,2048]{2,1,0:T(8,128)(2,1)S(1)}, bf16[1,256,2048]{2,1,0:T(8,128)(2,1)}, u32[]{:S(2)}) copy-start(bf16[1,256,2048]{2,1,0:T(8,128)(2,1)} %param.15) | copy-start | bytes 3145732
  2758.9 31.9 %copy-start.12 = (bf16[16,128,256]{2,1,0:T(8,128)(2,1)S(1)}, bf16[16,128,256]{2,1,0:T(8,128)(2,1)}, u32[]{:S(2)}) copy-start(bf16[16,128,256]{2,1,0:T(8,128)(2,1)} %copy-done.11) | copy-start | bytes 3145732
  2758.9 31.9 %copy-start.15 = (bf16[1,256,2048]{1,2,0:T(8,128)(2,1)S(1)}, bf16[1,256,2048]{1,2,0:T(8,128)(2,1)}, u32[]{:S(2)}) copy-start(bf16[1,256,2048]{1,2,0:T(8,128)(2,1)} %reduce-scatter.7.cloned.1.call-done) | copy-start | bytes 3145732
  2759.0 31.9 %copy-start.20 = (f32[16,1,128]{2,1,0:T(1,128)S(1)}, f32[16,1,128]{2,1,0:T(1,128)}, u32[]{:S(2)}) copy-start(f32[16,1,128]{2,1,0:T(1,128)} %copy-done.18) | copy-start | bytes 24580
  2759.0 31.9 %copy-start.29 = (f32[256]{0:T(256)S(1)}, f32[256]{0:T(256)}, u32[]{:S(2)}) copy-start(f32[256]{0:T(256)} %copy-done.27) | copy-start | bytes 3076
  2759.0 31.9 %copy-start.32 = (f32[256]{0:T(256)S(1)}, f32[256]{0:T(256)}, u32[]{:S(2)}) copy-start(f32[256]{0:T(256)} %copy-done.30) | copy-start | bytes 3076
  2790.9 14.0 copy-start.37
  2790.9 14.0 copy-start.38
  2790.9 14.0 copy-start.39
  2791.0 14.0 copy-start.40
  2791.0 14.0 copy-start.41
  2791.0 14.0 copy-start.42
  2791.0 86.3 %copy-start.10 = (f32[256,2048]{1,0:T(8,128)S(1)}, f32[256,2048]{1,0:T(8,128)}, u32[]{:S(2)}) copy-start(f32[256,2048]{1,0:T(8,128)} %copy-done.8) | copy-start | bytes 6291460
  2912.6 9.7 copy-start.14
Sparse Core Ops, SparseCore 0:
  10.7 139.1 all-gather.17
  163.4 34.4 all-gather.27
  200.0 34.5 all-gather.25
  237.2 74.9 all-gather.19
  314.2 176.3 all-gather.21
  492.6 177.9 all-gather.23
  729.7 44.4 reduce-scatter.8
  776.9 44.4 reduce-scatter.6
  825.5 178.5 reduce-scatter.12
  1008.2 466.8 reduce-scatter.10
  1479.3 635.7 reduce-scatter.16
  2119.2 635.8 reduce-scatter.14
  2759.0 153.5 all-reduce.13
where the time goes:
time: 2940 us; the launch traced here: 2930 us
  waiting for transfers between devices  2210 us (75%)
  blocking collectives  338 us (11%)
  matrix products  273 us (9%)
  other arithmetic  72.3 us (2%)
    reduce_scatter x1, waiting for transfers between devices, on_device(): lax.psum_scatter(grad_output_matrix, ('seq', 'shard'), scatter_dimension=...  637 us
    reduce_scatter x1, waiting for transfers between devices, on_device(): lax.psum_scatter(grad_hidden_matrix, ('seq', 'shard'), scatter_dimension=...  636 us
    reduce_scatter x1, waiting for transfers between devices, on_device(): lax.psum_scatter(grad_qkv_matrix, ('seq', 'shard'), scatter_dimension=0,...  469 us
    all_gather x1, waiting for transfers between devices, on_device(): lax.all_gather(halves[11], ('seq', 'shard'), axis=0, tiled=True)  162 us
    all_gather x1, waiting for transfers between devices, on_device(): lax.all_gather(halves[9], ('seq', 'shard'), axis=0, tiled=True)  158 us
    unnamed x1, blocking collectives  61.7 us
    reduce_scatter x1, waiting for transfers between devices, on_device(): lax.psum_scatter(grad_attn_matrix, ('seq', 'shard'), scatter_dimension=0,...  59.6 us
  transfers between devices with their start and end apart: 13, of which 9 were waited for; matrix products, arithmetic and copies ran while one was open for 9% of the time, Pallas kernels for 0%

commit v1 on v0

v1 whole, which is shorter than its diff:
```python
import jax
import jax.numpy as jnp
from jax import lax
from jax.experimental import pallas as pl
from jax.experimental.pallas import tpu as pltpu
from jax.sharding import PartitionSpec as P

HEAD_DIM = 128
bf16 = jnp.bfloat16
fp32 = jnp.float32

CORE = ("seq", 1)
ROW = ("seq", 2)
COL = ("replica", 1)


def normalize(values):
    mean_row = jnp.mean(values, axis=1, keepdims=True)
    centred = values - mean_row
    scale_row = lax.rsqrt(jnp.mean(centred * centred, axis=1, keepdims=True) + 1e-05)
    return (centred * scale_row, scale_row)


def norm_back(grad_normed, normed, scale_row):
    first_mean = jnp.mean(grad_normed, axis=1, keepdims=True)
    second_mean = jnp.mean(grad_normed * normed, axis=1, keepdims=True)
    return scale_row * (grad_normed - first_mean - normed * second_mean)


def gelu_slope(values):
    normal_cdf = 0.5 * (1.0 + lax.erf(values * 0.7071067811865476))
    return normal_cdf + values * jnp.exp(-0.5 * values * values) * 0.3989422804014327


def column_sums(values):
    return jnp.sum(values.astype(fp32), axis=0)


def flip(v, link):
    axis, bit = link
    return lax.ppermute(v, axis, [(i, i ^ bit) for i in range(lax.axis_size(axis))])


def hop(v, seq_bits, rep_bit):
    if rep_bit == 0:
        return flip(v, ("seq", seq_bits)) if seq_bits else v
    if seq_bits == 0:
        return flip(v, COL)
    S, R = lax.axis_size("seq"), lax.axis_size("replica")
    pairs = [(s * R + r, (s ^ seq_bits) * R + (r ^ rep_bit)) for s in range(S) for r in range(R)]
    return lax.ppermute(v, ("seq", "replica"), pairs)


def plane_gather(v):
    h = v.shape[0] // 2
    near = flip(v, CORE)
    py, px = flip(v, ROW), flip(v, COL)
    da, db = flip(py[:h], COL), flip(px[h:], ROW)
    cy, cx = flip(py, CORE), flip(px, CORE)
    ca, cb = flip(da, CORE), flip(db, CORE)
    return [jnp.concatenate(p) for p in ([v, near], [py, cy], [px, cx], [da, db, ca, cb])]


def plane_scatter(parts):
    n = parts[0].shape[0] // 2
    h = n // 2
    got = [flip(p[n:], CORE) for p in parts]
    sums = [p[:n].astype(fp32) + g.astype(fp32) for p, g in zip(parts, got)]
    py, px, pd = (v.astype(bf16) for v in sums[1:])
    ra, rb = flip(pd[:h], COL), flip(pd[h:], ROW)
    x_top, y_bot = flip(px[:h], COL), flip(py[h:], ROW)
    x_bot = flip((sums[2][h:] + rb.astype(fp32)).astype(bf16), COL)
    y_top = flip((sums[1][:h] + ra.astype(fp32)).astype(bf16), ROW)
    top = sums[0][:h] + x_top.astype(fp32) + y_top.astype(fp32)
    bot = sums[0][h:] + x_bot.astype(fp32) + y_bot.astype(fp32)
    return jnp.concatenate([top, bot])


def line_gather(v):
    Z, z = lax.axis_size("shard"), lax.axis_index("shard")
    up, down = [v], [v]
    for k in range(1, Z):
        up.append(lax.ppermute(up[-1], "shard", [(i, i + 1) for i in range(k - 1, Z - 1)]))
        down.append(lax.ppermute(down[-1], "shard", [(i, i - 1) for i in range(1, Z - k + 1)]))
    out = jnp.zeros((Z,) + v.shape, v.dtype)
    out = lax.dynamic_update_index_in_dim(out, v, z, 0)
    for k in range(1, Z):
        piece = jnp.where(z >= k, up[k], down[Z - k])
        out = lax.dynamic_update_index_in_dim(out, piece, lax.rem(z - k + Z, Z), 0)
    return out


def line_scatter(v):
    Z, z = lax.axis_size("shard"), lax.axis_index("shard")
    up = down = 0.0
    for k in range(1, Z):
        send_up = lax.dynamic_index_in_dim(v, jnp.minimum(z + Z - k, Z - 1), 0, keepdims=False)
        send_down = lax.dynamic_index_in_dim(v, jnp.maximum(z - (Z - k), 0), 0, keepdims=False)
        if k > 1:
            send_up = send_up.astype(fp32) + up
            send_down = send_down.astype(fp32) + down
        up = lax.ppermute(send_up.astype(bf16), "shard", [(i, i + 1) for i in range(0, k)]).astype(fp32)
        down = lax.ppermute(send_down.astype(bf16), "shard", [(i, i - 1) for i in range(Z - k, Z)]).astype(fp32)
    own = lax.dynamic_index_in_dim(v, z, 0, keepdims=False)
    return own.astype(fp32) + up + down


def in_order(pieces, index):
    bit = 1
    while bit < len(pieces):
        odd = (index & bit) != 0
        pieces = [jnp.where(odd, pieces[j ^ bit], pieces[j]) for j in range(len(pieces))]
        bit *= 2
    return jnp.stack(pieces)


def seq_exchange(v):
    S, s = lax.axis_size("seq"), lax.axis_index("seq")
    got = [hop(lax.dynamic_index_in_dim(v, s ^ j, 0, keepdims=False), j, 0) for j in range(S)]
    return in_order(got, s)


def gather_table(v):
    table = v[None]
    for axis in ("shard", "seq"):
        index, bit = lax.axis_index(axis), 1
        while bit < lax.axis_size(axis):
            other = flip(table, (axis, bit))
            odd = (index & bit) != 0
            table = jnp.concatenate([jnp.where(odd, other, table), jnp.where(odd, table, other)])
            bit *= 2
    return table


def total(v):
    for axis in ("seq", "replica", "shard"):
        bit = 1
        while bit < lax.axis_size(axis):
            v = v + flip(v, (axis, bit))
            bit *= 2
    return v


def attend_kernel(heads, own_ref, qkv_ref, out_ref, k_ref, v_ref):
    own = own_ref[0]
    _, blocks, length, _ = qkv_ref.shape
    width = heads * HEAD_DIM
    for h in range(heads):
        cols = slice(h * HEAD_DIM, (h + 1) * HEAD_DIM)
        for b in range(blocks):
            rows = slice(b * length, (b + 1) * length)
            k_ref[rows, :] = qkv_ref[0, own ^ b, :, width + h * HEAD_DIM : width + (h + 1) * HEAD_DIM]
            v_ref[rows, :] = qkv_ref[0, own ^ b, :, 2 * width + h * HEAD_DIM : 2 * width + (h + 1) * HEAD_DIM]
        for a in range(blocks):
            upto = (a + 1) * length
            q = qkv_ref[0, own ^ a, :, cols]
            scores = lax.dot_general(q, k_ref[:upto, :], (((1,), (1,)), ((), ())), preferred_element_type=fp32)
            scores = scores * HEAD_DIM ** (-0.5)
            expons = jnp.exp(scores - jnp.max(scores, axis=-1, keepdims=True))
            probs = (expons / jnp.sum(expons, axis=-1, keepdims=True)).astype(bf16)
            out_ref[0, own ^ a, :, cols] = jnp.dot(probs, v_ref[:upto, :], preferred_element_type=fp32).astype(bf16)


def attend_back_kernel(heads, own_ref, qkv_ref, grad_ref, out_ref, k_ref, v_ref, gk_ref, gv_ref):
    own = own_ref[0]
    _, blocks, length, _ = qkv_ref.shape
    width = heads * HEAD_DIM
    scaling = HEAD_DIM ** (-0.5)
    across = (((1,), (1,)), ((), ()))
    down = (((0,), (0,)), ((), ()))
    for h in range(heads):
        cols = slice(h * HEAD_DIM, (h + 1) * HEAD_DIM)
        k_cols = slice(width + h * HEAD_DIM, width + (h + 1) * HEAD_DIM)
        v_cols = slice(2 * width + h * HEAD_DIM, 2 * width + (h + 1) * HEAD_DIM)
        for b in range(blocks):
            rows = slice(b * length, (b + 1) * length)
            k_ref[rows, :] = qkv_ref[0, own ^ b, :, k_cols]
            v_ref[rows, :] = qkv_ref[0, own ^ b, :, v_cols]
        for a in reversed(range(blocks)):
            upto = (a + 1) * length
            q = qkv_ref[0, own ^ a, :, cols]
            g = grad_ref[0, own ^ a, :, cols]
            k = k_ref[:upto, :]
            v = v_ref[:upto, :]
            scores = lax.dot_general(q, k, across, preferred_element_type=fp32) * scaling
            expons = jnp.exp(scores - jnp.max(scores, axis=-1, keepdims=True))
            probs = expons / jnp.sum(expons, axis=-1, keepdims=True)
            grad_probs = lax.dot_general(g, v, across, preferred_element_type=fp32)
            inner = jnp.sum(probs * grad_probs, axis=-1, keepdims=True)
            grad_scores = (probs * (grad_probs - inner)).astype(bf16)
            gq = jnp.dot(grad_scores, k, preferred_element_type=fp32) * scaling
            out_ref[0, own ^ a, :, cols] = gq.astype(bf16)
            gk = lax.dot_general(grad_scores, q, down, preferred_element_type=fp32)
            gv = lax.dot_general(probs.astype(bf16), g, down, preferred_element_type=fp32)
            if a == blocks - 1:
                gk_ref[...] = gk
                gv_ref[...] = gv
            else:
                gk_ref[:upto, :] += gk
                gv_ref[:upto, :] += gv
        for b in range(blocks):
            rows = slice(b * length, (b + 1) * length)
            out_ref[0, own ^ b, :, k_cols] = (gk_ref[rows, :] * scaling).astype(bf16)
            out_ref[0, own ^ b, :, v_cols] = gv_ref[rows, :].astype(bf16)


def attention_call(kernel, own, operands, out_width, scratch, flops):
    seqs, blocks, length, _ = operands[0].shape

    def block(width):
        return pl.BlockSpec((1, blocks, length, width), lambda i, own_ref: (i, 0, 0, 0))

    return pl.pallas_call(
        kernel,
        out_shape=jax.ShapeDtypeStruct((seqs, blocks, length, out_width), bf16),
        grid_spec=pltpu.PrefetchScalarGridSpec(
            num_scalar_prefetch=1,
            grid=(seqs,),
            in_specs=[block(v.shape[-1]) for v in operands],
            out_specs=block(out_width),
            scratch_shapes=[pltpu.VMEM((blocks * length, HEAD_DIM), kind) for kind in scratch],
        ),
        compiler_params=pltpu.CompilerParams(vmem_limit_bytes=40 * 2**20),
        cost_estimate=pl.CostEstimate(flops=flops, bytes_accessed=sum(v.size * 2 for v in operands), transcendentals=0),
    )(own.reshape(1), *operands)


def on_device(
    inputs,
    cotangent,
    norm1_gain,
    norm1_bias,
    w_qkv,
    query_bias,
    value_bias,
    w_attn_out,
    attn_out_bias,
    norm2_gain,
    norm2_bias,
    w_hidden,
    hidden_bias,
    w_output,
    output_bias,
):
    S, Z, R = lax.axis_size("seq"), lax.axis_size("shard"), lax.axis_size("replica")
    s, z, r = lax.axis_index("seq"), lax.axis_index("shard"), lax.axis_index("replica")
    odd = r != 0
    _, n, D = inputs.shape
    rows = norm1_gain.shape[0]
    F = hidden_bias.shape[0] * S * Z
    T = S * R
    hw = D // T
    fw = F // T
    fr = fw // Z
    heads = hw // HEAD_DIM

    def by_shard(v):
        return v.reshape(-1, S, Z, rows).swapaxes(1, 2).reshape(-1, D)

    def by_seq(v):
        return v.reshape(-1, Z, S, rows).swapaxes(1, 2).reshape(-1, D)

    small = (norm1_gain, norm1_bias, query_bias, value_bias, attn_out_bias, norm2_gain, norm2_bias, output_bias, hidden_bias)
    table = gather_table(jnp.concatenate([v.astype(bf16) for v in small])).astype(fp32)
    gain_one, shift_one, query_shift, value_shift, attn_shift, gain_two, shift_two, output_shift = (
        table[:, i * rows : (i + 1) * rows].reshape(D) for i in range(8)
    )
    hidden_shift = lax.dynamic_index_in_dim(
        lax.dynamic_index_in_dim(table[:, 8 * rows :].reshape(S, Z, R, fr), s, 0, keepdims=False), r, 1, keepdims=False
    ).reshape(fw)

    t = s * R + r
    qkv_pieces = lax.dynamic_index_in_dim(w_qkv.astype(bf16).reshape(rows, 3, S, R, hw), r, 3, keepdims=False)
    qkv_matrix = seq_exchange(qkv_pieces.transpose(2, 0, 1, 3).reshape(S, rows, 3 * hw))
    qkv_matrix = line_gather(qkv_matrix.reshape(S * rows, 3 * hw)).reshape(D, 3 * hw)
    attn_part = lax.dynamic_index_in_dim(w_attn_out.astype(bf16).reshape(rows, R, D // R), r, 1, keepdims=False)
    attn_part = plane_gather(line_gather(attn_part).reshape(D // S, D // R))
    attn_matrix = jnp.concatenate([jnp.concatenate(attn_part[:2]), jnp.concatenate(attn_part[2:])], axis=1)
    hidden_pieces = lax.dynamic_index_in_dim(w_hidden.astype(bf16).reshape(rows, S, Z, R, fr), r, 3, keepdims=False)
    hidden_matrix = seq_exchange(hidden_pieces.transpose(1, 0, 2, 3).reshape(S, rows, fw))
    hidden_matrix = line_gather(hidden_matrix.reshape(S * rows, fw)).reshape(D, fw)
    output_part = lax.dynamic_index_in_dim(w_output.astype(bf16).reshape(R, fr, D), r, 0, keepdims=False)
    output_matrix = line_gather(output_part).reshape(fw, D)

    flat_in = inputs.reshape(n, D).astype(fp32)
    normed_one, inverse_one = normalize(flat_in)
    hidden_in = (normed_one * gain_one + shift_one).astype(bf16)
    hidden_in_parts = plane_gather(by_shard(hidden_in))
    grad_low = cotangent.reshape(n, D)
    grad_low_parts = plane_gather(grad_low)
    bias_row = jnp.concatenate(
        [
            lax.dynamic_slice_in_dim(query_shift, t * hw, hw),
            jnp.zeros((hw,), fp32),
            lax.dynamic_slice_in_dim(value_shift, t * hw, hw),
        ]
    )
    qkv_parts = [
        (jnp.dot(v, qkv_matrix, preferred_element_type=fp32) + bias_row).astype(bf16) for v in hidden_in_parts
    ]
    qkv = jnp.concatenate(qkv_parts).reshape(R, S, n, 3 * hw)
    half_pairs = R * heads * (S * (S + 1) // 2) * n * n * HEAD_DIM * 2
    attended_heads = attention_call(
        lambda *refs: attend_kernel(heads, *refs), s, (qkv,), hw, (bf16, bf16), 2 * half_pairs
    )
    att = [[hop(attended_heads[jr, js], js, jr) for jr in range(R)] for js in range(S)]
    attended = jnp.concatenate(
        [jnp.where(odd, att[js][1 - i], att[js][i]) for js in range(S) for i in range(R)], axis=1
    )

    def swap_halves(v):
        first, second = v[:, : D // R], v[:, D // R :]
        return jnp.concatenate([jnp.where(odd, second, first), jnp.where(odd, first, second)], axis=1)

    mid_rows = flat_in + (
        swap_halves(jnp.dot(attended, attn_matrix, preferred_element_type=fp32)) + attn_shift
    )

    normed_two, inverse_two = normalize(mid_rows)
    hidden_two = (normed_two * gain_two + shift_two).astype(bf16)
    hidden_two_parts = plane_gather(by_shard(hidden_two))
    activated_parts, grad_pre_parts, grad_hidden_two_parts, out_parts = [], [], [], []
    for h2, g in zip(hidden_two_parts, grad_low_parts):
        preactive = jnp.dot(h2, hidden_matrix, preferred_element_type=fp32) + hidden_shift
        grad_activated = lax.dot_general(g, output_matrix, (((1,), (1,)), ((), ())), preferred_element_type=fp32)
        grad_pre = (grad_activated * gelu_slope(preactive)).astype(bf16)
        grad_hidden_two_parts.append(
            lax.dot_general(grad_pre, hidden_matrix, (((1,), (1,)), ((), ())), preferred_element_type=fp32).astype(bf16)
        )
        activated = jax.nn.gelu(preactive, approximate=False).astype(bf16)
        activated_parts.append(activated)
        grad_pre_parts.append(grad_pre)
    for activated in activated_parts:
        out_parts.append(jnp.dot(activated, output_matrix, preferred_element_type=fp32).astype(bf16))
    grad_hidden_two = by_seq(plane_scatter(grad_hidden_two_parts))
    out_rows = mid_rows + (plane_scatter(out_parts) + output_shift)
    layer_out = out_rows.astype(bf16).reshape(inputs.shape)

    down = (((0,), (0,)), ((), ()))
    grad_pre_all = jnp.concatenate(grad_pre_parts)
    grad_output = lax.dot_general(
        jnp.concatenate(activated_parts), jnp.concatenate(grad_low_parts), down, preferred_element_type=fp32
    ).astype(bf16)
    grad_output = line_scatter(grad_output.reshape(Z, fr, D)).astype(bf16)
    other = flip(grad_output, COL)
    grad_output_matrix = jnp.concatenate(
        [jnp.where(odd, other, grad_output), jnp.where(odd, grad_output, other)]
    ).astype(fp32)

    def to_rows(v, width):
        v = line_scatter(v.reshape(Z, S, rows, width)).astype(bf16)
        v = seq_exchange(v)
        other = flip(v, COL)
        return jnp.stack([jnp.where(odd, other, v), jnp.where(odd, v, other)])

    grad_hidden = lax.dot_general(
        jnp.concatenate(hidden_two_parts), grad_pre_all, down, preferred_element_type=fp32
    ).astype(bf16)
    grad_hidden_matrix = (
        to_rows(grad_hidden, fw).reshape(R, S, rows, Z, fr).transpose(2, 1, 3, 0, 4).reshape(rows, F).astype(fp32)
    )

    grad_out = grad_low.astype(fp32)
    grad_mid = grad_out + norm_back(grad_hidden_two * gain_two, normed_two, inverse_two)
    grad_mid_low = grad_mid.astype(bf16)
    grad_mid_swapped = swap_halves(grad_mid_low)
    grad_attended = lax.dot_general(
        grad_mid_swapped, attn_matrix, (((1,), (1,)), ((), ())), preferred_element_type=fp32
    ).astype(bf16)
    grad_attended = grad_attended.reshape(n, S, R, hw)
    sent = [
        [jnp.where(odd, grad_attended[:, js, 1 - jr], grad_attended[:, js, jr]) for js in range(S)] for jr in range(R)
    ]
    grad_heads = jnp.stack([jnp.stack([hop(sent[jr][js], js, jr) for js in range(S)]) for jr in range(R)])
    grad_qkv = attention_call(
        lambda *refs: attend_back_kernel(heads, *refs),
        s,
        (qkv, grad_heads),
        3 * hw,
        (bf16, bf16, fp32, fp32),
        5 * half_pairs,
    )
    pairs = grad_qkv.reshape(2 * R, 2 * n, 3 * hw)
    grad_hidden_in = by_seq(
        plane_scatter(
            [
                lax.dot_general(pairs[i], qkv_matrix, (((1,), (1,)), ((), ())), preferred_element_type=fp32).astype(bf16)
                for i in range(2 * R)
            ]
        )
    )
    grad_qkv = grad_qkv.reshape(T * n, 3 * hw)
    grad_qkv_cols = lax.dot_general(
        jnp.concatenate(hidden_in_parts), grad_qkv, down, preferred_element_type=fp32
    ).astype(bf16)
    grad_qkv_matrix = (
        to_rows(grad_qkv_cols, 3 * hw)
        .reshape(R, S, rows, 3, hw)
        .transpose(2, 3, 1, 0, 4)
        .reshape(rows, 3 * D)
        .astype(fp32)
    )
    grad_attn = lax.dot_general(attended, grad_mid_swapped, down, preferred_element_type=fp32).astype(bf16)
    top, bot = slice(0, D // 2), slice(D // 2, D)
    left, right = slice(0, D // R), slice(D // R, D)
    grad_attn = plane_scatter([grad_attn[top, left], grad_attn[bot, left], grad_attn[top, right], grad_attn[bot, right]])
    grad_attn = line_scatter(grad_attn.astype(bf16).reshape(Z, rows, D // R)).astype(bf16)
    other = flip(grad_attn, COL)
    grad_attn_matrix = jnp.concatenate(
        [jnp.where(odd, other, grad_attn), jnp.where(odd, grad_attn, other)], axis=1
    ).astype(fp32)
    grad_input_rows = grad_mid + norm_back(grad_hidden_in * gain_one, normed_one, inverse_one)
    grad_input_out = grad_input_rows.reshape(inputs.shape)

    hidden_sums = column_sums(grad_pre_all).reshape(1, Z, 1, fr)
    hidden_sums = lax.dynamic_update_slice(jnp.zeros((S, Z, R, fr), fp32), hidden_sums, (s, 0, r, 0))
    early = total(
        jnp.concatenate(
            [
                jnp.sum(grad_hidden_two * normed_two, axis=0).reshape(S * Z, rows),
                jnp.sum(grad_hidden_two, axis=0).reshape(S * Z, rows),
                column_sums(grad_mid_low).reshape(S * Z, rows),
                column_sums(grad_low).reshape(S * Z, rows),
                hidden_sums.reshape(S * Z, R * fr),
            ],
            axis=1,
        )
    )
    qkv_sums = column_sums(grad_qkv)
    none = jnp.zeros((D,), fp32)
    late = total(
        jnp.concatenate(
            [
                jnp.sum(grad_hidden_in * normed_one, axis=0).reshape(S * Z, rows),
                jnp.sum(grad_hidden_in, axis=0).reshape(S * Z, rows),
                lax.dynamic_update_slice_in_dim(none, qkv_sums[:hw], t * hw, 0).reshape(S * Z, rows),
                lax.dynamic_update_slice_in_dim(none, qkv_sums[2 * hw :], t * hw, 0).reshape(S * Z, rows),
            ],
            axis=1,
        )
    )
    early = lax.dynamic_index_in_dim(early, s * Z + z, 0, keepdims=False)
    late = lax.dynamic_index_in_dim(late, s * Z + z, 0, keepdims=False)

    def part(v, i):
        return v[i * rows : (i + 1) * rows]

    return (
        layer_out,
        grad_input_out,
        part(late, 0),
        part(late, 1),
        grad_qkv_matrix,
        part(late, 2),
        part(late, 3),
        grad_attn_matrix,
        part(early, 2),
        part(early, 0),
        part(early, 1),
        grad_hidden_matrix,
        early[4 * rows :],
        grad_output_matrix,
        part(early, 3),
    )


def solution(mesh):
    tokens = P(("shard", "replica"), "seq", None)
    vector = P(("seq", "shard"))
    matrix = P(("seq", "shard"), None)
    weights = (
        vector,
        vector,
        matrix,
        vector,
        vector,
        matrix,
        vector,
        vector,
        vector,
        matrix,
        vector,
        matrix,
        vector,
    )
    return jax.shard_map(
        on_device,
        mesh=mesh,
        in_specs=(tokens, tokens) + weights,
        out_specs=(tokens, tokens) + weights,
        check_vma=False,
    )
```

time: 2940 us -> 1090 us (0.37)
  waiting for transfers between devices: 2210 us -> 378 us
  blocking collectives: 338 us -> 0 us
  starting transfers between devices: 0.54 us -> 264 us
  matrix products: 273 us -> 126 us
  local copies, waits for them, and re-layouts: 22.6 us -> 156 us
  other arithmetic: 72.3 us -> 127 us
    reduce_scatter x6 -> x0, waiting for transfers between devices: 1840 us -> none  [the longest x1 637 us: on_device(): lax.psum_scatter(grad_output_matrix, ('seq', 'shard'), scatter_dimension=...]
    ppermute x0 -> x168, waiting for transfers between devices: none -> 378 us  [the longest x114 195 us: flip(): lax.ppermute(v, axis, [(i, i ^ bit) for i in range(lax.axis_size(axis))])]
    all_gather x6 -> x0, waiting for transfers between devices: 333 us -> none  [the longest x1 162 us: on_device(): lax.all_gather(halves[11], ('seq', 'shard'), axis=0, tiled=True)]
    all_gather x9 -> x0, blocking collectives: 271 us -> none  [the longest x1 33.7 us: on_device(): lax.all_gather(halves[4], ('seq', 'shard'), axis=0, tiled=True)]
    ppermute x0 -> x168, starting transfers between devices: none -> 264 us  [the longest x114 93.1 us: flip(): lax.ppermute(v, axis, [(i, i ^ bit) for i in range(lax.axis_size(axis))])]
    dot_general x17 -> x29, matrix products: 266 us -> 124 us  [the longest x4 30.3 us: on_device(): jnp.dot(h2, hidden_matrix, preferred_element_type=fp32) + hidden_shift]
    unnamed x1 -> x0, blocking collectives: 61.7 us -> none
    unnamed x109 -> x398, local copies, waits for them, and re-layouts: 13.4 us -> 67.7 us
  transfers between devices with their start and end apart: 13 -> 168, of which waited for: 9 -> 51; matrix products, arithmetic and copies ran while one was open for 9% -> 36% of each run, Pallas kernels for 0% -> 2%
where the time goes in v1:
time: 1090 us; the launch traced here: 1080 us
  waiting for transfers between devices  378 us (35%)
  starting transfers between devices  264 us (24%)
  local copies, waits for them, and re-layouts  156 us (14%)
  other arithmetic  127 us (12%)
  matrix products  126 us (12%)
  Pallas kernels  22.5 us (2%)
    ppermute x114, waiting for transfers between devices, flip(): lax.ppermute(v, axis, [(i, i ^ bit) for i in range(lax.axis_size(axis))])  195 us
    ppermute x114, starting transfers between devices, flip(): lax.ppermute(v, axis, [(i, i ^ bit) for i in range(lax.axis_size(axis))])  93.1 us
    ppermute x12, starting transfers between devices, line_gather(): lax.ppermute(up[-1], 'shard', [(i, i + 1) for i in range(k - 1, Z - 1)])  71.7 us
    ppermute x12, waiting for transfers between devices, line_scatter(): lax.ppermute(send_up.astype(bf16), 'shard', [(i, i + 1) for i in range(0,...  69.6 us
    unnamed x398, local copies, waits for them, and re-layouts  67.7 us
    ppermute x12, waiting for transfers between devices, line_gather(): lax.ppermute(down[-1], 'shard', [(i, i - 1) for i in range(1, Z - k + 1)])  56.7 us
    ppermute x12, starting transfers between devices, line_scatter(): lax.ppermute(send_up.astype(bf16), 'shard', [(i, i + 1) for i in range(0,...  51.5 us
    ppermute x12, waiting for transfers between devices, line_scatter(): lax.ppermute(send_down.astype(bf16), 'shard', [(i, i - 1) for i in range(...  38.1 us
  transfers between devices with their start and end apart: 168, of which 51 were waited for; matrix products, arithmetic and copies ran while one was open for 36% of the time, Pallas kernels for 2%

profile of v1, /device:TPU:0, one launch (start us, length us, event | category | flops | bytes accessed | tf_op | source)
XLA Modules:
  0.0 1078.9 jit_solution(4721504122594228726)
XLA Ops:
  2.5 5.7 collective-permute-start.29
  56.9 4.4 collective-permute-done.45
  75.1 7.6 collective-permute-done.32
  85.4 4.8 collective-permute-done.84
  96.7 19.4 %collective-permute-done.16 = bf16[256,2048]{0,1:T(8,128)(2,1)S(1)} collective-permute-done((bf16[256,2048]{0,1:T(8,128)(2,1)S(1)}, bf16[256,2048]{0,1:T(8,128)(2,1)S(1)}, u32[]{:S(2)}, u32[]{:S(2)}) %collective-permute-start.16) | collective-permute-done | bytes 1048608 | tf_op jit(solution)/shard_map/ppermute | solution.py:41
  119.7 18.5 %collective-permute-done.38 = bf16[512,1024]{1,0:T(8,128)(2,1)S(1)} collective-permute-done((bf16[512,1024]{1,0:T(8,128)(2,1)}, bf16[512,1024]{1,0:T(8,128)(2,1)S(1)}, u32[]{:S(2)}, u32[]{:S(2)}) %collective-permute-start.38) | collective-permute-done | bytes 1048608 | tf_op jit(solution)/shard_map/ppermute | solution.py:41
  146.0 5.8 collective-permute-done.87
  154.2 4.5 collective-permute-done.8
  168.4 9.4 collective-permute-done.18
  177.8 6.8 collective-permute-start.54
  187.8 5.3 collective-permute-start.48
  194.0 12.9 %collective-permute-done.11 = bf16[512,768]{1,0:T(8,128)(2,1)S(1)} collective-permute-done((bf16[512,768]{1,0:T(8,128)(2,1)S(1)}, bf16[512,768]{1,0:T(8,128)(2,1)S(1)}, u32[]{:S(2)}, u32[]{:S(2)}) %collective-permute-start.11) | collective-permute-done | bytes 786464 | tf_op jit(solution)/shard_map/ppermute | solution.py:84
  216.9 8.8 shard_map.262
  229.0 13.3 %collective-permute-start.49 = (bf16[512,1024]{1,0:T(8,128)(2,1)S(1)}, bf16[512,1024]{1,0:T(8,128)(2,1)S(1)}, u32[]{:S(2)}, u32[]{:S(2)}) collective-permute-start(bf16[512,1024]{1,0:T(8,128)(2,1)S(1)} %bitcast.483), channel_id=1, source_target_pairs={{2,0},{4,2},{6,4},{3,1},{5,3},{7,5},{10,8},{12,10},{14,12},{11,9},... | collective-permute-start | bytes 3145736 | tf_op jit(solution)/shard_map/ppermute | solution.py:84
  243.7 4.8 collective-permute-done.23
  250.6 4.7 collective-permute-done.25
  259.9 4.3 collective-permute-done.27
  267.6 43.4 %collective-permute-start.58 = (bf16[256,2048]{1,0:T(8,128)(2,1)S(1)}, bf16[256,2048]{1,0:T(8,128)(2,1)}, u32[]{:S(2)}, u32[]{:S(2)}) collective-permute-start(bf16[256,2048]{1,0:T(8,128)(2,1)S(1)} %collective-permute-done.54), channel_id=1, source_target_pairs={{2,4},{4,6},{3,5},{5,7},{10,12},{12,14},{11,13},{13,15},{18,20},{2... | collective-permute-start | bytes 3145736 | tf_op jit(solution)/shard_map/ppermute | solution.py:83
  317.0 6.3 collective-permute-done.56
  326.2 19.5 %collective-permute-done.50 = bf16[512,1024]{1,0:T(8,128)(2,1)} collective-permute-done((bf16[512,1024]{1,0:T(8,128)(2,1)S(1)}, bf16[512,1024]{1,0:T(8,128)(2,1)}, u32[]{:S(2)}, u32[]{:S(2)}) %collective-permute-start.50) | collective-permute-done | bytes 1048608 | tf_op jit(solution)/shard_map/ppermute | solution.py:84
  348.7 14.1 %pad_maximum_fusion = bf16[2048,2048]{1,0:T(8,128)(2,1)S(1)} fusion(bf16[2048,1024]{1,0:T(8,128)(2,1)S(1)} %constant_dynamic-update-slice_fusion, bf16[512,1024]{1,0:T(8,128)(2,1)S(1)} %collective-permute-done.37, bf16[512,1024]{1,0:T(8,128)(2,1)S(1)} %collective-permute-done.36, bf16[512,1024]{1,0:T(8,128)(2,1)S(1)} %collective-permute-done.35, ...), kind=kLoop, calls=%fused_computation | loop fusion | flops 41943040 | bytes 16777216 | tf_op jit(solution)/shard_map/concatenate | solution.py:278
  393.4 9.7 collective-permute-done.61
  410.1 4.2 fusion.29
  427.4 23.2 %fusion.23 = (bf16[512,1024]{1,0:T(8,128)(2,1)S(1)}, bf16[512,1024]{1,0:T(8,128)(2,1)S(1)}, bf16[512,1024]{1,0:T(8,128)(2,1)S(1)}, bf16[512,1024]{1,0:T(8,128)(2,1)S(1)}, f32[512,1024]{1,0:T(8,128)S(1)}) fusion(f32[1024]{0:T(1024)S(1)} %bitcast.560, f32[512,1024]{1,0:T(8,128)S(1)} %fusion.77, f32[512,1024]{1,0:T(8,128)S(1)} %fusion.81, ...), kind=kOutput, calls=%fused_computation.54 | convolution fusion | flops 2294284288 | bytes 18878464 | tf_op jit(solution)/shard_map/dot_general | solution.py:324
  466.0 3.8 fusion.35
  472.3 3.8 fusion.41
  476.2 4.7 fusion.47
  488.3 12.6 %convolution_convert_fusion.1 = bf16[2048,1024]{1,0:T(8,128)(2,1)} fusion(bf16[2048,2048]{0,1:T(8,128)(2,1)} %constant_dynamic-update-slice_fusion.21, bf16[512,1024]{1,0:T(8,128)(2,1)S(1)} %fusion.47, bf16[512,1024]{1,0:T(8,128)(2,1)S(1)} %fusion.35, bf16[512,1024]{1,0:T(8,128)(2,1)S(1)} %fusion.41, bf16[512,1024]{1,0:T(8,128)(2,1)S(1)} %fusion.29), kind=kOutput, calls=%fused_computation.15 | convolution fusion | flops 8608808960 | bytes 16777216 | tf_op jit(solution)/shard_map/dot_general | solution.py:356
  501.0 12.0 %fusion.8 = bf16[1024,2048]{1,0:T(8,128)(2,1)} fusion(bf16[2048,2048]{1,0:T(8,128)(2,1)S(1)} %bitcast.540, bf16[512,1024]{1,0:T(8,128)(2,1)S(1)} %copy-done.162, bf16[512,1024]{1,0:T(8,128)(2,1)} %copy-done.163, bf16[512,1024]{1,0:T(8,128)(2,1)} %copy-done.164, bf16[512,1024]{1,0:T(8,128)(2,1)} %copy-done.165), kind=kOutput, calls=%fused_computation.14 | convolution fusion | flops 8608808960 | bytes 16777216 | tf_op jit(solution)/shard_map/dot_general | solution.py:341
  529.5 17.4 %collective-permute-start.91 = (bf16[256,2048]{1,0:T(8,128)(2,1)S(1)}, bf16[256,2048]{1,0:T(8,128)(2,1)S(1)}, u32[]{:S(2)}, u32[]{:S(2)}) collective-permute-start(bf16[256,2048]{1,0:T(8,128)(2,1)S(1)} %copy-done.92), channel_id=1, source_target_pairs={{0,8},{8,0},{16,24},{24,16},{1,9},{9,1},{17,25},{25,17},{2,10},{10... | collective-permute-start | bytes 3145736 | tf_op jit(solution)/shard_map/ppermute | solution.py:41
  550.7 3.8 collective-permute-start.161
  557.9 20.0 %collective-permute-done.161 = bf16[256,2048]{1,0:T(8,128)(2,1)S(1)} collective-permute-done((bf16[256,2048]{1,0:T(8,128)(2,1)S(1)}, bf16[256,2048]{1,0:T(8,128)(2,1)S(1)}, u32[]{:S(2)}, u32[]{:S(2)}) %collective-permute-start.161) | collective-permute-done | bytes 1048608 | tf_op jit(solution)/shard_map/ppermute | solution.py:102
  582.0 17.8 %collective-permute-done.151 = bf16[4,128,1024]{2,1,0:T(8,128)(2,1)S(1)} collective-permute-done((bf16[4,128,1024]{2,1,0:T(8,128)(2,1)S(1)}, bf16[4,128,1024]{2,1,0:T(8,128)(2,1)S(1)}, u32[]{:S(2)}, u32[]{:S(2)}) %collective-permute-start.151) | collective-permute-done | bytes 1048608 | tf_op jit(solution)/shard_map/ppermute | solution.py:102
  606.6 8.0 collective-permute-done.73
  618.5 4.4 collective-permute-start.152
  624.4 4.4 collective-permute-start.162
  631.3 15.2 %collective-permute-done.152 = bf16[4,128,1024]{2,1,0:T(8,128)(2,1)S(1)} collective-permute-done((bf16[4,128,1024]{2,1,0:T(8,128)(2,1)S(1)}, bf16[4,128,1024]{2,1,0:T(8,128)(2,1)S(1)}, u32[]{:S(2)}, u32[]{:S(2)}) %collective-permute-start.152) | collective-permute-done | bytes 1048608 | tf_op jit(solution)/shard_map/ppermute | solution.py:102
  650.9 13.6 %collective-permute-done.162 = bf16[256,2048]{1,0:T(8,128)(2,1)S(1)} collective-permute-done((bf16[256,2048]{1,0:T(8,128)(2,1)S(1)}, bf16[256,2048]{1,0:T(8,128)(2,1)S(1)}, u32[]{:S(2)}, u32[]{:S(2)}) %collective-permute-start.162) | collective-permute-done | bytes 1048608 | tf_op jit(solution)/shard_map/ppermute | solution.py:102
  670.8 8.6 collective-permute-done.95
  691.8 4.0 convert_reduce_fusion.4
  696.8 6.7 convolution_convert_fusion.15
  758.2 13.8 %shard_map.263 = bf16[2,4,256,768]{3,2,1,0:T(8,128)(2,1)S(1)} custom-call(s32[1]{0:T(128)} %bitcast.refs_0_, bf16[2,4,256,768]{3,2,1,0:T(8,128)(2,1)S(1)} %bitcast.431, bf16[2,4,256,256]{3,2,1,0:T(8,128)(2,1)S(1)} %pad_maximum_fusion.7.refs_2_), custom_call_target="tpu_custom_call" | custom-call | flops 3355443200 | bytes 4194304 | tf_op jit(solution)/shard_map/pallas_call | solution.py:213
  777.6 9.8 convolution_convert_fusion.2
  790.2 3.9 collective-permute-start.119
  798.7 14.1 %collective-permute-done.149 = f32[16,1024]{1,0:T(8,128)S(1)} collective-permute-done((f32[16,1024]{1,0:T(8,128)S(1)}, f32[16,1024]{1,0:T(8,128)S(1)}, u32[]{:S(2)}, u32[]{:S(2)}) %collective-permute-start.149) | collective-permute-done | bytes 65568 | tf_op jit(solution)/shard_map/ppermute | solution.py:41
  827.1 5.3 collective-permute-start.153
  835.0 5.7 add_convert_fusion
  853.5 9.5 collective-permute-done.134
  865.9 10.5 collective-permute-done.109
  878.2 4.9 collective-permute-start.163
  887.5 17.2 %collective-permute-done.156 = bf16[4,128,1024]{2,1,0:T(8,128)(2,1)S(1)} collective-permute-done((bf16[4,128,1024]{2,1,0:T(8,128)(2,1)S(1)}, bf16[4,128,1024]{2,1,0:T(8,128)(2,1)S(1)}, u32[]{:S(2)}, u32[]{:S(2)}) %collective-permute-start.156) | collective-permute-done | bytes 1048608 | tf_op jit(solution)/shard_map/ppermute | solution.py:103
  908.6 16.0 %collective-permute-done.166 = bf16[256,2048]{1,0:T(8,128)(2,1)S(1)} collective-permute-done((bf16[256,2048]{1,0:T(8,128)(2,1)S(1)}, bf16[256,2048]{1,0:T(8,128)(2,1)S(1)}, u32[]{:S(2)}, u32[]{:S(2)}) %collective-permute-start.166) | collective-permute-done | bytes 1048608 | tf_op jit(solution)/shard_map/ppermute | solution.py:103
  930.1 9.3 collective-permute-done.137
  944.1 7.2 collective-permute-done.110
  956.1 3.9 multiply_reduce_fusion.5
  971.2 4.8 fusion.131
  983.2 19.5 %collective-permute-done.117 = f32[16,512]{1,0:T(8,128)S(1)} collective-permute-done((f32[16,512]{1,0:T(8,128)S(1)}, f32[16,512]{1,0:T(8,128)S(1)}, u32[]{:S(2)}, u32[]{:S(2)}) %collective-permute-start.117) | collective-permute-done | bytes 32800 | tf_op jit(solution)/shard_map/ppermute | solution.py:41
  1003.7 4.9 collective-permute-done.118
  1008.6 4.2 collective-permute-start.140
  1020.2 12.1 %collective-permute-start.141 = (bf16[128,1024]{1,0:T(8,128)(2,1)S(1)}, bf16[128,1024]{1,0:T(8,128)(2,1)S(1)}, u32[]{:S(2)}, u32[]{:S(2)}) collective-permute-start(bf16[128,1024]{1,0:T(8,128)(2,1)S(1)} %get-tuple-element.137), channel_id=1, source_target_pairs={{0,2},{2,4},{4,6},{1,3},{3,5},{5,7},{8,10},{10,12},{12,14},{9,11},... | collective-permute-start | bytes 786440 | tf_op jit(solution)/shard_map/ppermute | solution.py:102
  1036.6 4.4 collective-permute-done.124
  1048.6 4.3 collective-permute-done.126
  1058.9 5.6 copy.252
  1066.7 7.2 collective-permute-done.128
  (960 shorter events, 453.8 us)
Async XLA Ops:
  2.5 60.7 %collective-permute-start.29 = (bf16[128,1024]{1,0:T(8,128)(2,1)S(1)}, bf16[128,1024]{1,0:T(8,128)(2,1)}, u32[]{:S(2)}, u32[]{:S(2)}) collective-permute-start(bf16[128,1024]{1,0:T(8,128)(2,1)S(1)} %bitcast.524), channel_id=1, source_target_pairs={{0,2},{2,4},{4,6},{1,3},{3,5},{5,7},{8,10},{10,12},{12,14},{9,11},... | collective-permute-start | bytes 786440 | tf_op jit(solution)/shard_map/ppermute | solution.py:83
  8.1 53.8 %collective-permute-start.30 = (bf16[128,1024]{1,0:T(8,128)(2,1)S(1)}, bf16[128,1024]{1,0:T(8,128)(2,1)}, u32[]{:S(2)}, u32[]{:S(2)}) collective-permute-start(bf16[128,1024]{1,0:T(8,128)(2,1)S(1)} %bitcast.525), channel_id=1, source_target_pairs={{2,0},{4,2},{6,4},{3,1},{5,3},{7,5},{10,8},{12,10},{14,12},{11,9},... | collective-permute-start | bytes 786440 | tf_op jit(solution)/shard_map/ppermute | solution.py:84
  18.1 34.9 %collective-permute-start.5 = (bf16[128,768]{1,0:T(8,128)(2,1)}, bf16[128,768]{1,0:T(8,128)(2,1)}, u32[]{:S(2)}, u32[]{:S(2)}) collective-permute-start(bf16[128,768]{1,0:T(8,128)(2,1)} %bitcast.12), channel_id=1, source_target_pairs={{0,24},{8,16},{16,8},{24,0},{1,25},{9,17},{17,9},{25,1},{2,26},{10... | collective-permute-start | bytes 589832 | tf_op jit(solution)/shard_map/ppermute | solution.py:41
  19.1 34.6 %collective-permute-start.6 = (bf16[128,768]{1,0:T(8,128)(2,1)}, bf16[128,768]{1,0:T(8,128)(2,1)}, u32[]{:S(2)}, u32[]{:S(2)}) collective-permute-start(bf16[128,768]{1,0:T(8,128)(2,1)} %bitcast.13), channel_id=1, source_target_pairs={{0,16},{8,24},{16,0},{24,8},{1,17},{9,25},{17,1},{25,9},{2,18},{10... | collective-permute-start | bytes 589832 | tf_op jit(solution)/shard_map/ppermute | solution.py:41
  55.0 35.2 %collective-permute-start.84 = (bf16[256,2048]{1,0:T(8,128)(2,1)S(1)}, bf16[256,2048]{1,0:T(8,128)(2,1)S(1)}, u32[]{:S(2)}, u32[]{:S(2)}) collective-permute-start(bf16[256,2048]{1,0:T(8,128)(2,1)S(1)} %bitcast.464), channel_id=1, source_target_pairs={{0,16},{8,24},{16,0},{24,8},{1,17},{9,25},{17,1},{25,9},{2,18},{10... | collective-permute-start | bytes 3145736 | tf_op jit(solution)/shard_map/ppermute | solution.py:41
  72.2 43.9 %collective-permute-start.16 = (bf16[256,2048]{0,1:T(8,128)(2,1)S(1)}, bf16[256,2048]{0,1:T(8,128)(2,1)S(1)}, u32[]{:S(2)}, u32[]{:S(2)}) collective-permute-start(bf16[256,2048]{0,1:T(8,128)(2,1)S(1)} %bitcast.502), channel_id=1, source_target_pairs={{0,1},{1,0},{2,3},{3,2},{4,5},{5,4},{6,7},{7,6},{8,9},{9,8},{10,11... | collective-permute-start | bytes 3145736 | tf_op jit(solution)/shard_map/ppermute | solution.py:41
  84.7 33.7 %collective-permute-start.14 = (bf16[256,2048]{0,1:T(8,128)(2,1)S(1)}, bf16[256,2048]{0,1:T(8,128)(2,1)S(1)}, u32[]{:S(2)}, u32[]{:S(2)}) collective-permute-start(bf16[256,2048]{0,1:T(8,128)(2,1)S(1)} %bitcast.503), channel_id=1, source_target_pairs={{0,16},{8,24},{16,0},{24,8},{1,17},{9,25},{17,1},{25,9},{2,18},{10... | collective-permute-start | bytes 3145736 | tf_op jit(solution)/shard_map/ppermute | solution.py:41
  93.6 44.6 %collective-permute-start.38 = (bf16[512,1024]{1,0:T(8,128)(2,1)}, bf16[512,1024]{1,0:T(8,128)(2,1)S(1)}, u32[]{:S(2)}, u32[]{:S(2)}) collective-permute-start(bf16[512,1024]{1,0:T(8,128)(2,1)} %bitcast.43), channel_id=1, source_target_pairs={{0,1},{1,0},{2,3},{3,2},{4,5},{5,4},{6,7},{7,6},{8,9},{9,8},{10,11... | collective-permute-start | bytes 3145736 | tf_op jit(solution)/shard_map/ppermute | solution.py:41
  95.9 43.9 %collective-permute-start.36 = (bf16[512,1024]{1,0:T(8,128)(2,1)}, bf16[512,1024]{1,0:T(8,128)(2,1)S(1)}, u32[]{:S(2)}, u32[]{:S(2)}) collective-permute-start(bf16[512,1024]{1,0:T(8,128)(2,1)} %bitcast.43), channel_id=1, source_target_pairs={{0,16},{8,24},{16,0},{24,8},{1,17},{9,25},{17,1},{25,9},{2,18},{10... | collective-permute-start | bytes 3145736 | tf_op jit(solution)/shard_map/ppermute | solution.py:41
  119.1 32.6 %collective-permute-start.81 = (bf16[256,2048]{1,0:T(8,128)(2,1)S(1)}, bf16[256,2048]{1,0:T(8,128)(2,1)S(1)}, u32[]{:S(2)}, u32[]{:S(2)}) collective-permute-start(bf16[256,2048]{1,0:T(8,128)(2,1)S(1)} %collective-permute-done.80), channel_id=1, source_target_pairs={{0,8},{8,0},{16,24},{24,16},{1,9},{9,1},{17,25},{25,17},{2,10},{10... | collective-permute-start | bytes 3145736 | tf_op jit(solution)/shard_map/ppermute | solution.py:41
  177.8 48.0 %collective-permute-start.54 = (bf16[256,2048]{1,0:T(8,128)(2,1)S(1)}, bf16[256,2048]{1,0:T(8,128)(2,1)S(1)}, u32[]{:S(2)}, u32[]{:S(2)}) collective-permute-start(bf16[256,2048]{1,0:T(8,128)(2,1)S(1)} %copy-done.73), channel_id=1, source_target_pairs={{0,2},{2,4},{4,6},{1,3},{3,5},{5,7},{8,10},{10,12},{12,14},{9,11},... | collective-permute-start | bytes 3145736 | tf_op jit(solution)/shard_map/ppermute | solution.py:83
  186.3 42.6 %collective-permute-start.55 = (bf16[256,2048]{1,0:T(8,128)(2,1)S(1)}, bf16[256,2048]{1,0:T(8,128)(2,1)S(1)}, u32[]{:S(2)}, u32[]{:S(2)}) collective-permute-start(bf16[256,2048]{1,0:T(8,128)(2,1)S(1)} %copy-done.73), channel_id=1, source_target_pairs={{2,0},{4,2},{6,4},{3,1},{5,3},{7,5},{10,8},{12,10},{14,12},{11,9},... | collective-permute-start | bytes 3145736 | tf_op jit(solution)/shard_map/ppermute | solution.py:84
  187.8 54.6 %collective-permute-start.48 = (bf16[512,1024]{1,0:T(8,128)(2,1)S(1)}, bf16[512,1024]{1,0:T(8,128)(2,1)S(1)}, u32[]{:S(2)}, u32[]{:S(2)}) collective-permute-start(bf16[512,1024]{1,0:T(8,128)(2,1)S(1)} %bitcast.482), channel_id=1, source_target_pairs={{0,2},{2,4},{4,6},{1,3},{3,5},{5,7},{8,10},{10,12},{12,14},{9,11},... | collective-permute-start | bytes 3145736 | tf_op jit(solution)/shard_map/ppermute | solution.py:83
  207.4 35.6 %collective-permute-start.40 = (bf16[256,1024]{1,0:T(8,128)(2,1)S(1)}, bf16[256,1024]{1,0:T(8,128)(2,1)}, u32[]{:S(2)}, u32[]{:S(2)}) collective-permute-start(bf16[256,1024]{1,0:T(8,128)(2,1)S(1)} %slice.530), channel_id=1, source_target_pairs={{0,1},{1,0},{2,3},{3,2},{4,5},{5,4},{6,7},{7,6},{8,9},{9,8},{10,11... | collective-permute-start | bytes 1572872 | tf_op jit(solution)/shard_map/ppermute | solution.py:41
  212.0 31.2 %collective-permute-start.41 = (bf16[256,1024]{1,0:T(8,128)(2,1)S(1)}, bf16[256,1024]{1,0:T(8,128)(2,1)}, u32[]{:S(2)}, u32[]{:S(2)}) collective-permute-start(bf16[256,1024]{1,0:T(8,128)(2,1)S(1)} %slice.531), channel_id=1, source_target_pairs={{0,16},{8,24},{16,0},{24,8},{1,17},{9,25},{17,1},{25,9},{2,18},{10... | collective-permute-start | bytes 1572872 | tf_op jit(solution)/shard_map/ppermute | solution.py:41
  229.0 29.1 %collective-permute-start.49 = (bf16[512,1024]{1,0:T(8,128)(2,1)S(1)}, bf16[512,1024]{1,0:T(8,128)(2,1)S(1)}, u32[]{:S(2)}, u32[]{:S(2)}) collective-permute-start(bf16[512,1024]{1,0:T(8,128)(2,1)S(1)} %bitcast.483), channel_id=1, source_target_pairs={{2,0},{4,2},{6,4},{3,1},{5,3},{7,5},{10,8},{12,10},{14,12},{11,9},... | collective-permute-start | bytes 3145736 | tf_op jit(solution)/shard_map/ppermute | solution.py:84
  242.4 68.6 %collective-permute-start.39 = (bf16[512,1024]{1,0:T(8,128)(2,1)S(1)}, bf16[512,1024]{1,0:T(8,128)(2,1)S(1)}, u32[]{:S(2)}, u32[]{:S(2)}) collective-permute-start(bf16[512,1024]{1,0:T(8,128)(2,1)S(1)} %collective-permute-done.38), channel_id=1, source_target_pairs={{0,8},{8,0},{16,24},{24,16},{1,9},{9,1},{17,25},{25,17},{2,10},{10... | collective-permute-start | bytes 3145736 | tf_op jit(solution)/shard_map/ppermute | solution.py:41
  255.3 57.0 %collective-permute-start.42 = (bf16[256,1024]{1,0:T(8,128)(2,1)}, bf16[256,1024]{1,0:T(8,128)(2,1)S(1)}, u32[]{:S(2)}, u32[]{:S(2)}) collective-permute-start(bf16[256,1024]{1,0:T(8,128)(2,1)} %collective-permute-done.40), channel_id=1, source_target_pairs={{0,8},{8,0},{16,24},{24,16},{1,9},{9,1},{17,25},{25,17},{2,10},{10... | collective-permute-start | bytes 1572872 | tf_op jit(solution)/shard_map/ppermute | solution.py:41
  257.9 56.0 %collective-permute-start.43 = (bf16[256,1024]{1,0:T(8,128)(2,1)}, bf16[256,1024]{1,0:T(8,128)(2,1)S(1)}, u32[]{:S(2)}, u32[]{:S(2)}) collective-permute-start(bf16[256,1024]{1,0:T(8,128)(2,1)} %collective-permute-done.41), channel_id=1, source_target_pairs={{0,8},{8,0},{16,24},{24,16},{1,9},{9,1},{17,25},{25,17},{2,10},{10... | collective-permute-start | bytes 1572872 | tf_op jit(solution)/shard_map/ppermute | solution.py:41
  264.3 59.0 %collective-permute-start.56 = (bf16[256,2048]{1,0:T(8,128)(2,1)S(1)}, bf16[256,2048]{1,0:T(8,128)(2,1)}, u32[]{:S(2)}, u32[]{:S(2)}) collective-permute-start(bf16[256,2048]{1,0:T(8,128)(2,1)S(1)} %collective-permute-done.55), channel_id=1, source_target_pairs={{2,0},{4,2},{3,1},{5,3},{10,8},{12,10},{11,9},{13,11},{18,16},{20,... | collective-permute-start | bytes 3145736 | tf_op jit(solution)/shard_map/ppermute | solution.py:84
  267.6 57.0 %collective-permute-start.58 = (bf16[256,2048]{1,0:T(8,128)(2,1)S(1)}, bf16[256,2048]{1,0:T(8,128)(2,1)}, u32[]{:S(2)}, u32[]{:S(2)}) collective-permute-start(bf16[256,2048]{1,0:T(8,128)(2,1)S(1)} %collective-permute-done.54), channel_id=1, source_target_pairs={{2,4},{4,6},{3,5},{5,7},{10,12},{12,14},{11,13},{13,15},{18,20},{2... | collective-permute-start | bytes 3145736 | tf_op jit(solution)/shard_map/ppermute | solution.py:83
  311.0 34.8 %collective-permute-start.50 = (bf16[512,1024]{1,0:T(8,128)(2,1)S(1)}, bf16[512,1024]{1,0:T(8,128)(2,1)}, u32[]{:S(2)}, u32[]{:S(2)}) collective-permute-start(bf16[512,1024]{1,0:T(8,128)(2,1)S(1)} %collective-permute-done.49), channel_id=1, source_target_pairs={{2,0},{4,2},{3,1},{5,3},{10,8},{12,10},{11,9},{13,11},{18,16},{20,... | collective-permute-start | bytes 3145736 | tf_op jit(solution)/shard_map/ppermute | solution.py:84
  312.3 34.8 %collective-permute-start.52 = (bf16[512,1024]{1,0:T(8,128)(2,1)S(1)}, bf16[512,1024]{1,0:T(8,128)(2,1)}, u32[]{:S(2)}, u32[]{:S(2)}) collective-permute-start(bf16[512,1024]{1,0:T(8,128)(2,1)S(1)} %collective-permute-done.48), channel_id=1, source_target_pairs={{2,4},{4,6},{3,5},{5,7},{10,12},{12,14},{11,13},{13,15},{18,20},{2... | collective-permute-start | bytes 3145736 | tf_op jit(solution)/shard_map/ppermute | solution.py:83
  313.9 34.8 %collective-permute-start.37 = (bf16[512,1024]{1,0:T(8,128)(2,1)S(1)}, bf16[512,1024]{1,0:T(8,128)(2,1)S(1)}, u32[]{:S(2)}, u32[]{:S(2)}) collective-permute-start(bf16[512,1024]{1,0:T(8,128)(2,1)S(1)} %collective-permute-done.36), channel_id=1, source_target_pairs={{0,8},{8,0},{16,24},{24,16},{1,9},{9,1},{17,25},{25,17},{2,10},{10... | collective-permute-start | bytes 3145736 | tf_op jit(solution)/shard_map/ppermute | solution.py:41
  323.3 57.8 %collective-permute-start.57 = (bf16[256,2048]{1,0:T(8,128)(2,1)}, bf16[256,2048]{1,0:T(8,128)(2,1)}, u32[]{:S(2)}, u32[]{:S(2)}) collective-permute-start(bf16[256,2048]{1,0:T(8,128)(2,1)} %collective-permute-done.56), channel_id=1, source_target_pairs={{2,0},{3,1},{10,8},{11,9},{18,16},{19,17},{26,24},{27,25}} | collective-permute-start | bytes 3145736 | tf_op jit(solution)/shard_map/ppermute | solution.py:84
  324.6 61.1 %collective-permute-start.59 = (bf16[256,2048]{1,0:T(8,128)(2,1)}, bf16[256,2048]{1,0:T(8,128)(2,1)}, u32[]{:S(2)}, u32[]{:S(2)}) collective-permute-start(bf16[256,2048]{1,0:T(8,128)(2,1)} %collective-permute-done.58), channel_id=1, source_target_pairs={{4,6},{5,7},{12,14},{13,15},{20,22},{21,23},{28,30},{29,31}} | collective-permute-start | bytes 3145736 | tf_op jit(solution)/shard_map/ppermute | solution.py:83
  345.8 43.8 %collective-permute-start.51 = (bf16[512,1024]{1,0:T(8,128)(2,1)}, bf16[512,1024]{1,0:T(8,128)(2,1)}, u32[]{:S(2)}, u32[]{:S(2)}) collective-permute-start(bf16[512,1024]{1,0:T(8,128)(2,1)} %collective-permute-done.50), channel_id=1, source_target_pairs={{2,0},{3,1},{10,8},{11,9},{18,16},{19,17},{26,24},{27,25}} | collective-permute-start | bytes 3145736 | tf_op jit(solution)/shard_map/ppermute | solution.py:84
  347.1 45.9 %collective-permute-start.53 = (bf16[512,1024]{1,0:T(8,128)(2,1)}, bf16[512,1024]{1,0:T(8,128)(2,1)}, u32[]{:S(2)}, u32[]{:S(2)}) collective-permute-start(bf16[512,1024]{1,0:T(8,128)(2,1)} %collective-permute-done.52), channel_id=1, source_target_pairs={{4,6},{5,7},{12,14},{13,15},{20,22},{21,23},{28,30},{29,31}} | collective-permute-start | bytes 3145736 | tf_op jit(solution)/shard_map/ppermute | solution.py:83
  417.9 108.4 %collective-permute-start.79 = (bf16[256,2048]{1,0:T(8,128)(2,1)}, bf16[256,2048]{1,0:T(8,128)(2,1)}, u32[]{:S(2)}, u32[]{:S(2)}) collective-permute-start(bf16[256,2048]{1,0:T(8,128)(2,1)} %slice.553), channel_id=1, source_target_pairs={{0,8},{8,0},{16,24},{24,16},{1,9},{9,1},{17,25},{25,17},{2,10},{10... | collective-permute-start | bytes 3145736 | tf_op jit(solution)/shard_map/ppermute | solution.py:41
  454.1 75.4 %collective-permute-start.60 = (bf16[256,2048]{1,0:T(8,128)(2,1)}, bf16[256,2048]{1,0:T(8,128)(2,1)}, u32[]{:S(2)}, u32[]{:S(2)}) collective-permute-start(bf16[256,2048]{1,0:T(8,128)(2,1)} %slice.535), channel_id=1, source_target_pairs={{0,8},{8,0},{16,24},{24,16},{1,9},{9,1},{17,25},{25,17},{2,10},{10... | collective-permute-start | bytes 3145736 | tf_op jit(solution)/shard_map/ppermute | solution.py:41
  460.4 89.5 %collective-permute-start.72 = (bf16[256,2048]{1,0:T(8,128)(2,1)}, bf16[256,2048]{1,0:T(8,128)(2,1)S(1)}, u32[]{:S(2)}, u32[]{:S(2)}) collective-permute-start(bf16[256,2048]{1,0:T(8,128)(2,1)} %slice.546), channel_id=1, source_target_pairs={{0,8},{8,0},{16,24},{24,16},{1,9},{9,1},{17,25},{25,17},{2,10},{10... | collective-permute-start | bytes 3145736 | tf_op jit(solution)/shard_map/ppermute | solution.py:41
  465.5 113.5 %collective-permute-start.63 = (bf16[256,2048]{1,0:T(8,128)(2,1)}, bf16[256,2048]{1,0:T(8,128)(2,1)}, u32[]{:S(2)}, u32[]{:S(2)}) collective-permute-start(bf16[256,2048]{1,0:T(8,128)(2,1)} %slice.538), channel_id=1, source_target_pairs={{0,8},{8,0},{16,24},{24,16},{1,9},{9,1},{17,25},{25,17},{2,10},{10... | collective-permute-start | bytes 3145736 | tf_op jit(solution)/shard_map/ppermute | solution.py:41
  518.9 36.0 %collective-permute-start.67 = (bf16[256,2048]{1,0:T(8,128)(2,1)}, bf16[256,2048]{1,0:T(8,128)(2,1)}, u32[]{:S(2)}, u32[]{:S(2)}) collective-permute-start(bf16[256,2048]{1,0:T(8,128)(2,1)} %slice.541), channel_id=1, source_target_pairs={{0,8},{8,0},{16,24},{24,16},{1,9},{9,1},{17,25},{25,17},{2,10},{10... | collective-permute-start | bytes 3145736 | tf_op jit(solution)/shard_map/ppermute | solution.py:41
  527.2 76.3 %collective-permute-start.86 = (bf16[256,2048]{1,0:T(8,128)(2,1)S(1)}, bf16[256,2048]{1,0:T(8,128)(2,1)S(1)}, u32[]{:S(2)}, u32[]{:S(2)}) collective-permute-start(bf16[256,2048]{1,0:T(8,128)(2,1)S(1)} %copy-done.91), channel_id=1, source_target_pairs={{0,8},{8,0},{16,24},{24,16},{1,9},{9,1},{17,25},{25,17},{2,10},{10... | collective-permute-start | bytes 3145736 | tf_op jit(solution)/shard_map/ppermute | solution.py:41
  549.9 55.6 %collective-permute-start.82 = (bf16[256,2048]{1,0:T(8,128)(2,1)S(1)}, bf16[256,2048]{1,0:T(8,128)(2,1)S(1)}, u32[]{:S(2)}, u32[]{:S(2)}) collective-permute-start(bf16[256,2048]{1,0:T(8,128)(2,1)S(1)} %copy-done.90), channel_id=1, source_target_pairs={{0,8},{8,0},{16,24},{24,16},{1,9},{9,1},{17,25},{25,17},{2,10},{10... | collective-permute-start | bytes 3145736 | tf_op jit(solution)/shard_map/ppermute | solution.py:41
  554.9 44.9 %collective-permute-start.151 = (bf16[4,128,1024]{2,1,0:T(8,128)(2,1)S(1)}, bf16[4,128,1024]{2,1,0:T(8,128)(2,1)S(1)}, u32[]{:S(2)}, u32[]{:S(2)}) collective-permute-start(bf16[4,128,1024]{2,1,0:T(8,128)(2,1)S(1)} %get-tuple-element.101), channel_id=1, source_target_pairs={{0,2},{1,3},{8,10},{9,11},{16,18},{17,19},{24,26},{25,27}} | collective-permute-start | bytes 3145736 | tf_op jit(solution)/shard_map/ppermute | solution.py:102
  577.9 52.8 %collective-permute-start.154 = (bf16[4,128,1024]{2,1,0:T(8,128)(2,1)S(1)}, bf16[4,128,1024]{2,1,0:T(8,128)(2,1)S(1)}, u32[]{:S(2)}, u32[]{:S(2)}) collective-permute-start(bf16[4,128,1024]{2,1,0:T(8,128)(2,1)S(1)} %get-tuple-element.102), channel_id=1, source_target_pairs={{6,4},{7,5},{14,12},{15,13},{22,20},{23,21},{30,28},{31,29}} | collective-permute-start | bytes 3145736 | tf_op jit(solution)/shard_map/ppermute | solution.py:103
  579.1 71.3 %collective-permute-start.164 = (bf16[256,2048]{1,0:T(8,128)(2,1)S(1)}, bf16[256,2048]{1,0:T(8,128)(2,1)S(1)}, u32[]{:S(2)}, u32[]{:S(2)}) collective-permute-start(bf16[256,2048]{1,0:T(8,128)(2,1)S(1)} %get-tuple-element.98), channel_id=1, source_target_pairs={{6,4},{7,5},{14,12},{15,13},{22,20},{23,21},{30,28},{31,29}} | collective-permute-start | bytes 3145736 | tf_op jit(solution)/shard_map/ppermute | solution.py:103
  624.4 40.1 %collective-permute-start.162 = (bf16[256,2048]{1,0:T(8,128)(2,1)S(1)}, bf16[256,2048]{1,0:T(8,128)(2,1)S(1)}, u32[]{:S(2)}, u32[]{:S(2)}) collective-permute-start(bf16[256,2048]{1,0:T(8,128)(2,1)S(1)} %fusion.117), channel_id=1, source_target_pairs={{0,2},{2,4},{1,3},{3,5},{8,10},{10,12},{9,11},{11,13},{16,18},{18,... | collective-permute-start | bytes 3145736 | tf_op jit(solution)/shard_map/ppermute | solution.py:102
  629.0 100.5 %collective-permute-start.64 = (bf16[128,2048]{1,0:T(8,128)(2,1)}, bf16[128,2048]{1,0:T(8,128)(2,1)}, u32[]{:S(2)}, u32[]{:S(2)}) collective-permute-start(bf16[128,2048]{1,0:T(8,128)(2,1)} %slice.750), channel_id=1, source_target_pairs={{0,1},{1,0},{2,3},{3,2},{4,5},{5,4},{6,7},{7,6},{8,9},{9,8},{10,11... | collective-permute-start | bytes 1572872 | tf_op jit(solution)/shard_map/ppermute | solution.py:41
  630.7 36.6 %collective-permute-start.83 = (bf16[128,2048]{1,0:T(8,128)(2,1)S(1)}, bf16[128,2048]{1,0:T(8,128)(2,1)S(1)}, u32[]{:S(2)}, u32[]{:S(2)}) collective-permute-start(bf16[128,2048]{1,0:T(8,128)(2,1)S(1)} %slice.748), channel_id=1, source_target_pairs={{0,1},{1,0},{2,3},{3,2},{4,5},{5,4},{6,7},{7,6},{8,9},{9,8},{10,11... | collective-permute-start | bytes 1572872 | tf_op jit(solution)/shard_map/ppermute | solution.py:41
  667.3 63.8 %collective-permute-start.77 = (bf16[128,2048]{1,0:T(8,128)(2,1)}, bf16[128,2048]{1,0:T(8,128)(2,1)}, u32[]{:S(2)}, u32[]{:S(2)}) collective-permute-start(bf16[128,2048]{1,0:T(8,128)(2,1)} %slice.749), channel_id=1, source_target_pairs={{0,16},{8,24},{16,0},{24,8},{1,17},{9,25},{17,1},{25,9},{2,18},{10... | collective-permute-start | bytes 1572872 | tf_op jit(solution)/shard_map/ppermute | solution.py:41
  668.7 63.8 %collective-permute-start.74 = (bf16[128,2048]{1,0:T(8,128)(2,1)}, bf16[128,2048]{1,0:T(8,128)(2,1)}, u32[]{:S(2)}, u32[]{:S(2)}) collective-permute-start(bf16[128,2048]{1,0:T(8,128)(2,1)} %fusion.201), channel_id=1, source_target_pairs={{0,16},{8,24},{16,0},{24,8},{1,17},{9,25},{17,1},{25,9},{2,18},{10... | collective-permute-start | bytes 1572872 | tf_op jit(solution)/shard_map/ppermute | solution.py:41
  669.3 64.7 %collective-permute-start.76 = (bf16[128,2048]{1,0:T(8,128)(2,1)}, bf16[128,2048]{1,0:T(8,128)(2,1)}, u32[]{:S(2)}, u32[]{:S(2)}) collective-permute-start(bf16[128,2048]{1,0:T(8,128)(2,1)} %fusion.198), channel_id=1, source_target_pairs={{0,1},{1,0},{2,3},{3,2},{4,5},{5,4},{6,7},{7,6},{8,9},{9,8},{10,11... | collective-permute-start | bytes 1572872 | tf_op jit(solution)/shard_map/ppermute | solution.py:41
  713.0 29.4 %collective-permute-start.103 = (bf16[256,256]{1,0:T(8,128)(2,1)}, bf16[256,256]{1,0:T(8,128)(2,1)}, u32[]{:S(2)}, u32[]{:S(2)}) collective-permute-start(bf16[256,256]{1,0:T(8,128)(2,1)} %get-tuple-element.194), channel_id=1, source_target_pairs={{0,25},{1,24},{8,17},{9,16},{16,9},{17,8},{24,1},{25,0},{2,27},{3,... | collective-permute-start | bytes 393224 | tf_op jit(solution)/shard_map/ppermute | solution.py:51
  750.3 73.8 %collective-permute-start.155 = (bf16[4,128,1024]{2,1,0:T(8,128)(2,1)}, bf16[4,128,1024]{2,1,0:T(8,128)(2,1)}, u32[]{:S(2)}, u32[]{:S(2)}) collective-permute-start(bf16[4,128,1024]{2,1,0:T(8,128)(2,1)} %get-tuple-element.100), channel_id=1, source_target_pairs={{4,2},{6,4},{5,3},{7,5},{12,10},{14,12},{13,11},{15,13},{20,18},{2... | collective-permute-start | bytes 3145736 | tf_op jit(solution)/shard_map/ppermute | solution.py:103
  751.9 66.8 %collective-permute-start.165 = (bf16[256,2048]{1,0:T(8,128)(2,1)}, bf16[256,2048]{1,0:T(8,128)(2,1)}, u32[]{:S(2)}, u32[]{:S(2)}) collective-permute-start(bf16[256,2048]{1,0:T(8,128)(2,1)} %get-tuple-element.96), channel_id=1, source_target_pairs={{4,2},{6,4},{5,3},{7,5},{12,10},{14,12},{13,11},{15,13},{20,18},{2... | collective-permute-start | bytes 3145736 | tf_op jit(solution)/shard_map/ppermute | solution.py:103
  755.0 72.1 %collective-permute-start.133 = (bf16[512,1024]{1,0:T(8,128)(2,1)}, bf16[512,1024]{1,0:T(8,128)(2,1)}, u32[]{:S(2)}, u32[]{:S(2)}) collective-permute-start(bf16[512,1024]{1,0:T(8,128)(2,1)} %get-tuple-element.91), channel_id=1, source_target_pairs={{0,8},{8,0},{16,24},{24,16},{1,9},{9,1},{17,25},{25,17},{2,10},{10... | collective-permute-start | bytes 3145736 | tf_op jit(solution)/shard_map/ppermute | solution.py:41
  755.5 38.6 %collective-permute-start.147 = (f32[16,1024]{1,0:T(8,128)S(1)}, f32[16,1024]{1,0:T(8,128)S(1)}, u32[]{:S(2)}, u32[]{:S(2)}) collective-permute-start(f32[16,1024]{1,0:T(8,128)S(1)} %add.711), channel_id=1, source_target_pairs={{0,16},{8,24},{16,0},{24,8},{1,17},{9,25},{17,1},{25,9},{2,18},{10... | collective-permute-start | bytes 196616 | tf_op jit(solution)/shard_map/ppermute | solution.py:41
  827.1 59.8 %collective-permute-start.153 = (bf16[4,128,1024]{2,1,0:T(8,128)(2,1)}, bf16[4,128,1024]{2,1,0:T(8,128)(2,1)}, u32[]{:S(2)}, u32[]{:S(2)}) collective-permute-start(bf16[4,128,1024]{2,1,0:T(8,128)(2,1)} %get-tuple-element.99), channel_id=1, source_target_pairs={{0,2},{2,4},{4,6},{1,3},{3,5},{5,7},{8,10},{10,12},{12,14},{9,11},... | collective-permute-start | bytes 3145736 | tf_op jit(solution)/shard_map/ppermute | solution.py:102
  843.2 35.0 %collective-permute-start.122 = (bf16[4,128,768]{2,1,0:T(8,128)(2,1)S(1)}, bf16[4,128,768]{2,1,0:T(8,128)(2,1)S(1)}, u32[]{:S(2)}, u32[]{:S(2)}) collective-permute-start(bf16[4,128,768]{2,1,0:T(8,128)(2,1)S(1)} %copy-done.105), channel_id=1, source_target_pairs={{6,4},{7,5},{14,12},{15,13},{22,20},{23,21},{30,28},{31,29}} | collective-permute-start | bytes 2359304 | tf_op jit(solution)/shard_map/ppermute | solution.py:103
  845.7 38.8 %collective-permute-start.120 = (bf16[4,128,768]{2,1,0:T(8,128)(2,1)S(1)}, bf16[4,128,768]{2,1,0:T(8,128)(2,1)S(1)}, u32[]{:S(2)}, u32[]{:S(2)}) collective-permute-start(bf16[4,128,768]{2,1,0:T(8,128)(2,1)S(1)} %copy-done.102), channel_id=1, source_target_pairs={{0,2},{2,4},{1,3},{3,5},{8,10},{10,12},{9,11},{11,13},{16,18},{18,... | collective-permute-start | bytes 2359304 | tf_op jit(solution)/shard_map/ppermute | solution.py:102
  878.2 29.8 %collective-permute-start.163 = (bf16[256,2048]{1,0:T(8,128)(2,1)S(1)}, bf16[256,2048]{1,0:T(8,128)(2,1)S(1)}, u32[]{:S(2)}, u32[]{:S(2)}) collective-permute-start(bf16[256,2048]{1,0:T(8,128)(2,1)S(1)} %copy-done.93), channel_id=1, source_target_pairs={{0,2},{2,4},{4,6},{1,3},{3,5},{5,7},{8,10},{10,12},{12,14},{9,11},... | collective-permute-start | bytes 3145736 | tf_op jit(solution)/shard_map/ppermute | solution.py:102
  883.1 41.5 %collective-permute-start.166 = (bf16[256,2048]{1,0:T(8,128)(2,1)S(1)}, bf16[256,2048]{1,0:T(8,128)(2,1)S(1)}, u32[]{:S(2)}, u32[]{:S(2)}) collective-permute-start(bf16[256,2048]{1,0:T(8,128)(2,1)S(1)} %copy-done.88), channel_id=1, source_target_pairs={{2,0},{4,2},{6,4},{3,1},{5,3},{7,5},{10,8},{12,10},{14,12},{11,9},... | collective-permute-start | bytes 3145736 | tf_op jit(solution)/shard_map/ppermute | solution.py:103
  884.5 42.1 %collective-permute-start.131 = (bf16[256,1024]{1,0:T(8,128)(2,1)S(1)}, bf16[256,1024]{1,0:T(8,128)(2,1)S(1)}, u32[]{:S(2)}, u32[]{:S(2)}) collective-permute-start(bf16[256,1024]{1,0:T(8,128)(2,1)S(1)} %slice.744), channel_id=1, source_target_pairs={{0,1},{1,0},{2,3},{3,2},{4,5},{5,4},{6,7},{7,6},{8,9},{9,8},{10,11... | collective-permute-start | bytes 1572872 | tf_op jit(solution)/shard_map/ppermute | solution.py:41
  886.9 40.3 %collective-permute-start.138 = (bf16[256,1024]{1,0:T(8,128)(2,1)S(1)}, bf16[256,1024]{1,0:T(8,128)(2,1)S(1)}, u32[]{:S(2)}, u32[]{:S(2)}) collective-permute-start(bf16[256,1024]{1,0:T(8,128)(2,1)S(1)} %slice.743), channel_id=1, source_target_pairs={{0,16},{8,24},{16,0},{24,8},{1,17},{9,25},{17,1},{25,9},{2,18},{10... | collective-permute-start | bytes 1572872 | tf_op jit(solution)/shard_map/ppermute | solution.py:41
  904.6 38.8 %collective-permute-start.106 = (bf16[128,2048]{1,0:T(8,128)(2,1)S(1)}, bf16[128,2048]{1,0:T(8,128)(2,1)S(1)}, u32[]{:S(2)}, u32[]{:S(2)}) collective-permute-start(bf16[128,2048]{1,0:T(8,128)(2,1)S(1)} %slice.746), channel_id=1, source_target_pairs={{0,1},{1,0},{2,3},{3,2},{4,5},{5,4},{6,7},{7,6},{8,9},{9,8},{10,11... | collective-permute-start | bytes 1572872 | tf_op jit(solution)/shard_map/ppermute | solution.py:41
  939.4 78.1 %collective-permute-start.123 = (bf16[4,128,768]{2,1,0:T(8,128)(2,1)}, bf16[4,128,768]{2,1,0:T(8,128)(2,1)}, u32[]{:S(2)}, u32[]{:S(2)}) collective-permute-start(bf16[4,128,768]{2,1,0:T(8,128)(2,1)} %get-tuple-element.104), channel_id=1, source_target_pairs={{4,2},{6,4},{5,3},{7,5},{12,10},{14,12},{13,11},{15,13},{20,18},{2... | collective-permute-start | bytes 2359304 | tf_op jit(solution)/shard_map/ppermute | solution.py:103
  943.5 36.2 %collective-permute-start.157 = (bf16[128,1024]{1,0:T(8,128)(2,1)}, bf16[128,1024]{1,0:T(8,128)(2,1)}, u32[]{:S(2)}, u32[]{:S(2)}) collective-permute-start(bf16[128,1024]{1,0:T(8,128)(2,1)} %get-tuple-element.135), channel_id=1, source_target_pairs={{0,24},{8,16},{16,8},{24,0},{1,25},{9,17},{17,9},{25,1},{2,26},{10... | collective-permute-start | bytes 786440 | tf_op jit(solution)/shard_map/ppermute | solution.py:41
  943.5 36.3 %collective-permute-start.158 = (bf16[128,1024]{1,0:T(8,128)(2,1)}, bf16[128,1024]{1,0:T(8,128)(2,1)}, u32[]{:S(2)}, u32[]{:S(2)}) collective-permute-start(bf16[128,1024]{1,0:T(8,128)(2,1)} %get-tuple-element.134), channel_id=1, source_target_pairs={{0,16},{8,24},{16,0},{24,8},{1,17},{9,25},{17,1},{25,9},{2,18},{10... | collective-permute-start | bytes 786440 | tf_op jit(solution)/shard_map/ppermute | solution.py:41
  951.3 30.5 %collective-permute-start.159 = (bf16[128,1024]{1,0:T(8,128)(2,1)S(1)}, bf16[128,1024]{1,0:T(8,128)(2,1)}, u32[]{:S(2)}, u32[]{:S(2)}) collective-permute-start(bf16[128,1024]{1,0:T(8,128)(2,1)S(1)} %get-tuple-element.133), channel_id=1, source_target_pairs={{0,8},{8,0},{16,24},{24,16},{1,9},{9,1},{17,25},{25,17},{2,10},{10... | collective-permute-start | bytes 786440 | tf_op jit(solution)/shard_map/ppermute | solution.py:41
  976.1 60.5 %collective-permute-start.121 = (bf16[4,128,768]{2,1,0:T(8,128)(2,1)S(1)}, bf16[4,128,768]{2,1,0:T(8,128)(2,1)S(1)}, u32[]{:S(2)}, u32[]{:S(2)}) collective-permute-start(bf16[4,128,768]{2,1,0:T(8,128)(2,1)S(1)} %copy-done.101), channel_id=1, source_target_pairs={{0,2},{2,4},{4,6},{1,3},{3,5},{5,7},{8,10},{10,12},{12,14},{9,11},... | collective-permute-start | bytes 2359304 | tf_op jit(solution)/shard_map/ppermute | solution.py:102
  979.7 52.7 %collective-permute-start.167 = (bf16[256,2048]{1,0:T(8,128)(2,1)S(1)}, bf16[256,2048]{1,0:T(8,128)(2,1)S(1)}, u32[]{:S(2)}, u32[]{:S(2)}) collective-permute-start(bf16[256,2048]{1,0:T(8,128)(2,1)S(1)} %copy-done.27), channel_id=1, source_target_pairs={{0,1},{1,0},{2,3},{3,2},{4,5},{5,4},{6,7},{7,6},{8,9},{9,8},{10,11... | collective-permute-start | bytes 3145736 | tf_op jit(solution)/shard_map/ppermute | solution.py:41
  1013.3 41.4 %collective-permute-start.160 = (bf16[4,128,1024]{2,1,0:T(8,128)(2,1)S(1)}, bf16[4,128,1024]{2,1,0:T(8,128)(2,1)S(1)}, u32[]{:S(2)}, u32[]{:S(2)}) collective-permute-start(bf16[4,128,1024]{2,1,0:T(8,128)(2,1)S(1)} %pad_maximum_fusion.9), channel_id=1, source_target_pairs={{0,1},{1,0},{2,3},{3,2},{4,5},{5,4},{6,7},{7,6},{8,9},{9,8},{10,11... | collective-permute-start | bytes 3145736 | tf_op jit(solution)/shard_map/ppermute | solution.py:41
  (274 other events, 4085.6 us)

commit v2 on v1

v2 whole, which is shorter than its diff:
```python
import jax
import jax.numpy as jnp
from jax import lax
from jax.experimental import pallas as pl
from jax.experimental.pallas import tpu as pltpu
from jax.sharding import PartitionSpec as P

HEAD_DIM = 128
bf16 = jnp.bfloat16
fp32 = jnp.float32

CORE = ("seq", 1)
ROW = ("seq", 2)
COL = ("replica", 1)


PARTS = ((0, 2, 4), (1, 3, 5), (6,), (7,))
ACROSS = (((1,), (1,)), ((), ()))
DOWN = (((0,), (0,)), ((), ()))
WHOLE = pl.BlockSpec(memory_space=pltpu.VMEM)
SCALARS = pl.BlockSpec(memory_space=pltpu.SMEM)


def place(j):
    return next((i, part.index(j)) for i, part in enumerate(PARTS) if j in part)


def gelu_slope(values):
    normal_cdf = 0.5 * (1.0 + lax.erf(values * 0.7071067811865476))
    return normal_cdf + values * jnp.exp(-0.5 * values * values) * 0.3989422804014327


def after(v, *others):
    return lax.optimization_barrier((v, others))[0]


def flip(v, link):
    axis, bit = link
    return lax.ppermute(v, axis, [(i, i ^ bit) for i in range(lax.axis_size(axis))])


def plane_gather(v):
    h = v.shape[0] // 2
    py, px = flip(v, ROW), flip(v, COL)
    first = jnp.concatenate([v, py, px])
    da, db = flip(py[:h], COL), flip(px[h:], ROW)
    second = jnp.concatenate([da, db])
    return first, flip(first, CORE), second, flip(second, CORE)


def relay_kernel(y_ref, gy_ref, x_ref, gx_ref, ra_ref, rb_ref, ys_ref, xs_ref):
    h = ra_ref.shape[0]
    top, bot = slice(0, h), slice(h, 2 * h)
    ys_ref[top, :] = (
        y_ref[top, :].astype(fp32) + gy_ref[top, :].astype(fp32) + ra_ref[...].astype(fp32)
    ).astype(bf16)
    ys_ref[bot, :] = (y_ref[bot, :].astype(fp32) + gy_ref[bot, :].astype(fp32)).astype(bf16)
    xs_ref[top, :] = (x_ref[top, :].astype(fp32) + gx_ref[top, :].astype(fp32)).astype(bf16)
    xs_ref[bot, :] = (
        x_ref[bot, :].astype(fp32) + gx_ref[bot, :].astype(fp32) + rb_ref[...].astype(fp32)
    ).astype(bf16)


def plane_scatter(parts):
    mine, theirs, far, far_theirs = parts
    n, width = far.shape
    h = n // 2
    far_got = flip(far_theirs, CORE)
    got = flip(theirs, CORE)
    far = (far.astype(fp32) + far_got.astype(fp32)).astype(bf16)
    ra, rb = flip(far[:h], COL), flip(far[h:], ROW)

    def rows(i):
        return pl.BlockSpec((n, width), lambda g: (i, 0))

    half = pl.BlockSpec((h, width), lambda g: (0, 0))
    y_send, x_send = pl.pallas_call(
        relay_kernel,
        grid=(1,),
        in_specs=[rows(1), rows(1), rows(2), rows(2), half, half],
        out_specs=[rows(0), rows(0)],
        out_shape=[jax.ShapeDtypeStruct((n, width), bf16)] * 2,
        compiler_params=pltpu.CompilerParams(vmem_limit_bytes=40 * 2**20),
        cost_estimate=pl.CostEstimate(flops=6 * n * width, bytes_accessed=14 * n * width, transcendentals=0),
    )(mine, got, mine, got, ra, rb)
    return mine, got, flip(y_send, ROW), flip(x_send, COL)


def line_gather(v):
    return lax.all_gather(v, "shard", axis=0, tiled=True)


def line_scatter(v):
    return lax.psum_scatter(v, "shard", scatter_dimension=0, tiled=True)


def in_order(pieces, index):
    bit = 1
    while bit < len(pieces):
        odd = (index & bit) != 0
        pieces = [jnp.where(odd, pieces[j ^ bit], pieces[j]) for j in range(len(pieces))]
        bit *= 2
    return jnp.stack(pieces)


def seq_exchange(v):
    S, s = lax.axis_size("seq"), lax.axis_index("seq")
    pieces = [lax.dynamic_index_in_dim(v, s ^ j, 0, keepdims=False) for j in range(S)]
    got = [flip(v, ("seq", j)) if j else v for j, v in enumerate(pieces)]
    return in_order(got, s)


def gather_table(v):
    table = v[None]
    for axis in ("shard", "seq"):
        index, bit = lax.axis_index(axis), 1
        while bit < lax.axis_size(axis):
            other = flip(table, (axis, bit))
            odd = (index & bit) != 0
            table = jnp.concatenate([jnp.where(odd, other, table), jnp.where(odd, table, other)])
            bit *= 2
    return table


def total(v):
    for axis in ("seq", "replica", "shard"):
        bit = 1
        while bit < lax.axis_size(axis):
            v = v + flip(v, (axis, bit))
            bit *= 2
    return v


def row_loop(n):
    step = 32 if n % 32 == 0 else n
    return pl.loop(0, n, step=step), step


def statistics(v):
    centred = v - jnp.mean(v, axis=1, keepdims=True)
    scale = lax.rsqrt(jnp.mean(centred * centred, axis=1, keepdims=True) + 1e-05)
    return centred * scale, scale


def norm_back(grad, normed, scale):
    first = jnp.mean(grad, axis=1, keepdims=True)
    second = jnp.mean(grad * normed, axis=1, keepdims=True)
    return scale * (grad - first - normed * second)


def transposed_columns(v, grid, rows):
    a, b = grid
    if rows % 128 or a == 1 or b == 1:
        return v
    return jnp.concatenate(
        [v[:, (i * b + k) * rows : (i * b + k + 1) * rows] for k in range(b) for i in range(a)], axis=1
    )


def norm_kernel(grid, rows, x_ref, gain_ref, shift_ref, out_ref):
    loop, step = row_loop(x_ref.shape[0])

    @loop
    def _(i):
        at = pl.ds(pl.multiple_of(i, step), step)
        normed, _ = statistics(x_ref[at, :].astype(fp32))
        hidden = (normed * gain_ref[...] + shift_ref[...]).astype(bf16)
        out_ref[at, :] = transposed_columns(hidden, grid, rows)


def mid_kernel(
    grid, rows, own_ref, att_ref, a_ref, b_ref, c_ref, d_ref, x_ref, bias_ref, gain_ref, shift_ref,
    mid_ref, hidden_ref, rel_ref,
):
    S = grid[0]
    T, n, hw = att_ref.shape
    R = T // S
    s, r = own_ref[0], own_ref[1]
    parts = (a_ref, b_ref, c_ref, d_ref)
    deep, wide = d_ref.shape
    for js in range(S):
        for i in range(R):
            rel_ref[:, (js * R + i) * hw : (js * R + i + 1) * hw] = att_ref[(s ^ js) * R + i]
    for jr in range(R):
        acc = jnp.zeros((n, wide), fp32)
        for js in range(S):
            part, k = place(js + 4 * jr)
            acc += jnp.dot(
                rel_ref[:, js * deep : (js + 1) * deep],
                parts[part][k * deep : (k + 1) * deep, :],
                preferred_element_type=fp32,
            )
        mid_ref[:, pl.ds(pl.multiple_of((r ^ jr) * wide, 128), wide)] = acc
    loop, step = row_loop(n)

    @loop
    def _(i):
        at = pl.ds(pl.multiple_of(i, step), step)
        mid = x_ref[at, :].astype(fp32) + (mid_ref[at, :] + bias_ref[...])
        mid_ref[at, :] = mid
        normed, _ = statistics(mid)
        hidden = (normed * gain_ref[...] + shift_ref[...]).astype(bf16)
        hidden_ref[at, :] = transposed_columns(hidden, grid, rows)


def back_mid_kernel(
    grid, rows, own_ref, p_ref, q_ref, u_ref, w_ref, mid_ref, g_ref, gain_ref, a_ref, b_ref, c_ref, d_ref,
    grad_ref, rel_ref, att_ref, sums_ref,
):
    S = grid[0]
    T, n, hw = att_ref.shape
    R = T // S
    s, r = own_ref[0], own_ref[1]
    parts = (a_ref, b_ref, c_ref, d_ref)
    deep, wide = d_ref.shape
    sums_ref[...] = jnp.zeros_like(sums_ref)
    loop, step = row_loop(n)

    @loop
    def _(i):
        at = pl.ds(pl.multiple_of(i, step), step)
        grad = p_ref[at, :].astype(fp32) + q_ref[at, :].astype(fp32)
        grad += u_ref[at, :].astype(fp32) + w_ref[at, :].astype(fp32)
        grad = transposed_columns(grad, grid[::-1], rows)
        normed, scale = statistics(mid_ref[at, :])
        g = g_ref[at, :].astype(fp32)
        sums_ref[0:1, :] += jnp.sum(grad * normed, axis=0, keepdims=True)
        sums_ref[1:2, :] += jnp.sum(grad, axis=0, keepdims=True)
        grad_mid = g + norm_back(grad * gain_ref[...], normed, scale)
        grad_ref[at, :] = grad_mid
        low = grad_mid.astype(bf16)
        sums_ref[2:3, :] += jnp.sum(low.astype(fp32), axis=0, keepdims=True)
        sums_ref[3:4, :] += jnp.sum(g, axis=0, keepdims=True)
        for k in range(R):
            rel_ref[at, pl.ds(pl.multiple_of((r ^ k) * wide, 128), wide)] = low[:, k * wide : (k + 1) * wide]

    for js in range(S):
        acc = jnp.zeros((n, deep), fp32)
        for jr in range(R):
            part, k = place(js + 4 * jr)
            acc += lax.dot_general(
                rel_ref[:, jr * wide : (jr + 1) * wide],
                parts[part][k * deep : (k + 1) * deep, :],
                ACROSS,
                preferred_element_type=fp32,
            )
        for i in range(R):
            att_ref[(s ^ js) * R + i] = acc[:, i * hw : (i + 1) * hw].astype(bf16)


def back_in_kernel(grid, rows, p_ref, q_ref, u_ref, w_ref, x_ref, g_ref, gain_ref, out_ref, sums_ref):
    sums_ref[...] = jnp.zeros_like(sums_ref)
    loop, step = row_loop(x_ref.shape[0])

    @loop
    def _(i):
        at = pl.ds(pl.multiple_of(i, step), step)
        grad = p_ref[at, :].astype(fp32) + q_ref[at, :].astype(fp32)
        grad += u_ref[at, :].astype(fp32) + w_ref[at, :].astype(fp32)
        grad = transposed_columns(grad, grid[::-1], rows)
        normed, scale = statistics(x_ref[at, :].astype(fp32))
        sums_ref[0:1, :] += jnp.sum(grad * normed, axis=0, keepdims=True)
        sums_ref[1:2, :] += jnp.sum(grad, axis=0, keepdims=True)
        out_ref[at, :] = g_ref[at, :] + norm_back(grad * gain_ref[...], normed, scale)


def out_kernel(p_ref, q_ref, u_ref, w_ref, mid_ref, bias_ref, out_ref):
    loop, step = row_loop(mid_ref.shape[0])

    @loop
    def _(i):
        at = pl.ds(pl.multiple_of(i, step), step)
        term = p_ref[at, :].astype(fp32) + q_ref[at, :].astype(fp32)
        term += u_ref[at, :].astype(fp32) + w_ref[at, :].astype(fp32)
        out_ref[at, :] = (mid_ref[at, :] + (term + bias_ref[...])).astype(bf16)


def outer_kernel(rel_ref, low_ref, *outs):
    deep, wide = outs[3].shape
    for out_ref, part in zip(outs, PARTS):
        for k, j in enumerate(part):
            js, jr = j & 3, j >> 2
            out_ref[k * deep : (k + 1) * deep, :] = lax.dot_general(
                rel_ref[:, js * deep : (js + 1) * deep],
                low_ref[:, jr * wide : (jr + 1) * wide],
                DOWN,
                preferred_element_type=fp32,
            ).astype(bf16)


def tall_kernel(*refs):
    half = len(refs) // 2
    acc = 0.0
    for left, right in zip(refs[:half], refs[half:-1]):
        acc += lax.dot_general(left[...], right[...], DOWN, preferred_element_type=fp32)
    refs[-1][...] = acc.astype(bf16)


def tall_product(lefts, rights):
    deep, wide = lefts[0].shape[1], rights[0].shape[1]
    tokens = sum(v.shape[0] for v in lefts)
    tile = min(256, deep)
    return pl.pallas_call(
        tall_kernel,
        grid=(deep // tile,),
        in_specs=[pl.BlockSpec((v.shape[0], tile), lambda i: (0, i)) for v in lefts]
        + [pl.BlockSpec(v.shape, lambda i: (0, 0)) for v in rights],
        out_specs=pl.BlockSpec((tile, wide), lambda i: (i, 0)),
        out_shape=jax.ShapeDtypeStruct((deep, wide), bf16),
        compiler_params=pltpu.CompilerParams(vmem_limit_bytes=48 * 2**20),
        cost_estimate=pl.CostEstimate(
            flops=2 * tokens * deep * wide,
            bytes_accessed=2 * (tokens * (deep + wide) + deep * wide),
            transcendentals=0,
        ),
    )(*lefts, *rights)


def attend_kernel(heads, own_ref, a_ref, b_ref, c_ref, d_ref, out_ref, q_ref, k_ref, v_ref):
    s, r = own_ref[0], own_ref[1]
    T, n, width = out_ref.shape
    S = q_ref.shape[0] // n
    parts = (a_ref, b_ref, c_ref, d_ref)
    for jr in range(T // S):
        for h in range(heads):
            cols = slice(h * HEAD_DIM, (h + 1) * HEAD_DIM)
            for js in range(S):
                part, k = place(js + 4 * jr)
                at = pl.ds(pl.multiple_of((s ^ js) * n, n), n)
                for i, ref in enumerate((q_ref, k_ref, v_ref)):
                    first = i * width + h * HEAD_DIM
                    ref[at, :] = parts[part][k * n : (k + 1) * n, first : first + HEAD_DIM]
            for a in range(S):
                upto = (a + 1) * n
                q = q_ref[a * n : upto, :]
                scores = lax.dot_general(q, k_ref[:upto, :], ACROSS, preferred_element_type=fp32)
                scores = scores * HEAD_DIM ** (-0.5)
                expons = jnp.exp(scores - jnp.max(scores, axis=-1, keepdims=True))
                probs = (expons / jnp.sum(expons, axis=-1, keepdims=True)).astype(bf16)
                out_ref[a * (T // S) + (r ^ jr), :, cols] = jnp.dot(
                    probs, v_ref[:upto, :], preferred_element_type=fp32
                ).astype(bf16)


def attend_back_kernel(
    heads, own_ref, a_ref, b_ref, c_ref, d_ref, grad_ref, oa_ref, ob_ref, oc_ref, od_ref, sums_ref,
    q_ref, k_ref, v_ref, gq_ref, gk_ref, gv_ref,
):
    s, r = own_ref[0], own_ref[1]
    T, n, width = grad_ref.shape
    S = q_ref.shape[0] // n
    parts = (a_ref, b_ref, c_ref, d_ref)
    outs = (oa_ref, ob_ref, oc_ref, od_ref)
    scaling = HEAD_DIM ** (-0.5)
    sums_ref[...] = jnp.zeros_like(sums_ref)
    for jr in range(T // S):
        for h in range(heads):
            cols = slice(h * HEAD_DIM, (h + 1) * HEAD_DIM)
            for js in range(S):
                part, k = place(js + 4 * jr)
                at = pl.ds(pl.multiple_of((s ^ js) * n, n), n)
                for i, ref in enumerate((q_ref, k_ref, v_ref)):
                    first = i * width + h * HEAD_DIM
                    ref[at, :] = parts[part][k * n : (k + 1) * n, first : first + HEAD_DIM]
            for a in reversed(range(S)):
                upto = (a + 1) * n
                q = q_ref[a * n : upto, :]
                g = grad_ref[a * (T // S) + (r ^ jr), :, cols]
                k = k_ref[:upto, :]
                v = v_ref[:upto, :]
                scores = lax.dot_general(q, k, ACROSS, preferred_element_type=fp32) * scaling
                expons = jnp.exp(scores - jnp.max(scores, axis=-1, keepdims=True))
                probs = expons / jnp.sum(expons, axis=-1, keepdims=True)
                grad_probs = lax.dot_general(g, v, ACROSS, preferred_element_type=fp32)
                inner = jnp.sum(probs * grad_probs, axis=-1, keepdims=True)
                grad_scores = (probs * (grad_probs - inner)).astype(bf16)
                gq_ref[a * n : upto, :] = jnp.dot(grad_scores, k, preferred_element_type=fp32)
                gk = lax.dot_general(grad_scores, q, DOWN, preferred_element_type=fp32)
                gv = lax.dot_general(probs.astype(bf16), g, DOWN, preferred_element_type=fp32)
                if a == S - 1:
                    gk_ref[...] = gk
                    gv_ref[...] = gv
                else:
                    gk_ref[:upto, :] += gk
                    gv_ref[:upto, :] += gv
            for js in range(S):
                part, k = place(js + 4 * jr)
                at = pl.ds(pl.multiple_of((s ^ js) * n, n), n)
                for i, (ref, factor) in enumerate(((gq_ref, scaling), (gk_ref, scaling), (gv_ref, 1.0))):
                    first = i * width + h * HEAD_DIM
                    low = (ref[at, :] * factor).astype(bf16)
                    outs[part][k * n : (k + 1) * n, first : first + HEAD_DIM] = low
                    sums_ref[0:1, first : first + HEAD_DIM] += jnp.sum(low.astype(fp32), axis=0, keepdims=True)


def small_call(kernel, out_shape, operands, scratch=(), flops=0, first_rows=()):
    specs = []
    for i, v in enumerate(operands):
        if v.dtype == jnp.int32:
            specs.append(SCALARS)
        elif dict(first_rows).get(i, v.shape[0]) != v.shape[0]:
            specs.append(pl.BlockSpec((dict(first_rows)[i], v.shape[1]), lambda g: (0, 0)))
        else:
            specs.append(pl.BlockSpec(v.shape, lambda g, rank=v.ndim: (0,) * rank))
    many = isinstance(out_shape, list)
    outs = out_shape if many else [out_shape]
    out_specs = [pl.BlockSpec(v.shape, lambda g, rank=len(v.shape): (0,) * rank) for v in outs]
    moved = sum(v.size * v.dtype.itemsize for v in operands) + sum(
        v.size * jnp.dtype(v.dtype).itemsize for v in outs
    )
    return pl.pallas_call(
        kernel,
        grid=(1,),
        in_specs=specs,
        out_specs=out_specs if many else out_specs[0],
        out_shape=out_shape,
        scratch_shapes=scratch,
        compiler_params=pltpu.CompilerParams(vmem_limit_bytes=56 * 2**20),
        cost_estimate=pl.CostEstimate(flops=flops, bytes_accessed=moved, transcendentals=0),
    )(*operands)


def on_device(
    inputs,
    cotangent,
    norm1_gain,
    norm1_bias,
    w_qkv,
    query_bias,
    value_bias,
    w_attn_out,
    attn_out_bias,
    norm2_gain,
    norm2_bias,
    w_hidden,
    hidden_bias,
    w_output,
    output_bias,
):
    S, Z, R = lax.axis_size("seq"), lax.axis_size("shard"), lax.axis_size("replica")
    s, z, r = lax.axis_index("seq"), lax.axis_index("shard"), lax.axis_index("replica")
    odd = r != 0
    _, n, D = inputs.shape
    rows = norm1_gain.shape[0]
    F = hidden_bias.shape[0] * S * Z
    T = S * R
    hw = D // T
    fw = F // T
    fr = fw // Z
    heads = hw // HEAD_DIM
    grid = (S, Z)
    own = jnp.stack([s, r]).astype(jnp.int32)

    def shape(*dims, kind=bf16):
        return jax.ShapeDtypeStruct(dims, kind)

    def by_shard(v):
        return v if rows % 128 == 0 else v.reshape(-1, S, Z, rows).swapaxes(1, 2).reshape(-1, D)

    def by_seq(v):
        return v if rows % 128 == 0 else v.reshape(-1, Z, S, rows).swapaxes(1, 2).reshape(-1, D)

    t = s * R + r
    attn_part = lax.dynamic_index_in_dim(w_attn_out.reshape(rows, R, D // R), r, 1, keepdims=False).astype(bf16)
    attn_part = line_gather(attn_part)
    qkv_pieces = lax.dynamic_index_in_dim(w_qkv.reshape(rows, 3, S, R, hw), r, 3, keepdims=False).astype(bf16)
    qkv_rows = seq_exchange(qkv_pieces.transpose(2, 0, 1, 3).reshape(S, rows, 3 * hw)).reshape(S * rows, 3 * hw)
    qkv_matrix = line_gather(qkv_rows)
    hidden_pieces = lax.dynamic_index_in_dim(w_hidden.reshape(rows, S, Z, R, fr), r, 3, keepdims=False).astype(bf16)
    hidden_pieces = after(hidden_pieces.transpose(1, 0, 2, 3).reshape(S, rows, fw), qkv_rows)
    hidden_rows = seq_exchange(hidden_pieces).reshape(S * rows, fw)
    hidden_matrix = line_gather(hidden_rows)
    output_part = lax.dynamic_index_in_dim(w_output.reshape(R, fr, D), r, 0, keepdims=False).astype(bf16)
    output_matrix = line_gather(after(output_part, hidden_rows))

    small = (norm1_gain, norm1_bias, query_bias, value_bias, attn_out_bias, norm2_gain, norm2_bias, output_bias, hidden_bias)
    table = gather_table(jnp.concatenate([v.astype(bf16) for v in small])).astype(fp32)
    gain_one, shift_one, query_shift, value_shift, attn_shift, gain_two, shift_two, output_shift = (
        table[:, i * rows : (i + 1) * rows].reshape(1, D) for i in range(8)
    )
    hidden_shift = lax.dynamic_index_in_dim(
        lax.dynamic_index_in_dim(table[:, 8 * rows :].reshape(S, Z, R, fr), s, 0, keepdims=False), r, 1, keepdims=False
    ).reshape(fw)
    bias_row = jnp.concatenate(
        [
            lax.dynamic_slice_in_dim(query_shift[0], t * hw, hw),
            jnp.zeros((hw,), fp32),
            lax.dynamic_slice_in_dim(value_shift[0], t * hw, hw),
        ]
    )

    x = inputs.reshape(n, D)
    g_low = cotangent.reshape(n, D)
    hidden_in = small_call(
        lambda *refs: norm_kernel(grid, rows, *refs), shape(n, D), (x, gain_one, shift_one), flops=10 * n * D
    )
    hidden_in_parts = plane_gather(by_shard(hidden_in))
    attn_parts = plane_gather(after(attn_part, hidden_in_parts[2]))
    qkv_parts = [
        (jnp.dot(v, qkv_matrix, preferred_element_type=fp32) + bias_row).astype(bf16) for v in hidden_in_parts
    ]
    half_pairs = R * heads * (S * (S + 1) // 2) * n * n * HEAD_DIM * 2
    head_block = pltpu.VMEM((S * n, HEAD_DIM), bf16)
    head_sums = pltpu.VMEM((S * n, HEAD_DIM), fp32)
    attended = small_call(
        lambda *refs: attend_kernel(heads, *refs),
        shape(T, n, hw),
        (own, *qkv_parts),
        [head_block] * 3,
        flops=2 * half_pairs,
    )
    attended = lax.all_to_all(attended, ("seq", "replica"), 0, 0, tiled=True)
    mid_rows, hidden_two, attended_rel = small_call(
        lambda *refs: mid_kernel(grid, rows, *refs),
        [shape(n, D, kind=fp32), shape(n, D), shape(n, D)],
        (own, attended, *attn_parts, x, attn_shift, gain_two, shift_two),
        flops=2 * n * D * D,
    )

    hidden_two_parts = plane_gather(by_shard(hidden_two))
    g_parts = plane_gather(after(g_low, hidden_two_parts[2]))
    activated_parts, grad_pre_parts, grad_two_parts = [], [], []
    for h2, g in zip(hidden_two_parts, g_parts):
        preactive = jnp.dot(h2, hidden_matrix, preferred_element_type=fp32) + hidden_shift
        activated_parts.append(jax.nn.gelu(preactive, approximate=False).astype(bf16))
        grad_activated = lax.dot_general(g, output_matrix, ACROSS, preferred_element_type=fp32)
        grad_pre = (grad_activated * gelu_slope(preactive)).astype(bf16)
        grad_pre_parts.append(grad_pre)
        grad_two_parts.append(
            lax.dot_general(grad_pre, hidden_matrix, ACROSS, preferred_element_type=fp32).astype(bf16)
        )
    grad_output = line_scatter(tall_product(activated_parts, g_parts))
    grad_two = plane_scatter(grad_two_parts)
    grad_hidden = line_scatter(tall_product(hidden_two_parts, grad_pre_parts))

    first = ((1, n), (2, n))
    grad_mid, grad_mid_rel, grad_heads, sums_two = small_call(
        lambda *refs: back_mid_kernel(grid, rows, *refs),
        [shape(n, D, kind=fp32), shape(n, D), shape(T, n, hw), shape(8, D, kind=fp32)],
        (own, *map(by_seq, grad_two), mid_rows, g_low, gain_two, *attn_parts),
        flops=2 * n * D * D,
        first_rows=first,
    )
    grad_heads = lax.all_to_all(grad_heads, ("seq", "replica"), 0, 0, tiled=True)
    *grad_qkv_parts, sums_qkv = small_call(
        lambda *refs: attend_back_kernel(heads, *refs),
        [shape(v.shape[0], 3 * hw) for v in qkv_parts] + [shape(8, 3 * hw, kind=fp32)],
        (own, *qkv_parts, grad_heads),
        [head_block] * 3 + [head_sums] * 3,
        flops=5 * half_pairs,
    )
    grad_attn_parts = small_call(
        outer_kernel,
        [shape(*v.shape) for v in attn_parts],
        (after(attended_rel, grad_heads), grad_mid_rel),
        flops=2 * n * D * D,
    )
    grad_attn = plane_scatter(grad_attn_parts)
    grad_in_parts = [
        lax.dot_general(v, qkv_matrix, ACROSS, preferred_element_type=fp32).astype(bf16) for v in grad_qkv_parts
    ]
    grad_qkv = line_scatter(tall_product(hidden_in_parts, grad_qkv_parts)).reshape(S, rows, 3 * hw)
    grad_in = plane_scatter(grad_in_parts)
    grad_inputs, sums_one = small_call(
        lambda *refs: back_in_kernel(grid, rows, *refs),
        [shape(n, D, kind=fp32), shape(8, D, kind=fp32)],
        (*map(by_seq, grad_in), x, grad_mid, gain_one),
        flops=20 * n * D,
        first_rows=((0, n), (1, n)),
    )

    out_parts = [
        jnp.dot(after(v, grad_qkv_parts[3]), output_matrix, preferred_element_type=fp32).astype(bf16)
        for v in activated_parts
    ]
    layer_out = small_call(
        out_kernel,
        shape(n, D),
        (*plane_scatter(out_parts), mid_rows, output_shift),
        flops=6 * n * D,
        first_rows=((0, n), (1, n)),
    )

    def both(v):
        other = flip(v, COL)
        return jnp.where(odd, other, v), jnp.where(odd, v, other)

    grad_output_matrix = jnp.concatenate(both(grad_output)).astype(fp32)
    grad_hidden = jnp.stack(both(seq_exchange(grad_hidden.reshape(S, rows, fw)))).reshape(R, S, rows, Z, fr)
    grad_hidden_matrix = grad_hidden.transpose(2, 1, 3, 0, 4).reshape(rows, F).astype(fp32)
    grad_qkv = jnp.stack(both(seq_exchange(grad_qkv))).reshape(R, S, rows, 3, hw)
    grad_qkv_matrix = grad_qkv.transpose(2, 3, 1, 0, 4).reshape(rows, 3 * D).astype(fp32)
    deep = D // S
    p, q, u, w = (v[:deep].astype(fp32) for v in grad_attn)
    grad_attn = line_scatter((p + q + u + w).astype(bf16))
    grad_attn_matrix = jnp.concatenate(both(grad_attn), axis=1).astype(fp32)

    hidden_sums = sum(jnp.sum(v.astype(fp32), axis=0) for v in grad_pre_parts).reshape(1, Z, 1, fr)
    hidden_sums = lax.dynamic_update_slice(jnp.zeros((S, Z, R, fr), fp32), hidden_sums, (s, 0, r, 0))
    none = jnp.zeros((D,), fp32)
    sums = total(
        jnp.concatenate(
            [sums_one[i].reshape(S * Z, rows) for i in range(2)]
            + [
                lax.dynamic_update_slice_in_dim(none, sums_qkv[0, i * hw : (i + 1) * hw], t * hw, 0).reshape(S * Z, rows)
                for i in (0, 2)
            ]
            + [sums_two[i].reshape(S * Z, rows) for i in range(4)]
            + [hidden_sums.reshape(S * Z, R * fr)],
            axis=1,
        )
    )
    sums = lax.dynamic_index_in_dim(sums, s * Z + z, 0, keepdims=False)

    def part(i):
        return sums[i * rows : (i + 1) * rows]

    return (
        layer_out.reshape(inputs.shape),
        grad_inputs.reshape(inputs.shape),
        part(0),
        part(1),
        grad_qkv_matrix,
        part(2),
        part(3),
        grad_attn_matrix,
        part(6),
        part(4),
        part(5),
        grad_hidden_matrix,
        sums[8 * rows :],
        grad_output_matrix,
        part(7),
    )


def solution(mesh):
    tokens = P(("shard", "replica"), "seq", None)
    vector = P(("seq", "shard"))
    matrix = P(("seq", "shard"), None)
    weights = (
        vector,
        vector,
        matrix,
        vector,
        vector,
        matrix,
        vector,
        vector,
        vector,
        matrix,
        vector,
        matrix,
        vector,
    )
    return jax.shard_map(
        on_device,
        mesh=mesh,
        in_specs=(tokens, tokens) + weights,
        out_specs=(tokens, tokens) + weights,
        check_vma=False,
    )
```

time: 1090 us -> 735 us (0.67)
  starting transfers between devices: 264 us -> 70.1 us
  other arithmetic: 127 us -> 22.1 us
  Pallas kernels: 22.5 us -> 122 us
  local copies, waits for them, and re-layouts: 156 us -> 79.2 us
  waiting for transfers between devices: 378 us -> 305 us
  matrix products: 126 us -> 114 us
  between operations: 4.9 us -> 15.8 us
    ppermute x54 -> x0, waiting for transfers between devices: 183 us -> none  [the longest x12 69.6 us: line_scatter(): lax.ppermute(send_up.astype(bf16), 'shard', [(i, i + 1) for i in range(0,...]
    ppermute x54 -> x0, starting transfers between devices: 171 us -> none  [the longest x12 71.7 us: line_gather(): lax.ppermute(up[-1], 'shard', [(i, i + 1) for i in range(k - 1, Z - 1)])]
    pallas_call x2 -> x15, Pallas kernels: 22.5 us -> 122 us  [the longest x8 75.6 us: small_call(): pl.pallas_call(kernel, grid=(1,), in_specs=specs, out_specs=out_specs if...]
    ppermute x114 -> x73, waiting for transfers between devices: 195 us -> 276 us  [flip(): lax.ppermute(v, axis, [(i, i ^ bit) for i in range(lax.axis_size(axis))])]
    convert_element_type x36 -> x7, other arithmetic: 42.8 us -> 9.19 us  [the longest x1 4.04 us: on_device(): grad_attn = line_scatter((p + q + u + w).astype(bf16))]
    ppermute x114 -> x73, starting transfers between devices: 93.1 us -> 62.6 us  [flip(): lax.ppermute(v, axis, [(i, i ^ bit) for i in range(lax.axis_size(axis))])]
    all_to_all x0 -> x2, waiting for transfers between devices: none -> 28.4 us  [the longest x1 14.8 us: on_device(): attended = lax.all_to_all(attended, ('seq', 'replica'), 0, 0, tiled=True)]
    dot_general x22 -> x16, matrix products: 88.8 us -> 63.8 us  [the longest x4 19.8 us: on_device(): jnp.dot(after(v, grad_qkv_parts[3]), output_matrix, preferred_element_typ...]
  transfers between devices with their start and end apart: 168 -> 83, of which waited for: 51 -> 36; matrix products, arithmetic and copies ran while one was open for 36% -> 25% of each run, Pallas kernels for 2% -> 15%
where the time goes in v2:
time: 735 us; the launch traced here: 728 us
  waiting for transfers between devices  305 us (41%)
  Pallas kernels  122 us (17%)
  matrix products  114 us (16%)
  local copies, waits for them, and re-layouts  79.2 us (11%)
  starting transfers between devices  70.1 us (10%)
  other arithmetic  22.1 us (3%)
  between operations  15.8 us (2%)
    ppermute x73, waiting for transfers between devices, flip(): lax.ppermute(v, axis, [(i, i ^ bit) for i in range(lax.axis_size(axis))])  276 us
    pallas_call x8, Pallas kernels, small_call(): pl.pallas_call(kernel, grid=(1,), in_specs=specs, out_specs=out_specs if...  75.6 us
    ppermute x73, starting transfers between devices, flip(): lax.ppermute(v, axis, [(i, i ^ bit) for i in range(lax.axis_size(axis))])  62.6 us
    unnamed x175, local copies, waits for them, and re-layouts  49.1 us
    pallas_call x3, Pallas kernels, tall_product(): pl.pallas_call(tall_kernel, grid=(deep // tile,), in_specs=[pl.BlockSpec(...  38.1 us
    dot_general x4, matrix products, on_device(): jnp.dot(h2, hidden_matrix, preferred_element_type=fp32) + hidden_shift  36.5 us
    dot_general x4, matrix products, on_device(): jnp.dot(after(v, grad_qkv_parts[3]), output_matrix, preferred_element_typ...  19.8 us
    dot_general x4, matrix products, on_device(): lax.dot_general(g, output_matrix, ACROSS, preferred_element_type=fp32)  19.2 us
  transfers between devices with their start and end apart: 83, of which 36 were waited for; matrix products, arithmetic and copies ran while one was open for 25% of the time, Pallas kernels for 15%

profile of v2, /device:TPU:0, one launch (start us, length us, event | category | flops | bytes accessed | tf_op | source)
XLA Modules:
  0.0 727.7 jit_solution(9343284217474689218)
XLA Ops:
  12.4 2.5 collective-permute-start.6
  16.1 4.0 collective-permute-done.6
  20.1 4.4 collective-permute-done.7
  25.7 3.7 copy.71
  38.9 5.9 collective-permute-done.22
  46.1 3.1 collective-permute-start.1
  56.7 4.1 shard_map.262
  64.2 21.5 %collective-permute-done.5 = bf16[256,2048]{1,0:T(8,128)(2,1)S(1)} collective-permute-done((bf16[256,2048]{1,0:T(8,128)(2,1)}, bf16[256,2048]{1,0:T(8,128)(2,1)S(1)}, u32[]{:S(2)}, u32[]{:S(2)}) %collective-permute-start.5) | collective-permute-done | bytes 1048608 | tf_op jit(solution)/shard_map/ppermute | solution.py:39
  87.1 3.3 pad_maximum_fusion.refs_0_
  92.8 12.1 %collective-permute-done.10 = bf16[128,2048]{1,0:T(8,128)(2,1)S(1)} collective-permute-done((bf16[128,2048]{1,0:T(8,128)(2,1)S(1)}, bf16[128,2048]{1,0:T(8,128)(2,1)S(1)}, u32[]{:S(2)}, u32[]{:S(2)}) %collective-permute-start.10) | collective-permute-done | bytes 524320 | tf_op jit(solution)/shard_map/ppermute | solution.py:39
  109.0 2.8 fusion.53
  112.0 18.2 %collective-permute-done.13 = bf16[512,1024]{1,0:T(8,128)(2,1)S(1)} collective-permute-done((bf16[512,1024]{1,0:T(8,128)(2,1)}, bf16[512,1024]{1,0:T(8,128)(2,1)S(1)}, u32[]{:S(2)}, u32[]{:S(2)}) %collective-permute-start.13) | collective-permute-done | bytes 1048608 | tf_op jit(solution)/shard_map/ppermute | solution.py:39
  141.2 2.9 collective-permute-done.16
  145.1 3.0 collective-permute-done.17
  148.3 6.8 add_convert_fusion.refs_2_
  155.2 3.6 add_convert_fusion.1.refs_1_
  162.3 11.8 %shard_map.263 = bf16[8,256,256]{2,1,0:T(8,128)(2,1)} custom-call(s32[2]{0:T(128)} %pad_add_fusion.refs_0_, bf16[768,768]{1,0:T(8,128)(2,1)} %add_convert_fusion.1.refs_1_, bf16[768,768]{1,0:T(8,128)(2,1)} %add_convert_fusion.refs_2_, bf16[256,768]{1,0:T(8,128)(2,1)} %fusion.37.refs_3_, bf16[256,768]{1,0:T(8,128)(2,1)} %fusion.38.refs_4_), custom_call_target="tpu_custom_call" | custom-call | flops 1342177280 | bytes 4194312 | tf_op jit(solution)/shard_map/pallas_call | solution.py:411
  174.1 3.6 all-to-all-start
  177.7 14.8 %all-to-all-done.refs_1_ = bf16[8,256,256]{2,1,0:T(8,128)(2,1)S(1)} async-done(((bf16[8,256,256]{2,1,0:T(8,128)(2,1)}), bf16[8,256,256]{2,1,0:T(8,128)(2,1)S(1)}, u32[]{:S(2)}, u32[]{:S(2)}) %all-to-all-start) | async-done | bytes 1048608 | tf_op jit(solution)/shard_map/all_to_all | solution.py:512
  193.5 11.1 %shard_map.264 = (f32[256,2048]{1,0:T(8,128)}, bf16[256,2048]{1,0:T(8,128)(2,1)}, bf16[256,2048]{1,0:T(8,128)(2,1)}) custom-call(s32[2]{0:T(128)} %pad_add_fusion.refs_0_, bf16[8,256,256]{2,1,0:T(8,128)(2,1)} %copy-done.32, bf16[1536,1024]{1,0:T(8,128)(2,1)} %constant_dynamic-update-slice_fusion.2.refs_2_.refs_8_, ...), custom_call_target="tpu_custom_call" | custom-call | flops 2147483648 | bytes 14704648 | tf_op jit(solution)/shard_map/pallas_call | solution.py:411
  208.3 21.2 %collective-permute-done.20 = bf16[256,2048]{1,0:T(8,128)(2,1)S(1)} collective-permute-done((bf16[256,2048]{1,0:T(8,128)(2,1)}, bf16[256,2048]{1,0:T(8,128)(2,1)S(1)}, u32[]{:S(2)}, u32[]{:S(2)}) %collective-permute-start.20) | collective-permute-done | bytes 1048608 | tf_op jit(solution)/shard_map/ppermute | solution.py:39
  234.7 8.4 %fusion.77 = f32[768,1024]{1,0:T(8,128)} fusion(bf16[768,2048]{1,0:T(8,128)(2,1)} %constant_dynamic-update-slice_fusion.7.refs_0_, bf16[2048,1024]{1,0:T(8,128)(2,1)} %all-gather.8.cloned.1.call-done), kind=kOutput, calls=%fused_computation.273 | convolution fusion | flops 3221225472 | bytes 10485760 | tf_op jit(solution)/shard_map/dot_general | solution.py:524
  243.0 2.7 collective-permute-done.24
  250.3 4.5 fusion.49
  254.8 17.2 %collective-permute-done.27 = bf16[256,2048]{1,0:T(8,128)(2,1)S(1)} collective-permute-done((bf16[256,2048]{1,0:T(8,128)(2,1)S(1)}, bf16[256,2048]{1,0:T(8,128)(2,1)S(1)}, u32[]{:S(2)}, u32[]{:S(2)}) %collective-permute-start.27) | collective-permute-done | bytes 1048608 | tf_op jit(solution)/shard_map/ppermute | solution.py:39
  276.9 8.6 %convert_reduce_fusion.1 = (f32[1024]{0:T(1024)S(1)}, bf16[768,1024]{1,0:T(8,128)(2,1)S(1)}) fusion(f32[768,1024]{1,0:T(8,128)} %fusion.77, f32[1024]{0:T(1024)S(1)} %bitcast.275, bf16[768,2048]{1,0:T(8,128)(2,1)} %constant_dynamic-update-slice_fusion.12.refs_4_, bf16[1024,2048]{1,0:T(8,128)(2,1)} %all-gather.10.cloned.1.call-done), kind=kOutput, calls=%fused_computation.32 | convolution fusion | flops 3231448064 | bytes 12066816 | tf_op jit(solution)/shard_map/dot_general | solution.py:526
  288.7 4.4 fusion.52
  297.2 19.2 %fusion.17 = (bf16[768,1024]{1,0:T(8,128)(2,1)}, bf16[768,1024]{1,0:T(8,128)(2,1)}, f32[768,1024]{1,0:T(8,128)S(1)}) fusion(f32[1024]{0:T(1024)S(1)} %bitcast.277, f32[768,1024]{1,0:T(8,128)S(1)} %copy-done.68, bf16[768,2048]{1,0:T(8,128)(2,1)} %collective-permute-done.29.refs_1_, bf16[2048,1024]{1,0:T(8,128)(2,1)S(1)} %copy-done.54), kind=kOutput, calls=%fused_computation.28 | convolution fusion | flops 3325034496 | bytes 16781312 | tf_op jit(solution)/shard_map/dot_general | solution.py:524
  316.3 7.5 %convert_reduce_fusion = (f32[1024]{0:T(1024)S(1)}, bf16[768,1024]{1,0:T(8,128)(2,1)}) fusion(f32[768,1024]{1,0:T(8,128)S(1)} %get-tuple-element.195, f32[1024]{0:T(1024)S(1)} %bitcast.278, bf16[768,2048]{1,0:T(8,128)(2,1)} %collective-permute-done.28.refs_5_, bf16[1024,2048]{1,0:T(8,128)(2,1)S(1)} %copy-done.50), kind=kOutput, calls=%fused_computation.31 | convolution fusion | flops 3231448064 | bytes 12066816 | tf_op jit(solution)/shard_map/dot_general | solution.py:526
  323.8 13.2 %shard_map.275 = bf16[2048,1024]{1,0:T(8,128)(2,1)} custom-call(bf16[768,2048]{1,0:T(8,128)(2,1)} %constant_dynamic-update-slice_fusion.7.refs_0_, bf16[768,2048]{1,0:T(8,128)(2,1)} %collective-permute-done.29.refs_1_, bf16[256,2048]{1,0:T(8,128)(2,1)S(1)} %constant_dynamic-update-slice_fusion.10.refs_2_, ...), custom_call_target="tpu_custom_call" | custom-call | flops 8589934592 | bytes 16777216 | tf_op jit(solution)/shard_map/pallas_call | solution.py:303
  339.9 13.9 %shard_map.276 = bf16[1024,2048]{1,0:T(8,128)(2,1)} custom-call(bf16[768,1024]{1,0:T(8,128)(2,1)S(1)} %copy-done.28, bf16[768,1024]{1,0:T(8,128)(2,1)} %get-tuple-element.61.refs_1_, bf16[256,1024]{1,0:T(8,128)(2,1)S(1)} %copy-done.18, bf16[256,1024]{1,0:T(8,128)(2,1)S(1)} %copy-done.22, bf16[768,2048]{1,0:T(8,128)(2,1)} %constant_dynamic-update-slice_fusion.12.refs_4_, ...), custom_call_target="tpu_custom_call" | custom-call | flops 8589934592 | bytes 16777216 | tf_op jit(solution)/shard_map/pallas_call | solution.py:303
  355.3 6.0 convolution_convert_fusion.4
  363.2 5.3 collective-permute-done.35
  372.2 3.7 convolution_convert_fusion.5.y_ref.x_ref.refs_1_
  375.9 8.1 %collective-permute-done.37.rb_ref = bf16[128,2048]{1,0:T(8,128)(2,1)S(1)} collective-permute-done((bf16[128,2048]{1,0:T(8,128)(2,1)S(1)}, bf16[128,2048]{1,0:T(8,128)(2,1)S(1)}, u32[]{:S(2)}, u32[]{:S(2)}) %collective-permute-start.37) | collective-permute-done | bytes 524320 | tf_op jit(solution)/shard_map/ppermute | solution.py:39
  388.3 22.3 %collective-permute-done.38.refs_3_ = bf16[256,2048]{1,0:T(8,128)(2,1)S(1)} collective-permute-done((bf16[256,2048]{1,0:T(8,128)(2,1)S(1)}, bf16[256,2048]{1,0:T(8,128)(2,1)S(1)}, u32[]{:S(2)}, u32[]{:S(2)}) %collective-permute-start.38) | collective-permute-done | bytes 1048608 | tf_op jit(solution)/shard_map/ppermute | solution.py:39
  412.2 12.5 %shard_map.266 = (f32[256,2048]{1,0:T(8,128)}, bf16[256,2048]{1,0:T(8,128)(2,1)}, bf16[8,256,256]{2,1,0:T(8,128)(2,1)}, f32[8,2048]{1,0:T(8,128)}) custom-call(s32[2]{0:T(128)} %pad_add_fusion.refs_0_, bf16[768,2048]{1,0:T(8,128)(2,1)} %copy-done.4, bf16[768,2048]{1,0:T(8,128)(2,1)} %copy-done.3, bf16[256,2048]{1,0:T(8,128)(2,1)} %copy-done.42, ...), custom_call_target="tpu_custom_call" | custom-call | flops 2147483648 | bytes 24190984 | tf_op jit(solution)/shard_map/pallas_call | solution.py:411
  424.7 3.6 all-to-all-start.1
  429.5 13.6 %all-to-all-done.1.refs_5_ = bf16[8,256,256]{2,1,0:T(8,128)(2,1)S(1)} async-done(((bf16[8,256,256]{2,1,0:T(8,128)(2,1)}), bf16[8,256,256]{2,1,0:T(8,128)(2,1)S(1)}, u32[]{:S(2)}, u32[]{:S(2)}) %all-to-all-start.1) | async-done | bytes 1048608 | tf_op jit(solution)/shard_map/all_to_all | solution.py:544
  444.1 18.0 %shard_map.267 = (bf16[768,768]{1,0:T(8,128)(2,1)}, bf16[768,768]{1,0:T(8,128)(2,1)}, bf16[256,768]{1,0:T(8,128)(2,1)}, bf16[256,768]{1,0:T(8,128)(2,1)}, f32[8,768]{1,0:T(8,128)}) custom-call(s32[2]{0:T(128)} %pad_add_fusion.refs_0_, bf16[768,768]{1,0:T(8,128)(2,1)} %add_convert_fusion.1.refs_1_, bf16[768,768]{1,0:T(8,128)(2,1)} %add_convert_fusion.refs_2_, ...), custom_call_target="tpu_custom_call" | custom-call | flops 3355443200 | bytes 7364616 | tf_op jit(solution)/shard_map/pallas_call | solution.py:411
  462.1 3.1 convolution_convert_fusion.10
  468.1 4.0 convolution_convert_fusion
  472.1 11.0 %shard_map.272 = bf16[2048,768]{1,0:T(8,128)(2,1)} custom-call(bf16[768,2048]{1,0:T(8,128)(2,1)} %pad_maximum_fusion.refs_0_, bf16[768,2048]{1,0:T(8,128)(2,1)} %collective-permute-done.9.refs_1_, bf16[256,2048]{1,0:T(8,128)(2,1)S(1)} %copy-done.9, bf16[256,2048]{1,0:T(8,128)(2,1)S(1)} %copy-done.11, bf16[768,768]{1,0:T(8,128)(2,1)S(1)} %copy-done.25, ...), custom_call_target="tpu_custom_call" | custom-call | flops 6442450944 | bytes 14680064 | tf_op jit(solution)/shard_map/pallas_call | solution.py:303
  484.6 6.9 convolution_convert_fusion.2
  492.0 6.0 shard_map.273
  499.2 2.5 add_convert_fusion.4
  502.6 2.8 add_convert_fusion.5
  507.1 8.6 %collective-permute-done.49.rb_ref = bf16[128,2048]{1,0:T(8,128)(2,1)S(1)} collective-permute-done((bf16[128,2048]{1,0:T(8,128)(2,1)S(1)}, bf16[128,2048]{1,0:T(8,128)(2,1)S(1)}, u32[]{:S(2)}, u32[]{:S(2)}) %collective-permute-start.49) | collective-permute-done | bytes 524320 | tf_op jit(solution)/shard_map/ppermute | solution.py:39
  520.8 8.3 %collective-permute-done.43.rb_ref = bf16[128,2048]{1,0:T(8,128)(2,1)S(1)} collective-permute-done((bf16[128,2048]{1,0:T(8,128)(2,1)S(1)}, bf16[128,2048]{1,0:T(8,128)(2,1)S(1)}, u32[]{:S(2)}, u32[]{:S(2)}) %collective-permute-start.43) | collective-permute-done | bytes 524320 | tf_op jit(solution)/shard_map/ppermute | solution.py:39
  531.7 2.9 convolution_convert_fusion.1.y_ref.x_ref.refs_0_
  548.4 7.8 %convolution_convert_fusion.3.y_ref.x_ref.p_ref = bf16[768,2048]{1,0:T(8,128)(2,1)} fusion(bf16[768,1024]{1,0:T(8,128)(2,1)} %get-tuple-element.60.refs_0_, bf16[1024,2048]{1,0:T(8,128)(2,1)} %all-gather.10.cloned.1.call-done), kind=kOutput, calls=%fused_computation.8 | convolution fusion | flops 3222798336 | bytes 8912896 | tf_op jit(solution)/shard_map/dot_general | solution.py:573
  560.5 2.9 shard_map.268
  566.4 8.0 %collective-permute-done.69 = bf16[128,1024]{1,0:T(8,128)(2,1)} collective-permute-done((bf16[128,1024]{1,0:T(8,128)(2,1)}, bf16[128,1024]{1,0:T(8,128)(2,1)}, u32[]{:S(2)}, u32[]{:S(2)}) %collective-permute-start.69) | collective-permute-done | bytes 262176 | tf_op jit(solution)/shard_map/ppermute | solution.py:39
  575.4 3.0 collective-permute-done.68
  584.2 7.4 %shard_map.271 = (f32[256,2048]{1,0:T(8,128)}, f32[8,2048]{1,0:T(8,128)}) custom-call(bf16[768,2048]{1,0:T(8,128)(2,1)} %copy-done.2, bf16[768,2048]{1,0:T(8,128)(2,1)} %collective-permute-done.46.gy_ref.gx_ref.refs_1_, bf16[256,2048]{1,0:T(8,128)(2,1)} %collective-permute-done.50.refs_2_, bf16[256,2048]{1,0:T(8,128)(2,1)} %collective-permute-done.51.refs_3_, ...), custom_call_target="tpu_custom_call" | custom-call | flops 10485760 | bytes 13705216 | tf_op jit(solution)/shard_map/pallas_call | solution.py:411
  592.5 30.4 %collective-permute-done.65 = bf16[512,1024]{1,0:T(8,128)(2,1)} collective-permute-done((bf16[512,1024]{1,0:T(8,128)(2,1)S(1)}, bf16[512,1024]{1,0:T(8,128)(2,1)}, u32[]{:S(2)}, u32[]{:S(2)}) %collective-permute-start.65) | collective-permute-done | bytes 1048608 | tf_op jit(solution)/shard_map/ppermute | solution.py:39
  624.6 4.0 add_convert_fusion.2
  628.9 4.6 shard_map.269
  633.9 15.0 %collective-permute-done.72 = bf16[256,2048]{1,0:T(8,128)(2,1)} collective-permute-done((bf16[256,2048]{1,0:T(8,128)(2,1)}, bf16[256,2048]{1,0:T(8,128)(2,1)}, u32[]{:S(2)}, u32[]{:S(2)}) %collective-permute-start.72) | collective-permute-done | bytes 1048608 | tf_op jit(solution)/shard_map/ppermute | solution.py:39
  651.2 2.6 maximum_convert_fusion
  653.7 19.6 %collective-permute-done.54 = f32[16,1536]{1,0:T(8,128)S(1)} collective-permute-done((f32[16,1536]{1,0:T(8,128)S(1)}, f32[16,1536]{1,0:T(8,128)S(1)}, u32[]{:S(2)}, u32[]{:S(2)}) %collective-permute-start.54) | collective-permute-done | bytes 98336 | tf_op jit(solution)/shard_map/ppermute | solution.py:39
  683.3 5.6 copy.85
  694.5 2.7 collective-permute-done.56
  701.7 15.2 %collective-permute-done.60 = bf16[4,128,768]{2,1,0:T(8,128)(2,1)S(1)} collective-permute-done((bf16[4,128,768]{2,1,0:T(8,128)(2,1)S(1)}, bf16[4,128,768]{2,1,0:T(8,128)(2,1)S(1)}, u32[]{:S(2)}, u32[]{:S(2)}) %collective-permute-start.60) | collective-permute-done | bytes 786464 | tf_op jit(solution)/shard_map/ppermute | solution.py:39
  (430 shorter events, 169.8 us)
Async XLA Ops:
  7.2 98.1 %all-gather.12.cloned.1.call-start = ((), (), s32[]{:S(2)}) async-start(), calls=%async_computation.13 | async-start | bytes 1310720 | tf_op jit(solution)/shard_map/all_gather | solution.py:90
  9.7 138.6 %all-gather.6.cloned.1.call-start = ((), (), s32[]{:S(2)}) async-start(), calls=%async_computation.6 | async-start | bytes 3932160 | tf_op jit(solution)/shard_map/all_gather | solution.py:90
  25.6 209.1 %all-gather.8.cloned.1.call-start = ((), (), s32[]{:S(2)}) async-start(), calls=%async_computation.7 | async-start | bytes 5242880 | tf_op jit(solution)/shard_map/all_gather | solution.py:90
  46.0 230.8 %all-gather.10.cloned.1.call-start = ((), (), s32[]{:S(2)}) async-start(), calls=%async_computation.8 | async-start | bytes 5242880 | tf_op jit(solution)/shard_map/all_gather | solution.py:90
  60.8 24.8 %collective-permute-start.5 = (bf16[256,2048]{1,0:T(8,128)(2,1)}, bf16[256,2048]{1,0:T(8,128)(2,1)S(1)}, u32[]{:S(2)}, u32[]{:S(2)}) collective-permute-start(bf16[256,2048]{1,0:T(8,128)(2,1)} %shard_map.262), channel_id=1, source_target_pairs={{0,1},{1,0},{2,3},{3,2},{4,5},{5,4},{6,7},{7,6},{8,9},{9,8},{10,11... | collective-permute-start | bytes 3145736 | tf_op jit(solution)/shard_map/ppermute | solution.py:39
  62.7 24.4 %collective-permute-start.4 = (bf16[256,2048]{1,0:T(8,128)(2,1)}, bf16[256,2048]{1,0:T(8,128)(2,1)S(1)}, u32[]{:S(2)}, u32[]{:S(2)}) collective-permute-start(bf16[256,2048]{1,0:T(8,128)(2,1)} %shard_map.262), channel_id=1, source_target_pairs={{0,16},{8,24},{16,0},{24,8},{1,17},{9,25},{17,1},{25,9},{2,18},{10... | collective-permute-start | bytes 3145736 | tf_op jit(solution)/shard_map/ppermute | solution.py:39
  90.4 57.8 %collective-permute-start.9 = (bf16[768,2048]{1,0:T(8,128)(2,1)}, bf16[768,2048]{1,0:T(8,128)(2,1)}, u32[]{:S(2)}, u32[]{:S(2)}) collective-permute-start(bf16[768,2048]{1,0:T(8,128)(2,1)} %pad_maximum_fusion.refs_0_), channel_id=1, source_target_pairs={{0,8},{8,0},{16,24},{24,16},{1,9},{9,1},{17,25},{25,17},{2,10},{10... | collective-permute-start | bytes 9437192 | tf_op jit(solution)/shard_map/ppermute | solution.py:39
  90.6 14.4 %collective-permute-start.10 = (bf16[128,2048]{1,0:T(8,128)(2,1)S(1)}, bf16[128,2048]{1,0:T(8,128)(2,1)S(1)}, u32[]{:S(2)}, u32[]{:S(2)}) collective-permute-start(bf16[128,2048]{1,0:T(8,128)(2,1)S(1)} %slice.212), channel_id=1, source_target_pairs={{0,1},{1,0},{2,3},{3,2},{4,5},{5,4},{6,7},{7,6},{8,9},{9,8},{10,11... | collective-permute-start | bytes 1572872 | tf_op jit(solution)/shard_map/ppermute | solution.py:39
  91.1 14.1 %collective-permute-start.11 = (bf16[128,2048]{1,0:T(8,128)(2,1)S(1)}, bf16[128,2048]{1,0:T(8,128)(2,1)S(1)}, u32[]{:S(2)}, u32[]{:S(2)}) collective-permute-start(bf16[128,2048]{1,0:T(8,128)(2,1)S(1)} %slice.213), channel_id=1, source_target_pairs={{0,16},{8,24},{16,0},{24,8},{1,17},{9,25},{17,1},{25,9},{2,18},{10... | collective-permute-start | bytes 1572872 | tf_op jit(solution)/shard_map/ppermute | solution.py:39
  105.2 25.0 %collective-permute-start.13 = (bf16[512,1024]{1,0:T(8,128)(2,1)}, bf16[512,1024]{1,0:T(8,128)(2,1)S(1)}, u32[]{:S(2)}, u32[]{:S(2)}) collective-permute-start(bf16[512,1024]{1,0:T(8,128)(2,1)} %bitcast.245), channel_id=1, source_target_pairs={{0,16},{8,24},{16,0},{24,8},{1,17},{9,25},{17,1},{25,9},{2,18},{10... | collective-permute-start | bytes 3145736 | tf_op jit(solution)/shard_map/ppermute | solution.py:39
  107.0 25.6 %collective-permute-start.14 = (bf16[512,1024]{1,0:T(8,128)(2,1)}, bf16[512,1024]{1,0:T(8,128)(2,1)}, u32[]{:S(2)}, u32[]{:S(2)}) collective-permute-start(bf16[512,1024]{1,0:T(8,128)(2,1)} %bitcast.246), channel_id=1, source_target_pairs={{0,1},{1,0},{2,3},{3,2},{4,5},{5,4},{6,7},{7,6},{8,9},{9,8},{10,11... | collective-permute-start | bytes 3145736 | tf_op jit(solution)/shard_map/ppermute | solution.py:39
  132.6 28.0 %collective-permute-start.12 = (bf16[256,2048]{1,0:T(8,128)(2,1)S(1)}, bf16[256,2048]{1,0:T(8,128)(2,1)S(1)}, u32[]{:S(2)}, u32[]{:S(2)}) collective-permute-start(bf16[256,2048]{1,0:T(8,128)(2,1)S(1)} %constant_dynamic-update-slice_fusion.refs_2_), channel_id=1, source_target_pairs={{0,8},{8,0},{16,24},{24,16},{1,9},{9,1},{17,25},{25,17},{2,10},{10... | collective-permute-start | bytes 3145736 | tf_op jit(solution)/shard_map/ppermute | solution.py:39
  133.7 14.4 %collective-permute-start.17 = (bf16[256,1024]{1,0:T(8,128)(2,1)S(1)}, bf16[256,1024]{1,0:T(8,128)(2,1)S(1)}, u32[]{:S(2)}, u32[]{:S(2)}) collective-permute-start(bf16[256,1024]{1,0:T(8,128)(2,1)S(1)} %slice.215), channel_id=1, source_target_pairs={{0,16},{8,24},{16,0},{24,8},{1,17},{9,25},{17,1},{25,9},{2,18},{10... | collective-permute-start | bytes 1572872 | tf_op jit(solution)/shard_map/ppermute | solution.py:39
  140.9 36.8 %collective-permute-start.15 = (bf16[1536,1024]{1,0:T(8,128)(2,1)}, bf16[1536,1024]{1,0:T(8,128)(2,1)}, u32[]{:S(2)}, u32[]{:S(2)}) collective-permute-start(bf16[1536,1024]{1,0:T(8,128)(2,1)} %constant_dynamic-update-slice_fusion.2.refs_2_.refs_8_), channel_id=1, source_target_pairs={{0,8},{8,0},{16,24},{24,16},{1,9},{9,1},{17,25},{25,17},{2,10},{10... | collective-permute-start | bytes 9437192 | tf_op jit(solution)/shard_map/ppermute | solution.py:39
  148.2 29.5 %collective-permute-start.18 = (bf16[512,1024]{1,0:T(8,128)(2,1)S(1)}, bf16[512,1024]{1,0:T(8,128)(2,1)}, u32[]{:S(2)}, u32[]{:S(2)}) collective-permute-start(bf16[512,1024]{1,0:T(8,128)(2,1)S(1)} %constant_dynamic-update-slice_fusion.5.refs_4_.refs_10_), channel_id=1, source_target_pairs={{0,8},{8,0},{16,24},{24,16},{1,9},{9,1},{17,25},{25,17},{2,10},{10... | collective-permute-start | bytes 3145736 | tf_op jit(solution)/shard_map/ppermute | solution.py:39
  174.1 18.4 %all-to-all-start = ((bf16[8,256,256]{2,1,0:T(8,128)(2,1)}), bf16[8,256,256]{2,1,0:T(8,128)(2,1)S(1)}, u32[]{:S(2)}, u32[]{:S(2)}) async-start(bf16[8,256,256]{2,1,0:T(8,128)(2,1)} %shard_map.263), calls=%async_computation | async-start | bytes 2097152 | tf_op jit(solution)/shard_map/all_to_all | solution.py:512
  177.7 362.8 %reduce-scatter.9.cloned.1.call-start = ((), (), s32[]{:S(2)}) async-start(), calls=%async_computation.11 | async-start | bytes 5242880 | tf_op jit(solution)/shard_map/reduce_scatter | solution.py:94
  204.6 25.0 %collective-permute-start.20 = (bf16[256,2048]{1,0:T(8,128)(2,1)}, bf16[256,2048]{1,0:T(8,128)(2,1)S(1)}, u32[]{:S(2)}, u32[]{:S(2)}) collective-permute-start(bf16[256,2048]{1,0:T(8,128)(2,1)} %get-tuple-element.51), channel_id=1, source_target_pairs={{0,1},{1,0},{2,3},{3,2},{4,5},{5,4},{6,7},{7,6},{8,9},{9,8},{10,11... | collective-permute-start | bytes 3145736 | tf_op jit(solution)/shard_map/ppermute | solution.py:39
  205.6 25.9 %collective-permute-start.19 = (bf16[256,2048]{1,0:T(8,128)(2,1)}, bf16[256,2048]{1,0:T(8,128)(2,1)S(1)}, u32[]{:S(2)}, u32[]{:S(2)}) collective-permute-start(bf16[256,2048]{1,0:T(8,128)(2,1)} %get-tuple-element.51), channel_id=1, source_target_pairs={{0,16},{8,24},{16,0},{24,8},{1,17},{9,25},{17,1},{25,9},{2,18},{10... | collective-permute-start | bytes 3145736 | tf_op jit(solution)/shard_map/ppermute | solution.py:39
  230.4 16.5 %collective-permute-start.25 = (bf16[128,2048]{1,0:T(8,128)(2,1)}, bf16[128,2048]{1,0:T(8,128)(2,1)}, u32[]{:S(2)}, u32[]{:S(2)}) collective-permute-start(bf16[128,2048]{1,0:T(8,128)(2,1)} %slice.217), channel_id=1, source_target_pairs={{0,16},{8,24},{16,0},{24,8},{1,17},{9,25},{17,1},{25,9},{2,18},{10... | collective-permute-start | bytes 1572872 | tf_op jit(solution)/shard_map/ppermute | solution.py:39
  232.3 13.5 %collective-permute-start.24 = (bf16[128,2048]{1,0:T(8,128)(2,1)}, bf16[128,2048]{1,0:T(8,128)(2,1)}, u32[]{:S(2)}, u32[]{:S(2)}) collective-permute-start(bf16[128,2048]{1,0:T(8,128)(2,1)} %slice.216), channel_id=1, source_target_pairs={{0,1},{1,0},{2,3},{3,2},{4,5},{5,4},{6,7},{7,6},{8,9},{9,8},{10,11... | collective-permute-start | bytes 1572872 | tf_op jit(solution)/shard_map/ppermute | solution.py:39
  234.7 61.6 %collective-permute-start.29 = (bf16[768,2048]{1,0:T(8,128)(2,1)}, bf16[768,2048]{1,0:T(8,128)(2,1)}, u32[]{:S(2)}, u32[]{:S(2)}) collective-permute-start(bf16[768,2048]{1,0:T(8,128)(2,1)} %constant_dynamic-update-slice_fusion.7.refs_0_), channel_id=1, source_target_pairs={{0,8},{8,0},{16,24},{24,16},{1,9},{9,1},{17,25},{25,17},{2,10},{10... | collective-permute-start | bytes 9437192 | tf_op jit(solution)/shard_map/ppermute | solution.py:39
  248.0 24.0 %collective-permute-start.27 = (bf16[256,2048]{1,0:T(8,128)(2,1)S(1)}, bf16[256,2048]{1,0:T(8,128)(2,1)S(1)}, u32[]{:S(2)}, u32[]{:S(2)}) collective-permute-start(bf16[256,2048]{1,0:T(8,128)(2,1)S(1)} %bitcast.233), channel_id=1, source_target_pairs={{0,1},{1,0},{2,3},{3,2},{4,5},{5,4},{6,7},{7,6},{8,9},{9,8},{10,11... | collective-permute-start | bytes 3145736 | tf_op jit(solution)/shard_map/ppermute | solution.py:39
  248.3 25.1 %collective-permute-start.26 = (bf16[256,2048]{1,0:T(8,128)(2,1)S(1)}, bf16[256,2048]{1,0:T(8,128)(2,1)S(1)}, u32[]{:S(2)}, u32[]{:S(2)}) collective-permute-start(bf16[256,2048]{1,0:T(8,128)(2,1)S(1)} %bitcast.234), channel_id=1, source_target_pairs={{0,16},{8,24},{16,0},{24,8},{1,17},{9,25},{17,1},{25,9},{2,18},{10... | collective-permute-start | bytes 3145736 | tf_op jit(solution)/shard_map/ppermute | solution.py:39
  249.2 39.4 %collective-permute-start.34 = (bf16[256,2048]{1,0:T(8,128)(2,1)S(1)}, bf16[256,2048]{1,0:T(8,128)(2,1)S(1)}, u32[]{:S(2)}, u32[]{:S(2)}) collective-permute-start(bf16[256,2048]{1,0:T(8,128)(2,1)S(1)} %constant_dynamic-update-slice_fusion.10.refs_2_), channel_id=1, source_target_pairs={{0,8},{8,0},{16,24},{24,16},{1,9},{9,1},{17,25},{25,17},{2,10},{10... | collective-permute-start | bytes 3145736 | tf_op jit(solution)/shard_map/ppermute | solution.py:39
  272.8 14.2 %collective-permute-start.32 = (bf16[128,2048]{1,0:T(8,128)(2,1)}, bf16[128,2048]{1,0:T(8,128)(2,1)}, u32[]{:S(2)}, u32[]{:S(2)}) collective-permute-start(bf16[128,2048]{1,0:T(8,128)(2,1)} %slice.219), channel_id=1, source_target_pairs={{0,16},{8,24},{16,0},{24,8},{1,17},{9,25},{17,1},{25,9},{2,18},{10... | collective-permute-start | bytes 1572872 | tf_op jit(solution)/shard_map/ppermute | solution.py:39
  276.9 39.5 %collective-permute-start.28 = (bf16[768,2048]{1,0:T(8,128)(2,1)}, bf16[768,2048]{1,0:T(8,128)(2,1)}, u32[]{:S(2)}, u32[]{:S(2)}) collective-permute-start(bf16[768,2048]{1,0:T(8,128)(2,1)} %constant_dynamic-update-slice_fusion.12.refs_4_), channel_id=1, source_target_pairs={{0,8},{8,0},{16,24},{24,16},{1,9},{9,1},{17,25},{25,17},{2,10},{10... | collective-permute-start | bytes 9437192 | tf_op jit(solution)/shard_map/ppermute | solution.py:39
  337.1 245.8 %reduce-scatter.11.cloned.1.call-start = ((), (), s32[]{:S(2)}) async-start(), calls=%async_computation.12 | async-start | bytes 5242880 | tf_op jit(solution)/shard_map/reduce_scatter | solution.py:94
  361.3 23.4 %collective-permute-start.30 = (bf16[768,2048]{1,0:T(8,128)(2,1)S(1)}, bf16[768,2048]{1,0:T(8,128)(2,1)S(1)}, u32[]{:S(2)}, u32[]{:S(2)}) collective-permute-start(bf16[768,2048]{1,0:T(8,128)(2,1)S(1)} %convolution_convert_fusion.4), channel_id=1, source_target_pairs={{0,8},{8,0},{16,24},{24,16},{1,9},{9,1},{17,25},{25,17},{2,10},{10... | collective-permute-start | bytes 9437192 | tf_op jit(solution)/shard_map/ppermute | solution.py:39
  369.9 14.0 %collective-permute-start.37 = (bf16[128,2048]{1,0:T(8,128)(2,1)S(1)}, bf16[128,2048]{1,0:T(8,128)(2,1)S(1)}, u32[]{:S(2)}, u32[]{:S(2)}) collective-permute-start(bf16[128,2048]{1,0:T(8,128)(2,1)S(1)} %get-tuple-element.138), channel_id=1, source_target_pairs={{0,16},{8,24},{16,0},{24,8},{1,17},{9,25},{17,1},{25,9},{2,18},{10... | collective-permute-start | bytes 1572872 | tf_op jit(solution)/shard_map/ppermute | solution.py:39
  371.0 13.7 %collective-permute-start.36 = (bf16[128,2048]{1,0:T(8,128)(2,1)S(1)}, bf16[128,2048]{1,0:T(8,128)(2,1)S(1)}, u32[]{:S(2)}, u32[]{:S(2)}) collective-permute-start(bf16[128,2048]{1,0:T(8,128)(2,1)S(1)} %get-tuple-element.139), channel_id=1, source_target_pairs={{0,1},{1,0},{2,3},{3,2},{4,5},{5,4},{6,7},{7,6},{8,9},{9,8},{10,11... | collective-permute-start | bytes 1572872 | tf_op jit(solution)/shard_map/ppermute | solution.py:39
  386.4 24.2 %collective-permute-start.38 = (bf16[256,2048]{1,0:T(8,128)(2,1)S(1)}, bf16[256,2048]{1,0:T(8,128)(2,1)S(1)}, u32[]{:S(2)}, u32[]{:S(2)}) collective-permute-start(bf16[256,2048]{1,0:T(8,128)(2,1)S(1)} %get-tuple-element.55), channel_id=1, source_target_pairs={{0,16},{8,24},{16,0},{24,8},{1,17},{9,25},{17,1},{25,9},{2,18},{10... | collective-permute-start | bytes 3145736 | tf_op jit(solution)/shard_map/ppermute | solution.py:39
  387.4 23.9 %collective-permute-start.39 = (bf16[256,2048]{1,0:T(8,128)(2,1)S(1)}, bf16[256,2048]{1,0:T(8,128)(2,1)S(1)}, u32[]{:S(2)}, u32[]{:S(2)}) collective-permute-start(bf16[256,2048]{1,0:T(8,128)(2,1)S(1)} %get-tuple-element.56), channel_id=1, source_target_pairs={{0,1},{1,0},{2,3},{3,2},{4,5},{5,4},{6,7},{7,6},{8,9},{9,8},{10,11... | collective-permute-start | bytes 3145736 | tf_op jit(solution)/shard_map/ppermute | solution.py:39
  424.7 18.4 %all-to-all-start.1 = ((bf16[8,256,256]{2,1,0:T(8,128)(2,1)}), bf16[8,256,256]{2,1,0:T(8,128)(2,1)S(1)}, u32[]{:S(2)}, u32[]{:S(2)}) async-start(bf16[8,256,256]{2,1,0:T(8,128)(2,1)} %get-tuple-element.58), calls=%async_computation.1 | async-start | bytes 2097152 | tf_op jit(solution)/shard_map/all_to_all | solution.py:544
  428.3 249.3 %reduce-scatter.5.cloned.1.call-start = ((), (), s32[]{:S(2)}) async-start(), calls=%async_computation.9 | async-start | bytes 3932160 | tf_op jit(solution)/shard_map/reduce_scatter | solution.py:94
  465.2 33.4 %collective-permute-start.47 = (bf16[256,2048]{1,0:T(8,128)(2,1)}, bf16[256,2048]{1,0:T(8,128)(2,1)}, u32[]{:S(2)}, u32[]{:S(2)}) collective-permute-start(bf16[256,2048]{1,0:T(8,128)(2,1)} %convolution_convert_fusion.10), channel_id=1, source_target_pairs={{0,8},{8,0},{16,24},{24,16},{1,9},{9,1},{17,25},{25,17},{2,10},{10... | collective-permute-start | bytes 3145736 | tf_op jit(solution)/shard_map/ppermute | solution.py:39
  467.5 34.3 %collective-permute-start.41 = (bf16[256,2048]{1,0:T(8,128)(2,1)}, bf16[256,2048]{1,0:T(8,128)(2,1)}, u32[]{:S(2)}, u32[]{:S(2)}) collective-permute-start(bf16[256,2048]{1,0:T(8,128)(2,1)} %convolution_convert_fusion.6), channel_id=1, source_target_pairs={{0,8},{8,0},{16,24},{24,16},{1,9},{9,1},{17,25},{25,17},{2,10},{10... | collective-permute-start | bytes 3145736 | tf_op jit(solution)/shard_map/ppermute | solution.py:39
  472.1 59.6 %collective-permute-start.46 = (bf16[768,2048]{1,0:T(8,128)(2,1)}, bf16[768,2048]{1,0:T(8,128)(2,1)}, u32[]{:S(2)}, u32[]{:S(2)}) collective-permute-start(bf16[768,2048]{1,0:T(8,128)(2,1)} %convolution_convert_fusion), channel_id=1, source_target_pairs={{0,8},{8,0},{16,24},{24,16},{1,9},{9,1},{17,25},{25,17},{2,10},{10... | collective-permute-start | bytes 9437192 | tf_op jit(solution)/shard_map/ppermute | solution.py:39
  483.2 208.1 %reduce-scatter.7.cloned.1.call-start = ((), (), s32[]{:S(2)}) async-start(), calls=%async_computation.10 | async-start | bytes 1310720 | tf_op jit(solution)/shard_map/reduce_scatter | solution.py:94
  491.5 55.0 %collective-permute-start.40 = (bf16[768,2048]{1,0:T(8,128)(2,1)}, bf16[768,2048]{1,0:T(8,128)(2,1)S(1)}, u32[]{:S(2)}, u32[]{:S(2)}) collective-permute-start(bf16[768,2048]{1,0:T(8,128)(2,1)} %convolution_convert_fusion.2), channel_id=1, source_target_pairs={{0,8},{8,0},{16,24},{24,16},{1,9},{9,1},{17,25},{25,17},{2,10},{10... | collective-permute-start | bytes 9437192 | tf_op jit(solution)/shard_map/ppermute | solution.py:39
  498.0 48.6 %collective-permute-start.61 = (bf16[1536,1024]{1,0:T(8,128)(2,1)}, bf16[1536,1024]{1,0:T(8,128)(2,1)}, u32[]{:S(2)}, u32[]{:S(2)}) collective-permute-start(bf16[1536,1024]{1,0:T(8,128)(2,1)} %get-tuple-element.80), channel_id=1, source_target_pairs={{0,8},{8,0},{16,24},{24,16},{1,9},{9,1},{17,25},{25,17},{2,10},{10... | collective-permute-start | bytes 9437192 | tf_op jit(solution)/shard_map/ppermute | solution.py:39
  501.9 13.8 %collective-permute-start.49 = (bf16[128,2048]{1,0:T(8,128)(2,1)S(1)}, bf16[128,2048]{1,0:T(8,128)(2,1)S(1)}, u32[]{:S(2)}, u32[]{:S(2)}) collective-permute-start(bf16[128,2048]{1,0:T(8,128)(2,1)S(1)} %get-tuple-element.134), channel_id=1, source_target_pairs={{0,16},{8,24},{16,0},{24,8},{1,17},{9,25},{17,1},{25,9},{2,18},{10... | collective-permute-start | bytes 1572872 | tf_op jit(solution)/shard_map/ppermute | solution.py:39
  506.4 14.2 %collective-permute-start.48 = (bf16[128,2048]{1,0:T(8,128)(2,1)S(1)}, bf16[128,2048]{1,0:T(8,128)(2,1)S(1)}, u32[]{:S(2)}, u32[]{:S(2)}) collective-permute-start(bf16[128,2048]{1,0:T(8,128)(2,1)S(1)} %get-tuple-element.135), channel_id=1, source_target_pairs={{0,1},{1,0},{2,3},{3,2},{4,5},{5,4},{6,7},{7,6},{8,9},{9,8},{10,11... | collective-permute-start | bytes 1572872 | tf_op jit(solution)/shard_map/ppermute | solution.py:39
  515.7 13.5 %collective-permute-start.43 = (bf16[128,2048]{1,0:T(8,128)(2,1)S(1)}, bf16[128,2048]{1,0:T(8,128)(2,1)S(1)}, u32[]{:S(2)}, u32[]{:S(2)}) collective-permute-start(bf16[128,2048]{1,0:T(8,128)(2,1)S(1)} %get-tuple-element.136), channel_id=1, source_target_pairs={{0,16},{8,24},{16,0},{24,8},{1,17},{9,25},{17,1},{25,9},{2,18},{10... | collective-permute-start | bytes 1572872 | tf_op jit(solution)/shard_map/ppermute | solution.py:39
  520.5 21.9 %collective-permute-start.42 = (bf16[128,2048]{1,0:T(8,128)(2,1)}, bf16[128,2048]{1,0:T(8,128)(2,1)}, u32[]{:S(2)}, u32[]{:S(2)}) collective-permute-start(bf16[128,2048]{1,0:T(8,128)(2,1)} %get-tuple-element.137), channel_id=1, source_target_pairs={{0,1},{1,0},{2,3},{3,2},{4,5},{5,4},{6,7},{7,6},{8,9},{9,8},{10,11... | collective-permute-start | bytes 1572872 | tf_op jit(solution)/shard_map/ppermute | solution.py:39
  529.9 13.4 %collective-permute-start.64 = (bf16[256,1024]{1,0:T(8,128)(2,1)}, bf16[256,1024]{1,0:T(8,128)(2,1)}, u32[]{:S(2)}, u32[]{:S(2)}) collective-permute-start(bf16[256,1024]{1,0:T(8,128)(2,1)} %get-tuple-element.132), channel_id=1, source_target_pairs={{0,16},{8,24},{16,0},{24,8},{1,17},{9,25},{17,1},{25,9},{2,18},{10... | collective-permute-start | bytes 1572872 | tf_op jit(solution)/shard_map/ppermute | solution.py:39
  531.7 14.9 %collective-permute-start.63 = (bf16[256,1024]{1,0:T(8,128)(2,1)}, bf16[256,1024]{1,0:T(8,128)(2,1)}, u32[]{:S(2)}, u32[]{:S(2)}) collective-permute-start(bf16[256,1024]{1,0:T(8,128)(2,1)} %get-tuple-element.133), channel_id=1, source_target_pairs={{0,1},{1,0},{2,3},{3,2},{4,5},{5,4},{6,7},{7,6},{8,9},{9,8},{10,11... | collective-permute-start | bytes 1572872 | tf_op jit(solution)/shard_map/ppermute | solution.py:39
  542.4 39.8 %collective-permute-start.50 = (bf16[256,2048]{1,0:T(8,128)(2,1)}, bf16[256,2048]{1,0:T(8,128)(2,1)}, u32[]{:S(2)}, u32[]{:S(2)}) collective-permute-start(bf16[256,2048]{1,0:T(8,128)(2,1)} %copy-done.13), channel_id=1, source_target_pairs={{0,16},{8,24},{16,0},{24,8},{1,17},{9,25},{17,1},{25,9},{2,18},{10... | collective-permute-start | bytes 3145736 | tf_op jit(solution)/shard_map/ppermute | solution.py:39
  543.4 39.5 %collective-permute-start.51 = (bf16[256,2048]{1,0:T(8,128)(2,1)}, bf16[256,2048]{1,0:T(8,128)(2,1)}, u32[]{:S(2)}, u32[]{:S(2)}) collective-permute-start(bf16[256,2048]{1,0:T(8,128)(2,1)} %copy-done.12), channel_id=1, source_target_pairs={{0,1},{1,0},{2,3},{3,2},{4,5},{5,4},{6,7},{7,6},{8,9},{9,8},{10,11... | collective-permute-start | bytes 3145736 | tf_op jit(solution)/shard_map/ppermute | solution.py:39
  546.5 19.4 %collective-permute-start.70 = (bf16[128,1024]{1,0:T(8,128)(2,1)}, bf16[128,1024]{1,0:T(8,128)(2,1)}, u32[]{:S(2)}, u32[]{:S(2)}) collective-permute-start(bf16[128,1024]{1,0:T(8,128)(2,1)} %get-tuple-element.129), channel_id=1, source_target_pairs={{0,8},{8,0},{16,24},{24,16},{1,9},{9,1},{17,25},{25,17},{2,10},{10... | collective-permute-start | bytes 786440 | tf_op jit(solution)/shard_map/ppermute | solution.py:39
  546.5 27.9 %collective-permute-start.69 = (bf16[128,1024]{1,0:T(8,128)(2,1)}, bf16[128,1024]{1,0:T(8,128)(2,1)}, u32[]{:S(2)}, u32[]{:S(2)}) collective-permute-start(bf16[128,1024]{1,0:T(8,128)(2,1)} %get-tuple-element.130), channel_id=1, source_target_pairs={{0,16},{8,24},{16,0},{24,8},{1,17},{9,25},{17,1},{25,9},{2,18},{10... | collective-permute-start | bytes 786440 | tf_op jit(solution)/shard_map/ppermute | solution.py:39
  546.6 31.8 %collective-permute-start.68 = (bf16[128,1024]{1,0:T(8,128)(2,1)S(1)}, bf16[128,1024]{1,0:T(8,128)(2,1)}, u32[]{:S(2)}, u32[]{:S(2)}) collective-permute-start(bf16[128,1024]{1,0:T(8,128)(2,1)S(1)} %get-tuple-element.131), channel_id=1, source_target_pairs={{0,24},{8,16},{16,8},{24,0},{1,25},{9,17},{17,9},{25,1},{2,26},{10... | collective-permute-start | bytes 786440 | tf_op jit(solution)/shard_map/ppermute | solution.py:39
  565.9 63.0 %collective-permute-start.44 = (bf16[256,2048]{1,0:T(8,128)(2,1)}, bf16[256,2048]{1,0:T(8,128)(2,1)}, u32[]{:S(2)}, u32[]{:S(2)}) collective-permute-start(bf16[256,2048]{1,0:T(8,128)(2,1)} %get-tuple-element.64), channel_id=1, source_target_pairs={{0,16},{8,24},{16,0},{24,8},{1,17},{9,25},{17,1},{25,9},{2,18},{10... | collective-permute-start | bytes 3145736 | tf_op jit(solution)/shard_map/ppermute | solution.py:39
  574.4 48.5 %collective-permute-start.65 = (bf16[512,1024]{1,0:T(8,128)(2,1)S(1)}, bf16[512,1024]{1,0:T(8,128)(2,1)}, u32[]{:S(2)}, u32[]{:S(2)}) collective-permute-start(bf16[512,1024]{1,0:T(8,128)(2,1)S(1)} %get-tuple-element.83), channel_id=1, source_target_pairs={{0,16},{8,24},{16,0},{24,8},{1,17},{9,25},{17,1},{25,9},{2,18},{10... | collective-permute-start | bytes 3145736 | tf_op jit(solution)/shard_map/ppermute | solution.py:39
  578.4 46.2 %collective-permute-start.66 = (bf16[512,1024]{1,0:T(8,128)(2,1)S(1)}, bf16[512,1024]{1,0:T(8,128)(2,1)}, u32[]{:S(2)}, u32[]{:S(2)}) collective-permute-start(bf16[512,1024]{1,0:T(8,128)(2,1)S(1)} %get-tuple-element.84), channel_id=1, source_target_pairs={{0,1},{1,0},{2,3},{3,2},{4,5},{5,4},{6,7},{7,6},{8,9},{9,8},{10,11... | collective-permute-start | bytes 3145736 | tf_op jit(solution)/shard_map/ppermute | solution.py:39
  582.1 46.8 %collective-permute-start.45 = (bf16[256,2048]{1,0:T(8,128)(2,1)}, bf16[256,2048]{1,0:T(8,128)(2,1)}, u32[]{:S(2)}, u32[]{:S(2)}) collective-permute-start(bf16[256,2048]{1,0:T(8,128)(2,1)} %get-tuple-element.65), channel_id=1, source_target_pairs={{0,1},{1,0},{2,3},{3,2},{4,5},{5,4},{6,7},{7,6},{8,9},{9,8},{10,11... | collective-permute-start | bytes 3145736 | tf_op jit(solution)/shard_map/ppermute | solution.py:39
  582.8 66.0 %collective-permute-start.72 = (bf16[256,2048]{1,0:T(8,128)(2,1)}, bf16[256,2048]{1,0:T(8,128)(2,1)}, u32[]{:S(2)}, u32[]{:S(2)}) collective-permute-start(bf16[256,2048]{1,0:T(8,128)(2,1)} %reduce-scatter.11.cloned.1.call-done), channel_id=1, source_target_pairs={{0,1},{1,0},{2,3},{3,2},{4,5},{5,4},{6,7},{7,6},{8,9},{9,8},{10,11... | collective-permute-start | bytes 3145736 | tf_op jit(solution)/shard_map/ppermute | solution.py:39
  622.9 51.9 %collective-permute-start.71 = (bf16[4,128,1024]{2,1,0:T(8,128)(2,1)}, bf16[4,128,1024]{2,1,0:T(8,128)(2,1)}, u32[]{:S(2)}, u32[]{:S(2)}) collective-permute-start(bf16[4,128,1024]{2,1,0:T(8,128)(2,1)} %pad_maximum_fusion.2), channel_id=1, source_target_pairs={{0,1},{1,0},{2,3},{3,2},{4,5},{5,4},{6,7},{7,6},{8,9},{9,8},{10,11... | collective-permute-start | bytes 3145736 | tf_op jit(solution)/shard_map/ppermute | solution.py:39
  633.5 16.7 %collective-permute-start.53 = (f32[16,1536]{1,0:T(8,128)S(1)}, f32[16,1536]{1,0:T(8,128)S(1)}, u32[]{:S(2)}, u32[]{:S(2)}) collective-permute-start(f32[16,1536]{1,0:T(8,128)S(1)} %add.258), channel_id=1, source_target_pairs={{0,16},{8,24},{16,0},{24,8},{1,17},{9,25},{17,1},{25,9},{2,18},{10... | collective-permute-start | bytes 294920 | tf_op jit(solution)/shard_map/ppermute | solution.py:39
  650.3 23.1 %collective-permute-start.54 = (f32[16,1536]{1,0:T(8,128)S(1)}, f32[16,1536]{1,0:T(8,128)S(1)}, u32[]{:S(2)}, u32[]{:S(2)}) collective-permute-start(f32[16,1536]{1,0:T(8,128)S(1)} %add.259), channel_id=1, source_target_pairs={{0,1},{1,0},{2,3},{3,2},{4,5},{5,4},{6,7},{7,6},{8,9},{9,8},{10,11... | collective-permute-start | bytes 294920 | tf_op jit(solution)/shard_map/ppermute | solution.py:39
  673.3 15.6 %collective-permute-start.55 = (f32[16,1536]{1,0:T(8,128)S(1)}, f32[16,1536]{1,0:T(8,128)S(1)}, u32[]{:S(2)}, u32[]{:S(2)}) collective-permute-start(f32[16,1536]{1,0:T(8,128)S(1)} %add.260), channel_id=1, source_target_pairs={{0,2},{2,0},{4,6},{6,4},{1,3},{3,1},{5,7},{7,5},{8,10},{10,8},{12,... | collective-permute-start | bytes 294920 | tf_op jit(solution)/shard_map/ppermute | solution.py:39
  678.8 14.5 %collective-permute-start.59 = (bf16[128,768]{1,0:T(8,128)(2,1)S(1)}, bf16[128,768]{1,0:T(8,128)(2,1)S(1)}, u32[]{:S(2)}, u32[]{:S(2)}) collective-permute-start(bf16[128,768]{1,0:T(8,128)(2,1)S(1)} %get-tuple-element.148), channel_id=1, source_target_pairs={{0,8},{8,0},{16,24},{24,16},{1,9},{9,1},{17,25},{25,17},{2,10},{10... | collective-permute-start | bytes 589832 | tf_op jit(solution)/shard_map/ppermute | solution.py:39
  679.1 14.2 %collective-permute-start.58 = (bf16[128,768]{1,0:T(8,128)(2,1)S(1)}, bf16[128,768]{1,0:T(8,128)(2,1)S(1)}, u32[]{:S(2)}, u32[]{:S(2)}) collective-permute-start(bf16[128,768]{1,0:T(8,128)(2,1)S(1)} %get-tuple-element.149), channel_id=1, source_target_pairs={{0,16},{8,24},{16,0},{24,8},{1,17},{9,25},{17,1},{25,9},{2,18},{10... | collective-permute-start | bytes 589832 | tf_op jit(solution)/shard_map/ppermute | solution.py:39
  694.4 22.5 %collective-permute-start.60 = (bf16[4,128,768]{2,1,0:T(8,128)(2,1)S(1)}, bf16[4,128,768]{2,1,0:T(8,128)(2,1)S(1)}, u32[]{:S(2)}, u32[]{:S(2)}) collective-permute-start(bf16[4,128,768]{2,1,0:T(8,128)(2,1)S(1)} %pad_maximum_fusion.4), channel_id=1, source_target_pairs={{0,1},{1,0},{2,3},{3,2},{4,5},{5,4},{6,7},{7,6},{8,9},{9,8},{10,11... | collective-permute-start | bytes 2359304 | tf_op jit(solution)/shard_map/ppermute | solution.py:39
  (90 other events, 762.0 us)
Sparse Core Ops, SparseCore 0:
  9.8 30.5 all-gather.11
  42.5 63.1 all-gather.5
  107.9 79.4 all-gather.7
  188.8 79.2 all-gather.9
  337.2 77.1 reduce-scatter.8
  417.2 77.2 reduce-scatter.10
  496.8 60.7 reduce-scatter.4
  628.8 26.2 reduce-scatter.6

commit v3 on v2

--- a/solution.py
+++ b/solution.py
@@ -21,17 +21,22 @@
 SCALARS = pl.BlockSpec(memory_space=pltpu.SMEM)
 
 
+LIGHT = pl.CostEstimate(flops=1, bytes_accessed=1, transcendentals=0)
+
+
 def place(j):
     return next((i, part.index(j)) for i, part in enumerate(PARTS) if j in part)
 
 
-def gelu_slope(values):
-    normal_cdf = 0.5 * (1.0 + lax.erf(values * 0.7071067811865476))
-    return normal_cdf + values * jnp.exp(-0.5 * values * values) * 0.3989422804014327
-
-
-def after(v, *others):
-    return lax.optimization_barrier((v, others))[0]
+def tie(*groups):
+    return lax.optimization_barrier(groups)
+
+
+def ordered(kernel, count, deps):
+    return lambda *refs: kernel(*refs[:count], *refs[count + len(deps) :])
+
+
+UNREAD = pl.BlockSpec(memory_space=pl.ANY)
 
 
 def flip(v, link):
@@ -39,12 +44,17 @@
     return lax.ppermute(v, axis, [(i, i ^ bit) for i in range(lax.axis_size(axis))])
 
 
-def plane_gather(v):
+def gather_near(v):
+    return v, flip(v, ROW), flip(v, COL)
+
+
+def gather_diagonal(v, py, px):
     h = v.shape[0] // 2
-    py, px = flip(v, ROW), flip(v, COL)
-    first = jnp.concatenate([v, py, px])
-    da, db = flip(py[:h], COL), flip(px[h:], ROW)
-    second = jnp.concatenate([da, db])
+    return flip(py[:h], COL), flip(px[h:], ROW)
+
+
+def gather_parts(near, diagonal):
+    first, second = jnp.concatenate(near), jnp.concatenate(diagonal)
     return first, flip(first, CORE), second, flip(second, CORE)
 
 
@@ -61,28 +71,45 @@
     ).astype(bf16)
 
 
-def plane_scatter(parts):
-    mine, theirs, far, far_theirs = parts
-    n, width = far.shape
-    h = n // 2
-    far_got = flip(far_theirs, CORE)
-    got = flip(theirs, CORE)
-    far = (far.astype(fp32) + far_got.astype(fp32)).astype(bf16)
-    ra, rb = flip(far[:h], COL), flip(far[h:], ROW)
+def relay_by_row_kernel(y_ref, gy_ref, x_ref, gx_ref, rb_ref, ys_ref, xs_ref):
+    ys_ref[...] = (y_ref[...].astype(fp32) + gy_ref[...].astype(fp32)).astype(bf16)
+    xs_ref[...] = (x_ref[...].astype(fp32) + gx_ref[...].astype(fp32) + rb_ref[...].astype(fp32)).astype(bf16)
+
+
+def far_sum(far, far_theirs):
+    return (far.astype(fp32) + flip(far_theirs, CORE).astype(fp32)).astype(bf16)
+
+
+def scatter_diagonal(far):
+    h = far.shape[0] // 2
+    return flip(far[:h], COL), flip(far[h:], ROW)
+
+
+def scatter_diagonal_by_row(far):
+    return (flip(far, ROW),)
+
+
+def scatter_relay(mine, got, diagonal):
+    width = diagonal[0].shape[1]
+    n = sum(v.shape[0] for v in diagonal)
 
     def rows(i):
         return pl.BlockSpec((n, width), lambda g: (i, 0))
 
-    half = pl.BlockSpec((h, width), lambda g: (0, 0))
+    diagonal_specs = [pl.BlockSpec(v.shape, lambda g: (0, 0)) for v in diagonal]
     y_send, x_send = pl.pallas_call(
-        relay_kernel,
+        relay_kernel if len(diagonal) == 2 else relay_by_row_kernel,
         grid=(1,),
-        in_specs=[rows(1), rows(1), rows(2), rows(2), half, half],
+        in_specs=[rows(1), rows(1), rows(2), rows(2), *diagonal_specs],
         out_specs=[rows(0), rows(0)],
         out_shape=[jax.ShapeDtypeStruct((n, width), bf16)] * 2,
         compiler_params=pltpu.CompilerParams(vmem_limit_bytes=40 * 2**20),
-        cost_estimate=pl.CostEstimate(flops=6 * n * width, bytes_accessed=14 * n * width, transcendentals=0),
-    )(mine, got, mine, got, ra, rb)
+        cost_estimate=LIGHT,
+    )(mine, got, mine, got, *diagonal)
+    return mine, got, y_send, x_send
+
+
+def scatter_last(mine, got, y_send, x_send):
     return mine, got, flip(y_send, ROW), flip(x_send, COL)
 
 
@@ -94,36 +121,22 @@
     return lax.psum_scatter(v, "shard", scatter_dimension=0, tiled=True)
 
 
-def in_order(pieces, index):
-    bit = 1
-    while bit < len(pieces):
+def seq_exchange(v):
+    return lax.all_to_all(v, "seq", 0, 0, tiled=True)
+
+
+def gather_table(table, axis):
+    index, bit = lax.axis_index(axis), 1
+    while bit < lax.axis_size(axis):
+        other = flip(table, (axis, bit))
         odd = (index & bit) != 0
-        pieces = [jnp.where(odd, pieces[j ^ bit], pieces[j]) for j in range(len(pieces))]
+        table = jnp.concatenate([jnp.where(odd, other, table), jnp.where(odd, table, other)])
         bit *= 2
-    return jnp.stack(pieces)
-
-
-def seq_exchange(v):
-    S, s = lax.axis_size("seq"), lax.axis_index("seq")
-    pieces = [lax.dynamic_index_in_dim(v, s ^ j, 0, keepdims=False) for j in range(S)]
-    got = [flip(v, ("seq", j)) if j else v for j, v in enumerate(pieces)]
-    return in_order(got, s)
-
-
-def gather_table(v):
-    table = v[None]
-    for axis in ("shard", "seq"):
-        index, bit = lax.axis_index(axis), 1
-        while bit < lax.axis_size(axis):
-            other = flip(table, (axis, bit))
-            odd = (index & bit) != 0
-            table = jnp.concatenate([jnp.where(odd, other, table), jnp.where(odd, table, other)])
-            bit *= 2
     return table
 
 
 def total(v):
-    for axis in ("seq", "replica", "shard"):
+    for axis in ("shard", "seq", "replica"):
         bit = 1
         while bit < lax.axis_size(axis):
             v = v + flip(v, (axis, bit))
@@ -296,24 +309,106 @@
     refs[-1][...] = acc.astype(bf16)
 
 
-def tall_product(lefts, rights):
+def tall_product(lefts, rights, deps=()):
     deep, wide = lefts[0].shape[1], rights[0].shape[1]
     tokens = sum(v.shape[0] for v in lefts)
     tile = min(256, deep)
     return pl.pallas_call(
-        tall_kernel,
+        ordered(tall_kernel, 2 * len(lefts), deps),
         grid=(deep // tile,),
         in_specs=[pl.BlockSpec((v.shape[0], tile), lambda i: (0, i)) for v in lefts]
-        + [pl.BlockSpec(v.shape, lambda i: (0, 0)) for v in rights],
+        + [pl.BlockSpec(v.shape, lambda i: (0, 0)) for v in rights]
+        + [UNREAD] * len(deps),
         out_specs=pl.BlockSpec((tile, wide), lambda i: (i, 0)),
         out_shape=jax.ShapeDtypeStruct((deep, wide), bf16),
         compiler_params=pltpu.CompilerParams(vmem_limit_bytes=48 * 2**20),
-        cost_estimate=pl.CostEstimate(
-            flops=2 * tokens * deep * wide,
-            bytes_accessed=2 * (tokens * (deep + wide) + deep * wide),
-            transcendentals=0,
-        ),
-    )(*lefts, *rights)
+        cost_estimate=LIGHT,
+    )(*lefts, *rights, *deps)
+
+
+def up_kernel(h_ref, w_ref, bias_ref, act_ref, slope_ref):
+    u = jnp.dot(h_ref[...], w_ref[...], preferred_element_type=fp32) + bias_ref[...]
+    cdf = 0.5 * (1.0 + lax.erf(u * 0.7071067811865476))
+    act_ref[...] = (u * cdf).astype(bf16)
+    slope_ref[...] = cdf + u * jnp.exp(-0.5 * u * u) * 0.3989422804014327
+
+
+def up_product(h, w, bias):
+    tile = min(256, h.shape[0])
+    deep, wide = w.shape
+    return pl.pallas_call(
+        up_kernel,
+        grid=(h.shape[0] // tile,),
+        in_specs=[
+            pl.BlockSpec((tile, deep), lambda i: (i, 0)),
+            pl.BlockSpec((deep, wide), lambda i: (0, 0)),
+            pl.BlockSpec((1, wide), lambda i: (0, 0)),
+        ],
+        out_specs=[pl.BlockSpec((tile, wide), lambda i: (i, 0))] * 2,
+        out_shape=[jax.ShapeDtypeStruct((h.shape[0], wide), kind) for kind in (bf16, fp32)],
+        compiler_params=pltpu.CompilerParams(vmem_limit_bytes=48 * 2**20),
+        cost_estimate=LIGHT,
+    )(h, w, bias)
+
+
+def product_kernel(dims, *refs):
+    term = lax.dot_general(refs[0][...], refs[1][...], dims, preferred_element_type=fp32)
+    refs[-1][...] = (term + refs[2][...] if len(refs) == 4 else term).astype(bf16)
+
+
+def product(v, w, dims=(((1,), (0,)), ((), ())), bias=(), deps=()):
+    tile = min(256, v.shape[0])
+    wide = w.shape[1 - dims[0][1][0]]
+    return pl.pallas_call(
+        ordered(lambda *refs: product_kernel(dims, *refs), 2 + len(bias), deps),
+        grid=(v.shape[0] // tile,),
+        in_specs=[pl.BlockSpec((tile, v.shape[1]), lambda i: (i, 0)), pl.BlockSpec(w.shape, lambda i: (0, 0))]
+        + [pl.BlockSpec((1, wide), lambda i: (0, 0))] * len(bias)
+        + [UNREAD] * len(deps),
+        out_specs=pl.BlockSpec((tile, wide), lambda i: (i, 0)),
+        out_shape=jax.ShapeDtypeStruct((v.shape[0], wide), bf16),
+        compiler_params=pltpu.CompilerParams(vmem_limit_bytes=48 * 2**20),
+        cost_estimate=LIGHT,
+    )(v, w, *bias, *deps)
+
+
+def down_kernel(g_ref, out_w_ref, slope_ref, up_w_ref, pre_ref, two_ref, sums_ref):
+    grad = lax.dot_general(g_ref[...], out_w_ref[...], ACROSS, preferred_element_type=fp32)
+    low = (grad * slope_ref[...]).astype(bf16)
+    pre_ref[...] = low
+    two_ref[...] = lax.dot_general(low, up_w_ref[...], ACROSS, preferred_element_type=fp32).astype(bf16)
+
+    @pl.when(pl.program_id(0) == 0)
+    def _():
+        sums_ref[...] = jnp.zeros_like(sums_ref)
+
+    sums_ref[0:1, :] += jnp.sum(low.astype(fp32), axis=0, keepdims=True)
+
+
+def down_product(g, out_w, slope, up_w, deps=()):
+    tile = min(256, g.shape[0])
+    wide, deep = out_w.shape
+    tokens = g.shape[0]
+
+    def tiles(width):
+        return pl.BlockSpec((tile, width), lambda i: (i, 0))
+
+    def whole(a, b):
+        return pl.BlockSpec((a, b), lambda i: (0, 0))
+
+    return pl.pallas_call(
+        ordered(down_kernel, 4, deps),
+        grid=(tokens // tile,),
+        in_specs=[tiles(deep), whole(wide, deep), tiles(wide), whole(deep, wide)] + [UNREAD] * len(deps),
+        out_specs=[tiles(wide), tiles(deep), whole(8, wide)],
+        out_shape=[
+            jax.ShapeDtypeStruct((tokens, wide), bf16),
+            jax.ShapeDtypeStruct((tokens, deep), bf16),
+            jax.ShapeDtypeStruct((8, wide), fp32),
+        ],
+        compiler_params=pltpu.CompilerParams(vmem_limit_bytes=48 * 2**20),
+        cost_estimate=LIGHT,
+    )(g, out_w, slope, up_w, *deps)
 
 
 def attend_kernel(heads, own_ref, a_ref, b_ref, c_ref, d_ref, out_ref, q_ref, k_ref, v_ref):
@@ -334,9 +429,8 @@
                 upto = (a + 1) * n
                 q = q_ref[a * n : upto, :]
                 scores = lax.dot_general(q, k_ref[:upto, :], ACROSS, preferred_element_type=fp32)
-                scores = scores * HEAD_DIM ** (-0.5)
-                expons = jnp.exp(scores - jnp.max(scores, axis=-1, keepdims=True))
-                probs = (expons / jnp.sum(expons, axis=-1, keepdims=True)).astype(bf16)
+                expons = jnp.exp((scores - jnp.max(scores, axis=-1, keepdims=True)) * HEAD_DIM ** (-0.5))
+                probs = (expons * (1.0 / jnp.sum(expons, axis=-1, keepdims=True))).astype(bf16)
                 out_ref[a * (T // S) + (r ^ jr), :, cols] = jnp.dot(
                     probs, v_ref[:upto, :], preferred_element_type=fp32
                 ).astype(bf16)
@@ -368,9 +462,9 @@
                 g = grad_ref[a * (T // S) + (r ^ jr), :, cols]
                 k = k_ref[:upto, :]
                 v = v_ref[:upto, :]
-                scores = lax.dot_general(q, k, ACROSS, preferred_element_type=fp32) * scaling
-                expons = jnp.exp(scores - jnp.max(scores, axis=-1, keepdims=True))
-                probs = expons / jnp.sum(expons, axis=-1, keepdims=True)
+                scores = lax.dot_general(q, k, ACROSS, preferred_element_type=fp32)
+                expons = jnp.exp((scores - jnp.max(scores, axis=-1, keepdims=True)) * scaling)
+                probs = expons * (1.0 / jnp.sum(expons, axis=-1, keepdims=True))
                 grad_probs = lax.dot_general(g, v, ACROSS, preferred_element_type=fp32)
                 inner = jnp.sum(probs * grad_probs, axis=-1, keepdims=True)
                 grad_scores = (probs * (grad_probs - inner)).astype(bf16)
@@ -393,7 +487,26 @@
                     sums_ref[0:1, first : first + HEAD_DIM] += jnp.sum(low.astype(fp32), axis=0, keepdims=True)
 
 
-def small_call(kernel, out_shape, operands, scratch=(), flops=0, first_rows=()):
+def unpack_rows_kernel(own_ref, mine_ref, other_ref, out_ref):
+    r, n = own_ref[1], mine_ref.shape[0]
+    out_ref[pl.ds(pl.multiple_of(r * n, n), n), :] = mine_ref[...].astype(fp32)
+    out_ref[pl.ds(pl.multiple_of((r ^ 1) * n, n), n), :] = other_ref[...].astype(fp32)
+
+
+def unpack_columns_kernel(groups, S, R, own_ref, mine_ref, other_ref, out_ref):
+    r = own_ref[1]
+    a, c = groups
+    width = mine_ref.shape[-1] // (a * c)
+    for s in range(S):
+        for i in range(a):
+            for k in range(c):
+                cols = slice((i * c + k) * width, (i * c + k + 1) * width)
+                base = ((i * S + s) * c + k) * R
+                for ref, at in ((mine_ref, r), (other_ref, r ^ 1)):
+                    out_ref[:, pl.ds(pl.multiple_of((base + at) * width, 128), width)] = ref[s, :, cols].astype(fp32)
+
+
+def small_call(kernel, out_shape, operands, scratch=(), first_rows=(), deps=()):
     specs = []
     for i, v in enumerate(operands):
         if v.dtype == jnp.int32:
@@ -405,19 +518,16 @@
     many = isinstance(out_shape, list)
     outs = out_shape if many else [out_shape]
     out_specs = [pl.BlockSpec(v.shape, lambda g, rank=len(v.shape): (0,) * rank) for v in outs]
-    moved = sum(v.size * v.dtype.itemsize for v in operands) + sum(
-        v.size * jnp.dtype(v.dtype).itemsize for v in outs
-    )
     return pl.pallas_call(
-        kernel,
+        ordered(kernel, len(operands), deps),
         grid=(1,),
-        in_specs=specs,
+        in_specs=specs + [UNREAD] * len(deps),
         out_specs=out_specs if many else out_specs[0],
         out_shape=out_shape,
         scratch_shapes=scratch,
         compiler_params=pltpu.CompilerParams(vmem_limit_bytes=56 * 2**20),
-        cost_estimate=pl.CostEstimate(flops=flops, bytes_accessed=moved, transcendentals=0),
-    )(*operands)
+        cost_estimate=LIGHT,
+    )(*operands, *deps)
 
 
 def on_device(
@@ -460,142 +570,182 @@
     def by_seq(v):
         return v if rows % 128 == 0 else v.reshape(-1, Z, S, rows).swapaxes(1, 2).reshape(-1, D)
 
+    x = inputs.reshape(n, D)
+    g_low = cotangent.reshape(n, D)
     t = s * R + r
     attn_part = lax.dynamic_index_in_dim(w_attn_out.reshape(rows, R, D // R), r, 1, keepdims=False).astype(bf16)
+    small = (norm1_gain, norm1_bias, query_bias, value_bias, attn_out_bias, norm2_gain, norm2_bias, output_bias, hidden_bias)
+    attn_part, *small = tie(attn_part, *small)
     attn_part = line_gather(attn_part)
+    table = jnp.concatenate([v.astype(bf16) for v in small])[None]
+    table = gather_table(gather_table(table, "shard"), "seq")
     qkv_pieces = lax.dynamic_index_in_dim(w_qkv.reshape(rows, 3, S, R, hw), r, 3, keepdims=False).astype(bf16)
     qkv_rows = seq_exchange(qkv_pieces.transpose(2, 0, 1, 3).reshape(S, rows, 3 * hw)).reshape(S * rows, 3 * hw)
+    hidden_pieces = lax.dynamic_index_in_dim(w_hidden.reshape(rows, S, Z, R, fr), r, 3, keepdims=False).astype(bf16)
+    hidden_pieces, qkv_rows = tie(hidden_pieces.transpose(1, 0, 2, 3).reshape(S, rows, fw), qkv_rows)
     qkv_matrix = line_gather(qkv_rows)
-    hidden_pieces = lax.dynamic_index_in_dim(w_hidden.reshape(rows, S, Z, R, fr), r, 3, keepdims=False).astype(bf16)
-    hidden_pieces = after(hidden_pieces.transpose(1, 0, 2, 3).reshape(S, rows, fw), qkv_rows)
     hidden_rows = seq_exchange(hidden_pieces).reshape(S * rows, fw)
-    hidden_matrix = line_gather(hidden_rows)
     output_part = lax.dynamic_index_in_dim(w_output.reshape(R, fr, D), r, 0, keepdims=False).astype(bf16)
-    output_matrix = line_gather(after(output_part, hidden_rows))
-
-    small = (norm1_gain, norm1_bias, query_bias, value_bias, attn_out_bias, norm2_gain, norm2_bias, output_bias, hidden_bias)
-    table = gather_table(jnp.concatenate([v.astype(bf16) for v in small])).astype(fp32)
+
+    table = table.astype(fp32)
     gain_one, shift_one, query_shift, value_shift, attn_shift, gain_two, shift_two, output_shift = (
         table[:, i * rows : (i + 1) * rows].reshape(1, D) for i in range(8)
     )
     hidden_shift = lax.dynamic_index_in_dim(
         lax.dynamic_index_in_dim(table[:, 8 * rows :].reshape(S, Z, R, fr), s, 0, keepdims=False), r, 1, keepdims=False
-    ).reshape(fw)
+    ).reshape(1, fw)
     bias_row = jnp.concatenate(
         [
             lax.dynamic_slice_in_dim(query_shift[0], t * hw, hw),
             jnp.zeros((hw,), fp32),
             lax.dynamic_slice_in_dim(value_shift[0], t * hw, hw),
         ]
-    )
-
-    x = inputs.reshape(n, D)
-    g_low = cotangent.reshape(n, D)
-    hidden_in = small_call(
-        lambda *refs: norm_kernel(grid, rows, *refs), shape(n, D), (x, gain_one, shift_one), flops=10 * n * D
-    )
-    hidden_in_parts = plane_gather(by_shard(hidden_in))
-    attn_parts = plane_gather(after(attn_part, hidden_in_parts[2]))
-    qkv_parts = [
-        (jnp.dot(v, qkv_matrix, preferred_element_type=fp32) + bias_row).astype(bf16) for v in hidden_in_parts
-    ]
-    half_pairs = R * heads * (S * (S + 1) // 2) * n * n * HEAD_DIM * 2
+    ).reshape(1, 3 * hw)
+
+    hidden_in = by_shard(
+        small_call(lambda *refs: norm_kernel(grid, rows, *refs), shape(n, D), (x, gain_one, shift_one), deps=(qkv_rows,))
+    )
+    in_near = gather_near(hidden_in)
+    hidden_rows, output_part, in_near = tie(hidden_rows, output_part, in_near)
+    hidden_matrix = line_gather(hidden_rows)
+    output_matrix = line_gather(output_part)
+    hidden_in_parts = gather_parts(in_near, gather_diagonal(*in_near))
+    hidden_in_parts, attn_part = tie(hidden_in_parts, attn_part)
+    attn_near = gather_near(attn_part)
+    qkv_parts = [product(v, qkv_matrix, bias=(bias_row,)) for v in hidden_in_parts]
+    qkv_parts, attn_near = tie(qkv_parts, attn_near)
+    attn_far = gather_diagonal(*attn_near)
     head_block = pltpu.VMEM((S * n, HEAD_DIM), bf16)
     head_sums = pltpu.VMEM((S * n, HEAD_DIM), fp32)
     attended = small_call(
-        lambda *refs: attend_kernel(heads, *refs),
-        shape(T, n, hw),
-        (own, *qkv_parts),
-        [head_block] * 3,
-        flops=2 * half_pairs,
-    )
+        lambda *refs: attend_kernel(heads, *refs), shape(T, n, hw), (own, *qkv_parts), [head_block] * 3
+    )
+    attended, attn_far, attn_near = tie(attended, attn_far, attn_near)
+    attn_parts = gather_parts(attn_near, attn_far)
     attended = lax.all_to_all(attended, ("seq", "replica"), 0, 0, tiled=True)
+    attended, g_low = tie(attended, g_low)
+    g_near = gather_near(g_low)
     mid_rows, hidden_two, attended_rel = small_call(
         lambda *refs: mid_kernel(grid, rows, *refs),
         [shape(n, D, kind=fp32), shape(n, D), shape(n, D)],
         (own, attended, *attn_parts, x, attn_shift, gain_two, shift_two),
-        flops=2 * n * D * D,
-    )
-
-    hidden_two_parts = plane_gather(by_shard(hidden_two))
-    g_parts = plane_gather(after(g_low, hidden_two_parts[2]))
-    activated_parts, grad_pre_parts, grad_two_parts = [], [], []
-    for h2, g in zip(hidden_two_parts, g_parts):
-        preactive = jnp.dot(h2, hidden_matrix, preferred_element_type=fp32) + hidden_shift
-        activated_parts.append(jax.nn.gelu(preactive, approximate=False).astype(bf16))
-        grad_activated = lax.dot_general(g, output_matrix, ACROSS, preferred_element_type=fp32)
-        grad_pre = (grad_activated * gelu_slope(preactive)).astype(bf16)
-        grad_pre_parts.append(grad_pre)
-        grad_two_parts.append(
-            lax.dot_general(grad_pre, hidden_matrix, ACROSS, preferred_element_type=fp32).astype(bf16)
-        )
-    grad_output = line_scatter(tall_product(activated_parts, g_parts))
-    grad_two = plane_scatter(grad_two_parts)
-    grad_hidden = line_scatter(tall_product(hidden_two_parts, grad_pre_parts))
-
-    first = ((1, n), (2, n))
+    )
+
+    two_near = gather_near(by_shard(hidden_two))
+    two_near, g_near = tie(two_near, g_near)
+    two_diagonal = gather_diagonal(*two_near)
+    two_first = jnp.concatenate(two_near)
+    up_first = up_product(two_first, hidden_matrix, hidden_shift)
+    up_first, two_diagonal = tie(up_first, two_diagonal)
+    two_second = jnp.concatenate(two_diagonal)
+    hidden_two_parts = (two_first, flip(two_first, CORE), two_second, flip(two_second, CORE))
+    two_second, g_near = tie(two_second, g_near)
+    g_far = gather_diagonal(*g_near)
+    ups = [up_first] + [up_product(v, hidden_matrix, hidden_shift) for v in hidden_two_parts[1:]]
+    ups[1:], g_far = tie(ups[1:], g_far)
+    activated_parts, slope_parts = zip(*ups)
+    g_parts = gather_parts(g_near, g_far)
+    grad_output = tall_product(activated_parts, g_parts)
+    down = [None] * 4
+    down[3] = down_product(g_parts[3], output_matrix, slope_parts[3], hidden_matrix, (grad_output,))
+    down[2] = down_product(g_parts[2], output_matrix, slope_parts[2], hidden_matrix, (down[3][0],))
+    two_far = far_sum(down[2][1], down[3][1])
+    down[1] = down_product(g_parts[1], output_matrix, slope_parts[1], hidden_matrix, (two_far,))
+    two_got = flip(down[1][1], CORE)
+    down[0] = down_product(g_parts[0], output_matrix, slope_parts[0], hidden_matrix, (down[1][0],))
+    grad_pre_parts, grad_two_parts, hidden_sums = zip(*down)
+    grad_output = line_scatter(grad_output)
+    grad_two = scatter_relay(grad_two_parts[0], two_got, scatter_diagonal(two_far))
+    out_parts = [None] * 4
+    deps = ()
+    for i in (3, 2):
+        out_parts[i] = product(activated_parts[i], output_matrix, deps=(grad_two[3], *deps))
+        deps = (out_parts[i],)
+    grad_hidden = tall_product(hidden_two_parts, grad_pre_parts, deps)
+    out_far = far_sum(out_parts[2], out_parts[3])
+    grad_two = scatter_last(*grad_two)
+
     grad_mid, grad_mid_rel, grad_heads, sums_two = small_call(
         lambda *refs: back_mid_kernel(grid, rows, *refs),
         [shape(n, D, kind=fp32), shape(n, D), shape(T, n, hw), shape(8, D, kind=fp32)],
         (own, *map(by_seq, grad_two), mid_rows, g_low, gain_two, *attn_parts),
-        flops=2 * n * D * D,
-        first_rows=first,
-    )
+        first_rows=((1, n), (2, n)),
+        deps=(out_far, grad_hidden),
+    )
+    grad_hidden, grad_mid = tie(grad_hidden, grad_mid)
+    grad_hidden = line_scatter(grad_hidden)
+    out_parts[1] = product(activated_parts[1], output_matrix, deps=(grad_mid,))
     grad_heads = lax.all_to_all(grad_heads, ("seq", "replica"), 0, 0, tiled=True)
+    grad_heads, out_theirs, grad_output, out_far = tie(grad_heads, out_parts[1], grad_output, out_far)
+    out_diagonal = scatter_diagonal_by_row(out_far)
     *grad_qkv_parts, sums_qkv = small_call(
         lambda *refs: attend_back_kernel(heads, *refs),
         [shape(v.shape[0], 3 * hw) for v in qkv_parts] + [shape(8, 3 * hw, kind=fp32)],
         (own, *qkv_parts, grad_heads),
         [head_block] * 3 + [head_sums] * 3,
-        flops=5 * half_pairs,
-    )
+        deps=(out_parts[1],),
+    )
+    out_got = flip(out_theirs, CORE)
+    other_output = flip(grad_output, COL)
+    into = [None] * 4
+    into[3] = product(grad_qkv_parts[3], qkv_matrix, ACROSS, deps=(other_output, *out_diagonal))
+    into[2] = product(grad_qkv_parts[2], qkv_matrix, ACROSS, deps=(into[3],))
+    into_far = far_sum(into[2], into[3])
+    into[1] = product(grad_qkv_parts[1], qkv_matrix, ACROSS, deps=(into_far,))
+    into[0] = product(grad_qkv_parts[0], qkv_matrix, ACROSS, deps=(into[1],))
+    into_got = flip(into[1], CORE)
+    grad_qkv = tall_product(hidden_in_parts, grad_qkv_parts, (into[0],))
+    grad_in = scatter_relay(into[0], into_got, scatter_diagonal(into_far))
+    *grad_in, grad_qkv = tie(*grad_in, grad_qkv)
+    grad_qkv = line_scatter(grad_qkv).reshape(S, rows, 3 * hw)
     grad_attn_parts = small_call(
-        outer_kernel,
-        [shape(*v.shape) for v in attn_parts],
-        (after(attended_rel, grad_heads), grad_mid_rel),
-        flops=2 * n * D * D,
-    )
-    grad_attn = plane_scatter(grad_attn_parts)
-    grad_in_parts = [
-        lax.dot_general(v, qkv_matrix, ACROSS, preferred_element_type=fp32).astype(bf16) for v in grad_qkv_parts
-    ]
-    grad_qkv = line_scatter(tall_product(hidden_in_parts, grad_qkv_parts)).reshape(S, rows, 3 * hw)
-    grad_in = plane_scatter(grad_in_parts)
+        outer_kernel, [shape(*v.shape) for v in attn_parts], (attended_rel, grad_mid_rel), deps=(grad_in[3],)
+    )
+    attn_got = flip(grad_attn_parts[1], CORE)
+    attn_far = far_sum(grad_attn_parts[2], grad_attn_parts[3])
+    attn_diagonal = scatter_diagonal(attn_far)
+    grad_in = scatter_last(*grad_in)
     grad_inputs, sums_one = small_call(
         lambda *refs: back_in_kernel(grid, rows, *refs),
         [shape(n, D, kind=fp32), shape(8, D, kind=fp32)],
         (*map(by_seq, grad_in), x, grad_mid, gain_one),
-        flops=20 * n * D,
         first_rows=((0, n), (1, n)),
-    )
-
-    out_parts = [
-        jnp.dot(after(v, grad_qkv_parts[3]), output_matrix, preferred_element_type=fp32).astype(bf16)
-        for v in activated_parts
-    ]
+        deps=(),
+    )
+    out_parts[0] = product(activated_parts[0], output_matrix, deps=(sums_one,))
+    sums_one, attn_got, grad_hidden = tie(sums_one, attn_got, grad_hidden)
+    grad_attn = scatter_relay(grad_attn_parts[0], attn_got, attn_diagonal)
+    grad_attn = scatter_last(*grad_attn)
+    out_terms = scatter_last(*scatter_relay(out_parts[0], out_got, out_diagonal))
     layer_out = small_call(
-        out_kernel,
-        shape(n, D),
-        (*plane_scatter(out_parts), mid_rows, output_shift),
-        flops=6 * n * D,
-        first_rows=((0, n), (1, n)),
-    )
-
-    def both(v):
+        out_kernel, shape(n, D), (*out_terms, mid_rows, output_shift), first_rows=((0, n), (1, n))
+    )
+
+    def columns_of_both(v, groups):
+        v = v.reshape(-1, rows, v.shape[-1])
         other = flip(v, COL)
-        return jnp.where(odd, other, v), jnp.where(odd, v, other)
-
-    grad_output_matrix = jnp.concatenate(both(grad_output)).astype(fp32)
-    grad_hidden = jnp.stack(both(seq_exchange(grad_hidden.reshape(S, rows, fw)))).reshape(R, S, rows, Z, fr)
-    grad_hidden_matrix = grad_hidden.transpose(2, 1, 3, 0, 4).reshape(rows, F).astype(fp32)
-    grad_qkv = jnp.stack(both(seq_exchange(grad_qkv))).reshape(R, S, rows, 3, hw)
-    grad_qkv_matrix = grad_qkv.transpose(2, 3, 1, 0, 4).reshape(rows, 3 * D).astype(fp32)
+        a, c = groups
+        count, width = v.shape[0], v.shape[-1] // (a * c)
+        if width % 128 == 0:
+            return small_call(
+                lambda *refs: unpack_columns_kernel(groups, count, R, *refs),
+                shape(rows, count * R * v.shape[-1], kind=fp32),
+                (own, v, other),
+            )
+        pair = jnp.stack([jnp.where(odd, other, v), jnp.where(odd, v, other)]).reshape(R, count, rows, a, c, width)
+        return pair.transpose(2, 3, 1, 4, 0, 5).reshape(rows, -1).astype(fp32)
+
+    grad_output_matrix = small_call(
+        unpack_rows_kernel, shape(R * fr, D, kind=fp32), (own, grad_output, other_output)
+    )
+    grad_hidden_matrix = columns_of_both(seq_exchange(grad_hidden.reshape(S, rows, fw)), (1, Z))
+    grad_qkv_matrix = columns_of_both(seq_exchange(grad_qkv), (3, 1))
     deep = D // S
     p, q, u, w = (v[:deep].astype(fp32) for v in grad_attn)
     grad_attn = line_scatter((p + q + u + w).astype(bf16))
-    grad_attn_matrix = jnp.concatenate(both(grad_attn), axis=1).astype(fp32)
-
-    hidden_sums = sum(jnp.sum(v.astype(fp32), axis=0) for v in grad_pre_parts).reshape(1, Z, 1, fr)
+    grad_attn_matrix = columns_of_both(grad_attn, (1, 1))
+
+    hidden_sums = sum(v[0] for v in hidden_sums).reshape(1, Z, 1, fr)
     hidden_sums = lax.dynamic_update_slice(jnp.zeros((S, Z, R, fr), fp32), hidden_sums, (s, 0, r, 0))
     none = jnp.zeros((D,), fp32)
     sums = total(

time: 735 us -> 654 us (0.89)
  Pallas kernels: 122 us -> 249 us
  matrix products: 114 us -> 0 us
  waiting for transfers between devices: 305 us -> 200 us
  blocking collectives: 0 us -> 18.4 us
    ppermute x73 -> x60, waiting for transfers between devices: 276 us -> 127 us  [flip(): lax.ppermute(v, axis, [(i, i ^ bit) for i in range(lax.axis_size(axis))])]
    pallas_call x15 -> x39, Pallas kernels: 122 us -> 249 us  [the longest x12 87.1 us: small_call(): pl.pallas_call(ordered(kernel, len(operands), deps), grid=(1,), in_specs=...]
    dot_general x24 -> x0, matrix products: 114 us -> none  [the longest x4 36.5 us: on_device(): jnp.dot(h2, hidden_matrix, preferred_element_type=fp32) + hidden_shift]
    all_to_all x1 -> x4, waiting for transfers between devices: 14.8 us -> 66.8 us  [seq_exchange(): return lax.all_to_all(v, 'seq', 0, 0, tiled=True)]
    all_to_all x0 -> x1, blocking collectives: none -> 18.4 us  [on_device(): attended = lax.all_to_all(attended, ('seq', 'replica'), 0, 0, tiled=True)]
    ppermute x73 -> x60, starting transfers between devices: 62.6 us -> 45.1 us  [flip(): lax.ppermute(v, axis, [(i, i ^ bit) for i in range(lax.axis_size(axis))])]
    all_to_all x1 -> x4, starting transfers between devices: 3.56 us -> 14.8 us  [seq_exchange(): return lax.all_to_all(v, 'seq', 0, 0, tiled=True)]
    all_to_all x1, waiting for transfers between devices: 13.6 us -> 6.21 us  [on_device(): lax.all_to_all(grad_heads, ('seq', 'replica'), 0, 0, tiled=True)]
  transfers between devices with their start and end apart: 83 -> 73, of which waited for: 36 -> 35; matrix products, arithmetic and copies ran while one was open for 25% -> 8% of each run, Pallas kernels for 15% -> 38%
where the time goes in v3:
time: 654 us; the launch traced here: 642 us
  Pallas kernels  249 us (38%)
  waiting for transfers between devices  200 us (31%)
  local copies, waits for them, and re-layouts  78.1 us (12%)
  starting transfers between devices  64.8 us (10%)
  blocking collectives  18.4 us (3%)
  other arithmetic  16.1 us (2%)
  between operations  15.5 us (2%)
    ppermute x60, waiting for transfers between devices, flip(): lax.ppermute(v, axis, [(i, i ^ bit) for i in range(lax.axis_size(axis))])  127 us
    pallas_call x12, Pallas kernels, small_call(): pl.pallas_call(ordered(kernel, len(operands), deps), grid=(1,), in_specs=...  87.1 us
    all_to_all x4, waiting for transfers between devices, seq_exchange(): return lax.all_to_all(v, 'seq', 0, 0, tiled=True)  66.8 us
    unnamed x159, local copies, waits for them, and re-layouts  53.2 us
    pallas_call x12, Pallas kernels, product(): pl.pallas_call(ordered(lambda *refs: product_kernel(dims, *refs), 2 + len...  51.2 us
    ppermute x60, starting transfers between devices, flip(): lax.ppermute(v, axis, [(i, i ^ bit) for i in range(lax.axis_size(axis))])  45.1 us
    pallas_call x3, Pallas kernels, tall_product(): pl.pallas_call(ordered(tall_kernel, 2 * len(lefts), deps), grid=(deep //...  38.2 us
    pallas_call x4, Pallas kernels, down_product(): pl.pallas_call(ordered(down_kernel, 4, deps), grid=(tokens // tile,), in_...  36.6 us
  transfers between devices with their start and end apart: 73, of which 35 were waited for; matrix products, arithmetic and copies ran while one was open for 8% of the time, Pallas kernels for 38%

profile of v3, /device:TPU:0, one launch (start us, length us, event | category | flops | bytes accessed | tf_op | source)
XLA Modules:
  0.0 641.9 jit_solution(7164566695039373349)
XLA Ops:
  17.2 3.1 collective-permute-start
  26.3 3.5 all-to-all-start
  29.9 3.7 copy.40
  35.2 6.2 all-to-all-done
  43.1 3.5 collective-permute-done.3
  47.2 4.1 shard_map.262
  53.2 3.5 all-to-all-start.1
  56.8 2.9 fusion
  59.7 28.4 %all-to-all-done.1 = bf16[4,128,1024]{1,2,0:T(8,128)(2,1)S(1)} async-done(((bf16[4,128,1024]{1,2,0:T(8,128)(2,1)}), bf16[4,128,1024]{1,2,0:T(8,128)(2,1)S(1)}, u32[]{:S(2)}, u32[]{:S(2)}) %all-to-all-start.1) | async-done | bytes 1048608 | tf_op jit(solution)/shard_map/all_to_all | solution.py:125
  95.1 13.0 %collective-permute-done.7 = bf16[128,2048]{1,0:T(8,128)(2,1)S(1)} collective-permute-done((bf16[128,2048]{1,0:T(8,128)(2,1)S(1)}, bf16[128,2048]{1,0:T(8,128)(2,1)S(1)}, u32[]{:S(2)}, u32[]{:S(2)}) %collective-permute-start.7) | collective-permute-done | bytes 524320 | tf_op jit(solution)/shard_map/ppermute | solution.py:44
  110.0 2.7 collective-permute-done.9.refs_0_.refs_3_
  122.4 5.0 shard_map.263.refs_1_
  128.6 5.5 shard_map.264.refs_2_
  135.0 3.2 collective-permute-done.11
  143.4 11.4 %shard_map.267 = bf16[8,256,256]{2,1,0:T(8,128)(2,1)} custom-call(s32[2]{0:T(128)} %pad_add_fusion.refs_0_, bf16[768,768]{1,0:T(8,128)(2,1)} %copy-done.10, bf16[768,768]{1,0:T(8,128)(2,1)} %copy-done.11, bf16[256,768]{1,0:T(8,128)(2,1)} %copy-done.25, bf16[256,768]{1,0:T(8,128)(2,1)} %copy-done.26), custom_call_target="tpu_custom_call" | custom-call | flops 1 | bytes 1 | tf_op jit(solution)/shard_map/pallas_call | solution.py:521
  159.4 18.4 %all_to_all.30.refs_1_ = bf16[8,256,256]{2,1,0:T(8,128)(2,1)} all-to-all(bf16[8,256,256]{2,1,0:T(8,128)(2,1)S(1)} %copy-done.49), channel_id=1, replica_groups=mesh['seq'=4,'shard'=4,'replica'=2] {'seq','replica'}, dimensions={0} | all-to-all | bytes 2097152 | tf_op jit(solution)/shard_map/all_to_all | solution.py:625
  182.0 10.2 %shard_map.268 = (f32[256,2048]{1,0:T(8,128)}, bf16[256,2048]{1,0:T(8,128)(2,1)}, bf16[256,2048]{1,0:T(8,128)(2,1)}) custom-call(s32[2]{0:T(128)} %pad_add_fusion.refs_0_, bf16[8,256,256]{2,1,0:T(8,128)(2,1)} %all_to_all.30.refs_1_, bf16[1536,1024]{1,0:T(8,128)(2,1)} %copy-done.43, bf16[1536,1024]{1,0:T(8,128)(2,1)} %copy-done.45, ...), custom_call_target="tpu_custom_call" | custom-call | flops 1 | bytes 1 | tf_op jit(solution)/shard_map/pallas_call | solution.py:521
  194.7 9.3 %collective-permute-done.19 = bf16[256,2048]{1,0:T(8,128)(2,1)} collective-permute-done((bf16[256,2048]{1,0:T(8,128)(2,1)}, bf16[256,2048]{1,0:T(8,128)(2,1)}, u32[]{:S(2)}, u32[]{:S(2)}) %collective-permute-start.19) | collective-permute-done | bytes 1048608 | tf_op jit(solution)/shard_map/ppermute | solution.py:44
  205.2 20.5 %collective-permute-done.17 = bf16[256,2048]{1,0:T(8,128)(2,1)S(1)} collective-permute-done((bf16[256,2048]{1,0:T(8,128)(2,1)}, bf16[256,2048]{1,0:T(8,128)(2,1)S(1)}, u32[]{:S(2)}, u32[]{:S(2)}) %collective-permute-start.17) | collective-permute-done | bytes 1048608 | tf_op jit(solution)/shard_map/ppermute | solution.py:44
  233.3 7.5 %shard_map.269 = (bf16[768,1024]{1,0:T(8,128)(2,1)S(1)}, f32[768,1024]{1,0:T(8,128)S(1)}) custom-call(bf16[768,2048]{1,0:T(8,128)(2,1)} %constant_dynamic-update-slice_fusion.10.h_ref.refs_0_, bf16[2048,1024]{1,0:T(8,128)(2,1)} %all-gather.9.cloned.1.call-done.w_ref.refs_3_, f32[1,1024]{1,0:T(1,128)S(1)} %bitcast.74), custom_call_target="tpu_custom_call" | custom-call | flops 1 | bytes 1 | tf_op jit(solution)/shard_map/pallas_call | solution.py:339
  253.7 3.8 shard_map.271
  258.5 4.4 shard_map.272
  263.9 7.6 %shard_map.270 = (bf16[768,1024]{1,0:T(8,128)(2,1)S(1)}, f32[768,1024]{1,0:T(8,128)S(1)}) custom-call(bf16[768,2048]{1,0:T(8,128)(2,1)} %collective-permute-done.23.h_ref.refs_1_, bf16[2048,1024]{1,0:T(8,128)(2,1)} %all-gather.9.cloned.1.call-done.w_ref.refs_3_, f32[1,1024]{1,0:T(1,128)S(1)} %bitcast.77), custom_call_target="tpu_custom_call" | custom-call | flops 1 | bytes 1 | tf_op jit(solution)/shard_map/pallas_call | solution.py:339
  277.0 13.7 %shard_map.273.refs_4_ = bf16[1024,2048]{1,0:T(8,128)(2,1)} custom-call(bf16[768,1024]{1,0:T(8,128)(2,1)S(1)} %get-tuple-element.175.refs_0_, bf16[768,1024]{1,0:T(8,128)(2,1)} %copy-done.15, bf16[256,1024]{1,0:T(8,128)(2,1)S(1)} %get-tuple-element.198.refs_2_.refs_0_, bf16[256,1024]{1,0:T(8,128)(2,1)S(1)} %get-tuple-element.199.refs_3_.refs_0_, ...), custom_call_target="tpu_custom_call" | custom-call | flops 1 | bytes 1 | tf_op jit(solution)/shard_map/pallas_call | solution.py:316
  292.1 6.7 %shard_map.274 = (bf16[256,1024]{1,0:T(8,128)(2,1)S(1)}, bf16[256,2048]{1,0:T(8,128)(2,1)S(1)}, f32[8,1024]{1,0:T(8,128)S(1)}) custom-call(bf16[256,2048]{1,0:T(8,128)(2,1)S(1)} %collective-permute-done.27.refs_7_.refs_0_, bf16[1024,2048]{1,0:T(8,128)(2,1)} %all-gather.11.cloned.1.call-done.refs_1_, f32[256,1024]{1,0:T(8,128)S(1)} %copy-done.37, ...), custom_call_target="tpu_custom_call" | custom-call | flops 1 | bytes 1 | tf_op jit(solution)/shard_map/pallas_call | solution.py:399
  298.8 5.8 shard_map.275
  305.1 11.7 %shard_map.276 = (bf16[768,1024]{1,0:T(8,128)(2,1)S(1)}, bf16[768,2048]{1,0:T(8,128)(2,1)S(1)}, f32[8,1024]{1,0:T(8,128)S(1)}) custom-call(bf16[768,2048]{1,0:T(8,128)(2,1)} %collective-permute-done.22.refs_5_.refs_0_, bf16[1024,2048]{1,0:T(8,128)(2,1)} %all-gather.11.cloned.1.call-done.refs_1_, f32[768,1024]{1,0:T(8,128)} %copy-done.28, ...), custom_call_target="tpu_custom_call" | custom-call | flops 1 | bytes 1 | tf_op jit(solution)/shard_map/pallas_call | solution.py:399
  318.9 12.4 %shard_map.277 = (bf16[768,1024]{1,0:T(8,128)(2,1)S(1)}, bf16[768,2048]{1,0:T(8,128)(2,1)}, f32[8,1024]{1,0:T(8,128)S(1)}) custom-call(bf16[768,2048]{1,0:T(8,128)(2,1)} %copy-done.44, bf16[1024,2048]{1,0:T(8,128)(2,1)} %all-gather.11.cloned.1.call-done.refs_1_, f32[768,1024]{1,0:T(8,128)} %copy-done.27, ...), custom_call_target="tpu_custom_call" | custom-call | flops 1 | bytes 1 | tf_op jit(solution)/shard_map/pallas_call | solution.py:399
  332.0 3.0 copy-done.6
  336.4 4.5 shard_map.279.refs_3_
  342.9 3.4 shard_map.280.refs_8_
  346.4 13.2 %shard_map.281.refs_13_ = bf16[2048,1024]{1,0:T(8,128)(2,1)} custom-call(bf16[768,2048]{1,0:T(8,128)(2,1)} %constant_dynamic-update-slice_fusion.10.h_ref.refs_0_, bf16[768,2048]{1,0:T(8,128)(2,1)} %collective-permute-done.23.h_ref.refs_1_, bf16[256,2048]{1,0:T(8,128)(2,1)S(1)} %constant_dynamic-update-slice_fusion.13.h_ref.refs_2_, ...), custom_call_target="tpu_custom_call" | custom-call | flops 1 | bytes 1 | tf_op jit(solution)/shard_map/pallas_call | solution.py:316
  362.2 4.6 collective-permute-done.32.refs_3_
  367.4 12.5 %shard_map.282 = (f32[256,2048]{1,0:T(8,128)}, bf16[256,2048]{1,0:T(8,128)(2,1)}, bf16[8,256,256]{2,1,0:T(8,128)(2,1)}, f32[8,2048]{1,0:T(8,128)}) custom-call(s32[2]{0:T(128)} %pad_add_fusion.refs_0_, bf16[768,2048]{1,0:T(8,128)(2,1)} %get-tuple-element.204.y_ref.x_ref.refs_1_, bf16[768,2048]{1,0:T(8,128)(2,1)} %copy-done.5, ...), custom_call_target="tpu_custom_call" | custom-call | flops 1 | bytes 1 | tf_op jit(solution)/shard_map/pallas_call | solution.py:521
  380.0 4.4 all-to-all-start.3
  385.9 7.2 %shard_map.283.refs_6_ = bf16[768,2048]{1,0:T(8,128)(2,1)} custom-call(bf16[768,1024]{1,0:T(8,128)(2,1)S(1)} %copy-done.16, bf16[1024,2048]{1,0:T(8,128)(2,1)} %all-gather.11.cloned.1.call-done.refs_1_, f32[256,2048]{1,0:T(8,128)S(1)} %copy-done.12), custom_call_target="tpu_custom_call" | custom-call | flops 1 | bytes 1 | tf_op jit(solution)/shard_map/pallas_call | solution.py:362
  393.1 6.2 all-to-all-done.3.refs_5_
  400.9 17.9 %shard_map.284 = (bf16[768,768]{1,0:T(8,128)(2,1)}, bf16[768,768]{1,0:T(8,128)(2,1)}, bf16[256,768]{1,0:T(8,128)(2,1)}, bf16[256,768]{1,0:T(8,128)(2,1)}, f32[8,768]{1,0:T(8,128)}) custom-call(s32[2]{0:T(128)} %pad_add_fusion.refs_0_, bf16[768,768]{1,0:T(8,128)(2,1)} %copy-done.10, bf16[768,768]{1,0:T(8,128)(2,1)} %copy-done.11, ...), custom_call_target="tpu_custom_call" | custom-call | flops 1 | bytes 1 | tf_op jit(solution)/shard_map/pallas_call | solution.py:521
  418.8 5.2 collective-permute-done.36.refs_3_.rb_ref
  426.7 3.0 shard_map.285.refs_2_
  432.9 6.0 shard_map.287.refs_2_
  441.8 5.0 shard_map.288.y_ref.x_ref.refs_8_.refs_0_
  448.5 11.3 %shard_map.290 = bf16[2048,768]{1,0:T(8,128)(2,1)} custom-call(bf16[768,2048]{1,0:T(8,128)(2,1)} %copy-done.8, bf16[768,2048]{1,0:T(8,128)(2,1)} %collective-permute-done.6.refs_0_.refs_1_, bf16[256,2048]{1,0:T(8,128)(2,1)} %constant_dynamic-update-slice_fusion.3.refs_0_.refs_2_, bf16[256,2048]{1,0:T(8,128)(2,1)} %collective-permute-done.9.refs_0_.refs_3_, ...), custom_call_target="tpu_custom_call" | custom-call | flops 1 | bytes 1 | tf_op jit(solution)/shard_map/pallas_call | solution.py:316
  461.8 3.2 shard_map.289
  466.0 6.0 shard_map.295
  475.0 5.5 collective-permute-done.53
  484.0 14.5 %collective-permute-done.41.refs_2_ = bf16[256,2048]{1,0:T(8,128)(2,1)S(1)} collective-permute-done((bf16[256,2048]{1,0:T(8,128)(2,1)S(1)}, bf16[256,2048]{1,0:T(8,128)(2,1)S(1)}, u32[]{:S(2)}, u32[]{:S(2)}) %collective-permute-start.41) | collective-permute-done | bytes 1048608 | tf_op jit(solution)/shard_map/ppermute | solution.py:44
  500.5 7.4 %shard_map.291 = (f32[256,2048]{1,0:T(8,128)}, f32[8,2048]{1,0:T(8,128)}) custom-call(bf16[768,2048]{1,0:T(8,128)(2,1)} %copy-done.2, bf16[768,2048]{1,0:T(8,128)(2,1)} %copy-done.7, bf16[256,2048]{1,0:T(8,128)(2,1)} %copy-done.56, bf16[256,2048]{1,0:T(8,128)(2,1)} %copy-done.57, bf16[256,2048]{1,0:T(8,128)(2,1)} %bitcast.80, ...), custom_call_target="tpu_custom_call" | custom-call | flops 1 | bytes 1 | tf_op jit(solution)/shard_map/pallas_call | solution.py:521
  512.1 3.5 shard_map.297
  521.1 6.1 shard_map.292.y_ref.x_ref.refs_0_
  527.1 4.2 shard_map.293
  532.9 4.2 all-to-all-start.5
  537.1 4.8 collective-permute-done.56
  542.8 3.7 add_convert_fusion
  546.6 26.6 %all-to-all-done.5.refs_1_ = bf16[4,128,1024]{2,1,0:T(8,128)(2,1)} async-done(((bf16[4,128,1024]{2,1,0:T(8,128)(2,1)}), bf16[4,128,1024]{2,1,0:T(8,128)(2,1)}, u32[]{:S(2)}, u32[]{:S(2)}) %all-to-all-start.5) | async-done | bytes 1048608 | tf_op jit(solution)/shard_map/all_to_all | solution.py:125
  573.2 3.5 all-to-all-start.4
  578.4 4.3 collective-permute-done.47
  582.8 5.5 all-to-all-done.4.refs_1_
  592.6 3.4 collective-permute-done.50
  597.1 3.8 shard_map.300
  600.9 4.5 shard_map.294
  606.5 15.5 %collective-permute-done.51 = f32[16,1536]{1,0:T(8,128)S(1)} collective-permute-done((f32[16,1536]{1,0:T(8,128)S(1)}, f32[16,1536]{1,0:T(8,128)S(1)}, u32[]{:S(2)}, u32[]{:S(2)}) %collective-permute-start.51) | collective-permute-done | bytes 98336 | tf_op jit(solution)/shard_map/ppermute | solution.py:44
  624.1 3.9 shard_map.299
  631.6 3.3 shard_map.296
  (366 shorter events, 149.5 us)
Async XLA Ops:
  7.2 102.8 %all-gather.5.cloned.1.call-start = ((), (), s32[]{:S(2)}) async-start(), calls=%async_computation.10 | async-start | bytes 1310720 | tf_op jit(solution)/shard_map/all_gather | solution.py:117
  22.7 10.9 %collective-permute-start.1 = (bf16[2,1536]{1,0:T(2,128)(2,1)S(1)}, bf16[2,1536]{1,0:T(2,128)(2,1)S(1)}, u32[]{:S(2)}, u32[]{:S(2)}) collective-permute-start(bf16[2,1536]{1,0:T(2,128)(2,1)S(1)} %pad_maximum_fusion.2), channel_id=1, source_target_pairs={{0,4},{2,6},{4,0},{6,2},{1,5},{3,7},{5,1},{7,3},{8,12},{10,14},{12... | collective-permute-start | bytes 18440 | tf_op jit(solution)/shard_map/ppermute | solution.py:44
  26.3 15.2 %all-to-all-start = ((bf16[4,128,768]{1,2,0:T(8,128)(2,1)}), bf16[4,128,768]{1,2,0:T(8,128)(2,1)S(1)}, u32[]{:S(2)}, u32[]{:S(2)}) async-start(bf16[4,128,768]{1,2,0:T(8,128)(2,1)} %bitcast.11), calls=%async_computation | async-start | bytes 1572864 | tf_op jit(solution)/shard_map/all_to_all | solution.py:125
  29.9 84.7 %all-gather.7.cloned.1.call-start = ((), (), s32[]{:S(2)}) async-start(), calls=%async_computation.11 | async-start | bytes 3932160 | tf_op jit(solution)/shard_map/all_gather | solution.py:117
  51.4 38.0 %collective-permute-start.5 = (bf16[256,2048]{1,0:T(8,128)(2,1)}, bf16[256,2048]{1,0:T(8,128)(2,1)S(1)}, u32[]{:S(2)}, u32[]{:S(2)}) collective-permute-start(bf16[256,2048]{1,0:T(8,128)(2,1)} %shard_map.262), channel_id=1, source_target_pairs={{0,1},{1,0},{2,3},{3,2},{4,5},{5,4},{6,7},{7,6},{8,9},{9,8},{10,11... | collective-permute-start | bytes 3145736 | tf_op jit(solution)/shard_map/ppermute | solution.py:44
  52.8 36.5 %collective-permute-start.4 = (bf16[256,2048]{1,0:T(8,128)(2,1)}, bf16[256,2048]{1,0:T(8,128)(2,1)S(1)}, u32[]{:S(2)}, u32[]{:S(2)}) collective-permute-start(bf16[256,2048]{1,0:T(8,128)(2,1)} %shard_map.262), channel_id=1, source_target_pairs={{0,16},{8,24},{16,0},{24,8},{1,17},{9,25},{17,1},{25,9},{2,18},{10... | collective-permute-start | bytes 3145736 | tf_op jit(solution)/shard_map/ppermute | solution.py:44
  53.2 34.9 %all-to-all-start.1 = ((bf16[4,128,1024]{1,2,0:T(8,128)(2,1)}), bf16[4,128,1024]{1,2,0:T(8,128)(2,1)S(1)}, u32[]{:S(2)}, u32[]{:S(2)}) async-start(bf16[4,128,1024]{1,2,0:T(8,128)(2,1)} %bitcast.6), calls=%async_computation.1 | async-start | bytes 2097152 | tf_op jit(solution)/shard_map/all_to_all | solution.py:125
  56.7 176.6 %all-gather.9.cloned.1.call-start = ((), (), s32[]{:S(2)}) async-start(), calls=%async_computation.12 | async-start | bytes 5242880 | tf_op jit(solution)/shard_map/all_gather | solution.py:117
  93.5 19.2 %collective-permute-start.6 = (bf16[768,2048]{1,0:T(8,128)(2,1)S(1)}, bf16[768,2048]{1,0:T(8,128)(2,1)}, u32[]{:S(2)}, u32[]{:S(2)}) collective-permute-start(bf16[768,2048]{1,0:T(8,128)(2,1)S(1)} %constant_dynamic-update-slice_fusion.refs_0_), channel_id=1, source_target_pairs={{0,8},{8,0},{16,24},{24,16},{1,9},{9,1},{17,25},{25,17},{2,10},{10... | collective-permute-start | bytes 9437192 | tf_op jit(solution)/shard_map/ppermute | solution.py:44
  93.7 14.4 %collective-permute-start.7 = (bf16[128,2048]{1,0:T(8,128)(2,1)S(1)}, bf16[128,2048]{1,0:T(8,128)(2,1)S(1)}, u32[]{:S(2)}, u32[]{:S(2)}) collective-permute-start(bf16[128,2048]{1,0:T(8,128)(2,1)S(1)} %slice.167), channel_id=1, source_target_pairs={{0,1},{1,0},{2,3},{3,2},{4,5},{5,4},{6,7},{7,6},{8,9},{9,8},{10,11... | collective-permute-start | bytes 1572872 | tf_op jit(solution)/shard_map/ppermute | solution.py:44
  94.4 14.5 %collective-permute-start.8 = (bf16[128,2048]{1,0:T(8,128)(2,1)S(1)}, bf16[128,2048]{1,0:T(8,128)(2,1)S(1)}, u32[]{:S(2)}, u32[]{:S(2)}) collective-permute-start(bf16[128,2048]{1,0:T(8,128)(2,1)S(1)} %slice.168), channel_id=1, source_target_pairs={{0,16},{8,24},{16,0},{24,8},{1,17},{9,25},{17,1},{25,9},{2,18},{10... | collective-permute-start | bytes 1572872 | tf_op jit(solution)/shard_map/ppermute | solution.py:44
  109.8 181.1 %all-gather.11.cloned.1.call-start = ((), (), s32[]{:S(2)}) async-start(), calls=%async_computation.13 | async-start | bytes 5242880 | tf_op jit(solution)/shard_map/all_gather | solution.py:117
  112.7 25.5 %collective-permute-start.11 = (bf16[512,1024]{1,0:T(8,128)(2,1)}, bf16[512,1024]{1,0:T(8,128)(2,1)}, u32[]{:S(2)}, u32[]{:S(2)}) collective-permute-start(bf16[512,1024]{1,0:T(8,128)(2,1)} %all-gather.5.cloned.1.call-done), channel_id=1, source_target_pairs={{0,1},{1,0},{2,3},{3,2},{4,5},{5,4},{6,7},{7,6},{8,9},{9,8},{10,11... | collective-permute-start | bytes 3145736 | tf_op jit(solution)/shard_map/ppermute | solution.py:44
  113.8 25.2 %collective-permute-start.10 = (bf16[512,1024]{1,0:T(8,128)(2,1)}, bf16[512,1024]{1,0:T(8,128)(2,1)}, u32[]{:S(2)}, u32[]{:S(2)}) collective-permute-start(bf16[512,1024]{1,0:T(8,128)(2,1)} %all-gather.5.cloned.1.call-done), channel_id=1, source_target_pairs={{0,16},{8,24},{16,0},{24,8},{1,17},{9,25},{17,1},{25,9},{2,18},{10... | collective-permute-start | bytes 3145736 | tf_op jit(solution)/shard_map/ppermute | solution.py:44
  141.2 13.6 %collective-permute-start.13 = (bf16[256,1024]{1,0:T(8,128)(2,1)S(1)}, bf16[256,1024]{1,0:T(8,128)(2,1)S(1)}, u32[]{:S(2)}, u32[]{:S(2)}) collective-permute-start(bf16[256,1024]{1,0:T(8,128)(2,1)S(1)} %slice.172), channel_id=1, source_target_pairs={{0,16},{8,24},{16,0},{24,8},{1,17},{9,25},{17,1},{25,9},{2,18},{10... | collective-permute-start | bytes 1572872 | tf_op jit(solution)/shard_map/ppermute | solution.py:44
  141.9 12.9 %collective-permute-start.12 = (bf16[256,1024]{1,0:T(8,128)(2,1)S(1)}, bf16[256,1024]{1,0:T(8,128)(2,1)}, u32[]{:S(2)}, u32[]{:S(2)}) collective-permute-start(bf16[256,1024]{1,0:T(8,128)(2,1)S(1)} %slice.171), channel_id=1, source_target_pairs={{0,1},{1,0},{2,3},{3,2},{4,5},{5,4},{6,7},{7,6},{8,9},{9,8},{10,11... | collective-permute-start | bytes 1572872 | tf_op jit(solution)/shard_map/ppermute | solution.py:44
  157.6 21.8 %collective-permute-start.14 = (bf16[1536,1024]{1,0:T(8,128)(2,1)S(1)}, bf16[1536,1024]{1,0:T(8,128)(2,1)S(1)}, u32[]{:S(2)}, u32[]{:S(2)}) collective-permute-start(bf16[1536,1024]{1,0:T(8,128)(2,1)S(1)} %constant_dynamic-update-slice_fusion.5.refs_2_.refs_8_), channel_id=1, source_target_pairs={{0,8},{8,0},{16,24},{24,16},{1,9},{9,1},{17,25},{25,17},{2,10},{10... | collective-permute-start | bytes 9437192 | tf_op jit(solution)/shard_map/ppermute | solution.py:44
  159.2 20.2 %collective-permute-start.15 = (bf16[512,1024]{1,0:T(8,128)(2,1)S(1)}, bf16[512,1024]{1,0:T(8,128)(2,1)S(1)}, u32[]{:S(2)}, u32[]{:S(2)}) collective-permute-start(bf16[512,1024]{1,0:T(8,128)(2,1)S(1)} %constant_dynamic-update-slice_fusion.8.refs_4_.refs_10_), channel_id=1, source_target_pairs={{0,8},{8,0},{16,24},{24,16},{1,9},{9,1},{17,25},{25,17},{2,10},{10... | collective-permute-start | bytes 3145736 | tf_op jit(solution)/shard_map/ppermute | solution.py:44
  177.7 26.3 %collective-permute-start.19 = (bf16[256,2048]{1,0:T(8,128)(2,1)}, bf16[256,2048]{1,0:T(8,128)(2,1)}, u32[]{:S(2)}, u32[]{:S(2)}) collective-permute-start(bf16[256,2048]{1,0:T(8,128)(2,1)} %bitcast.23.refs_6_), channel_id=1, source_target_pairs={{0,1},{1,0},{2,3},{3,2},{4,5},{5,4},{6,7},{7,6},{8,9},{9,8},{10,11... | collective-permute-start | bytes 3145736 | tf_op jit(solution)/shard_map/ppermute | solution.py:44
  178.8 26.4 %collective-permute-start.18 = (bf16[256,2048]{1,0:T(8,128)(2,1)}, bf16[256,2048]{1,0:T(8,128)(2,1)}, u32[]{:S(2)}, u32[]{:S(2)}) collective-permute-start(bf16[256,2048]{1,0:T(8,128)(2,1)} %bitcast.23.refs_6_), channel_id=1, source_target_pairs={{0,16},{8,24},{16,0},{24,8},{1,17},{9,25},{17,1},{25,9},{2,18},{10... | collective-permute-start | bytes 3145736 | tf_op jit(solution)/shard_map/ppermute | solution.py:44
  192.2 33.5 %collective-permute-start.17 = (bf16[256,2048]{1,0:T(8,128)(2,1)}, bf16[256,2048]{1,0:T(8,128)(2,1)S(1)}, u32[]{:S(2)}, u32[]{:S(2)}) collective-permute-start(bf16[256,2048]{1,0:T(8,128)(2,1)} %get-tuple-element.169), channel_id=1, source_target_pairs={{0,1},{1,0},{2,3},{3,2},{4,5},{5,4},{6,7},{7,6},{8,9},{9,8},{10,11... | collective-permute-start | bytes 3145736 | tf_op jit(solution)/shard_map/ppermute | solution.py:44
  193.2 32.9 %collective-permute-start.16 = (bf16[256,2048]{1,0:T(8,128)(2,1)}, bf16[256,2048]{1,0:T(8,128)(2,1)S(1)}, u32[]{:S(2)}, u32[]{:S(2)}) collective-permute-start(bf16[256,2048]{1,0:T(8,128)(2,1)} %get-tuple-element.169), channel_id=1, source_target_pairs={{0,16},{8,24},{16,0},{24,8},{1,17},{9,25},{17,1},{25,9},{2,18},{10... | collective-permute-start | bytes 3145736 | tf_op jit(solution)/shard_map/ppermute | solution.py:44
  194.7 204.6 %reduce-scatter.5.cloned.1.call-start = ((), (), s32[]{:S(2)}) async-start(), calls=%async_computation.14 | async-start | bytes 5242880 | tf_op jit(solution)/shard_map/reduce_scatter | solution.py:121
  227.7 13.3 %collective-permute-start.21 = (bf16[128,2048]{1,0:T(8,128)(2,1)}, bf16[128,2048]{1,0:T(8,128)(2,1)}, u32[]{:S(2)}, u32[]{:S(2)}) collective-permute-start(bf16[128,2048]{1,0:T(8,128)(2,1)} %slice.178), channel_id=1, source_target_pairs={{0,16},{8,24},{16,0},{24,8},{1,17},{9,25},{17,1},{25,9},{2,18},{10... | collective-permute-start | bytes 1572872 | tf_op jit(solution)/shard_map/ppermute | solution.py:44
  228.4 13.7 %collective-permute-start.20 = (bf16[128,2048]{1,0:T(8,128)(2,1)}, bf16[128,2048]{1,0:T(8,128)(2,1)}, u32[]{:S(2)}, u32[]{:S(2)}) collective-permute-start(bf16[128,2048]{1,0:T(8,128)(2,1)} %slice.177), channel_id=1, source_target_pairs={{0,1},{1,0},{2,3},{3,2},{4,5},{5,4},{6,7},{7,6},{8,9},{9,8},{10,11... | collective-permute-start | bytes 1572872 | tf_op jit(solution)/shard_map/ppermute | solution.py:44
  233.2 30.7 %collective-permute-start.23 = (bf16[768,2048]{1,0:T(8,128)(2,1)}, bf16[768,2048]{1,0:T(8,128)(2,1)}, u32[]{:S(2)}, u32[]{:S(2)}) collective-permute-start(bf16[768,2048]{1,0:T(8,128)(2,1)} %constant_dynamic-update-slice_fusion.10.h_ref.refs_0_), channel_id=1, source_target_pairs={{0,8},{8,0},{16,24},{24,16},{1,9},{9,1},{17,25},{25,17},{2,10},{10... | collective-permute-start | bytes 9437192 | tf_op jit(solution)/shard_map/ppermute | solution.py:44
  248.6 25.7 %collective-permute-start.22 = (bf16[768,2048]{1,0:T(8,128)(2,1)S(1)}, bf16[768,2048]{1,0:T(8,128)(2,1)}, u32[]{:S(2)}, u32[]{:S(2)}) collective-permute-start(bf16[768,2048]{1,0:T(8,128)(2,1)S(1)} %constant_dynamic-update-slice_fusion.15.refs_4_.refs_0_), channel_id=1, source_target_pairs={{0,8},{8,0},{16,24},{24,16},{1,9},{9,1},{17,25},{25,17},{2,10},{10... | collective-permute-start | bytes 9437192 | tf_op jit(solution)/shard_map/ppermute | solution.py:44
  248.7 9.9 %collective-permute-start.24 = (bf16[256,2048]{1,0:T(8,128)(2,1)S(1)}, bf16[256,2048]{1,0:T(8,128)(2,1)S(1)}, u32[]{:S(2)}, u32[]{:S(2)}) collective-permute-start(bf16[256,2048]{1,0:T(8,128)(2,1)S(1)} %constant_dynamic-update-slice_fusion.13.h_ref.refs_2_), channel_id=1, source_target_pairs={{0,8},{8,0},{16,24},{24,16},{1,9},{9,1},{17,25},{25,17},{2,10},{10... | collective-permute-start | bytes 3145736 | tf_op jit(solution)/shard_map/ppermute | solution.py:44
  251.8 21.4 %collective-permute-start.26 = (bf16[128,2048]{1,0:T(8,128)(2,1)S(1)}, bf16[128,2048]{1,0:T(8,128)(2,1)S(1)}, u32[]{:S(2)}, u32[]{:S(2)}) collective-permute-start(bf16[128,2048]{1,0:T(8,128)(2,1)S(1)} %slice.180), channel_id=1, source_target_pairs={{0,16},{8,24},{16,0},{24,8},{1,17},{9,25},{17,1},{25,9},{2,18},{10... | collective-permute-start | bytes 1572872 | tf_op jit(solution)/shard_map/ppermute | solution.py:44
  252.6 20.6 %collective-permute-start.25 = (bf16[128,2048]{1,0:T(8,128)(2,1)S(1)}, bf16[128,2048]{1,0:T(8,128)(2,1)S(1)}, u32[]{:S(2)}, u32[]{:S(2)}) collective-permute-start(bf16[128,2048]{1,0:T(8,128)(2,1)S(1)} %slice.179), channel_id=1, source_target_pairs={{0,1},{1,0},{2,3},{3,2},{4,5},{5,4},{6,7},{7,6},{8,9},{9,8},{10,11... | collective-permute-start | bytes 1572872 | tf_op jit(solution)/shard_map/ppermute | solution.py:44
  290.8 217.1 %reduce-scatter.7.cloned.1.call-start = ((), (), s32[]{:S(2)}) async-start(), calls=%async_computation.15 | async-start | bytes 5242880 | tf_op jit(solution)/shard_map/reduce_scatter | solution.py:121
  298.7 5.9 collective-permute-start.28
  316.8 15.2 %collective-permute-start.29 = (bf16[768,2048]{1,0:T(8,128)(2,1)S(1)}, bf16[768,2048]{1,0:T(8,128)(2,1)S(1)}, u32[]{:S(2)}, u32[]{:S(2)}) collective-permute-start(bf16[768,2048]{1,0:T(8,128)(2,1)S(1)} %get-tuple-element.205), channel_id=1, source_target_pairs={{0,8},{8,0},{16,24},{24,16},{1,9},{9,1},{17,25},{25,17},{2,10},{10... | collective-permute-start | bytes 9437192 | tf_op jit(solution)/shard_map/ppermute | solution.py:44
  317.5 13.9 %collective-permute-start.31 = (bf16[128,2048]{1,0:T(8,128)(2,1)S(1)}, bf16[128,2048]{1,0:T(8,128)(2,1)S(1)}, u32[]{:S(2)}, u32[]{:S(2)}) collective-permute-start(bf16[128,2048]{1,0:T(8,128)(2,1)S(1)} %get-tuple-element.255), channel_id=1, source_target_pairs={{0,16},{8,24},{16,0},{24,8},{1,17},{9,25},{17,1},{25,9},{2,18},{10... | collective-permute-start | bytes 1572872 | tf_op jit(solution)/shard_map/ppermute | solution.py:44
  318.4 13.6 %collective-permute-start.30 = (bf16[128,2048]{1,0:T(8,128)(2,1)S(1)}, bf16[128,2048]{1,0:T(8,128)(2,1)S(1)}, u32[]{:S(2)}, u32[]{:S(2)}) collective-permute-start(bf16[128,2048]{1,0:T(8,128)(2,1)S(1)} %get-tuple-element.256), channel_id=1, source_target_pairs={{0,1},{1,0},{2,3},{3,2},{4,5},{5,4},{6,7},{7,6},{8,9},{9,8},{10,11... | collective-permute-start | bytes 1572872 | tf_op jit(solution)/shard_map/ppermute | solution.py:44
  340.9 18.7 %collective-permute-start.34 = (bf16[256,2048]{1,0:T(8,128)(2,1)}, bf16[256,2048]{1,0:T(8,128)(2,1)}, u32[]{:S(2)}, u32[]{:S(2)}) collective-permute-start(bf16[256,2048]{1,0:T(8,128)(2,1)} %shard_map.279.refs_3_), channel_id=1, source_target_pairs={{0,8},{8,0},{16,24},{24,16},{1,9},{9,1},{17,25},{25,17},{2,10},{10... | collective-permute-start | bytes 3145736 | tf_op jit(solution)/shard_map/ppermute | solution.py:44
  340.9 25.9 %collective-permute-start.32 = (bf16[256,2048]{1,0:T(8,128)(2,1)}, bf16[256,2048]{1,0:T(8,128)(2,1)}, u32[]{:S(2)}, u32[]{:S(2)}) collective-permute-start(bf16[256,2048]{1,0:T(8,128)(2,1)} %get-tuple-element.206), channel_id=1, source_target_pairs={{0,16},{8,24},{16,0},{24,8},{1,17},{9,25},{17,1},{25,9},{2,18},{10... | collective-permute-start | bytes 3145736 | tf_op jit(solution)/shard_map/ppermute | solution.py:44
  342.0 25.4 %collective-permute-start.33 = (bf16[256,2048]{1,0:T(8,128)(2,1)S(1)}, bf16[256,2048]{1,0:T(8,128)(2,1)}, u32[]{:S(2)}, u32[]{:S(2)}) collective-permute-start(bf16[256,2048]{1,0:T(8,128)(2,1)S(1)} %get-tuple-element.207.refs_2_), channel_id=1, source_target_pairs={{0,1},{1,0},{2,3},{3,2},{4,5},{5,4},{6,7},{7,6},{8,9},{9,8},{10,11... | collective-permute-start | bytes 3145736 | tf_op jit(solution)/shard_map/ppermute | solution.py:44
  380.0 19.3 %all-to-all-start.3 = ((bf16[8,256,256]{2,1,0:T(8,128)(2,1)}), bf16[8,256,256]{2,1,0:T(8,128)(2,1)}, u32[]{:S(2)}, u32[]{:S(2)}) async-start(bf16[8,256,256]{2,1,0:T(8,128)(2,1)} %get-tuple-element.211), calls=%async_computation.3 | async-start | bytes 2097152 | tf_op jit(solution)/shard_map/all_to_all | solution.py:678
  384.4 188.8 %reduce-scatter.9.cloned.1.call-start = ((), (), s32[]{:S(2)}) async-start(), calls=%async_computation.16 | async-start | bytes 3932160 | tf_op jit(solution)/shard_map/reduce_scatter | solution.py:121
  399.3 24.7 %collective-permute-start.36 = (bf16[256,2048]{1,0:T(8,128)(2,1)S(1)}, bf16[256,2048]{1,0:T(8,128)(2,1)S(1)}, u32[]{:S(2)}, u32[]{:S(2)}) collective-permute-start(bf16[256,2048]{1,0:T(8,128)(2,1)S(1)} %copy-done.48), channel_id=1, source_target_pairs={{0,16},{8,24},{16,0},{24,8},{1,17},{9,25},{17,1},{25,9},{2,18},{10... | collective-permute-start | bytes 3145736 | tf_op jit(solution)/shard_map/ppermute | solution.py:44
  399.8 25.6 %collective-permute-start.35 = (bf16[256,2048]{1,0:T(8,128)(2,1)}, bf16[256,2048]{1,0:T(8,128)(2,1)S(1)}, u32[]{:S(2)}, u32[]{:S(2)}) collective-permute-start(bf16[256,2048]{1,0:T(8,128)(2,1)} %reduce-scatter.5.cloned.1.call-done.refs_1_), channel_id=1, source_target_pairs={{0,1},{1,0},{2,3},{3,2},{4,5},{5,4},{6,7},{7,6},{8,9},{9,8},{10,11... | collective-permute-start | bytes 3145736 | tf_op jit(solution)/shard_map/ppermute | solution.py:44
  439.0 20.9 %collective-permute-start.38 = (bf16[768,2048]{1,0:T(8,128)(2,1)}, bf16[768,2048]{1,0:T(8,128)(2,1)S(1)}, u32[]{:S(2)}, u32[]{:S(2)}) collective-permute-start(bf16[768,2048]{1,0:T(8,128)(2,1)} %shard_map.287.refs_2_), channel_id=1, source_target_pairs={{0,8},{8,0},{16,24},{24,16},{1,9},{9,1},{17,25},{25,17},{2,10},{10... | collective-permute-start | bytes 9437192 | tf_op jit(solution)/shard_map/ppermute | solution.py:44
  440.2 19.6 %collective-permute-start.40 = (bf16[128,2048]{1,0:T(8,128)(2,1)}, bf16[128,2048]{1,0:T(8,128)(2,1)}, u32[]{:S(2)}, u32[]{:S(2)}) collective-permute-start(bf16[128,2048]{1,0:T(8,128)(2,1)} %get-tuple-element.253), channel_id=1, source_target_pairs={{0,16},{8,24},{16,0},{24,8},{1,17},{9,25},{17,1},{25,9},{2,18},{10... | collective-permute-start | bytes 1572872 | tf_op jit(solution)/shard_map/ppermute | solution.py:44
  440.8 19.1 %collective-permute-start.39 = (bf16[128,2048]{1,0:T(8,128)(2,1)}, bf16[128,2048]{1,0:T(8,128)(2,1)}, u32[]{:S(2)}, u32[]{:S(2)}) collective-permute-start(bf16[128,2048]{1,0:T(8,128)(2,1)} %get-tuple-element.254), channel_id=1, source_target_pairs={{0,1},{1,0},{2,3},{3,2},{4,5},{5,4},{6,7},{7,6},{8,9},{9,8},{10,11... | collective-permute-start | bytes 1572872 | tf_op jit(solution)/shard_map/ppermute | solution.py:44
  472.0 35.9 %collective-permute-start.46 = (bf16[1536,1024]{1,0:T(8,128)(2,1)}, bf16[1536,1024]{1,0:T(8,128)(2,1)}, u32[]{:S(2)}, u32[]{:S(2)}) collective-permute-start(bf16[1536,1024]{1,0:T(8,128)(2,1)} %get-tuple-element.234), channel_id=1, source_target_pairs={{0,8},{8,0},{16,24},{24,16},{1,9},{9,1},{17,25},{25,17},{2,10},{10... | collective-permute-start | bytes 9437192 | tf_op jit(solution)/shard_map/ppermute | solution.py:44
  472.0 8.5 %collective-permute-start.53 = (bf16[512,1024]{1,0:T(8,128)(2,1)}, bf16[512,1024]{1,0:T(8,128)(2,1)S(1)}, u32[]{:S(2)}, u32[]{:S(2)}) collective-permute-start(bf16[512,1024]{1,0:T(8,128)(2,1)} %get-tuple-element.247), channel_id=1, source_target_pairs={{0,8},{8,0},{16,24},{24,16},{1,9},{9,1},{17,25},{25,17},{2,10},{10... | collective-permute-start | bytes 3145736 | tf_op jit(solution)/shard_map/ppermute | solution.py:44
  472.5 54.6 %collective-permute-start.43 = (bf16[768,2048]{1,0:T(8,128)(2,1)}, bf16[768,2048]{1,0:T(8,128)(2,1)}, u32[]{:S(2)}, u32[]{:S(2)}) collective-permute-start(bf16[768,2048]{1,0:T(8,128)(2,1)} %shard_map.283.refs_6_), channel_id=1, source_target_pairs={{0,8},{8,0},{16,24},{24,16},{1,9},{9,1},{17,25},{25,17},{2,10},{10... | collective-permute-start | bytes 9437192 | tf_op jit(solution)/shard_map/ppermute | solution.py:44
  472.5 26.0 %collective-permute-start.41 = (bf16[256,2048]{1,0:T(8,128)(2,1)S(1)}, bf16[256,2048]{1,0:T(8,128)(2,1)S(1)}, u32[]{:S(2)}, u32[]{:S(2)}) collective-permute-start(bf16[256,2048]{1,0:T(8,128)(2,1)S(1)} %copy-done.42), channel_id=1, source_target_pairs={{0,16},{8,24},{16,0},{24,8},{1,17},{9,25},{17,1},{25,9},{2,18},{10... | collective-permute-start | bytes 3145736 | tf_op jit(solution)/shard_map/ppermute | solution.py:44
  473.3 26.2 %collective-permute-start.42 = (bf16[256,2048]{1,0:T(8,128)(2,1)}, bf16[256,2048]{1,0:T(8,128)(2,1)S(1)}, u32[]{:S(2)}, u32[]{:S(2)}) collective-permute-start(bf16[256,2048]{1,0:T(8,128)(2,1)} %get-tuple-element.226.refs_2_), channel_id=1, source_target_pairs={{0,1},{1,0},{2,3},{3,2},{4,5},{5,4},{6,7},{7,6},{8,9},{9,8},{10,11... | collective-permute-start | bytes 3145736 | tf_op jit(solution)/shard_map/ppermute | solution.py:44
  483.2 26.2 %collective-permute-start.55 = (bf16[256,1024]{1,0:T(8,128)(2,1)}, bf16[256,1024]{1,0:T(8,128)(2,1)}, u32[]{:S(2)}, u32[]{:S(2)}) collective-permute-start(bf16[256,1024]{1,0:T(8,128)(2,1)} %get-tuple-element.251), channel_id=1, source_target_pairs={{0,16},{8,24},{16,0},{24,8},{1,17},{9,25},{17,1},{25,9},{2,18},{10... | collective-permute-start | bytes 1572872 | tf_op jit(solution)/shard_map/ppermute | solution.py:44
  498.5 13.6 %collective-permute-start.54 = (bf16[256,1024]{1,0:T(8,128)(2,1)}, bf16[256,1024]{1,0:T(8,128)(2,1)}, u32[]{:S(2)}, u32[]{:S(2)}) collective-permute-start(bf16[256,1024]{1,0:T(8,128)(2,1)} %get-tuple-element.252), channel_id=1, source_target_pairs={{0,1},{1,0},{2,3},{3,2},{4,5},{5,4},{6,7},{7,6},{8,9},{9,8},{10,11... | collective-permute-start | bytes 1572872 | tf_op jit(solution)/shard_map/ppermute | solution.py:44
  515.6 26.4 %collective-permute-start.56 = (bf16[512,1024]{1,0:T(8,128)(2,1)}, bf16[512,1024]{1,0:T(8,128)(2,1)}, u32[]{:S(2)}, u32[]{:S(2)}) collective-permute-start(bf16[512,1024]{1,0:T(8,128)(2,1)} %get-tuple-element.248), channel_id=1, source_target_pairs={{0,16},{8,24},{16,0},{24,8},{1,17},{9,25},{17,1},{25,9},{2,18},{10... | collective-permute-start | bytes 3145736 | tf_op jit(solution)/shard_map/ppermute | solution.py:44
  516.4 26.4 %collective-permute-start.57 = (bf16[512,1024]{1,0:T(8,128)(2,1)}, bf16[512,1024]{1,0:T(8,128)(2,1)}, u32[]{:S(2)}, u32[]{:S(2)}) collective-permute-start(bf16[512,1024]{1,0:T(8,128)(2,1)} %get-tuple-element.249), channel_id=1, source_target_pairs={{0,1},{1,0},{2,3},{3,2},{4,5},{5,4},{6,7},{7,6},{8,9},{9,8},{10,11... | collective-permute-start | bytes 3145736 | tf_op jit(solution)/shard_map/ppermute | solution.py:44
  531.4 69.5 %collective-permute-start.44 = (bf16[256,2048]{1,0:T(8,128)(2,1)}, bf16[256,2048]{1,0:T(8,128)(2,1)}, u32[]{:S(2)}, u32[]{:S(2)}) collective-permute-start(bf16[256,2048]{1,0:T(8,128)(2,1)} %get-tuple-element.229), channel_id=1, source_target_pairs={{0,16},{8,24},{16,0},{24,8},{1,17},{9,25},{17,1},{25,9},{2,18},{10... | collective-permute-start | bytes 3145736 | tf_op jit(solution)/shard_map/ppermute | solution.py:44
  531.9 69.0 %collective-permute-start.45 = (bf16[256,2048]{1,0:T(8,128)(2,1)}, bf16[256,2048]{1,0:T(8,128)(2,1)}, u32[]{:S(2)}, u32[]{:S(2)}) collective-permute-start(bf16[256,2048]{1,0:T(8,128)(2,1)} %get-tuple-element.230), channel_id=1, source_target_pairs={{0,1},{1,0},{2,3},{3,2},{4,5},{5,4},{6,7},{7,6},{8,9},{9,8},{10,11... | collective-permute-start | bytes 3145736 | tf_op jit(solution)/shard_map/ppermute | solution.py:44
  532.9 40.4 %all-to-all-start.5 = ((bf16[4,128,1024]{2,1,0:T(8,128)(2,1)}), bf16[4,128,1024]{2,1,0:T(8,128)(2,1)}, u32[]{:S(2)}, u32[]{:S(2)}) async-start(bf16[4,128,1024]{2,1,0:T(8,128)(2,1)} %bitcast.88), calls=%async_computation.9 | async-start | bytes 2097152 | tf_op jit(solution)/shard_map/all_to_all | solution.py:125
  537.1 68.4 %reduce-scatter.11.cloned.1.call-start = ((), (), s32[]{:S(2)}) async-start(), calls=%async_computation.17 | async-start | bytes 1310720 | tf_op jit(solution)/shard_map/reduce_scatter | solution.py:121
  573.2 15.1 %all-to-all-start.4 = ((bf16[4,128,768]{2,1,0:T(8,128)(2,1)}), bf16[4,128,768]{2,1,0:T(8,128)(2,1)S(1)}, u32[]{:S(2)}, u32[]{:S(2)}) async-start(bf16[4,128,768]{2,1,0:T(8,128)(2,1)} %bitcast.90), calls=%async_computation.7 | async-start | bytes 1572864 | tf_op jit(solution)/shard_map/all_to_all | solution.py:125
  576.7 46.4 %collective-permute-start.59 = (bf16[4,128,1024]{2,1,0:T(8,128)(2,1)}, bf16[4,128,1024]{2,1,0:T(8,128)(2,1)S(1)}, u32[]{:S(2)}, u32[]{:S(2)}) collective-permute-start(bf16[4,128,1024]{2,1,0:T(8,128)(2,1)} %all-to-all-done.5.refs_1_), channel_id=1, source_target_pairs={{0,1},{1,0},{2,3},{3,2},{4,5},{5,4},{6,7},{7,6},{8,9},{9,8},{10,11... | collective-permute-start | bytes 3145736 | tf_op jit(solution)/shard_map/ppermute | solution.py:44
  582.7 6.9 %collective-permute-start.48 = (f32[16,1536]{1,0:T(8,128)S(1)}, f32[16,1536]{1,0:T(8,128)S(1)}, u32[]{:S(2)}, u32[]{:S(2)}) collective-permute-start(f32[16,1536]{1,0:T(8,128)S(1)} %add.128), channel_id=1, source_target_pairs={{0,4},{2,6},{4,0},{6,2},{1,5},{3,7},{5,1},{7,3},{8,12},{10,14},{12... | collective-permute-start | bytes 294920 | tf_op jit(solution)/shard_map/ppermute | solution.py:44
  588.3 42.4 %collective-permute-start.52 = (bf16[4,128,768]{2,1,0:T(8,128)(2,1)S(1)}, bf16[4,128,768]{2,1,0:T(8,128)(2,1)S(1)}, u32[]{:S(2)}, u32[]{:S(2)}) collective-permute-start(bf16[4,128,768]{2,1,0:T(8,128)(2,1)S(1)} %all-to-all-done.4.refs_1_), channel_id=1, source_target_pairs={{0,1},{1,0},{2,3},{3,2},{4,5},{5,4},{6,7},{7,6},{8,9},{9,8},{10,11... | collective-permute-start | bytes 2359304 | tf_op jit(solution)/shard_map/ppermute | solution.py:44
  596.0 26.0 %collective-permute-start.51 = (f32[16,1536]{1,0:T(8,128)S(1)}, f32[16,1536]{1,0:T(8,128)S(1)}, u32[]{:S(2)}, u32[]{:S(2)}) collective-permute-start(f32[16,1536]{1,0:T(8,128)S(1)} %add.131), channel_id=1, source_target_pairs={{0,1},{1,0},{2,3},{3,2},{4,5},{5,4},{6,7},{7,6},{8,9},{9,8},{10,11... | collective-permute-start | bytes 294920 | tf_op jit(solution)/shard_map/ppermute | solution.py:44
  605.5 22.5 %collective-permute-start.58 = (bf16[1,128,1024]{2,1,0:T(8,128)(2,1)}, bf16[1,128,1024]{2,1,0:T(8,128)(2,1)S(1)}, u32[]{:S(2)}, u32[]{:S(2)}) collective-permute-start(bf16[1,128,1024]{2,1,0:T(8,128)(2,1)} %bitcast.92), channel_id=1, source_target_pairs={{0,1},{1,0},{2,3},{3,2},{4,5},{5,4},{6,7},{7,6},{8,9},{9,8},{10,11... | collective-permute-start | bytes 786440 | tf_op jit(solution)/shard_map/ppermute | solution.py:44
  (72 other events, 442.4 us)
Sparse Core Ops, SparseCore 0:
  20.4 28.1 all-gather.4
  50.8 62.9 all-gather.6
  116.0 79.3 all-gather.8
  196.8 79.2 all-gather.10
  290.9 74.5 reduce-scatter.4
  380.1 74.3 reduce-scatter.6
  466.1 57.9 reduce-scatter.8
  546.6 24.6 reduce-scatter.10

commit v4 on v3

--- a/solution.py
+++ b/solution.py
@@ -89,7 +89,7 @@
     return (flip(far, ROW),)
 
 
-def scatter_relay(mine, got, diagonal):
+def scatter_relay(mine, got, diagonal, deps=()):
     width = diagonal[0].shape[1]
     n = sum(v.shape[0] for v in diagonal)
 
@@ -98,14 +98,14 @@
 
     diagonal_specs = [pl.BlockSpec(v.shape, lambda g: (0, 0)) for v in diagonal]
     y_send, x_send = pl.pallas_call(
-        relay_kernel if len(diagonal) == 2 else relay_by_row_kernel,
+        ordered(relay_kernel if len(diagonal) == 2 else relay_by_row_kernel, 4 + len(diagonal), deps),
         grid=(1,),
-        in_specs=[rows(1), rows(1), rows(2), rows(2), *diagonal_specs],
+        in_specs=[rows(1), rows(1), rows(2), rows(2), *diagonal_specs] + [UNREAD] * len(deps),
         out_specs=[rows(0), rows(0)],
         out_shape=[jax.ShapeDtypeStruct((n, width), bf16)] * 2,
         compiler_params=pltpu.CompilerParams(vmem_limit_bytes=40 * 2**20),
         cost_estimate=LIGHT,
-    )(mine, got, mine, got, *diagonal)
+    )(mine, got, mine, got, *diagonal, *deps)
     return mine, got, y_send, x_send
 
 
@@ -145,7 +145,7 @@
 
 
 def row_loop(n):
-    step = 32 if n % 32 == 0 else n
+    step = 64 if n % 64 == 0 else n
     return pl.loop(0, n, step=step), step
 
 
@@ -487,6 +487,13 @@
                     sums_ref[0:1, first : first + HEAD_DIM] += jnp.sum(low.astype(fp32), axis=0, keepdims=True)
 
 
+def pack_kernel(*refs):
+    at = 0
+    for ref in refs[:-1]:
+        refs[-1][:, at : at + ref.shape[1]] = ref[...].astype(bf16)
+        at += ref.shape[1]
+
+
 def unpack_rows_kernel(own_ref, mine_ref, other_ref, out_ref):
     r, n = own_ref[1], mine_ref.shape[0]
     out_ref[pl.ds(pl.multiple_of(r * n, n), n), :] = mine_ref[...].astype(fp32)
@@ -577,7 +584,11 @@
     small = (norm1_gain, norm1_bias, query_bias, value_bias, attn_out_bias, norm2_gain, norm2_bias, output_bias, hidden_bias)
     attn_part, *small = tie(attn_part, *small)
     attn_part = line_gather(attn_part)
-    table = jnp.concatenate([v.astype(bf16) for v in small])[None]
+    small = [v.reshape(1, -1) for v in small]
+    if rows % 128 == 0:
+        table = small_call(pack_kernel, shape(1, sum(v.size for v in small)), small)
+    else:
+        table = jnp.concatenate([v.astype(bf16) for v in small], axis=1)
     table = gather_table(gather_table(table, "shard"), "seq")
     qkv_pieces = lax.dynamic_index_in_dim(w_qkv.reshape(rows, 3, S, R, hw), r, 3, keepdims=False).astype(bf16)
     qkv_rows = seq_exchange(qkv_pieces.transpose(2, 0, 1, 3).reshape(S, rows, 3 * hw)).reshape(S * rows, 3 * hw)
@@ -603,7 +614,7 @@
     ).reshape(1, 3 * hw)
 
     hidden_in = by_shard(
-        small_call(lambda *refs: norm_kernel(grid, rows, *refs), shape(n, D), (x, gain_one, shift_one), deps=(qkv_rows,))
+        small_call(lambda *refs: norm_kernel(grid, rows, *refs), shape(n, D), (x, gain_one, shift_one))
     )
     in_near = gather_near(hidden_in)
     hidden_rows, output_part, in_near = tie(hidden_rows, output_part, in_near)
@@ -675,55 +686,60 @@
     grad_hidden, grad_mid = tie(grad_hidden, grad_mid)
     grad_hidden = line_scatter(grad_hidden)
     out_parts[1] = product(activated_parts[1], output_matrix, deps=(grad_mid,))
+    out_parts[0] = product(activated_parts[0], output_matrix, deps=(grad_mid,))
     grad_heads = lax.all_to_all(grad_heads, ("seq", "replica"), 0, 0, tiled=True)
-    grad_heads, out_theirs, grad_output, out_far = tie(grad_heads, out_parts[1], grad_output, out_far)
+    grad_heads, out_theirs, out_mine, grad_output, out_far = tie(
+        grad_heads, out_parts[1], out_parts[0], grad_output, out_far
+    )
     out_diagonal = scatter_diagonal_by_row(out_far)
     *grad_qkv_parts, sums_qkv = small_call(
         lambda *refs: attend_back_kernel(heads, *refs),
         [shape(v.shape[0], 3 * hw) for v in qkv_parts] + [shape(8, 3 * hw, kind=fp32)],
         (own, *qkv_parts, grad_heads),
         [head_block] * 3 + [head_sums] * 3,
-        deps=(out_parts[1],),
     )
     out_got = flip(out_theirs, CORE)
     other_output = flip(grad_output, COL)
     into = [None] * 4
-    into[3] = product(grad_qkv_parts[3], qkv_matrix, ACROSS, deps=(other_output, *out_diagonal))
-    into[2] = product(grad_qkv_parts[2], qkv_matrix, ACROSS, deps=(into[3],))
+    into[3] = product(grad_qkv_parts[3], qkv_matrix, ACROSS)
+    into[2] = product(grad_qkv_parts[2], qkv_matrix, ACROSS, deps=(into[3], other_output, *out_diagonal))
+    out_terms = scatter_relay(out_mine, out_got, out_diagonal, deps=(into[2],))
     into_far = far_sum(into[2], into[3])
-    into[1] = product(grad_qkv_parts[1], qkv_matrix, ACROSS, deps=(into_far,))
+    into[1] = product(grad_qkv_parts[1], qkv_matrix, ACROSS, deps=(into_far, out_terms[3]))
     into[0] = product(grad_qkv_parts[0], qkv_matrix, ACROSS, deps=(into[1],))
     into_got = flip(into[1], CORE)
-    grad_qkv = tall_product(hidden_in_parts, grad_qkv_parts, (into[0],))
-    grad_in = scatter_relay(into[0], into_got, scatter_diagonal(into_far))
-    *grad_in, grad_qkv = tie(*grad_in, grad_qkv)
-    grad_qkv = line_scatter(grad_qkv).reshape(S, rows, 3 * hw)
     grad_attn_parts = small_call(
-        outer_kernel, [shape(*v.shape) for v in attn_parts], (attended_rel, grad_mid_rel), deps=(grad_in[3],)
-    )
+        outer_kernel, [shape(*v.shape) for v in attn_parts], (attended_rel, grad_mid_rel), deps=(into[0],)
+    )
+    grad_in = scatter_relay(into[0], into_got, scatter_diagonal(into_far), deps=(grad_attn_parts[0],))
+    grad_qkv = tall_product(hidden_in_parts, grad_qkv_parts, (grad_in[3],))
     attn_got = flip(grad_attn_parts[1], CORE)
     attn_far = far_sum(grad_attn_parts[2], grad_attn_parts[3])
+    attn_far, grad_qkv = tie(attn_far, grad_qkv)
+    grad_qkv = line_scatter(grad_qkv).reshape(S, rows, 3 * hw)
     attn_diagonal = scatter_diagonal(attn_far)
-    grad_in = scatter_last(*grad_in)
+    grad_attn = scatter_relay(grad_attn_parts[0], attn_got, attn_diagonal)
+    grad_hidden, in_send = tie(grad_hidden, grad_in[3])
+    grad_in = scatter_last(*grad_in[:3], in_send)
+    grad_hidden = seq_exchange(grad_hidden.reshape(S, rows, fw))
+    grad_hidden, attn_send = tie(grad_hidden, grad_attn[3])
+    grad_attn = scatter_last(*grad_attn[:3], attn_send)
+    other_hidden = flip(grad_hidden, COL)
     grad_inputs, sums_one = small_call(
         lambda *refs: back_in_kernel(grid, rows, *refs),
         [shape(n, D, kind=fp32), shape(8, D, kind=fp32)],
         (*map(by_seq, grad_in), x, grad_mid, gain_one),
         first_rows=((0, n), (1, n)),
-        deps=(),
-    )
-    out_parts[0] = product(activated_parts[0], output_matrix, deps=(sums_one,))
-    sums_one, attn_got, grad_hidden = tie(sums_one, attn_got, grad_hidden)
-    grad_attn = scatter_relay(grad_attn_parts[0], attn_got, attn_diagonal)
-    grad_attn = scatter_last(*grad_attn)
-    out_terms = scatter_last(*scatter_relay(out_parts[0], out_got, out_diagonal))
+        deps=(attn_send,),
+    )
+    out_terms = scatter_last(*out_terms)
     layer_out = small_call(
         out_kernel, shape(n, D), (*out_terms, mid_rows, output_shift), first_rows=((0, n), (1, n))
     )
 
-    def columns_of_both(v, groups):
+    def columns_of_both(v, groups, other=None):
         v = v.reshape(-1, rows, v.shape[-1])
-        other = flip(v, COL)
+        other = flip(v, COL) if other is None else other
         a, c = groups
         count, width = v.shape[0], v.shape[-1] // (a * c)
         if width % 128 == 0:
@@ -738,7 +754,7 @@
     grad_output_matrix = small_call(
         unpack_rows_kernel, shape(R * fr, D, kind=fp32), (own, grad_output, other_output)
     )
-    grad_hidden_matrix = columns_of_both(seq_exchange(grad_hidden.reshape(S, rows, fw)), (1, Z))
+    grad_hidden_matrix = columns_of_both(grad_hidden, (1, Z), other_hidden)
     grad_qkv_matrix = columns_of_both(seq_exchange(grad_qkv), (3, 1))
     deep = D // S
     p, q, u, w = (v[:deep].astype(fp32) for v in grad_attn)

time: 654 us -> 635 us (0.971)
  Pallas kernels: 249 us -> 242 us
  waiting for transfers between devices: 200 us -> 193 us
    all_to_all x4, waiting for transfers between devices: 66.8 us -> 47 us  [seq_exchange(): return lax.all_to_all(v, 'seq', 0, 0, tiled=True)]
    ppermute x60, waiting for transfers between devices: 127 us -> 145 us  [flip(): lax.ppermute(v, axis, [(i, i ^ bit) for i in range(lax.axis_size(axis))])]
    pallas_call x4, Pallas kernels: 12.4 us -> 5.53 us  [scatter_relay(): pl.pallas_call(ordered(relay_kernel if len(diagonal) == 2 else relay_by_r...]
    unnamed x159 -> x153, local copies, waits for them, and re-layouts: 53.2 us -> 55.2 us
    pallas_call x12 -> x13, Pallas kernels: 87.1 us -> 86.2 us  [small_call(): pl.pallas_call(ordered(kernel, len(operands), deps), grid=(1,), in_specs=...]
  transfers between devices with their start and end apart: 73 -> 73, of which waited for: 35 -> 28; matrix products, arithmetic and copies ran while one was open for 8% -> 9% of each run, Pallas kernels for 38% -> 38%
where the time goes in v4:
time: 635 us; the launch traced here: 629 us
  Pallas kernels  242 us (38%)
  waiting for transfers between devices  193 us (30%)
  local copies, waits for them, and re-layouts  80.3 us (13%)
  starting transfers between devices  69 us (11%)
  blocking collectives  18.4 us (3%)
  between operations  15.6 us (2%)
  other arithmetic  11.2 us (2%)
    ppermute x60, waiting for transfers between devices, flip(): lax.ppermute(v, axis, [(i, i ^ bit) for i in range(lax.axis_size(axis))])  145 us
    pallas_call x13, Pallas kernels, small_call(): pl.pallas_call(ordered(kernel, len(operands), deps), grid=(1,), in_specs=...  86.2 us
    unnamed x153, local copies, waits for them, and re-layouts  55.2 us
    pallas_call x12, Pallas kernels, product(): pl.pallas_call(ordered(lambda *refs: product_kernel(dims, *refs), 2 + len...  51.8 us
    ppermute x60, starting transfers between devices, flip(): lax.ppermute(v, axis, [(i, i ^ bit) for i in range(lax.axis_size(axis))])  49 us
    all_to_all x4, waiting for transfers between devices, seq_exchange(): return lax.all_to_all(v, 'seq', 0, 0, tiled=True)  47 us
    pallas_call x3, Pallas kernels, tall_product(): pl.pallas_call(ordered(tall_kernel, 2 * len(lefts), deps), grid=(deep //...  38.7 us
    pallas_call x4, Pallas kernels, down_product(): pl.pallas_call(ordered(down_kernel, 4, deps), grid=(tokens // tile,), in_...  35.9 us
  transfers between devices with their start and end apart: 73, of which 28 were waited for; matrix products, arithmetic and copies ran while one was open for 9% of the time, Pallas kernels for 38%

profile of v4, /device:TPU:0, one launch (start us, length us, event | category | flops | bytes accessed | tf_op | source)
XLA Modules:
  0.0 629.1 jit_solution(11453471196124714408)
XLA Ops:
  11.0 3.0 collective-permute-start
  16.5 2.7 collective-permute-start.1
  20.1 3.5 all-to-all-start
  23.7 3.7 copy.40
  29.0 6.2 all-to-all-done
  36.9 3.5 collective-permute-done.3
  41.0 3.4 shard_map.263
  46.2 3.5 all-to-all-start.1
  49.8 2.9 fusion
  52.7 28.4 %all-to-all-done.1 = bf16[4,128,1024]{1,2,0:T(8,128)(2,1)S(1)} async-done(((bf16[4,128,1024]{1,2,0:T(8,128)(2,1)}), bf16[4,128,1024]{1,2,0:T(8,128)(2,1)S(1)}, u32[]{:S(2)}, u32[]{:S(2)}) %all-to-all-start.1) | async-done | bytes 1048608 | tf_op jit(solution)/shard_map/all_to_all | solution.py:125
  88.1 13.0 %collective-permute-done.7 = bf16[128,2048]{1,0:T(8,128)(2,1)S(1)} collective-permute-done((bf16[128,2048]{1,0:T(8,128)(2,1)S(1)}, bf16[128,2048]{1,0:T(8,128)(2,1)S(1)}, u32[]{:S(2)}, u32[]{:S(2)}) %collective-permute-start.7) | collective-permute-done | bytes 524320 | tf_op jit(solution)/shard_map/ppermute | solution.py:44
  103.0 2.7 collective-permute-done.9.refs_0_.refs_3_
  115.5 5.2 shard_map.264.refs_1_
  121.7 5.4 shard_map.265.refs_2_
  128.2 3.1 collective-permute-done.11
  136.5 11.3 %shard_map.268 = bf16[8,256,256]{2,1,0:T(8,128)(2,1)} custom-call(s32[2]{0:T(128)} %pad_add_fusion.refs_0_, bf16[768,768]{1,0:T(8,128)(2,1)} %copy-done.13, bf16[768,768]{1,0:T(8,128)(2,1)} %copy-done.14, bf16[256,768]{1,0:T(8,128)(2,1)} %copy-done.29, bf16[256,768]{1,0:T(8,128)(2,1)} %copy-done.30), custom_call_target="tpu_custom_call" | custom-call | flops 1 | bytes 1 | tf_op jit(solution)/shard_map/pallas_call | solution.py:528
  152.4 18.4 %all_to_all.30.refs_1_ = bf16[8,256,256]{2,1,0:T(8,128)(2,1)} all-to-all(bf16[8,256,256]{2,1,0:T(8,128)(2,1)S(1)} %copy-done.52), channel_id=1, replica_groups=mesh['seq'=4,'shard'=4,'replica'=2] {'seq','replica'}, dimensions={0} | all-to-all | bytes 2097152 | tf_op jit(solution)/shard_map/all_to_all | solution.py:636
  175.1 9.3 %shard_map.269 = (f32[256,2048]{1,0:T(8,128)}, bf16[256,2048]{1,0:T(8,128)(2,1)}, bf16[256,2048]{1,0:T(8,128)(2,1)}) custom-call(s32[2]{0:T(128)} %pad_add_fusion.refs_0_, bf16[8,256,256]{2,1,0:T(8,128)(2,1)} %all_to_all.30.refs_1_, bf16[1536,1024]{1,0:T(8,128)(2,1)} %copy-done.47, bf16[1536,1024]{1,0:T(8,128)(2,1)} %copy-done.49, ...), custom_call_target="tpu_custom_call" | custom-call | flops 1 | bytes 1 | tf_op jit(solution)/shard_map/pallas_call | solution.py:528
  186.9 10.2 %collective-permute-done.19 = bf16[256,2048]{1,0:T(8,128)(2,1)} collective-permute-done((bf16[256,2048]{1,0:T(8,128)(2,1)}, bf16[256,2048]{1,0:T(8,128)(2,1)}, u32[]{:S(2)}, u32[]{:S(2)}) %collective-permute-start.19) | collective-permute-done | bytes 1048608 | tf_op jit(solution)/shard_map/ppermute | solution.py:44
  198.3 20.5 %collective-permute-done.17 = bf16[256,2048]{1,0:T(8,128)(2,1)S(1)} collective-permute-done((bf16[256,2048]{1,0:T(8,128)(2,1)}, bf16[256,2048]{1,0:T(8,128)(2,1)S(1)}, u32[]{:S(2)}, u32[]{:S(2)}) %collective-permute-start.17) | collective-permute-done | bytes 1048608 | tf_op jit(solution)/shard_map/ppermute | solution.py:44
  226.4 7.5 %shard_map.270 = (bf16[768,1024]{1,0:T(8,128)(2,1)S(1)}, f32[768,1024]{1,0:T(8,128)S(1)}) custom-call(bf16[768,2048]{1,0:T(8,128)(2,1)} %constant_dynamic-update-slice_fusion.10.h_ref.refs_0_, bf16[2048,1024]{1,0:T(8,128)(2,1)} %all-gather.9.cloned.1.call-done.w_ref.refs_3_, f32[1,1024]{1,0:T(1,128)S(1)} %bitcast.83), custom_call_target="tpu_custom_call" | custom-call | flops 1 | bytes 1 | tf_op jit(solution)/shard_map/pallas_call | solution.py:339
  247.5 3.8 shard_map.272
  251.4 4.7 shard_map.273
  256.2 7.6 %shard_map.271 = (bf16[768,1024]{1,0:T(8,128)(2,1)S(1)}, f32[768,1024]{1,0:T(8,128)S(1)}) custom-call(bf16[768,2048]{1,0:T(8,128)(2,1)} %collective-permute-done.23.h_ref.refs_1_, bf16[2048,1024]{1,0:T(8,128)(2,1)} %all-gather.9.cloned.1.call-done.w_ref.refs_3_, f32[1,1024]{1,0:T(1,128)S(1)} %bitcast.86), custom_call_target="tpu_custom_call" | custom-call | flops 1 | bytes 1 | tf_op jit(solution)/shard_map/pallas_call | solution.py:339
  266.7 2.7 collective-permute-done.27.refs_7_.refs_0_
  269.3 13.7 %shard_map.274.refs_4_ = bf16[1024,2048]{1,0:T(8,128)(2,1)} custom-call(bf16[768,1024]{1,0:T(8,128)(2,1)S(1)} %get-tuple-element.195.refs_0_, bf16[768,1024]{1,0:T(8,128)(2,1)} %copy-done.19, bf16[256,1024]{1,0:T(8,128)(2,1)S(1)} %get-tuple-element.197.refs_2_.refs_0_, bf16[256,1024]{1,0:T(8,128)(2,1)S(1)} %get-tuple-element.198.refs_3_.refs_0_, ...), custom_call_target="tpu_custom_call" | custom-call | flops 1 | bytes 1 | tf_op jit(solution)/shard_map/pallas_call | solution.py:316
  283.2 5.9 shard_map.275
  289.3 5.8 shard_map.276
  295.5 11.8 %shard_map.277 = (bf16[768,1024]{1,0:T(8,128)(2,1)S(1)}, bf16[768,2048]{1,0:T(8,128)(2,1)S(1)}, f32[8,1024]{1,0:T(8,128)S(1)}) custom-call(bf16[768,2048]{1,0:T(8,128)(2,1)} %collective-permute-done.22.refs_5_.refs_0_, bf16[1024,2048]{1,0:T(8,128)(2,1)} %all-gather.11.cloned.1.call-done.refs_1_, f32[768,1024]{1,0:T(8,128)} %copy-done.32, ...), custom_call_target="tpu_custom_call" | custom-call | flops 1 | bytes 1 | tf_op jit(solution)/shard_map/pallas_call | solution.py:399
  310.2 12.4 %shard_map.278 = (bf16[768,1024]{1,0:T(8,128)(2,1)S(1)}, bf16[768,2048]{1,0:T(8,128)(2,1)}, f32[8,1024]{1,0:T(8,128)S(1)}) custom-call(bf16[768,2048]{1,0:T(8,128)(2,1)} %copy-done.48, bf16[1024,2048]{1,0:T(8,128)(2,1)} %all-gather.11.cloned.1.call-done.refs_1_, f32[768,1024]{1,0:T(8,128)} %copy-done.31, ...), custom_call_target="tpu_custom_call" | custom-call | flops 1 | bytes 1 | tf_op jit(solution)/shard_map/pallas_call | solution.py:399
  322.6 3.0 copy-done.10
  327.1 3.6 shard_map.280.refs_3_
  333.2 3.5 shard_map.281.refs_8_
  336.7 13.2 %shard_map.282.refs_13_ = bf16[2048,1024]{1,0:T(8,128)(2,1)} custom-call(bf16[768,2048]{1,0:T(8,128)(2,1)} %constant_dynamic-update-slice_fusion.10.h_ref.refs_0_, bf16[768,2048]{1,0:T(8,128)(2,1)} %collective-permute-done.23.h_ref.refs_1_, bf16[256,2048]{1,0:T(8,128)(2,1)S(1)} %copy-done.16, bf16[256,2048]{1,0:T(8,128)(2,1)S(1)} %copy-done.28, ...), custom_call_target="tpu_custom_call" | custom-call | flops 1 | bytes 1 | tf_op jit(solution)/shard_map/pallas_call | solution.py:316
  352.5 4.0 collective-permute-done.32.refs_3_
  357.5 12.2 %shard_map.283 = (f32[256,2048]{1,0:T(8,128)}, bf16[256,2048]{1,0:T(8,128)(2,1)}, bf16[8,256,256]{2,1,0:T(8,128)(2,1)}, f32[8,2048]{1,0:T(8,128)}) custom-call(s32[2]{0:T(128)} %pad_add_fusion.refs_0_, bf16[768,2048]{1,0:T(8,128)(2,1)} %get-tuple-element.203.refs_0_.refs_2_.refs_1_, bf16[768,2048]{1,0:T(8,128)(2,1)} %copy-done.9, ...), custom_call_target="tpu_custom_call" | custom-call | flops 1 | bytes 1 | tf_op jit(solution)/shard_map/pallas_call | solution.py:528
  369.7 4.4 all-to-all-start.3
  376.0 7.1 %shard_map.285.refs_0_.refs_2_ = bf16[768,2048]{1,0:T(8,128)(2,1)} custom-call(bf16[768,1024]{1,0:T(8,128)(2,1)S(1)} %copy-done.18, bf16[1024,2048]{1,0:T(8,128)(2,1)} %all-gather.11.cloned.1.call-done.refs_1_, f32[256,2048]{1,0:T(8,128)S(1)} %copy-done.11), custom_call_target="tpu_custom_call" | custom-call | flops 1 | bytes 1 | tf_op jit(solution)/shard_map/pallas_call | solution.py:362
  383.1 7.4 %shard_map.284 = bf16[768,2048]{1,0:T(8,128)(2,1)} custom-call(bf16[768,1024]{1,0:T(8,128)(2,1)S(1)} %copy-done.20, bf16[1024,2048]{1,0:T(8,128)(2,1)} %all-gather.11.cloned.1.call-done.refs_1_, f32[256,2048]{1,0:T(8,128)S(1)} %copy-done.11), custom_call_target="tpu_custom_call" | custom-call | flops 1 | bytes 1 | tf_op jit(solution)/shard_map/pallas_call | solution.py:362
  394.0 17.8 %shard_map.286 = (bf16[768,768]{1,0:T(8,128)(2,1)}, bf16[768,768]{1,0:T(8,128)(2,1)}, bf16[256,768]{1,0:T(8,128)(2,1)}, bf16[256,768]{1,0:T(8,128)(2,1)}, f32[8,768]{1,0:T(8,128)}) custom-call(s32[2]{0:T(128)} %pad_add_fusion.refs_0_, bf16[768,768]{1,0:T(8,128)(2,1)} %copy-done.13, bf16[768,768]{1,0:T(8,128)(2,1)} %copy-done.14, ...), custom_call_target="tpu_custom_call" | custom-call | flops 1 | bytes 1 | tf_op jit(solution)/shard_map/pallas_call | solution.py:528
  418.1 2.9 shard_map.288.refs_5_
  426.8 6.4 %shard_map.291.refs_2_ = bf16[768,2048]{1,0:T(8,128)(2,1)} custom-call(bf16[768,768]{1,0:T(8,128)(2,1)S(1)} %copy-done.22, bf16[2048,768]{1,0:T(8,128)(2,1)} %all-gather.7.cloned.1.call-done.refs_1_, bf16[256,2048]{1,0:T(8,128)(2,1)S(1)} %add_convert_fusion.2.refs_2_, bf16[256,2048]{1,0:T(8,128)(2,1)S(1)} %get-tuple-element.221.refs_3_), custom_call_target="tpu_custom_call" | custom-call | flops 1 | bytes 1 | tf_op jit(solution)/shard_map/pallas_call | solution.py:362
  433.2 5.0 shard_map.292.refs_2_.refs_0_
  439.9 6.0 shard_map.293
  451.5 8.9 %collective-permute-done.43.refs_5_ = bf16[128,2048]{1,0:T(8,128)(2,1)S(1)} collective-permute-done((bf16[128,2048]{1,0:T(8,128)(2,1)S(1)}, bf16[128,2048]{1,0:T(8,128)(2,1)S(1)}, u32[]{:S(2)}, u32[]{:S(2)}) %collective-permute-start.43) | collective-permute-done | bytes 524320 | tf_op jit(solution)/shard_map/ppermute | solution.py:44
  460.7 3.0 copy-done.5
  465.3 11.9 %shard_map.295 = bf16[2048,768]{1,0:T(8,128)(2,1)} custom-call(bf16[768,2048]{1,0:T(8,128)(2,1)} %copy-done.12, bf16[768,2048]{1,0:T(8,128)(2,1)} %collective-permute-done.6.refs_0_.refs_1_, bf16[256,2048]{1,0:T(8,128)(2,1)} %constant_dynamic-update-slice_fusion.3.refs_0_.refs_2_, bf16[256,2048]{1,0:T(8,128)(2,1)} %collective-permute-done.9.refs_0_.refs_3_, ...), custom_call_target="tpu_custom_call" | custom-call | flops 1 | bytes 1 | tf_op jit(solution)/shard_map/pallas_call | solution.py:316
  478.3 4.5 all-to-all-start.4
  488.5 20.4 %collective-permute-done.49.refs_5_ = bf16[256,1024]{1,0:T(8,128)(2,1)S(1)} collective-permute-done((bf16[256,1024]{1,0:T(8,128)(2,1)S(1)}, bf16[256,1024]{1,0:T(8,128)(2,1)S(1)}, u32[]{:S(2)}, u32[]{:S(2)}) %collective-permute-start.49) | collective-permute-done | bytes 524320 | tf_op jit(solution)/shard_map/ppermute | solution.py:44
  508.9 2.9 shard_map.296
  516.5 7.3 %collective-permute-done.45.refs_3_ = bf16[256,2048]{1,0:T(8,128)(2,1)} collective-permute-done((bf16[256,2048]{1,0:T(8,128)(2,1)}, bf16[256,2048]{1,0:T(8,128)(2,1)}, u32[]{:S(2)}, u32[]{:S(2)}) %collective-permute-start.45) | collective-permute-done | bytes 1048608 | tf_op jit(solution)/shard_map/ppermute | solution.py:44
  523.8 7.7 %collective-permute-done.44.refs_2_ = bf16[256,2048]{1,0:T(8,128)(2,1)} collective-permute-done((bf16[256,2048]{1,0:T(8,128)(2,1)}, bf16[256,2048]{1,0:T(8,128)(2,1)}, u32[]{:S(2)}, u32[]{:S(2)}) %collective-permute-start.44) | collective-permute-done | bytes 1048608 | tf_op jit(solution)/shard_map/ppermute | solution.py:44
  532.9 7.2 %shard_map.297 = (f32[256,2048]{1,0:T(8,128)}, f32[8,2048]{1,0:T(8,128)}) custom-call(bf16[768,2048]{1,0:T(8,128)(2,1)} %copy-done.2, bf16[768,2048]{1,0:T(8,128)(2,1)} %copy-done.8, bf16[256,2048]{1,0:T(8,128)(2,1)} %collective-permute-done.44.refs_2_, bf16[256,2048]{1,0:T(8,128)(2,1)} %collective-permute-done.45.refs_3_, bf16[256,2048]{1,0:T(8,128)(2,1)} %bitcast.89, ...), custom_call_target="tpu_custom_call" | custom-call | flops 1 | bytes 1 | tf_op jit(solution)/shard_map/pallas_call | solution.py:528
  540.2 13.8 %collective-permute-done.56 = bf16[512,1024]{1,0:T(8,128)(2,1)} collective-permute-done((bf16[512,1024]{1,0:T(8,128)(2,1)}, bf16[512,1024]{1,0:T(8,128)(2,1)}, u32[]{:S(2)}, u32[]{:S(2)}) %collective-permute-start.56) | collective-permute-done | bytes 1048608 | tf_op jit(solution)/shard_map/ppermute | solution.py:44
  554.0 3.7 add_convert_fusion
  558.7 3.5 all-to-all-start.5
  563.8 8.0 %collective-permute-done.50 = f32[16,1536]{1,0:T(8,128)S(1)} collective-permute-done((f32[16,1536]{1,0:T(8,128)S(1)}, f32[16,1536]{1,0:T(8,128)S(1)}, u32[]{:S(2)}, u32[]{:S(2)}) %collective-permute-start.50) | collective-permute-done | bytes 98336 | tf_op jit(solution)/shard_map/ppermute | solution.py:44
  571.9 12.4 %all-to-all-done.5.refs_1_ = bf16[4,128,768]{2,1,0:T(8,128)(2,1)S(1)} async-done(((bf16[4,128,768]{2,1,0:T(8,128)(2,1)}), bf16[4,128,768]{2,1,0:T(8,128)(2,1)S(1)}, u32[]{:S(2)}, u32[]{:S(2)}) %all-to-all-start.5) | async-done | bytes 786464 | tf_op jit(solution)/shard_map/all_to_all | solution.py:125
  589.4 3.1 collective-permute-done.53
  594.1 3.8 shard_map.301
  597.9 4.5 shard_map.290
  603.0 7.0 %collective-permute-done.54 = f32[16,1536]{1,0:T(8,128)S(1)} collective-permute-done((f32[16,1536]{1,0:T(8,128)S(1)}, f32[16,1536]{1,0:T(8,128)S(1)}, u32[]{:S(2)}, u32[]{:S(2)}) %collective-permute-start.54) | collective-permute-done | bytes 98336 | tf_op jit(solution)/shard_map/ppermute | solution.py:44
  611.2 3.9 shard_map.300
  618.7 3.3 shard_map.298
  (350 shorter events, 140.2 us)
Async XLA Ops:
  7.2 95.9 %all-gather.5.cloned.1.call-start = ((), (), s32[]{:S(2)}) async-start(), calls=%async_computation.10 | async-start | bytes 1310720 | tf_op jit(solution)/shard_map/all_gather | solution.py:117
  16.5 11.0 %collective-permute-start.1 = (bf16[2,1536]{1,0:T(2,128)(2,1)S(1)}, bf16[2,1536]{1,0:T(2,128)(2,1)S(1)}, u32[]{:S(2)}, u32[]{:S(2)}) collective-permute-start(bf16[2,1536]{1,0:T(2,128)(2,1)S(1)} %pad_maximum_fusion.2), channel_id=1, source_target_pairs={{0,4},{2,6},{4,0},{6,2},{1,5},{3,7},{5,1},{7,3},{8,12},{10,14},{12... | collective-permute-start | bytes 18440 | tf_op jit(solution)/shard_map/ppermute | solution.py:44
  20.1 15.2 %all-to-all-start = ((bf16[4,128,768]{1,2,0:T(8,128)(2,1)}), bf16[4,128,768]{1,2,0:T(8,128)(2,1)S(1)}, u32[]{:S(2)}, u32[]{:S(2)}) async-start(bf16[4,128,768]{1,2,0:T(8,128)(2,1)} %bitcast.11), calls=%async_computation | async-start | bytes 1572864 | tf_op jit(solution)/shard_map/all_to_all | solution.py:125
  23.6 84.0 %all-gather.7.cloned.1.call-start = ((), (), s32[]{:S(2)}) async-start(), calls=%async_computation.11 | async-start | bytes 3932160 | tf_op jit(solution)/shard_map/all_gather | solution.py:117
  44.4 38.0 %collective-permute-start.5 = (bf16[256,2048]{1,0:T(8,128)(2,1)}, bf16[256,2048]{1,0:T(8,128)(2,1)S(1)}, u32[]{:S(2)}, u32[]{:S(2)}) collective-permute-start(bf16[256,2048]{1,0:T(8,128)(2,1)} %shard_map.263), channel_id=1, source_target_pairs={{0,1},{1,0},{2,3},{3,2},{4,5},{5,4},{6,7},{7,6},{8,9},{9,8},{10,11... | collective-permute-start | bytes 3145736 | tf_op jit(solution)/shard_map/ppermute | solution.py:44
  45.8 36.5 %collective-permute-start.4 = (bf16[256,2048]{1,0:T(8,128)(2,1)}, bf16[256,2048]{1,0:T(8,128)(2,1)S(1)}, u32[]{:S(2)}, u32[]{:S(2)}) collective-permute-start(bf16[256,2048]{1,0:T(8,128)(2,1)} %shard_map.263), channel_id=1, source_target_pairs={{0,16},{8,24},{16,0},{24,8},{1,17},{9,25},{17,1},{25,9},{2,18},{10... | collective-permute-start | bytes 3145736 | tf_op jit(solution)/shard_map/ppermute | solution.py:44
  46.2 34.9 %all-to-all-start.1 = ((bf16[4,128,1024]{1,2,0:T(8,128)(2,1)}), bf16[4,128,1024]{1,2,0:T(8,128)(2,1)S(1)}, u32[]{:S(2)}, u32[]{:S(2)}) async-start(bf16[4,128,1024]{1,2,0:T(8,128)(2,1)} %bitcast.6), calls=%async_computation.1 | async-start | bytes 2097152 | tf_op jit(solution)/shard_map/all_to_all | solution.py:125
  49.7 176.6 %all-gather.9.cloned.1.call-start = ((), (), s32[]{:S(2)}) async-start(), calls=%async_computation.12 | async-start | bytes 5242880 | tf_op jit(solution)/shard_map/all_gather | solution.py:117
  86.6 19.2 %collective-permute-start.6 = (bf16[768,2048]{1,0:T(8,128)(2,1)S(1)}, bf16[768,2048]{1,0:T(8,128)(2,1)}, u32[]{:S(2)}, u32[]{:S(2)}) collective-permute-start(bf16[768,2048]{1,0:T(8,128)(2,1)S(1)} %constant_dynamic-update-slice_fusion.refs_0_), channel_id=1, source_target_pairs={{0,8},{8,0},{16,24},{24,16},{1,9},{9,1},{17,25},{25,17},{2,10},{10... | collective-permute-start | bytes 9437192 | tf_op jit(solution)/shard_map/ppermute | solution.py:44
  86.7 14.4 %collective-permute-start.7 = (bf16[128,2048]{1,0:T(8,128)(2,1)S(1)}, bf16[128,2048]{1,0:T(8,128)(2,1)S(1)}, u32[]{:S(2)}, u32[]{:S(2)}) collective-permute-start(bf16[128,2048]{1,0:T(8,128)(2,1)S(1)} %slice.167), channel_id=1, source_target_pairs={{0,1},{1,0},{2,3},{3,2},{4,5},{5,4},{6,7},{7,6},{8,9},{9,8},{10,11... | collective-permute-start | bytes 1572872 | tf_op jit(solution)/shard_map/ppermute | solution.py:44
  87.4 14.5 %collective-permute-start.8 = (bf16[128,2048]{1,0:T(8,128)(2,1)S(1)}, bf16[128,2048]{1,0:T(8,128)(2,1)S(1)}, u32[]{:S(2)}, u32[]{:S(2)}) collective-permute-start(bf16[128,2048]{1,0:T(8,128)(2,1)S(1)} %slice.168), channel_id=1, source_target_pairs={{0,16},{8,24},{16,0},{24,8},{1,17},{9,25},{17,1},{25,9},{2,18},{10... | collective-permute-start | bytes 1572872 | tf_op jit(solution)/shard_map/ppermute | solution.py:44
  102.8 180.4 %all-gather.11.cloned.1.call-start = ((), (), s32[]{:S(2)}) async-start(), calls=%async_computation.13 | async-start | bytes 5242880 | tf_op jit(solution)/shard_map/all_gather | solution.py:117
  105.8 25.5 %collective-permute-start.11 = (bf16[512,1024]{1,0:T(8,128)(2,1)}, bf16[512,1024]{1,0:T(8,128)(2,1)}, u32[]{:S(2)}, u32[]{:S(2)}) collective-permute-start(bf16[512,1024]{1,0:T(8,128)(2,1)} %all-gather.5.cloned.1.call-done), channel_id=1, source_target_pairs={{0,1},{1,0},{2,3},{3,2},{4,5},{5,4},{6,7},{7,6},{8,9},{9,8},{10,11... | collective-permute-start | bytes 3145736 | tf_op jit(solution)/shard_map/ppermute | solution.py:44
  106.8 25.2 %collective-permute-start.10 = (bf16[512,1024]{1,0:T(8,128)(2,1)}, bf16[512,1024]{1,0:T(8,128)(2,1)}, u32[]{:S(2)}, u32[]{:S(2)}) collective-permute-start(bf16[512,1024]{1,0:T(8,128)(2,1)} %all-gather.5.cloned.1.call-done), channel_id=1, source_target_pairs={{0,16},{8,24},{16,0},{24,8},{1,17},{9,25},{17,1},{25,9},{2,18},{10... | collective-permute-start | bytes 3145736 | tf_op jit(solution)/shard_map/ppermute | solution.py:44
  134.2 13.6 %collective-permute-start.13 = (bf16[256,1024]{1,0:T(8,128)(2,1)S(1)}, bf16[256,1024]{1,0:T(8,128)(2,1)S(1)}, u32[]{:S(2)}, u32[]{:S(2)}) collective-permute-start(bf16[256,1024]{1,0:T(8,128)(2,1)S(1)} %slice.172), channel_id=1, source_target_pairs={{0,16},{8,24},{16,0},{24,8},{1,17},{9,25},{17,1},{25,9},{2,18},{10... | collective-permute-start | bytes 1572872 | tf_op jit(solution)/shard_map/ppermute | solution.py:44
  134.9 12.9 %collective-permute-start.12 = (bf16[256,1024]{1,0:T(8,128)(2,1)S(1)}, bf16[256,1024]{1,0:T(8,128)(2,1)}, u32[]{:S(2)}, u32[]{:S(2)}) collective-permute-start(bf16[256,1024]{1,0:T(8,128)(2,1)S(1)} %slice.171), channel_id=1, source_target_pairs={{0,1},{1,0},{2,3},{3,2},{4,5},{5,4},{6,7},{7,6},{8,9},{9,8},{10,11... | collective-permute-start | bytes 1572872 | tf_op jit(solution)/shard_map/ppermute | solution.py:44
  150.6 21.8 %collective-permute-start.14 = (bf16[1536,1024]{1,0:T(8,128)(2,1)S(1)}, bf16[1536,1024]{1,0:T(8,128)(2,1)S(1)}, u32[]{:S(2)}, u32[]{:S(2)}) collective-permute-start(bf16[1536,1024]{1,0:T(8,128)(2,1)S(1)} %constant_dynamic-update-slice_fusion.5.refs_2_.refs_8_), channel_id=1, source_target_pairs={{0,8},{8,0},{16,24},{24,16},{1,9},{9,1},{17,25},{25,17},{2,10},{10... | collective-permute-start | bytes 9437192 | tf_op jit(solution)/shard_map/ppermute | solution.py:44
  152.3 20.2 %collective-permute-start.15 = (bf16[512,1024]{1,0:T(8,128)(2,1)S(1)}, bf16[512,1024]{1,0:T(8,128)(2,1)S(1)}, u32[]{:S(2)}, u32[]{:S(2)}) collective-permute-start(bf16[512,1024]{1,0:T(8,128)(2,1)S(1)} %constant_dynamic-update-slice_fusion.8.refs_4_.refs_10_), channel_id=1, source_target_pairs={{0,8},{8,0},{16,24},{24,16},{1,9},{9,1},{17,25},{25,17},{2,10},{10... | collective-permute-start | bytes 3145736 | tf_op jit(solution)/shard_map/ppermute | solution.py:44
  170.8 26.3 %collective-permute-start.19 = (bf16[256,2048]{1,0:T(8,128)(2,1)}, bf16[256,2048]{1,0:T(8,128)(2,1)}, u32[]{:S(2)}, u32[]{:S(2)}) collective-permute-start(bf16[256,2048]{1,0:T(8,128)(2,1)} %bitcast.32.refs_6_), channel_id=1, source_target_pairs={{0,1},{1,0},{2,3},{3,2},{4,5},{5,4},{6,7},{7,6},{8,9},{9,8},{10,11... | collective-permute-start | bytes 3145736 | tf_op jit(solution)/shard_map/ppermute | solution.py:44
  171.9 26.4 %collective-permute-start.18 = (bf16[256,2048]{1,0:T(8,128)(2,1)}, bf16[256,2048]{1,0:T(8,128)(2,1)}, u32[]{:S(2)}, u32[]{:S(2)}) collective-permute-start(bf16[256,2048]{1,0:T(8,128)(2,1)} %bitcast.32.refs_6_), channel_id=1, source_target_pairs={{0,16},{8,24},{16,0},{24,8},{1,17},{9,25},{17,1},{25,9},{2,18},{10... | collective-permute-start | bytes 3145736 | tf_op jit(solution)/shard_map/ppermute | solution.py:44
  184.4 34.4 %collective-permute-start.17 = (bf16[256,2048]{1,0:T(8,128)(2,1)}, bf16[256,2048]{1,0:T(8,128)(2,1)S(1)}, u32[]{:S(2)}, u32[]{:S(2)}) collective-permute-start(bf16[256,2048]{1,0:T(8,128)(2,1)} %get-tuple-element.168), channel_id=1, source_target_pairs={{0,1},{1,0},{2,3},{3,2},{4,5},{5,4},{6,7},{7,6},{8,9},{9,8},{10,11... | collective-permute-start | bytes 3145736 | tf_op jit(solution)/shard_map/ppermute | solution.py:44
  185.4 33.7 %collective-permute-start.16 = (bf16[256,2048]{1,0:T(8,128)(2,1)}, bf16[256,2048]{1,0:T(8,128)(2,1)S(1)}, u32[]{:S(2)}, u32[]{:S(2)}) collective-permute-start(bf16[256,2048]{1,0:T(8,128)(2,1)} %get-tuple-element.168), channel_id=1, source_target_pairs={{0,16},{8,24},{16,0},{24,8},{1,17},{9,25},{17,1},{25,9},{2,18},{10... | collective-permute-start | bytes 3145736 | tf_op jit(solution)/shard_map/ppermute | solution.py:44
  186.9 203.7 %reduce-scatter.5.cloned.1.call-start = ((), (), s32[]{:S(2)}) async-start(), calls=%async_computation.14 | async-start | bytes 5242880 | tf_op jit(solution)/shard_map/reduce_scatter | solution.py:121
  220.8 14.7 %collective-permute-start.21 = (bf16[128,2048]{1,0:T(8,128)(2,1)}, bf16[128,2048]{1,0:T(8,128)(2,1)}, u32[]{:S(2)}, u32[]{:S(2)}) collective-permute-start(bf16[128,2048]{1,0:T(8,128)(2,1)} %slice.178), channel_id=1, source_target_pairs={{0,16},{8,24},{16,0},{24,8},{1,17},{9,25},{17,1},{25,9},{2,18},{10... | collective-permute-start | bytes 1572872 | tf_op jit(solution)/shard_map/ppermute | solution.py:44
  221.5 14.0 %collective-permute-start.20 = (bf16[128,2048]{1,0:T(8,128)(2,1)}, bf16[128,2048]{1,0:T(8,128)(2,1)}, u32[]{:S(2)}, u32[]{:S(2)}) collective-permute-start(bf16[128,2048]{1,0:T(8,128)(2,1)} %slice.177), channel_id=1, source_target_pairs={{0,1},{1,0},{2,3},{3,2},{4,5},{5,4},{6,7},{7,6},{8,9},{9,8},{10,11... | collective-permute-start | bytes 1572872 | tf_op jit(solution)/shard_map/ppermute | solution.py:44
  226.3 29.9 %collective-permute-start.23 = (bf16[768,2048]{1,0:T(8,128)(2,1)}, bf16[768,2048]{1,0:T(8,128)(2,1)}, u32[]{:S(2)}, u32[]{:S(2)}) collective-permute-start(bf16[768,2048]{1,0:T(8,128)(2,1)} %constant_dynamic-update-slice_fusion.10.h_ref.refs_0_), channel_id=1, source_target_pairs={{0,8},{8,0},{16,24},{24,16},{1,9},{9,1},{17,25},{25,17},{2,10},{10... | collective-permute-start | bytes 9437192 | tf_op jit(solution)/shard_map/ppermute | solution.py:44
  242.5 24.2 %collective-permute-start.22 = (bf16[768,2048]{1,0:T(8,128)(2,1)S(1)}, bf16[768,2048]{1,0:T(8,128)(2,1)}, u32[]{:S(2)}, u32[]{:S(2)}) collective-permute-start(bf16[768,2048]{1,0:T(8,128)(2,1)S(1)} %constant_dynamic-update-slice_fusion.15.refs_4_.refs_0_), channel_id=1, source_target_pairs={{0,8},{8,0},{16,24},{24,16},{1,9},{9,1},{17,25},{25,17},{2,10},{10... | collective-permute-start | bytes 9437192 | tf_op jit(solution)/shard_map/ppermute | solution.py:44
  243.0 8.4 %collective-permute-start.24 = (bf16[256,2048]{1,0:T(8,128)(2,1)S(1)}, bf16[256,2048]{1,0:T(8,128)(2,1)S(1)}, u32[]{:S(2)}, u32[]{:S(2)}) collective-permute-start(bf16[256,2048]{1,0:T(8,128)(2,1)S(1)} %constant_dynamic-update-slice_fusion.13.h_ref.refs_2_), channel_id=1, source_target_pairs={{0,8},{8,0},{16,24},{24,16},{1,9},{9,1},{17,25},{25,17},{2,10},{10... | collective-permute-start | bytes 3145736 | tf_op jit(solution)/shard_map/ppermute | solution.py:44
  245.7 19.8 %collective-permute-start.26 = (bf16[128,2048]{1,0:T(8,128)(2,1)S(1)}, bf16[128,2048]{1,0:T(8,128)(2,1)S(1)}, u32[]{:S(2)}, u32[]{:S(2)}) collective-permute-start(bf16[128,2048]{1,0:T(8,128)(2,1)S(1)} %slice.180), channel_id=1, source_target_pairs={{0,16},{8,24},{16,0},{24,8},{1,17},{9,25},{17,1},{25,9},{2,18},{10... | collective-permute-start | bytes 1572872 | tf_op jit(solution)/shard_map/ppermute | solution.py:44
  246.9 18.6 %collective-permute-start.25 = (bf16[128,2048]{1,0:T(8,128)(2,1)S(1)}, bf16[128,2048]{1,0:T(8,128)(2,1)S(1)}, u32[]{:S(2)}, u32[]{:S(2)}) collective-permute-start(bf16[128,2048]{1,0:T(8,128)(2,1)S(1)} %slice.179), channel_id=1, source_target_pairs={{0,1},{1,0},{2,3},{3,2},{4,5},{5,4},{6,7},{7,6},{8,9},{9,8},{10,11... | collective-permute-start | bytes 1572872 | tf_op jit(solution)/shard_map/ppermute | solution.py:44
  283.1 195.2 %reduce-scatter.7.cloned.1.call-start = ((), (), s32[]{:S(2)}) async-start(), calls=%async_computation.15 | async-start | bytes 5242880 | tf_op jit(solution)/shard_map/reduce_scatter | solution.py:121
  307.3 15.3 %collective-permute-start.29 = (bf16[768,2048]{1,0:T(8,128)(2,1)S(1)}, bf16[768,2048]{1,0:T(8,128)(2,1)S(1)}, u32[]{:S(2)}, u32[]{:S(2)}) collective-permute-start(bf16[768,2048]{1,0:T(8,128)(2,1)S(1)} %get-tuple-element.204), channel_id=1, source_target_pairs={{0,8},{8,0},{16,24},{24,16},{1,9},{9,1},{17,25},{25,17},{2,10},{10... | collective-permute-start | bytes 9437192 | tf_op jit(solution)/shard_map/ppermute | solution.py:44
  307.8 14.8 %collective-permute-start.31 = (bf16[128,2048]{1,0:T(8,128)(2,1)S(1)}, bf16[128,2048]{1,0:T(8,128)(2,1)S(1)}, u32[]{:S(2)}, u32[]{:S(2)}) collective-permute-start(bf16[128,2048]{1,0:T(8,128)(2,1)S(1)} %get-tuple-element.253), channel_id=1, source_target_pairs={{0,16},{8,24},{16,0},{24,8},{1,17},{9,25},{17,1},{25,9},{2,18},{10... | collective-permute-start | bytes 1572872 | tf_op jit(solution)/shard_map/ppermute | solution.py:44
  308.8 13.8 %collective-permute-start.30 = (bf16[128,2048]{1,0:T(8,128)(2,1)S(1)}, bf16[128,2048]{1,0:T(8,128)(2,1)S(1)}, u32[]{:S(2)}, u32[]{:S(2)}) collective-permute-start(bf16[128,2048]{1,0:T(8,128)(2,1)S(1)} %get-tuple-element.254), channel_id=1, source_target_pairs={{0,1},{1,0},{2,3},{3,2},{4,5},{5,4},{6,7},{7,6},{8,9},{9,8},{10,11... | collective-permute-start | bytes 1572872 | tf_op jit(solution)/shard_map/ppermute | solution.py:44
  330.7 19.2 %collective-permute-start.34 = (bf16[256,2048]{1,0:T(8,128)(2,1)S(1)}, bf16[256,2048]{1,0:T(8,128)(2,1)}, u32[]{:S(2)}, u32[]{:S(2)}) collective-permute-start(bf16[256,2048]{1,0:T(8,128)(2,1)S(1)} %shard_map.280.refs_3_), channel_id=1, source_target_pairs={{0,8},{8,0},{16,24},{24,16},{1,9},{9,1},{17,25},{25,17},{2,10},{10... | collective-permute-start | bytes 3145736 | tf_op jit(solution)/shard_map/ppermute | solution.py:44
  330.8 25.7 %collective-permute-start.32 = (bf16[256,2048]{1,0:T(8,128)(2,1)S(1)}, bf16[256,2048]{1,0:T(8,128)(2,1)}, u32[]{:S(2)}, u32[]{:S(2)}) collective-permute-start(bf16[256,2048]{1,0:T(8,128)(2,1)S(1)} %get-tuple-element.205), channel_id=1, source_target_pairs={{0,16},{8,24},{16,0},{24,8},{1,17},{9,25},{17,1},{25,9},{2,18},{10... | collective-permute-start | bytes 3145736 | tf_op jit(solution)/shard_map/ppermute | solution.py:44
  331.9 25.5 %collective-permute-start.33 = (bf16[256,2048]{1,0:T(8,128)(2,1)}, bf16[256,2048]{1,0:T(8,128)(2,1)}, u32[]{:S(2)}, u32[]{:S(2)}) collective-permute-start(bf16[256,2048]{1,0:T(8,128)(2,1)} %get-tuple-element.206.refs_2_), channel_id=1, source_target_pairs={{0,1},{1,0},{2,3},{3,2},{4,5},{5,4},{6,7},{7,6},{8,9},{9,8},{10,11... | collective-permute-start | bytes 3145736 | tf_op jit(solution)/shard_map/ppermute | solution.py:44
  369.7 20.8 %all-to-all-start.3 = ((bf16[8,256,256]{2,1,0:T(8,128)(2,1)}), bf16[8,256,256]{2,1,0:T(8,128)(2,1)}, u32[]{:S(2)}, u32[]{:S(2)}) async-start(bf16[8,256,256]{2,1,0:T(8,128)(2,1)} %get-tuple-element.210), calls=%async_computation.3 | async-start | bytes 2097152 | tf_op jit(solution)/shard_map/all_to_all | solution.py:690
  374.1 184.6 %reduce-scatter.9.cloned.1.call-start = ((), (), s32[]{:S(2)}) async-start(), calls=%async_computation.16 | async-start | bytes 3932160 | tf_op jit(solution)/shard_map/reduce_scatter | solution.py:121
  390.5 30.9 %collective-permute-start.35 = (bf16[768,2048]{1,0:T(8,128)(2,1)}, bf16[768,2048]{1,0:T(8,128)(2,1)S(1)}, u32[]{:S(2)}, u32[]{:S(2)}) collective-permute-start(bf16[768,2048]{1,0:T(8,128)(2,1)} %shard_map.284), channel_id=1, source_target_pairs={{0,8},{8,0},{16,24},{24,16},{1,9},{9,1},{17,25},{25,17},{2,10},{10... | collective-permute-start | bytes 9437192 | tf_op jit(solution)/shard_map/ppermute | solution.py:44
  390.9 25.6 %collective-permute-start.36 = (bf16[256,2048]{1,0:T(8,128)(2,1)}, bf16[256,2048]{1,0:T(8,128)(2,1)S(1)}, u32[]{:S(2)}, u32[]{:S(2)}) collective-permute-start(bf16[256,2048]{1,0:T(8,128)(2,1)} %add_convert_fusion.3.refs_12_), channel_id=1, source_target_pairs={{0,16},{8,24},{16,0},{24,8},{1,17},{9,25},{17,1},{25,9},{2,18},{10... | collective-permute-start | bytes 3145736 | tf_op jit(solution)/shard_map/ppermute | solution.py:44
  392.5 25.5 %collective-permute-start.37 = (bf16[256,2048]{1,0:T(8,128)(2,1)}, bf16[256,2048]{1,0:T(8,128)(2,1)}, u32[]{:S(2)}, u32[]{:S(2)}) collective-permute-start(bf16[256,2048]{1,0:T(8,128)(2,1)} %reduce-scatter.5.cloned.1.call-done.refs_1_), channel_id=1, source_target_pairs={{0,1},{1,0},{2,3},{3,2},{4,5},{5,4},{6,7},{7,6},{8,9},{9,8},{10,11... | collective-permute-start | bytes 3145736 | tf_op jit(solution)/shard_map/ppermute | solution.py:44
  413.8 7.2 %collective-permute-start.40 = (bf16[256,2048]{1,0:T(8,128)(2,1)S(1)}, bf16[256,2048]{1,0:T(8,128)(2,1)S(1)}, u32[]{:S(2)}, u32[]{:S(2)}) collective-permute-start(bf16[256,2048]{1,0:T(8,128)(2,1)S(1)} %shard_map.287.refs_2_), channel_id=1, source_target_pairs={{0,8},{8,0},{16,24},{24,16},{1,9},{9,1},{17,25},{25,17},{2,10},{10... | collective-permute-start | bytes 3145736 | tf_op jit(solution)/shard_map/ppermute | solution.py:44
  433.2 27.5 %collective-permute-start.41 = (bf16[768,2048]{1,0:T(8,128)(2,1)}, bf16[768,2048]{1,0:T(8,128)(2,1)S(1)}, u32[]{:S(2)}, u32[]{:S(2)}) collective-permute-start(bf16[768,2048]{1,0:T(8,128)(2,1)} %shard_map.291.refs_2_), channel_id=1, source_target_pairs={{0,8},{8,0},{16,24},{24,16},{1,9},{9,1},{17,25},{25,17},{2,10},{10... | collective-permute-start | bytes 9437192 | tf_op jit(solution)/shard_map/ppermute | solution.py:44
  446.4 14.0 %collective-permute-start.43 = (bf16[128,2048]{1,0:T(8,128)(2,1)S(1)}, bf16[128,2048]{1,0:T(8,128)(2,1)S(1)}, u32[]{:S(2)}, u32[]{:S(2)}) collective-permute-start(bf16[128,2048]{1,0:T(8,128)(2,1)S(1)} %get-tuple-element.251), channel_id=1, source_target_pairs={{0,16},{8,24},{16,0},{24,8},{1,17},{9,25},{17,1},{25,9},{2,18},{10... | collective-permute-start | bytes 1572872 | tf_op jit(solution)/shard_map/ppermute | solution.py:44
  447.2 13.6 %collective-permute-start.42 = (bf16[128,2048]{1,0:T(8,128)(2,1)S(1)}, bf16[128,2048]{1,0:T(8,128)(2,1)S(1)}, u32[]{:S(2)}, u32[]{:S(2)}) collective-permute-start(bf16[128,2048]{1,0:T(8,128)(2,1)S(1)} %get-tuple-element.252), channel_id=1, source_target_pairs={{0,1},{1,0},{2,3},{3,2},{4,5},{5,4},{6,7},{7,6},{8,9},{9,8},{10,11... | collective-permute-start | bytes 1572872 | tf_op jit(solution)/shard_map/ppermute | solution.py:44
  478.2 10.3 %collective-permute-start.46 = (bf16[1536,1024]{1,0:T(8,128)(2,1)}, bf16[1536,1024]{1,0:T(8,128)(2,1)}, u32[]{:S(2)}, u32[]{:S(2)}) collective-permute-start(bf16[1536,1024]{1,0:T(8,128)(2,1)} %get-tuple-element.232), channel_id=1, source_target_pairs={{0,8},{8,0},{16,24},{24,16},{1,9},{9,1},{17,25},{25,17},{2,10},{10... | collective-permute-start | bytes 9437192 | tf_op jit(solution)/shard_map/ppermute | solution.py:44
  478.3 34.5 %all-to-all-start.4 = ((bf16[4,128,1024]{2,1,0:T(8,128)(2,1)}), bf16[4,128,1024]{2,1,0:T(8,128)(2,1)}, u32[]{:S(2)}, u32[]{:S(2)}) async-start(bf16[4,128,1024]{2,1,0:T(8,128)(2,1)} %bitcast.96), calls=%async_computation.6 | async-start | bytes 2097152 | tf_op jit(solution)/shard_map/all_to_all | solution.py:125
  482.8 119.6 %reduce-scatter.11.cloned.1.call-start = ((), (), s32[]{:S(2)}) async-start(), calls=%async_computation.17 | async-start | bytes 1310720 | tf_op jit(solution)/shard_map/reduce_scatter | solution.py:121
  484.4 24.5 %collective-permute-start.49 = (bf16[256,1024]{1,0:T(8,128)(2,1)S(1)}, bf16[256,1024]{1,0:T(8,128)(2,1)S(1)}, u32[]{:S(2)}, u32[]{:S(2)}) collective-permute-start(bf16[256,1024]{1,0:T(8,128)(2,1)S(1)} %get-tuple-element.249), channel_id=1, source_target_pairs={{0,16},{8,24},{16,0},{24,8},{1,17},{9,25},{17,1},{25,9},{2,18},{10... | collective-permute-start | bytes 1572872 | tf_op jit(solution)/shard_map/ppermute | solution.py:44
  486.4 22.5 %collective-permute-start.48 = (bf16[256,1024]{1,0:T(8,128)(2,1)S(1)}, bf16[256,1024]{1,0:T(8,128)(2,1)S(1)}, u32[]{:S(2)}, u32[]{:S(2)}) collective-permute-start(bf16[256,1024]{1,0:T(8,128)(2,1)S(1)} %get-tuple-element.250), channel_id=1, source_target_pairs={{0,1},{1,0},{2,3},{3,2},{4,5},{5,4},{6,7},{7,6},{8,9},{9,8},{10,11... | collective-permute-start | bytes 1572872 | tf_op jit(solution)/shard_map/ppermute | solution.py:44
  487.8 36.0 %collective-permute-start.45 = (bf16[256,2048]{1,0:T(8,128)(2,1)}, bf16[256,2048]{1,0:T(8,128)(2,1)}, u32[]{:S(2)}, u32[]{:S(2)}) collective-permute-start(bf16[256,2048]{1,0:T(8,128)(2,1)} %copy-done.44), channel_id=1, source_target_pairs={{0,1},{1,0},{2,3},{3,2},{4,5},{5,4},{6,7},{7,6},{8,9},{9,8},{10,11... | collective-permute-start | bytes 3145736 | tf_op jit(solution)/shard_map/ppermute | solution.py:44
  488.4 43.1 %collective-permute-start.44 = (bf16[256,2048]{1,0:T(8,128)(2,1)}, bf16[256,2048]{1,0:T(8,128)(2,1)}, u32[]{:S(2)}, u32[]{:S(2)}) collective-permute-start(bf16[256,2048]{1,0:T(8,128)(2,1)} %copy-done.46), channel_id=1, source_target_pairs={{0,16},{8,24},{16,0},{24,8},{1,17},{9,25},{17,1},{25,9},{2,18},{10... | collective-permute-start | bytes 3145736 | tf_op jit(solution)/shard_map/ppermute | solution.py:44
  512.8 41.2 %collective-permute-start.56 = (bf16[512,1024]{1,0:T(8,128)(2,1)}, bf16[512,1024]{1,0:T(8,128)(2,1)}, u32[]{:S(2)}, u32[]{:S(2)}) collective-permute-start(bf16[512,1024]{1,0:T(8,128)(2,1)} %get-tuple-element.247), channel_id=1, source_target_pairs={{0,16},{8,24},{16,0},{24,8},{1,17},{9,25},{17,1},{25,9},{2,18},{10... | collective-permute-start | bytes 3145736 | tf_op jit(solution)/shard_map/ppermute | solution.py:44
  512.8 41.2 %collective-permute-start.57 = (bf16[512,1024]{1,0:T(8,128)(2,1)}, bf16[512,1024]{1,0:T(8,128)(2,1)}, u32[]{:S(2)}, u32[]{:S(2)}) collective-permute-start(bf16[512,1024]{1,0:T(8,128)(2,1)} %copy-done.41), channel_id=1, source_target_pairs={{0,1},{1,0},{2,3},{3,2},{4,5},{5,4},{6,7},{7,6},{8,9},{9,8},{10,11... | collective-permute-start | bytes 3145736 | tf_op jit(solution)/shard_map/ppermute | solution.py:44
  515.8 82.1 %collective-permute-start.39 = (bf16[256,2048]{1,0:T(8,128)(2,1)}, bf16[256,2048]{1,0:T(8,128)(2,1)}, u32[]{:S(2)}, u32[]{:S(2)}) collective-permute-start(bf16[256,2048]{1,0:T(8,128)(2,1)} %copy-done.40), channel_id=1, source_target_pairs={{0,1},{1,0},{2,3},{3,2},{4,5},{5,4},{6,7},{7,6},{8,9},{9,8},{10,11... | collective-permute-start | bytes 3145736 | tf_op jit(solution)/shard_map/ppermute | solution.py:44
  523.8 74.1 %collective-permute-start.38 = (bf16[256,2048]{1,0:T(8,128)(2,1)}, bf16[256,2048]{1,0:T(8,128)(2,1)}, u32[]{:S(2)}, u32[]{:S(2)}) collective-permute-start(bf16[256,2048]{1,0:T(8,128)(2,1)} %copy-done.45), channel_id=1, source_target_pairs={{0,16},{8,24},{16,0},{24,8},{1,17},{9,25},{17,1},{25,9},{2,18},{10... | collective-permute-start | bytes 3145736 | tf_op jit(solution)/shard_map/ppermute | solution.py:44
  531.5 79.7 %collective-permute-start.59 = (bf16[4,128,1024]{2,1,0:T(8,128)(2,1)}, bf16[4,128,1024]{2,1,0:T(8,128)(2,1)}, u32[]{:S(2)}, u32[]{:S(2)}) collective-permute-start(bf16[4,128,1024]{2,1,0:T(8,128)(2,1)} %all-to-all-done.4.refs_1_), channel_id=1, source_target_pairs={{0,1},{1,0},{2,3},{3,2},{4,5},{5,4},{6,7},{7,6},{8,9},{9,8},{10,11... | collective-permute-start | bytes 3145736 | tf_op jit(solution)/shard_map/ppermute | solution.py:44
  558.7 25.6 %all-to-all-start.5 = ((bf16[4,128,768]{2,1,0:T(8,128)(2,1)}), bf16[4,128,768]{2,1,0:T(8,128)(2,1)S(1)}, u32[]{:S(2)}, u32[]{:S(2)}) async-start(bf16[4,128,768]{2,1,0:T(8,128)(2,1)} %bitcast.98), calls=%async_computation.8 | async-start | bytes 1572864 | tf_op jit(solution)/shard_map/all_to_all | solution.py:125
  562.3 9.5 %collective-permute-start.50 = (f32[16,1536]{1,0:T(8,128)S(1)}, f32[16,1536]{1,0:T(8,128)S(1)}, u32[]{:S(2)}, u32[]{:S(2)}) collective-permute-start(f32[16,1536]{1,0:T(8,128)S(1)} %constant_dynamic-update-slice_fusion.20), channel_id=1, source_target_pairs={{0,2},{2,0},{4,6},{6,4},{1,3},{3,1},{5,7},{7,5},{8,10},{10,8},{12,... | collective-permute-start | bytes 294920 | tf_op jit(solution)/shard_map/ppermute | solution.py:44
  571.8 13.9 %collective-permute-start.51 = (f32[16,1536]{1,0:T(8,128)S(1)}, f32[16,1536]{1,0:T(8,128)S(1)}, u32[]{:S(2)}, u32[]{:S(2)}) collective-permute-start(f32[16,1536]{1,0:T(8,128)S(1)} %add.129), channel_id=1, source_target_pairs={{0,4},{2,6},{4,0},{6,2},{1,5},{3,7},{5,1},{7,3},{8,12},{10,14},{12... | collective-permute-start | bytes 294920 | tf_op jit(solution)/shard_map/ppermute | solution.py:44
  584.3 33.6 %collective-permute-start.55 = (bf16[4,128,768]{2,1,0:T(8,128)(2,1)S(1)}, bf16[4,128,768]{2,1,0:T(8,128)(2,1)S(1)}, u32[]{:S(2)}, u32[]{:S(2)}) collective-permute-start(bf16[4,128,768]{2,1,0:T(8,128)(2,1)S(1)} %all-to-all-done.5.refs_1_), channel_id=1, source_target_pairs={{0,1},{1,0},{2,3},{3,2},{4,5},{5,4},{6,7},{7,6},{8,9},{9,8},{10,11... | collective-permute-start | bytes 2359304 | tf_op jit(solution)/shard_map/ppermute | solution.py:44
  592.6 17.5 %collective-permute-start.54 = (f32[16,1536]{1,0:T(8,128)S(1)}, f32[16,1536]{1,0:T(8,128)S(1)}, u32[]{:S(2)}, u32[]{:S(2)}) collective-permute-start(f32[16,1536]{1,0:T(8,128)S(1)} %add.132), channel_id=1, source_target_pairs={{0,1},{1,0},{2,3},{3,2},{4,5},{5,4},{6,7},{7,6},{8,9},{9,8},{10,11... | collective-permute-start | bytes 294920 | tf_op jit(solution)/shard_map/ppermute | solution.py:44
  602.4 12.6 %collective-permute-start.58 = (bf16[1,128,1024]{2,1,0:T(8,128)(2,1)}, bf16[1,128,1024]{2,1,0:T(8,128)(2,1)S(1)}, u32[]{:S(2)}, u32[]{:S(2)}) collective-permute-start(bf16[1,128,1024]{2,1,0:T(8,128)(2,1)} %bitcast.100), channel_id=1, source_target_pairs={{0,1},{1,0},{2,3},{3,2},{4,5},{5,4},{6,7},{7,6},{8,9},{9,8},{10,11... | collective-permute-start | bytes 786440 | tf_op jit(solution)/shard_map/ppermute | solution.py:44
  (73 other events, 504.8 us)
Sparse Core Ops, SparseCore 0:
  14.2 28.1 all-gather.4
  44.5 62.9 all-gather.6
  109.7 79.3 all-gather.8
  190.6 79.2 all-gather.10
  283.2 74.9 reduce-scatter.4
  369.8 75.6 reduce-scatter.6
  478.3 59.7 reduce-scatter.8
  557.9 29.1 reduce-scatter.10

commit v5 on v4

--- a/solution.py
+++ b/solution.py
@@ -686,11 +686,14 @@
     grad_hidden, grad_mid = tie(grad_hidden, grad_mid)
     grad_hidden = line_scatter(grad_hidden)
     out_parts[1] = product(activated_parts[1], output_matrix, deps=(grad_mid,))
-    out_parts[0] = product(activated_parts[0], output_matrix, deps=(grad_mid,))
     grad_heads = lax.all_to_all(grad_heads, ("seq", "replica"), 0, 0, tiled=True)
-    grad_heads, out_theirs, out_mine, grad_output, out_far = tie(
-        grad_heads, out_parts[1], out_parts[0], grad_output, out_far
-    )
+    grad_attn_parts = small_call(
+        outer_kernel, [shape(*v.shape) for v in attn_parts], (attended_rel, grad_mid_rel), deps=(out_parts[1],)
+    )
+    grad_heads, out_theirs, grad_attn_parts, grad_output, out_far = tie(
+        grad_heads, out_parts[1], grad_attn_parts, grad_output, out_far
+    )
+    attn_far = far_sum(grad_attn_parts[2], grad_attn_parts[3])
     out_diagonal = scatter_diagonal_by_row(out_far)
     *grad_qkv_parts, sums_qkv = small_call(
         lambda *refs: attend_back_kernel(heads, *refs),
@@ -698,32 +701,32 @@
         (own, *qkv_parts, grad_heads),
         [head_block] * 3 + [head_sums] * 3,
     )
-    out_got = flip(out_theirs, CORE)
     other_output = flip(grad_output, COL)
     into = [None] * 4
     into[3] = product(grad_qkv_parts[3], qkv_matrix, ACROSS)
     into[2] = product(grad_qkv_parts[2], qkv_matrix, ACROSS, deps=(into[3], other_output, *out_diagonal))
-    out_terms = scatter_relay(out_mine, out_got, out_diagonal, deps=(into[2],))
     into_far = far_sum(into[2], into[3])
-    into[1] = product(grad_qkv_parts[1], qkv_matrix, ACROSS, deps=(into_far, out_terms[3]))
+    into[1] = product(grad_qkv_parts[1], qkv_matrix, ACROSS, deps=(into_far,))
     into[0] = product(grad_qkv_parts[0], qkv_matrix, ACROSS, deps=(into[1],))
     into_got = flip(into[1], CORE)
-    grad_attn_parts = small_call(
-        outer_kernel, [shape(*v.shape) for v in attn_parts], (attended_rel, grad_mid_rel), deps=(into[0],)
-    )
-    grad_in = scatter_relay(into[0], into_got, scatter_diagonal(into_far), deps=(grad_attn_parts[0],))
-    grad_qkv = tall_product(hidden_in_parts, grad_qkv_parts, (grad_in[3],))
-    attn_got = flip(grad_attn_parts[1], CORE)
-    attn_far = far_sum(grad_attn_parts[2], grad_attn_parts[3])
-    attn_far, grad_qkv = tie(attn_far, grad_qkv)
+    grad_qkv = tall_product(hidden_in_parts, grad_qkv_parts, (into[0],))
+    grad_in = scatter_relay(into[0], into_got, scatter_diagonal(into_far))
+    *grad_in, grad_qkv = tie(*grad_in, grad_qkv)
     grad_qkv = line_scatter(grad_qkv).reshape(S, rows, 3 * hw)
+    attn_far, in_send, attn_theirs = tie(attn_far, grad_in[3], grad_attn_parts[1])
+    grad_in[3] = in_send
     attn_diagonal = scatter_diagonal(attn_far)
+    attn_got = flip(attn_theirs, CORE)
     grad_attn = scatter_relay(grad_attn_parts[0], attn_got, attn_diagonal)
-    grad_hidden, in_send = tie(grad_hidden, grad_in[3])
-    grad_in = scatter_last(*grad_in[:3], in_send)
+    attn_send, out_theirs = tie(grad_attn[3], out_theirs)
+    grad_attn = (*grad_attn[:3], attn_send)
+    out_got = flip(out_theirs, CORE)
+    out_parts[0] = product(activated_parts[0], output_matrix, deps=(attn_send,))
+    grad_in = scatter_last(*grad_in)
+    out_terms = scatter_relay(out_parts[0], out_got, out_diagonal)
+    grad_hidden, attn_send = tie(grad_hidden, attn_send)
+    grad_attn = scatter_last(*grad_attn[:3], attn_send)
     grad_hidden = seq_exchange(grad_hidden.reshape(S, rows, fw))
-    grad_hidden, attn_send = tie(grad_hidden, grad_attn[3])
-    grad_attn = scatter_last(*grad_attn[:3], attn_send)
     other_hidden = flip(grad_hidden, COL)
     grad_inputs, sums_one = small_call(
         lambda *refs: back_in_kernel(grid, rows, *refs),
@@ -733,6 +736,8 @@
         deps=(attn_send,),
     )
     out_terms = scatter_last(*out_terms)
+    sums_one, out_last, other_hidden = tie(sums_one, out_terms[2:], other_hidden)
+    out_terms = (*out_terms[:2], *out_last)
     layer_out = small_call(
         out_kernel, shape(n, D), (*out_terms, mid_rows, output_shift), first_rows=((0, n), (1, n))
     )

time: 635 us -> 630 us (level)
  waiting for transfers between devices: 193 us -> 182 us
    ppermute x60, waiting for transfers between devices: 145 us -> 104 us  [flip(): lax.ppermute(v, axis, [(i, i ^ bit) for i in range(lax.axis_size(axis))])]
    all_to_all x4, waiting for transfers between devices: 47 us -> 77.8 us  [seq_exchange(): return lax.all_to_all(v, 'seq', 0, 0, tiled=True)]
    unnamed x153 -> x149, local copies, waits for them, and re-layouts: 55.2 us -> 53.2 us
  transfers between devices with their start and end apart: 73 -> 73, of which waited for: 28 -> 30; matrix products, arithmetic and copies ran while one was open for 9% -> 9% of each run, Pallas kernels for 38% -> 39%
where the time goes in v5:
time: 630 us; the launch traced here: 619 us
  Pallas kernels  245 us (39%)
  waiting for transfers between devices  182 us (29%)
  local copies, waits for them, and re-layouts  79 us (13%)
  starting transfers between devices  67.3 us (11%)
  blocking collectives  18.4 us (3%)
  between operations  15.5 us (2%)
  other arithmetic  12 us (2%)
    ppermute x60, waiting for transfers between devices, flip(): lax.ppermute(v, axis, [(i, i ^ bit) for i in range(lax.axis_size(axis))])  104 us
    pallas_call x13, Pallas kernels, small_call(): pl.pallas_call(ordered(kernel, len(operands), deps), grid=(1,), in_specs=...  86.2 us
    all_to_all x4, waiting for transfers between devices, seq_exchange(): return lax.all_to_all(v, 'seq', 0, 0, tiled=True)  77.8 us
    unnamed x149, local copies, waits for them, and re-layouts  53.2 us
    pallas_call x12, Pallas kernels, product(): pl.pallas_call(ordered(lambda *refs: product_kernel(dims, *refs), 2 + len...  51.4 us
    ppermute x60, starting transfers between devices, flip(): lax.ppermute(v, axis, [(i, i ^ bit) for i in range(lax.axis_size(axis))])  47.4 us
    pallas_call x3, Pallas kernels, tall_product(): pl.pallas_call(ordered(tall_kernel, 2 * len(lefts), deps), grid=(deep //...  38.2 us
    pallas_call x4, Pallas kernels, down_product(): pl.pallas_call(ordered(down_kernel, 4, deps), grid=(tokens // tile,), in_...  36.4 us
  transfers between devices with their start and end apart: 73, of which 30 were waited for; matrix products, arithmetic and copies ran while one was open for 9% of the time, Pallas kernels for 39%

profile of v5, /device:TPU:0, one launch (start us, length us, event | category | flops | bytes accessed | tf_op | source)
XLA Modules:
  0.0 619.2 jit_solution(10608253962149904021)
XLA Ops:
  11.0 3.0 collective-permute-start
  16.5 2.7 collective-permute-start.1
  20.1 3.5 all-to-all-start
  23.7 3.7 copy.40
  29.0 6.2 %all-to-all-done = bf16[4,128,768]{1,2,0:T(8,128)(2,1)S(1)} async-done(((bf16[4,128,768]{1,2,0:T(8,128)(2,1)}), bf16[4,128,768]{1,2,0:T(8,128)(2,1)S(1)}, u32[]{:S(2)}, u32[]{:S(2)}) %all-to-all-start) | async-done | bytes 786464 | tf_op jit(solution)/shard_map/all_to_all | solution.py:125
  36.9 3.5 collective-permute-done.3
  41.0 3.4 shard_map.263
  46.2 3.5 all-to-all-start.1
  49.8 2.9 fusion
  52.7 28.4 %all-to-all-done.1 = bf16[4,128,1024]{1,2,0:T(8,128)(2,1)S(1)} async-done(((bf16[4,128,1024]{1,2,0:T(8,128)(2,1)}), bf16[4,128,1024]{1,2,0:T(8,128)(2,1)S(1)}, u32[]{:S(2)}, u32[]{:S(2)}) %all-to-all-start.1) | async-done | bytes 1048608 | tf_op jit(solution)/shard_map/all_to_all | solution.py:125
  88.1 13.0 %collective-permute-done.7 = bf16[128,2048]{1,0:T(8,128)(2,1)S(1)} collective-permute-done((bf16[128,2048]{1,0:T(8,128)(2,1)S(1)}, bf16[128,2048]{1,0:T(8,128)(2,1)S(1)}, u32[]{:S(2)}, u32[]{:S(2)}) %collective-permute-start.7) | collective-permute-done | bytes 524320 | tf_op jit(solution)/shard_map/ppermute | solution.py:44
  103.0 2.7 collective-permute-done.9.refs_0_.refs_3_
  115.5 5.2 shard_map.264.refs_1_
  121.7 5.4 shard_map.265.refs_2_
  128.2 3.1 collective-permute-done.11
  136.5 11.3 %shard_map.268 = bf16[8,256,256]{2,1,0:T(8,128)(2,1)} custom-call(s32[2]{0:T(128)} %pad_add_fusion.refs_0_, bf16[768,768]{1,0:T(8,128)(2,1)} %copy-done.9, bf16[768,768]{1,0:T(8,128)(2,1)} %copy-done.10, bf16[256,768]{1,0:T(8,128)(2,1)} %copy-done.26, bf16[256,768]{1,0:T(8,128)(2,1)} %copy-done.27), custom_call_target="tpu_custom_call" | custom-call | flops 1 | bytes 1 | tf_op jit(solution)/shard_map/pallas_call | solution.py:528
  152.4 18.4 %all_to_all.30.refs_1_ = bf16[8,256,256]{2,1,0:T(8,128)(2,1)} all-to-all(bf16[8,256,256]{2,1,0:T(8,128)(2,1)S(1)} %copy-done.49), channel_id=1, replica_groups=mesh['seq'=4,'shard'=4,'replica'=2] {'seq','replica'}, dimensions={0} | all-to-all | bytes 2097152 | tf_op jit(solution)/shard_map/all_to_all | solution.py:636
  175.1 9.3 %shard_map.269 = (f32[256,2048]{1,0:T(8,128)}, bf16[256,2048]{1,0:T(8,128)(2,1)}, bf16[256,2048]{1,0:T(8,128)(2,1)}) custom-call(s32[2]{0:T(128)} %pad_add_fusion.refs_0_, bf16[8,256,256]{2,1,0:T(8,128)(2,1)} %all_to_all.30.refs_1_, bf16[1536,1024]{1,0:T(8,128)(2,1)} %copy-done.44, bf16[1536,1024]{1,0:T(8,128)(2,1)} %copy-done.46, ...), custom_call_target="tpu_custom_call" | custom-call | flops 1 | bytes 1 | tf_op jit(solution)/shard_map/pallas_call | solution.py:528
  186.9 10.2 %collective-permute-done.19 = bf16[256,2048]{1,0:T(8,128)(2,1)} collective-permute-done((bf16[256,2048]{1,0:T(8,128)(2,1)}, bf16[256,2048]{1,0:T(8,128)(2,1)}, u32[]{:S(2)}, u32[]{:S(2)}) %collective-permute-start.19) | collective-permute-done | bytes 1048608 | tf_op jit(solution)/shard_map/ppermute | solution.py:44
  198.3 20.5 %collective-permute-done.17 = bf16[256,2048]{1,0:T(8,128)(2,1)S(1)} collective-permute-done((bf16[256,2048]{1,0:T(8,128)(2,1)}, bf16[256,2048]{1,0:T(8,128)(2,1)S(1)}, u32[]{:S(2)}, u32[]{:S(2)}) %collective-permute-start.17) | collective-permute-done | bytes 1048608 | tf_op jit(solution)/shard_map/ppermute | solution.py:44
  226.4 7.5 %shard_map.270 = (bf16[768,1024]{1,0:T(8,128)(2,1)S(1)}, f32[768,1024]{1,0:T(8,128)S(1)}) custom-call(bf16[768,2048]{1,0:T(8,128)(2,1)} %constant_dynamic-update-slice_fusion.10.h_ref.refs_0_, bf16[2048,1024]{1,0:T(8,128)(2,1)} %all-gather.9.cloned.1.call-done.w_ref.refs_3_, f32[1,1024]{1,0:T(1,128)S(1)} %bitcast.83), custom_call_target="tpu_custom_call" | custom-call | flops 1 | bytes 1 | tf_op jit(solution)/shard_map/pallas_call | solution.py:339
  246.7 3.8 shard_map.272
  251.5 4.4 shard_map.273
  256.9 7.6 %shard_map.271 = (bf16[768,1024]{1,0:T(8,128)(2,1)S(1)}, f32[768,1024]{1,0:T(8,128)S(1)}) custom-call(bf16[768,2048]{1,0:T(8,128)(2,1)} %collective-permute-done.23.h_ref.refs_1_, bf16[2048,1024]{1,0:T(8,128)(2,1)} %all-gather.9.cloned.1.call-done.w_ref.refs_3_, f32[1,1024]{1,0:T(1,128)S(1)} %bitcast.86), custom_call_target="tpu_custom_call" | custom-call | flops 1 | bytes 1 | tf_op jit(solution)/shard_map/pallas_call | solution.py:339
  267.4 2.7 collective-permute-done.27.refs_7_.refs_0_
  270.0 13.7 %shard_map.274.refs_4_ = bf16[1024,2048]{1,0:T(8,128)(2,1)} custom-call(bf16[768,1024]{1,0:T(8,128)(2,1)S(1)} %get-tuple-element.187.refs_0_, bf16[768,1024]{1,0:T(8,128)(2,1)} %copy-done.14, bf16[256,1024]{1,0:T(8,128)(2,1)S(1)} %get-tuple-element.210.refs_2_.refs_0_, bf16[256,1024]{1,0:T(8,128)(2,1)S(1)} %get-tuple-element.211.refs_3_.refs_0_, ...), custom_call_target="tpu_custom_call" | custom-call | flops 1 | bytes 1 | tf_op jit(solution)/shard_map/pallas_call | solution.py:316
  285.1 6.5 %shard_map.275 = (bf16[256,1024]{1,0:T(8,128)(2,1)S(1)}, bf16[256,2048]{1,0:T(8,128)(2,1)S(1)}, f32[8,1024]{1,0:T(8,128)S(1)}) custom-call(bf16[256,2048]{1,0:T(8,128)(2,1)S(1)} %collective-permute-done.27.refs_7_.refs_0_, bf16[1024,2048]{1,0:T(8,128)(2,1)} %all-gather.11.cloned.1.call-done.refs_1_, f32[256,1024]{1,0:T(8,128)S(1)} %copy-done.38, ...), custom_call_target="tpu_custom_call" | custom-call | flops 1 | bytes 1 | tf_op jit(solution)/shard_map/pallas_call | solution.py:399
  291.7 5.8 shard_map.276
  298.0 11.7 %shard_map.277 = (bf16[768,1024]{1,0:T(8,128)(2,1)S(1)}, bf16[768,2048]{1,0:T(8,128)(2,1)S(1)}, f32[8,1024]{1,0:T(8,128)S(1)}) custom-call(bf16[768,2048]{1,0:T(8,128)(2,1)} %collective-permute-done.22.refs_5_.refs_0_, bf16[1024,2048]{1,0:T(8,128)(2,1)} %all-gather.11.cloned.1.call-done.refs_1_, f32[768,1024]{1,0:T(8,128)} %copy-done.29, ...), custom_call_target="tpu_custom_call" | custom-call | flops 1 | bytes 1 | tf_op jit(solution)/shard_map/pallas_call | solution.py:399
  312.0 12.4 %shard_map.278 = (bf16[768,1024]{1,0:T(8,128)(2,1)S(1)}, bf16[768,2048]{1,0:T(8,128)(2,1)}, f32[8,1024]{1,0:T(8,128)S(1)}) custom-call(bf16[768,2048]{1,0:T(8,128)(2,1)} %copy-done.45, bf16[1024,2048]{1,0:T(8,128)(2,1)} %all-gather.11.cloned.1.call-done.refs_1_, f32[768,1024]{1,0:T(8,128)} %copy-done.28, ...), custom_call_target="tpu_custom_call" | custom-call | flops 1 | bytes 1 | tf_op jit(solution)/shard_map/pallas_call | solution.py:399
  324.8 3.0 copy-done.6
  329.3 4.5 shard_map.280.refs_3_
  335.9 3.4 shard_map.281.refs_8_
  339.3 13.2 %shard_map.282.refs_13_ = bf16[2048,1024]{1,0:T(8,128)(2,1)} custom-call(bf16[768,2048]{1,0:T(8,128)(2,1)} %constant_dynamic-update-slice_fusion.10.h_ref.refs_0_, bf16[768,2048]{1,0:T(8,128)(2,1)} %collective-permute-done.23.h_ref.refs_1_, bf16[256,2048]{1,0:T(8,128)(2,1)S(1)} %constant_dynamic-update-slice_fusion.13.h_ref.refs_2_, ...), custom_call_target="tpu_custom_call" | custom-call | flops 1 | bytes 1 | tf_op jit(solution)/shard_map/pallas_call | solution.py:316
  352.5 2.6 add_convert_fusion.3.refs_12_
  355.1 4.5 collective-permute-done.32.refs_3_
  360.3 12.1 %shard_map.283 = (f32[256,2048]{1,0:T(8,128)}, bf16[256,2048]{1,0:T(8,128)(2,1)}, bf16[8,256,256]{2,1,0:T(8,128)(2,1)}, f32[8,2048]{1,0:T(8,128)}) custom-call(s32[2]{0:T(128)} %pad_add_fusion.refs_0_, bf16[768,2048]{1,0:T(8,128)(2,1)} %get-tuple-element.216.refs_0_.refs_2_.refs_1_, bf16[768,2048]{1,0:T(8,128)(2,1)} %copy-done.5, ...), custom_call_target="tpu_custom_call" | custom-call | flops 1 | bytes 1 | tf_op jit(solution)/shard_map/pallas_call | solution.py:528
  372.5 4.4 all-to-all-start.3
  378.5 7.1 %shard_map.284.refs_2_ = bf16[768,2048]{1,0:T(8,128)(2,1)} custom-call(bf16[768,1024]{1,0:T(8,128)(2,1)S(1)} %copy-done.15, bf16[1024,2048]{1,0:T(8,128)(2,1)} %all-gather.11.cloned.1.call-done.refs_1_, f32[256,2048]{1,0:T(8,128)S(1)} %copy-done.11), custom_call_target="tpu_custom_call" | custom-call | flops 1 | bytes 1 | tf_op jit(solution)/shard_map/pallas_call | solution.py:362
  385.6 6.0 shard_map.285
  395.0 17.9 %shard_map.286 = (bf16[768,768]{1,0:T(8,128)(2,1)}, bf16[768,768]{1,0:T(8,128)(2,1)}, bf16[256,768]{1,0:T(8,128)(2,1)}, bf16[256,768]{1,0:T(8,128)(2,1)}, f32[8,768]{1,0:T(8,128)}) custom-call(s32[2]{0:T(128)} %pad_add_fusion.refs_0_, bf16[768,768]{1,0:T(8,128)(2,1)} %copy-done.9, bf16[768,768]{1,0:T(8,128)(2,1)} %copy-done.10, bf16[256,768]{1,0:T(8,128)(2,1)} %copy-done.26, ...), custom_call_target="tpu_custom_call" | custom-call | flops 1 | bytes 1 | tf_op jit(solution)/shard_map/pallas_call | solution.py:528
  418.7 3.3 shard_map.288
  423.3 6.0 shard_map.289.refs_2_
  433.0 5.0 shard_map.290.refs_0_.refs_2_.refs_8_
  439.8 11.3 %shard_map.292 = bf16[2048,768]{1,0:T(8,128)(2,1)} custom-call(bf16[768,2048]{1,0:T(8,128)(2,1)} %copy-done.7, bf16[768,2048]{1,0:T(8,128)(2,1)} %collective-permute-done.6.refs_0_.refs_1_, bf16[256,2048]{1,0:T(8,128)(2,1)} %constant_dynamic-update-slice_fusion.3.refs_0_.refs_2_, bf16[256,2048]{1,0:T(8,128)(2,1)} %collective-permute-done.9.refs_0_.refs_3_, ...), custom_call_target="tpu_custom_call" | custom-call | flops 1 | bytes 1 | tf_op jit(solution)/shard_map/pallas_call | solution.py:316
  451.1 3.1 add_convert_fusion.2
  454.2 2.4 shard_map.291
  462.1 12.2 %collective-permute-done.44.refs_5_ = bf16[256,1024]{1,0:T(8,128)(2,1)S(1)} collective-permute-done((bf16[256,1024]{1,0:T(8,128)(2,1)S(1)}, bf16[256,1024]{1,0:T(8,128)(2,1)S(1)}, u32[]{:S(2)}, u32[]{:S(2)}) %collective-permute-start.44) | collective-permute-done | bytes 524320 | tf_op jit(solution)/shard_map/ppermute | solution.py:44
  480.8 4.4 all-to-all-start.4
  491.4 6.0 shard_map.294.refs_0_.refs_2_
  497.5 20.3 %all-to-all-done.4.refs_1_ = bf16[4,128,1024]{2,1,0:T(8,128)(2,1)} async-done(((bf16[4,128,1024]{2,1,0:T(8,128)(2,1)}), bf16[4,128,1024]{2,1,0:T(8,128)(2,1)}, u32[]{:S(2)}, u32[]{:S(2)}) %all-to-all-start.4) | async-done | bytes 1048608 | tf_op jit(solution)/shard_map/all_to_all | solution.py:125
  520.3 3.1 shard_map.296
  524.9 3.5 all-to-all-start.5
  528.5 4.0 add_convert_fusion
  533.7 6.5 %collective-permute-done.46.refs_2_ = bf16[256,2048]{1,0:T(8,128)(2,1)} collective-permute-done((bf16[256,2048]{1,0:T(8,128)(2,1)}, bf16[256,2048]{1,0:T(8,128)(2,1)}, u32[]{:S(2)}, u32[]{:S(2)}) %collective-permute-start.46) | collective-permute-done | bytes 1048608 | tf_op jit(solution)/shard_map/ppermute | solution.py:44
  540.2 7.2 %shard_map.295 = (f32[256,2048]{1,0:T(8,128)}, f32[8,2048]{1,0:T(8,128)}) custom-call(bf16[768,2048]{1,0:T(8,128)(2,1)} %copy-done.2, bf16[768,2048]{1,0:T(8,128)(2,1)} %collective-permute-done.39.refs_1_.refs_3_, bf16[256,2048]{1,0:T(8,128)(2,1)} %collective-permute-done.46.refs_2_, bf16[256,2048]{1,0:T(8,128)(2,1)} %collective-permute-done.47.refs_3_, ...), custom_call_target="tpu_custom_call" | custom-call | flops 1 | bytes 1 | tf_op jit(solution)/shard_map/pallas_call | solution.py:528
  547.4 22.9 %all-to-all-done.5.refs_1_ = bf16[4,128,768]{2,1,0:T(8,128)(2,1)S(1)} async-done(((bf16[4,128,768]{2,1,0:T(8,128)(2,1)}), bf16[4,128,768]{2,1,0:T(8,128)(2,1)S(1)}, u32[]{:S(2)}, u32[]{:S(2)}) %all-to-all-start.5) | async-done | bytes 786464 | tf_op jit(solution)/shard_map/all_to_all | solution.py:125
  575.5 3.4 collective-permute-done.51
  579.5 6.0 collective-permute-done.52
  587.7 4.1 collective-permute-done.54
  592.8 3.8 shard_map.301
  599.4 3.9 shard_map.300
  603.3 4.5 shard_map.297
  607.8 3.3 shard_map.298
  (346 shorter events, 138.5 us)
Async XLA Ops:
  7.2 95.9 %all-gather.5.cloned.1.call-start = ((), (), s32[]{:S(2)}) async-start(), calls=%async_computation.10 | async-start | bytes 1310720 | tf_op jit(solution)/shard_map/all_gather | solution.py:117
  16.5 11.0 %collective-permute-start.1 = (bf16[2,1536]{1,0:T(2,128)(2,1)S(1)}, bf16[2,1536]{1,0:T(2,128)(2,1)S(1)}, u32[]{:S(2)}, u32[]{:S(2)}) collective-permute-start(bf16[2,1536]{1,0:T(2,128)(2,1)S(1)} %pad_maximum_fusion.2), channel_id=1, source_target_pairs={{0,4},{2,6},{4,0},{6,2},{1,5},{3,7},{5,1},{7,3},{8,12},{10,14},{12... | collective-permute-start | bytes 18440 | tf_op jit(solution)/shard_map/ppermute | solution.py:44
  20.1 15.2 %all-to-all-start = ((bf16[4,128,768]{1,2,0:T(8,128)(2,1)}), bf16[4,128,768]{1,2,0:T(8,128)(2,1)S(1)}, u32[]{:S(2)}, u32[]{:S(2)}) async-start(bf16[4,128,768]{1,2,0:T(8,128)(2,1)} %bitcast.11), calls=%async_computation | async-start | bytes 1572864 | tf_op jit(solution)/shard_map/all_to_all | solution.py:125
  23.6 84.0 %all-gather.7.cloned.1.call-start = ((), (), s32[]{:S(2)}) async-start(), calls=%async_computation.11 | async-start | bytes 3932160 | tf_op jit(solution)/shard_map/all_gather | solution.py:117
  44.4 38.0 %collective-permute-start.5 = (bf16[256,2048]{1,0:T(8,128)(2,1)}, bf16[256,2048]{1,0:T(8,128)(2,1)S(1)}, u32[]{:S(2)}, u32[]{:S(2)}) collective-permute-start(bf16[256,2048]{1,0:T(8,128)(2,1)} %shard_map.263), channel_id=1, source_target_pairs={{0,1},{1,0},{2,3},{3,2},{4,5},{5,4},{6,7},{7,6},{8,9},{9,8},{10,11... | collective-permute-start | bytes 3145736 | tf_op jit(solution)/shard_map/ppermute | solution.py:44
  45.9 36.5 %collective-permute-start.4 = (bf16[256,2048]{1,0:T(8,128)(2,1)}, bf16[256,2048]{1,0:T(8,128)(2,1)S(1)}, u32[]{:S(2)}, u32[]{:S(2)}) collective-permute-start(bf16[256,2048]{1,0:T(8,128)(2,1)} %shard_map.263), channel_id=1, source_target_pairs={{0,16},{8,24},{16,0},{24,8},{1,17},{9,25},{17,1},{25,9},{2,18},{10... | collective-permute-start | bytes 3145736 | tf_op jit(solution)/shard_map/ppermute | solution.py:44
  46.2 34.9 %all-to-all-start.1 = ((bf16[4,128,1024]{1,2,0:T(8,128)(2,1)}), bf16[4,128,1024]{1,2,0:T(8,128)(2,1)S(1)}, u32[]{:S(2)}, u32[]{:S(2)}) async-start(bf16[4,128,1024]{1,2,0:T(8,128)(2,1)} %bitcast.6), calls=%async_computation.1 | async-start | bytes 2097152 | tf_op jit(solution)/shard_map/all_to_all | solution.py:125
  49.7 176.6 %all-gather.9.cloned.1.call-start = ((), (), s32[]{:S(2)}) async-start(), calls=%async_computation.12 | async-start | bytes 5242880 | tf_op jit(solution)/shard_map/all_gather | solution.py:117
  86.6 19.2 %collective-permute-start.6 = (bf16[768,2048]{1,0:T(8,128)(2,1)S(1)}, bf16[768,2048]{1,0:T(8,128)(2,1)}, u32[]{:S(2)}, u32[]{:S(2)}) collective-permute-start(bf16[768,2048]{1,0:T(8,128)(2,1)S(1)} %constant_dynamic-update-slice_fusion.refs_0_), channel_id=1, source_target_pairs={{0,8},{8,0},{16,24},{24,16},{1,9},{9,1},{17,25},{25,17},{2,10},{10... | collective-permute-start | bytes 9437192 | tf_op jit(solution)/shard_map/ppermute | solution.py:44
  86.7 14.4 %collective-permute-start.7 = (bf16[128,2048]{1,0:T(8,128)(2,1)S(1)}, bf16[128,2048]{1,0:T(8,128)(2,1)S(1)}, u32[]{:S(2)}, u32[]{:S(2)}) collective-permute-start(bf16[128,2048]{1,0:T(8,128)(2,1)S(1)} %slice.167), channel_id=1, source_target_pairs={{0,1},{1,0},{2,3},{3,2},{4,5},{5,4},{6,7},{7,6},{8,9},{9,8},{10,11... | collective-permute-start | bytes 1572872 | tf_op jit(solution)/shard_map/ppermute | solution.py:44
  87.4 14.5 %collective-permute-start.8 = (bf16[128,2048]{1,0:T(8,128)(2,1)S(1)}, bf16[128,2048]{1,0:T(8,128)(2,1)S(1)}, u32[]{:S(2)}, u32[]{:S(2)}) collective-permute-start(bf16[128,2048]{1,0:T(8,128)(2,1)S(1)} %slice.168), channel_id=1, source_target_pairs={{0,16},{8,24},{16,0},{24,8},{1,17},{9,25},{17,1},{25,9},{2,18},{10... | collective-permute-start | bytes 1572872 | tf_op jit(solution)/shard_map/ppermute | solution.py:44
  102.8 181.1 %all-gather.11.cloned.1.call-start = ((), (), s32[]{:S(2)}) async-start(), calls=%async_computation.13 | async-start | bytes 5242880 | tf_op jit(solution)/shard_map/all_gather | solution.py:117
  105.8 25.5 %collective-permute-start.11 = (bf16[512,1024]{1,0:T(8,128)(2,1)}, bf16[512,1024]{1,0:T(8,128)(2,1)}, u32[]{:S(2)}, u32[]{:S(2)}) collective-permute-start(bf16[512,1024]{1,0:T(8,128)(2,1)} %all-gather.5.cloned.1.call-done), channel_id=1, source_target_pairs={{0,1},{1,0},{2,3},{3,2},{4,5},{5,4},{6,7},{7,6},{8,9},{9,8},{10,11... | collective-permute-start | bytes 3145736 | tf_op jit(solution)/shard_map/ppermute | solution.py:44
  106.8 25.2 %collective-permute-start.10 = (bf16[512,1024]{1,0:T(8,128)(2,1)}, bf16[512,1024]{1,0:T(8,128)(2,1)}, u32[]{:S(2)}, u32[]{:S(2)}) collective-permute-start(bf16[512,1024]{1,0:T(8,128)(2,1)} %all-gather.5.cloned.1.call-done), channel_id=1, source_target_pairs={{0,16},{8,24},{16,0},{24,8},{1,17},{9,25},{17,1},{25,9},{2,18},{10... | collective-permute-start | bytes 3145736 | tf_op jit(solution)/shard_map/ppermute | solution.py:44
  134.2 13.6 %collective-permute-start.13 = (bf16[256,1024]{1,0:T(8,128)(2,1)S(1)}, bf16[256,1024]{1,0:T(8,128)(2,1)S(1)}, u32[]{:S(2)}, u32[]{:S(2)}) collective-permute-start(bf16[256,1024]{1,0:T(8,128)(2,1)S(1)} %slice.172), channel_id=1, source_target_pairs={{0,16},{8,24},{16,0},{24,8},{1,17},{9,25},{17,1},{25,9},{2,18},{10... | collective-permute-start | bytes 1572872 | tf_op jit(solution)/shard_map/ppermute | solution.py:44
  134.9 12.9 %collective-permute-start.12 = (bf16[256,1024]{1,0:T(8,128)(2,1)S(1)}, bf16[256,1024]{1,0:T(8,128)(2,1)}, u32[]{:S(2)}, u32[]{:S(2)}) collective-permute-start(bf16[256,1024]{1,0:T(8,128)(2,1)S(1)} %slice.171), channel_id=1, source_target_pairs={{0,1},{1,0},{2,3},{3,2},{4,5},{5,4},{6,7},{7,6},{8,9},{9,8},{10,11... | collective-permute-start | bytes 1572872 | tf_op jit(solution)/shard_map/ppermute | solution.py:44
  150.6 21.8 %collective-permute-start.14 = (bf16[1536,1024]{1,0:T(8,128)(2,1)S(1)}, bf16[1536,1024]{1,0:T(8,128)(2,1)S(1)}, u32[]{:S(2)}, u32[]{:S(2)}) collective-permute-start(bf16[1536,1024]{1,0:T(8,128)(2,1)S(1)} %constant_dynamic-update-slice_fusion.5.refs_2_.refs_8_), channel_id=1, source_target_pairs={{0,8},{8,0},{16,24},{24,16},{1,9},{9,1},{17,25},{25,17},{2,10},{10... | collective-permute-start | bytes 9437192 | tf_op jit(solution)/shard_map/ppermute | solution.py:44
  152.3 20.2 %collective-permute-start.15 = (bf16[512,1024]{1,0:T(8,128)(2,1)S(1)}, bf16[512,1024]{1,0:T(8,128)(2,1)S(1)}, u32[]{:S(2)}, u32[]{:S(2)}) collective-permute-start(bf16[512,1024]{1,0:T(8,128)(2,1)S(1)} %constant_dynamic-update-slice_fusion.8.refs_4_.refs_10_), channel_id=1, source_target_pairs={{0,8},{8,0},{16,24},{24,16},{1,9},{9,1},{17,25},{25,17},{2,10},{10... | collective-permute-start | bytes 3145736 | tf_op jit(solution)/shard_map/ppermute | solution.py:44
  170.8 26.3 %collective-permute-start.19 = (bf16[256,2048]{1,0:T(8,128)(2,1)}, bf16[256,2048]{1,0:T(8,128)(2,1)}, u32[]{:S(2)}, u32[]{:S(2)}) collective-permute-start(bf16[256,2048]{1,0:T(8,128)(2,1)} %bitcast.32.refs_6_), channel_id=1, source_target_pairs={{0,1},{1,0},{2,3},{3,2},{4,5},{5,4},{6,7},{7,6},{8,9},{9,8},{10,11... | collective-permute-start | bytes 3145736 | tf_op jit(solution)/shard_map/ppermute | solution.py:44
  171.9 26.4 %collective-permute-start.18 = (bf16[256,2048]{1,0:T(8,128)(2,1)}, bf16[256,2048]{1,0:T(8,128)(2,1)}, u32[]{:S(2)}, u32[]{:S(2)}) collective-permute-start(bf16[256,2048]{1,0:T(8,128)(2,1)} %bitcast.32.refs_6_), channel_id=1, source_target_pairs={{0,16},{8,24},{16,0},{24,8},{1,17},{9,25},{17,1},{25,9},{2,18},{10... | collective-permute-start | bytes 3145736 | tf_op jit(solution)/shard_map/ppermute | solution.py:44
  184.4 34.4 %collective-permute-start.17 = (bf16[256,2048]{1,0:T(8,128)(2,1)}, bf16[256,2048]{1,0:T(8,128)(2,1)S(1)}, u32[]{:S(2)}, u32[]{:S(2)}) collective-permute-start(bf16[256,2048]{1,0:T(8,128)(2,1)} %get-tuple-element.181), channel_id=1, source_target_pairs={{0,1},{1,0},{2,3},{3,2},{4,5},{5,4},{6,7},{7,6},{8,9},{9,8},{10,11... | collective-permute-start | bytes 3145736 | tf_op jit(solution)/shard_map/ppermute | solution.py:44
  185.4 33.7 %collective-permute-start.16 = (bf16[256,2048]{1,0:T(8,128)(2,1)}, bf16[256,2048]{1,0:T(8,128)(2,1)S(1)}, u32[]{:S(2)}, u32[]{:S(2)}) collective-permute-start(bf16[256,2048]{1,0:T(8,128)(2,1)} %get-tuple-element.181), channel_id=1, source_target_pairs={{0,16},{8,24},{16,0},{24,8},{1,17},{9,25},{17,1},{25,9},{2,18},{10... | collective-permute-start | bytes 3145736 | tf_op jit(solution)/shard_map/ppermute | solution.py:44
  186.9 204.9 %reduce-scatter.5.cloned.1.call-start = ((), (), s32[]{:S(2)}) async-start(), calls=%async_computation.14 | async-start | bytes 5242880 | tf_op jit(solution)/shard_map/reduce_scatter | solution.py:121
  220.8 13.3 %collective-permute-start.21 = (bf16[128,2048]{1,0:T(8,128)(2,1)}, bf16[128,2048]{1,0:T(8,128)(2,1)}, u32[]{:S(2)}, u32[]{:S(2)}) collective-permute-start(bf16[128,2048]{1,0:T(8,128)(2,1)} %slice.178), channel_id=1, source_target_pairs={{0,16},{8,24},{16,0},{24,8},{1,17},{9,25},{17,1},{25,9},{2,18},{10... | collective-permute-start | bytes 1572872 | tf_op jit(solution)/shard_map/ppermute | solution.py:44
  221.4 13.7 %collective-permute-start.20 = (bf16[128,2048]{1,0:T(8,128)(2,1)}, bf16[128,2048]{1,0:T(8,128)(2,1)}, u32[]{:S(2)}, u32[]{:S(2)}) collective-permute-start(bf16[128,2048]{1,0:T(8,128)(2,1)} %slice.177), channel_id=1, source_target_pairs={{0,1},{1,0},{2,3},{3,2},{4,5},{5,4},{6,7},{7,6},{8,9},{9,8},{10,11... | collective-permute-start | bytes 1572872 | tf_op jit(solution)/shard_map/ppermute | solution.py:44
  226.3 30.7 %collective-permute-start.23 = (bf16[768,2048]{1,0:T(8,128)(2,1)}, bf16[768,2048]{1,0:T(8,128)(2,1)}, u32[]{:S(2)}, u32[]{:S(2)}) collective-permute-start(bf16[768,2048]{1,0:T(8,128)(2,1)} %constant_dynamic-update-slice_fusion.10.h_ref.refs_0_), channel_id=1, source_target_pairs={{0,8},{8,0},{16,24},{24,16},{1,9},{9,1},{17,25},{25,17},{2,10},{10... | collective-permute-start | bytes 9437192 | tf_op jit(solution)/shard_map/ppermute | solution.py:44
  241.7 25.7 %collective-permute-start.22 = (bf16[768,2048]{1,0:T(8,128)(2,1)S(1)}, bf16[768,2048]{1,0:T(8,128)(2,1)}, u32[]{:S(2)}, u32[]{:S(2)}) collective-permute-start(bf16[768,2048]{1,0:T(8,128)(2,1)S(1)} %constant_dynamic-update-slice_fusion.15.refs_4_.refs_0_), channel_id=1, source_target_pairs={{0,8},{8,0},{16,24},{24,16},{1,9},{9,1},{17,25},{25,17},{2,10},{10... | collective-permute-start | bytes 9437192 | tf_op jit(solution)/shard_map/ppermute | solution.py:44
  241.7 9.8 %collective-permute-start.24 = (bf16[256,2048]{1,0:T(8,128)(2,1)S(1)}, bf16[256,2048]{1,0:T(8,128)(2,1)S(1)}, u32[]{:S(2)}, u32[]{:S(2)}) collective-permute-start(bf16[256,2048]{1,0:T(8,128)(2,1)S(1)} %constant_dynamic-update-slice_fusion.13.h_ref.refs_2_), channel_id=1, source_target_pairs={{0,8},{8,0},{16,24},{24,16},{1,9},{9,1},{17,25},{25,17},{2,10},{10... | collective-permute-start | bytes 3145736 | tf_op jit(solution)/shard_map/ppermute | solution.py:44
  244.8 21.4 %collective-permute-start.26 = (bf16[128,2048]{1,0:T(8,128)(2,1)S(1)}, bf16[128,2048]{1,0:T(8,128)(2,1)S(1)}, u32[]{:S(2)}, u32[]{:S(2)}) collective-permute-start(bf16[128,2048]{1,0:T(8,128)(2,1)S(1)} %slice.180), channel_id=1, source_target_pairs={{0,16},{8,24},{16,0},{24,8},{1,17},{9,25},{17,1},{25,9},{2,18},{10... | collective-permute-start | bytes 1572872 | tf_op jit(solution)/shard_map/ppermute | solution.py:44
  245.7 20.5 %collective-permute-start.25 = (bf16[128,2048]{1,0:T(8,128)(2,1)S(1)}, bf16[128,2048]{1,0:T(8,128)(2,1)S(1)}, u32[]{:S(2)}, u32[]{:S(2)}) collective-permute-start(bf16[128,2048]{1,0:T(8,128)(2,1)S(1)} %slice.179), channel_id=1, source_target_pairs={{0,1},{1,0},{2,3},{3,2},{4,5},{5,4},{6,7},{7,6},{8,9},{9,8},{10,11... | collective-permute-start | bytes 1572872 | tf_op jit(solution)/shard_map/ppermute | solution.py:44
  283.8 195.7 %reduce-scatter.7.cloned.1.call-start = ((), (), s32[]{:S(2)}) async-start(), calls=%async_computation.15 | async-start | bytes 5242880 | tf_op jit(solution)/shard_map/reduce_scatter | solution.py:121
  309.7 15.2 %collective-permute-start.29 = (bf16[768,2048]{1,0:T(8,128)(2,1)S(1)}, bf16[768,2048]{1,0:T(8,128)(2,1)S(1)}, u32[]{:S(2)}, u32[]{:S(2)}) collective-permute-start(bf16[768,2048]{1,0:T(8,128)(2,1)S(1)} %get-tuple-element.217), channel_id=1, source_target_pairs={{0,8},{8,0},{16,24},{24,16},{1,9},{9,1},{17,25},{25,17},{2,10},{10... | collective-permute-start | bytes 9437192 | tf_op jit(solution)/shard_map/ppermute | solution.py:44
  310.3 14.0 %collective-permute-start.31 = (bf16[128,2048]{1,0:T(8,128)(2,1)S(1)}, bf16[128,2048]{1,0:T(8,128)(2,1)S(1)}, u32[]{:S(2)}, u32[]{:S(2)}) collective-permute-start(bf16[128,2048]{1,0:T(8,128)(2,1)S(1)} %get-tuple-element.279), channel_id=1, source_target_pairs={{0,16},{8,24},{16,0},{24,8},{1,17},{9,25},{17,1},{25,9},{2,18},{10... | collective-permute-start | bytes 1572872 | tf_op jit(solution)/shard_map/ppermute | solution.py:44
  311.2 13.6 %collective-permute-start.30 = (bf16[128,2048]{1,0:T(8,128)(2,1)S(1)}, bf16[128,2048]{1,0:T(8,128)(2,1)S(1)}, u32[]{:S(2)}, u32[]{:S(2)}) collective-permute-start(bf16[128,2048]{1,0:T(8,128)(2,1)S(1)} %get-tuple-element.280), channel_id=1, source_target_pairs={{0,1},{1,0},{2,3},{3,2},{4,5},{5,4},{6,7},{7,6},{8,9},{9,8},{10,11... | collective-permute-start | bytes 1572872 | tf_op jit(solution)/shard_map/ppermute | solution.py:44
  333.8 18.7 %collective-permute-start.34 = (bf16[256,2048]{1,0:T(8,128)(2,1)}, bf16[256,2048]{1,0:T(8,128)(2,1)}, u32[]{:S(2)}, u32[]{:S(2)}) collective-permute-start(bf16[256,2048]{1,0:T(8,128)(2,1)} %shard_map.280.refs_3_), channel_id=1, source_target_pairs={{0,8},{8,0},{16,24},{24,16},{1,9},{9,1},{17,25},{25,17},{2,10},{10... | collective-permute-start | bytes 3145736 | tf_op jit(solution)/shard_map/ppermute | solution.py:44
  333.8 25.9 %collective-permute-start.32 = (bf16[256,2048]{1,0:T(8,128)(2,1)}, bf16[256,2048]{1,0:T(8,128)(2,1)}, u32[]{:S(2)}, u32[]{:S(2)}) collective-permute-start(bf16[256,2048]{1,0:T(8,128)(2,1)} %get-tuple-element.218), channel_id=1, source_target_pairs={{0,16},{8,24},{16,0},{24,8},{1,17},{9,25},{17,1},{25,9},{2,18},{10... | collective-permute-start | bytes 3145736 | tf_op jit(solution)/shard_map/ppermute | solution.py:44
  334.9 25.4 %collective-permute-start.33 = (bf16[256,2048]{1,0:T(8,128)(2,1)S(1)}, bf16[256,2048]{1,0:T(8,128)(2,1)}, u32[]{:S(2)}, u32[]{:S(2)}) collective-permute-start(bf16[256,2048]{1,0:T(8,128)(2,1)S(1)} %get-tuple-element.219.refs_2_), channel_id=1, source_target_pairs={{0,1},{1,0},{2,3},{3,2},{4,5},{5,4},{6,7},{7,6},{8,9},{9,8},{10,11... | collective-permute-start | bytes 3145736 | tf_op jit(solution)/shard_map/ppermute | solution.py:44
  372.5 19.3 %all-to-all-start.3 = ((bf16[8,256,256]{2,1,0:T(8,128)(2,1)}), bf16[8,256,256]{2,1,0:T(8,128)(2,1)}, u32[]{:S(2)}, u32[]{:S(2)}) async-start(bf16[8,256,256]{2,1,0:T(8,128)(2,1)} %get-tuple-element.223), calls=%async_computation.3 | async-start | bytes 2097152 | tf_op jit(solution)/shard_map/all_to_all | solution.py:689
  376.9 148.0 %reduce-scatter.9.cloned.1.call-start = ((), (), s32[]{:S(2)}) async-start(), calls=%async_computation.16 | async-start | bytes 3932160 | tf_op jit(solution)/shard_map/reduce_scatter | solution.py:121
  391.8 25.4 %collective-permute-start.37 = (bf16[256,2048]{1,0:T(8,128)(2,1)}, bf16[256,2048]{1,0:T(8,128)(2,1)S(1)}, u32[]{:S(2)}, u32[]{:S(2)}) collective-permute-start(bf16[256,2048]{1,0:T(8,128)(2,1)} %add_convert_fusion.3.refs_12_), channel_id=1, source_target_pairs={{0,16},{8,24},{16,0},{24,8},{1,17},{9,25},{17,1},{25,9},{2,18},{10... | collective-permute-start | bytes 3145736 | tf_op jit(solution)/shard_map/ppermute | solution.py:44
  393.5 25.2 %collective-permute-start.36 = (bf16[256,2048]{1,0:T(8,128)(2,1)}, bf16[256,2048]{1,0:T(8,128)(2,1)S(1)}, u32[]{:S(2)}, u32[]{:S(2)}) collective-permute-start(bf16[256,2048]{1,0:T(8,128)(2,1)} %reduce-scatter.5.cloned.1.call-done.refs_1_), channel_id=1, source_target_pairs={{0,1},{1,0},{2,3},{3,2},{4,5},{5,4},{6,7},{7,6},{8,9},{9,8},{10,11... | collective-permute-start | bytes 3145736 | tf_op jit(solution)/shard_map/ppermute | solution.py:44
  414.9 7.1 %collective-permute-start.38 = (bf16[256,2048]{1,0:T(8,128)(2,1)S(1)}, bf16[256,2048]{1,0:T(8,128)(2,1)S(1)}, u32[]{:S(2)}, u32[]{:S(2)}) collective-permute-start(bf16[256,2048]{1,0:T(8,128)(2,1)S(1)} %shard_map.287.refs_2_), channel_id=1, source_target_pairs={{0,8},{8,0},{16,24},{24,16},{1,9},{9,1},{17,25},{25,17},{2,10},{10... | collective-permute-start | bytes 3145736 | tf_op jit(solution)/shard_map/ppermute | solution.py:44
  429.3 24.9 %collective-permute-start.39 = (bf16[768,2048]{1,0:T(8,128)(2,1)}, bf16[768,2048]{1,0:T(8,128)(2,1)}, u32[]{:S(2)}, u32[]{:S(2)}) collective-permute-start(bf16[768,2048]{1,0:T(8,128)(2,1)} %shard_map.289.refs_2_), channel_id=1, source_target_pairs={{0,8},{8,0},{16,24},{24,16},{1,9},{9,1},{17,25},{25,17},{2,10},{10... | collective-permute-start | bytes 9437192 | tf_op jit(solution)/shard_map/ppermute | solution.py:44
  429.3 21.8 %collective-permute-start.35 = (bf16[512,1024]{1,0:T(8,128)(2,1)}, bf16[512,1024]{1,0:T(8,128)(2,1)}, u32[]{:S(2)}, u32[]{:S(2)}) collective-permute-start(bf16[512,1024]{1,0:T(8,128)(2,1)} %get-tuple-element.234), channel_id=1, source_target_pairs={{0,8},{8,0},{16,24},{24,16},{1,9},{9,1},{17,25},{25,17},{2,10},{10... | collective-permute-start | bytes 3145736 | tf_op jit(solution)/shard_map/ppermute | solution.py:44
  430.9 23.3 %collective-permute-start.41 = (bf16[128,2048]{1,0:T(8,128)(2,1)}, bf16[128,2048]{1,0:T(8,128)(2,1)}, u32[]{:S(2)}, u32[]{:S(2)}) collective-permute-start(bf16[128,2048]{1,0:T(8,128)(2,1)} %get-tuple-element.277), channel_id=1, source_target_pairs={{0,16},{8,24},{16,0},{24,8},{1,17},{9,25},{17,1},{25,9},{2,18},{10... | collective-permute-start | bytes 1572872 | tf_op jit(solution)/shard_map/ppermute | solution.py:44
  431.6 22.6 %collective-permute-start.40 = (bf16[128,2048]{1,0:T(8,128)(2,1)}, bf16[128,2048]{1,0:T(8,128)(2,1)}, u32[]{:S(2)}, u32[]{:S(2)}) collective-permute-start(bf16[128,2048]{1,0:T(8,128)(2,1)} %get-tuple-element.278), channel_id=1, source_target_pairs={{0,1},{1,0},{2,3},{3,2},{4,5},{5,4},{6,7},{7,6},{8,9},{9,8},{10,11... | collective-permute-start | bytes 1572872 | tf_op jit(solution)/shard_map/ppermute | solution.py:44
  458.6 16.8 %collective-permute-start.42 = (bf16[1536,1024]{1,0:T(8,128)(2,1)}, bf16[1536,1024]{1,0:T(8,128)(2,1)}, u32[]{:S(2)}, u32[]{:S(2)}) collective-permute-start(bf16[1536,1024]{1,0:T(8,128)(2,1)} %get-tuple-element.246), channel_id=1, source_target_pairs={{0,8},{8,0},{16,24},{24,16},{1,9},{9,1},{17,25},{25,17},{2,10},{10... | collective-permute-start | bytes 9437192 | tf_op jit(solution)/shard_map/ppermute | solution.py:44
  460.1 14.3 %collective-permute-start.44 = (bf16[256,1024]{1,0:T(8,128)(2,1)S(1)}, bf16[256,1024]{1,0:T(8,128)(2,1)S(1)}, u32[]{:S(2)}, u32[]{:S(2)}) collective-permute-start(bf16[256,1024]{1,0:T(8,128)(2,1)S(1)} %get-tuple-element.275), channel_id=1, source_target_pairs={{0,16},{8,24},{16,0},{24,8},{1,17},{9,25},{17,1},{25,9},{2,18},{10... | collective-permute-start | bytes 1572872 | tf_op jit(solution)/shard_map/ppermute | solution.py:44
  461.5 13.9 %collective-permute-start.43 = (bf16[256,1024]{1,0:T(8,128)(2,1)S(1)}, bf16[256,1024]{1,0:T(8,128)(2,1)S(1)}, u32[]{:S(2)}, u32[]{:S(2)}) collective-permute-start(bf16[256,1024]{1,0:T(8,128)(2,1)S(1)} %get-tuple-element.276), channel_id=1, source_target_pairs={{0,1},{1,0},{2,3},{3,2},{4,5},{5,4},{6,7},{7,6},{8,9},{9,8},{10,11... | collective-permute-start | bytes 1572872 | tf_op jit(solution)/shard_map/ppermute | solution.py:44
  479.5 38.2 %collective-permute-start.45 = (bf16[768,2048]{1,0:T(8,128)(2,1)}, bf16[768,2048]{1,0:T(8,128)(2,1)}, u32[]{:S(2)}, u32[]{:S(2)}) collective-permute-start(bf16[768,2048]{1,0:T(8,128)(2,1)} %shard_map.284.refs_2_), channel_id=1, source_target_pairs={{0,8},{8,0},{16,24},{24,16},{1,9},{9,1},{17,25},{25,17},{2,10},{10... | collective-permute-start | bytes 9437192 | tf_op jit(solution)/shard_map/ppermute | solution.py:44
  479.5 43.9 %collective-permute-start.58 = (bf16[512,1024]{1,0:T(8,128)(2,1)}, bf16[512,1024]{1,0:T(8,128)(2,1)}, u32[]{:S(2)}, u32[]{:S(2)}) collective-permute-start(bf16[512,1024]{1,0:T(8,128)(2,1)} %copy-done.22), channel_id=1, source_target_pairs={{0,1},{1,0},{2,3},{3,2},{4,5},{5,4},{6,7},{7,6},{8,9},{9,8},{10,11... | collective-permute-start | bytes 3145736 | tf_op jit(solution)/shard_map/ppermute | solution.py:44
  480.2 44.0 %collective-permute-start.57 = (bf16[512,1024]{1,0:T(8,128)(2,1)}, bf16[512,1024]{1,0:T(8,128)(2,1)}, u32[]{:S(2)}, u32[]{:S(2)}) collective-permute-start(bf16[512,1024]{1,0:T(8,128)(2,1)} %copy-done.43), channel_id=1, source_target_pairs={{0,16},{8,24},{16,0},{24,8},{1,17},{9,25},{17,1},{25,9},{2,18},{10... | collective-permute-start | bytes 3145736 | tf_op jit(solution)/shard_map/ppermute | solution.py:44
  480.8 36.9 %all-to-all-start.4 = ((bf16[4,128,1024]{2,1,0:T(8,128)(2,1)}), bf16[4,128,1024]{2,1,0:T(8,128)(2,1)}, u32[]{:S(2)}, u32[]{:S(2)}) async-start(bf16[4,128,1024]{2,1,0:T(8,128)(2,1)} %bitcast.96), calls=%async_computation.6 | async-start | bytes 2097152 | tf_op jit(solution)/shard_map/all_to_all | solution.py:125
  485.3 48.5 %collective-permute-start.47 = (bf16[256,2048]{1,0:T(8,128)(2,1)}, bf16[256,2048]{1,0:T(8,128)(2,1)}, u32[]{:S(2)}, u32[]{:S(2)}) collective-permute-start(bf16[256,2048]{1,0:T(8,128)(2,1)} %copy-done.42), channel_id=1, source_target_pairs={{0,1},{1,0},{2,3},{3,2},{4,5},{5,4},{6,7},{7,6},{8,9},{9,8},{10,11... | collective-permute-start | bytes 3145736 | tf_op jit(solution)/shard_map/ppermute | solution.py:44
  486.8 53.4 %collective-permute-start.46 = (bf16[256,2048]{1,0:T(8,128)(2,1)}, bf16[256,2048]{1,0:T(8,128)(2,1)}, u32[]{:S(2)}, u32[]{:S(2)}) collective-permute-start(bf16[256,2048]{1,0:T(8,128)(2,1)} %copy-done.41), channel_id=1, source_target_pairs={{0,16},{8,24},{16,0},{24,8},{1,17},{9,25},{17,1},{25,9},{2,18},{10... | collective-permute-start | bytes 3145736 | tf_op jit(solution)/shard_map/ppermute | solution.py:44
  517.7 53.9 %collective-permute-start.50 = (bf16[4,128,1024]{2,1,0:T(8,128)(2,1)}, bf16[4,128,1024]{2,1,0:T(8,128)(2,1)}, u32[]{:S(2)}, u32[]{:S(2)}) collective-permute-start(bf16[4,128,1024]{2,1,0:T(8,128)(2,1)} %all-to-all-done.4.refs_1_), channel_id=1, source_target_pairs={{0,1},{1,0},{2,3},{3,2},{4,5},{5,4},{6,7},{7,6},{8,9},{9,8},{10,11... | collective-permute-start | bytes 3145736 | tf_op jit(solution)/shard_map/ppermute | solution.py:44
  523.5 48.2 %collective-permute-start.48 = (bf16[256,2048]{1,0:T(8,128)(2,1)}, bf16[256,2048]{1,0:T(8,128)(2,1)S(1)}, u32[]{:S(2)}, u32[]{:S(2)}) collective-permute-start(bf16[256,2048]{1,0:T(8,128)(2,1)} %get-tuple-element.259), channel_id=1, source_target_pairs={{0,16},{8,24},{16,0},{24,8},{1,17},{9,25},{17,1},{25,9},{2,18},{10... | collective-permute-start | bytes 3145736 | tf_op jit(solution)/shard_map/ppermute | solution.py:44
  524.2 48.9 %collective-permute-start.49 = (bf16[256,2048]{1,0:T(8,128)(2,1)}, bf16[256,2048]{1,0:T(8,128)(2,1)S(1)}, u32[]{:S(2)}, u32[]{:S(2)}) collective-permute-start(bf16[256,2048]{1,0:T(8,128)(2,1)} %get-tuple-element.260), channel_id=1, source_target_pairs={{0,1},{1,0},{2,3},{3,2},{4,5},{5,4},{6,7},{7,6},{8,9},{9,8},{10,11... | collective-permute-start | bytes 3145736 | tf_op jit(solution)/shard_map/ppermute | solution.py:44
  524.9 45.4 %all-to-all-start.5 = ((bf16[4,128,768]{2,1,0:T(8,128)(2,1)}), bf16[4,128,768]{2,1,0:T(8,128)(2,1)S(1)}, u32[]{:S(2)}, u32[]{:S(2)}) async-start(bf16[4,128,768]{2,1,0:T(8,128)(2,1)} %bitcast.98), calls=%async_computation.8 | async-start | bytes 1572864 | tf_op jit(solution)/shard_map/all_to_all | solution.py:125
  528.4 57.3 %reduce-scatter.11.cloned.1.call-start = ((), (), s32[]{:S(2)}) async-start(), calls=%async_computation.17 | async-start | bytes 1310720 | tf_op jit(solution)/shard_map/reduce_scatter | solution.py:121
  570.3 37.5 %collective-permute-start.56 = (bf16[4,128,768]{2,1,0:T(8,128)(2,1)S(1)}, bf16[4,128,768]{2,1,0:T(8,128)(2,1)}, u32[]{:S(2)}, u32[]{:S(2)}) collective-permute-start(bf16[4,128,768]{2,1,0:T(8,128)(2,1)S(1)} %all-to-all-done.5.refs_1_), channel_id=1, source_target_pairs={{0,1},{1,0},{2,3},{3,2},{4,5},{5,4},{6,7},{7,6},{8,9},{9,8},{10,11... | collective-permute-start | bytes 2359304 | tf_op jit(solution)/shard_map/ppermute | solution.py:44
  578.9 6.6 %collective-permute-start.52 = (f32[16,1536]{1,0:T(8,128)S(1)}, f32[16,1536]{1,0:T(8,128)S(1)}, u32[]{:S(2)}, u32[]{:S(2)}) collective-permute-start(f32[16,1536]{1,0:T(8,128)S(1)} %add.129), channel_id=1, source_target_pairs={{0,4},{2,6},{4,0},{6,2},{1,5},{3,7},{5,1},{7,3},{8,12},{10,14},{12... | collective-permute-start | bytes 294920 | tf_op jit(solution)/shard_map/ppermute | solution.py:44
  585.7 11.0 %collective-permute-start.59 = (bf16[1,128,1024]{2,1,0:T(8,128)(2,1)}, bf16[1,128,1024]{2,1,0:T(8,128)(2,1)S(1)}, u32[]{:S(2)}, u32[]{:S(2)}) collective-permute-start(bf16[1,128,1024]{2,1,0:T(8,128)(2,1)} %bitcast.100), channel_id=1, source_target_pairs={{0,1},{1,0},{2,3},{3,2},{4,5},{5,4},{6,7},{7,6},{8,9},{9,8},{10,11... | collective-permute-start | bytes 786440 | tf_op jit(solution)/shard_map/ppermute | solution.py:44
  591.9 19.2 %collective-permute-start.55 = (f32[16,1536]{1,0:T(8,128)S(1)}, f32[16,1536]{1,0:T(8,128)S(1)}, u32[]{:S(2)}, u32[]{:S(2)}) collective-permute-start(f32[16,1536]{1,0:T(8,128)S(1)} %add.132), channel_id=1, source_target_pairs={{0,1},{1,0},{2,3},{3,2},{4,5},{5,4},{6,7},{7,6},{8,9},{9,8},{10,11... | collective-permute-start | bytes 294920 | tf_op jit(solution)/shard_map/ppermute | solution.py:44
  (71 other events, 552.4 us)
Sparse Core Ops, SparseCore 0:
  14.2 28.1 all-gather.4
  44.5 62.9 all-gather.6
  109.7 79.3 all-gather.8
  190.6 79.2 all-gather.10
  283.9 74.8 reduce-scatter.4
  372.6 74.7 reduce-scatter.6
  458.8 58.4 reduce-scatter.8
  532.7 26.6 reduce-scatter.10

commit v6 on v4

--- a/solution.py
+++ b/solution.py
@@ -145,7 +145,7 @@
 
 
 def row_loop(n):
-    step = 64 if n % 64 == 0 else n
+    step = 128 if n % 128 == 0 else n
     return pl.loop(0, n, step=step), step
 
 

time: 635 us -> 635 us (level)
  transfers between devices with their start and end apart: 73 -> 73, of which waited for: 28 -> 29; matrix products, arithmetic and copies ran while one was open for 9% -> 9% of each run, Pallas kernels for 38% -> 37%
where the time goes in v6:
time: 635 us; the launch traced here: 629 us
  Pallas kernels  240 us (38%)
  waiting for transfers between devices  193 us (30%)
  local copies, waits for them, and re-layouts  80.3 us (13%)
  starting transfers between devices  69.3 us (11%)
  blocking collectives  18.4 us (3%)
  between operations  15.6 us (2%)
  other arithmetic  11.2 us (2%)
    ppermute x60, waiting for transfers between devices, flip(): lax.ppermute(v, axis, [(i, i ^ bit) for i in range(lax.axis_size(axis))])  146 us
    pallas_call x13, Pallas kernels, small_call(): pl.pallas_call(ordered(kernel, len(operands), deps), grid=(1,), in_specs=...  85.2 us
    unnamed x153, local copies, waits for them, and re-layouts  55.2 us
    pallas_call x12, Pallas kernels, product(): pl.pallas_call(ordered(lambda *refs: product_kernel(dims, *refs), 2 + len...  51.4 us
    ppermute x60, starting transfers between devices, flip(): lax.ppermute(v, axis, [(i, i ^ bit) for i in range(lax.axis_size(axis))])  49.1 us
    all_to_all x4, waiting for transfers between devices, seq_exchange(): return lax.all_to_all(v, 'seq', 0, 0, tiled=True)  47 us
    pallas_call x3, Pallas kernels, tall_product(): pl.pallas_call(ordered(tall_kernel, 2 * len(lefts), deps), grid=(deep //...  38.8 us
    pallas_call x4, Pallas kernels, down_product(): pl.pallas_call(ordered(down_kernel, 4, deps), grid=(tokens // tile,), in_...  35.7 us
  transfers between devices with their start and end apart: 73, of which 29 were waited for; matrix products, arithmetic and copies ran while one was open for 9% of the time, Pallas kernels for 37%

profile of v6, /device:TPU:0, one launch (start us, length us, event | category | flops | bytes accessed | tf_op | source)
XLA Modules:
  0.0 628.5 jit_solution(5389487727330809031)
XLA Ops:
  11.0 3.0 collective-permute-start
  16.5 2.7 collective-permute-start.1
  20.1 3.5 all-to-all-start
  23.7 3.7 copy.40
  29.0 6.2 all-to-all-done
  36.9 3.5 collective-permute-done.3
  41.0 3.0 shard_map.263
  45.9 3.5 all-to-all-start.1
  49.4 2.9 fusion
  52.3 28.4 %all-to-all-done.1 = bf16[4,128,1024]{1,2,0:T(8,128)(2,1)S(1)} async-done(((bf16[4,128,1024]{1,2,0:T(8,128)(2,1)}), bf16[4,128,1024]{1,2,0:T(8,128)(2,1)S(1)}, u32[]{:S(2)}, u32[]{:S(2)}) %all-to-all-start.1) | async-done | bytes 1048608 | tf_op jit(solution)/shard_map/all_to_all | solution.py:125
  87.7 13.0 %collective-permute-done.7 = bf16[128,2048]{1,0:T(8,128)(2,1)S(1)} collective-permute-done((bf16[128,2048]{1,0:T(8,128)(2,1)S(1)}, bf16[128,2048]{1,0:T(8,128)(2,1)S(1)}, u32[]{:S(2)}, u32[]{:S(2)}) %collective-permute-start.7) | collective-permute-done | bytes 524320 | tf_op jit(solution)/shard_map/ppermute | solution.py:44
  102.7 2.7 collective-permute-done.9.refs_0_.refs_3_
  115.4 5.2 shard_map.264.refs_1_
  121.7 5.4 shard_map.265.refs_2_
  128.1 2.8 collective-permute-done.11
  136.1 11.3 %shard_map.268 = bf16[8,256,256]{2,1,0:T(8,128)(2,1)} custom-call(s32[2]{0:T(128)} %pad_add_fusion.refs_0_, bf16[768,768]{1,0:T(8,128)(2,1)} %copy-done.13, bf16[768,768]{1,0:T(8,128)(2,1)} %copy-done.14, bf16[256,768]{1,0:T(8,128)(2,1)} %copy-done.29, bf16[256,768]{1,0:T(8,128)(2,1)} %copy-done.30), custom_call_target="tpu_custom_call" | custom-call | flops 1 | bytes 1 | tf_op jit(solution)/shard_map/pallas_call | solution.py:528
  152.1 18.4 %all_to_all.30.refs_1_ = bf16[8,256,256]{2,1,0:T(8,128)(2,1)} all-to-all(bf16[8,256,256]{2,1,0:T(8,128)(2,1)S(1)} %copy-done.52), channel_id=1, replica_groups=mesh['seq'=4,'shard'=4,'replica'=2] {'seq','replica'}, dimensions={0} | all-to-all | bytes 2097152 | tf_op jit(solution)/shard_map/all_to_all | solution.py:636
  174.8 9.0 %shard_map.269 = (f32[256,2048]{1,0:T(8,128)}, bf16[256,2048]{1,0:T(8,128)(2,1)}, bf16[256,2048]{1,0:T(8,128)(2,1)}) custom-call(s32[2]{0:T(128)} %pad_add_fusion.refs_0_, bf16[8,256,256]{2,1,0:T(8,128)(2,1)} %all_to_all.30.refs_1_, bf16[1536,1024]{1,0:T(8,128)(2,1)} %copy-done.47, bf16[1536,1024]{1,0:T(8,128)(2,1)} %copy-done.49, ...), custom_call_target="tpu_custom_call" | custom-call | flops 1 | bytes 1 | tf_op jit(solution)/shard_map/pallas_call | solution.py:528
  186.3 10.5 %collective-permute-done.19 = bf16[256,2048]{1,0:T(8,128)(2,1)} collective-permute-done((bf16[256,2048]{1,0:T(8,128)(2,1)}, bf16[256,2048]{1,0:T(8,128)(2,1)}, u32[]{:S(2)}, u32[]{:S(2)}) %collective-permute-start.19) | collective-permute-done | bytes 1048608 | tf_op jit(solution)/shard_map/ppermute | solution.py:44
  198.0 20.5 %collective-permute-done.17 = bf16[256,2048]{1,0:T(8,128)(2,1)S(1)} collective-permute-done((bf16[256,2048]{1,0:T(8,128)(2,1)}, bf16[256,2048]{1,0:T(8,128)(2,1)S(1)}, u32[]{:S(2)}, u32[]{:S(2)}) %collective-permute-start.17) | collective-permute-done | bytes 1048608 | tf_op jit(solution)/shard_map/ppermute | solution.py:44
  226.1 7.5 %shard_map.270 = (bf16[768,1024]{1,0:T(8,128)(2,1)S(1)}, f32[768,1024]{1,0:T(8,128)S(1)}) custom-call(bf16[768,2048]{1,0:T(8,128)(2,1)} %constant_dynamic-update-slice_fusion.10.h_ref.refs_0_, bf16[2048,1024]{1,0:T(8,128)(2,1)} %all-gather.9.cloned.1.call-done.w_ref.refs_3_, f32[1,1024]{1,0:T(1,128)S(1)} %bitcast.83), custom_call_target="tpu_custom_call" | custom-call | flops 1 | bytes 1 | tf_op jit(solution)/shard_map/pallas_call | solution.py:339
  247.2 3.8 shard_map.272
  251.1 4.7 shard_map.273
  255.9 7.6 %shard_map.271 = (bf16[768,1024]{1,0:T(8,128)(2,1)S(1)}, f32[768,1024]{1,0:T(8,128)S(1)}) custom-call(bf16[768,2048]{1,0:T(8,128)(2,1)} %collective-permute-done.23.h_ref.refs_1_, bf16[2048,1024]{1,0:T(8,128)(2,1)} %all-gather.9.cloned.1.call-done.w_ref.refs_3_, f32[1,1024]{1,0:T(1,128)S(1)} %bitcast.86), custom_call_target="tpu_custom_call" | custom-call | flops 1 | bytes 1 | tf_op jit(solution)/shard_map/pallas_call | solution.py:339
  266.4 2.7 collective-permute-done.27.refs_7_.refs_0_
  269.0 13.7 %shard_map.274.refs_4_ = bf16[1024,2048]{1,0:T(8,128)(2,1)} custom-call(bf16[768,1024]{1,0:T(8,128)(2,1)S(1)} %get-tuple-element.195.refs_0_, bf16[768,1024]{1,0:T(8,128)(2,1)} %copy-done.19, bf16[256,1024]{1,0:T(8,128)(2,1)S(1)} %get-tuple-element.197.refs_2_.refs_0_, bf16[256,1024]{1,0:T(8,128)(2,1)S(1)} %get-tuple-element.198.refs_3_.refs_0_, ...), custom_call_target="tpu_custom_call" | custom-call | flops 1 | bytes 1 | tf_op jit(solution)/shard_map/pallas_call | solution.py:316
  283.0 5.9 shard_map.275
  289.2 5.8 shard_map.276
  295.4 11.6 %shard_map.277 = (bf16[768,1024]{1,0:T(8,128)(2,1)S(1)}, bf16[768,2048]{1,0:T(8,128)(2,1)S(1)}, f32[8,1024]{1,0:T(8,128)S(1)}) custom-call(bf16[768,2048]{1,0:T(8,128)(2,1)} %collective-permute-done.22.refs_5_.refs_0_, bf16[1024,2048]{1,0:T(8,128)(2,1)} %all-gather.11.cloned.1.call-done.refs_1_, f32[768,1024]{1,0:T(8,128)} %copy-done.32, ...), custom_call_target="tpu_custom_call" | custom-call | flops 1 | bytes 1 | tf_op jit(solution)/shard_map/pallas_call | solution.py:399
  309.9 12.4 %shard_map.278 = (bf16[768,1024]{1,0:T(8,128)(2,1)S(1)}, bf16[768,2048]{1,0:T(8,128)(2,1)}, f32[8,1024]{1,0:T(8,128)S(1)}) custom-call(bf16[768,2048]{1,0:T(8,128)(2,1)} %copy-done.48, bf16[1024,2048]{1,0:T(8,128)(2,1)} %all-gather.11.cloned.1.call-done.refs_1_, f32[768,1024]{1,0:T(8,128)} %copy-done.31, ...), custom_call_target="tpu_custom_call" | custom-call | flops 1 | bytes 1 | tf_op jit(solution)/shard_map/pallas_call | solution.py:399
  322.3 3.0 copy-done.10
  326.8 3.6 shard_map.280.refs_3_
  332.9 3.5 shard_map.281.refs_8_
  336.4 13.2 %shard_map.282.refs_13_ = bf16[2048,1024]{1,0:T(8,128)(2,1)} custom-call(bf16[768,2048]{1,0:T(8,128)(2,1)} %constant_dynamic-update-slice_fusion.10.h_ref.refs_0_, bf16[768,2048]{1,0:T(8,128)(2,1)} %collective-permute-done.23.h_ref.refs_1_, bf16[256,2048]{1,0:T(8,128)(2,1)S(1)} %copy-done.16, bf16[256,2048]{1,0:T(8,128)(2,1)S(1)} %copy-done.28, ...), custom_call_target="tpu_custom_call" | custom-call | flops 1 | bytes 1 | tf_op jit(solution)/shard_map/pallas_call | solution.py:316
  352.2 4.0 collective-permute-done.32.refs_3_
  357.2 12.5 %shard_map.283 = (f32[256,2048]{1,0:T(8,128)}, bf16[256,2048]{1,0:T(8,128)(2,1)}, bf16[8,256,256]{2,1,0:T(8,128)(2,1)}, f32[8,2048]{1,0:T(8,128)}) custom-call(s32[2]{0:T(128)} %pad_add_fusion.refs_0_, bf16[768,2048]{1,0:T(8,128)(2,1)} %get-tuple-element.203.refs_0_.refs_2_.refs_1_, bf16[768,2048]{1,0:T(8,128)(2,1)} %copy-done.9, ...), custom_call_target="tpu_custom_call" | custom-call | flops 1 | bytes 1 | tf_op jit(solution)/shard_map/pallas_call | solution.py:528
  369.7 4.4 all-to-all-start.3
  376.0 7.1 %shard_map.285.refs_0_.refs_2_ = bf16[768,2048]{1,0:T(8,128)(2,1)} custom-call(bf16[768,1024]{1,0:T(8,128)(2,1)S(1)} %copy-done.18, bf16[1024,2048]{1,0:T(8,128)(2,1)} %all-gather.11.cloned.1.call-done.refs_1_, f32[256,2048]{1,0:T(8,128)S(1)} %copy-done.11), custom_call_target="tpu_custom_call" | custom-call | flops 1 | bytes 1 | tf_op jit(solution)/shard_map/pallas_call | solution.py:362
  383.1 7.0 %shard_map.284 = bf16[768,2048]{1,0:T(8,128)(2,1)} custom-call(bf16[768,1024]{1,0:T(8,128)(2,1)S(1)} %copy-done.20, bf16[1024,2048]{1,0:T(8,128)(2,1)} %all-gather.11.cloned.1.call-done.refs_1_, f32[256,2048]{1,0:T(8,128)S(1)} %copy-done.11), custom_call_target="tpu_custom_call" | custom-call | flops 1 | bytes 1 | tf_op jit(solution)/shard_map/pallas_call | solution.py:362
  393.6 17.7 %shard_map.286 = (bf16[768,768]{1,0:T(8,128)(2,1)}, bf16[768,768]{1,0:T(8,128)(2,1)}, bf16[256,768]{1,0:T(8,128)(2,1)}, bf16[256,768]{1,0:T(8,128)(2,1)}, f32[8,768]{1,0:T(8,128)}) custom-call(s32[2]{0:T(128)} %pad_add_fusion.refs_0_, bf16[768,768]{1,0:T(8,128)(2,1)} %copy-done.13, bf16[768,768]{1,0:T(8,128)(2,1)} %copy-done.14, ...), custom_call_target="tpu_custom_call" | custom-call | flops 1 | bytes 1 | tf_op jit(solution)/shard_map/pallas_call | solution.py:528
  417.6 2.9 shard_map.288.refs_5_
  426.4 6.3 %shard_map.291.refs_2_ = bf16[768,2048]{1,0:T(8,128)(2,1)} custom-call(bf16[768,768]{1,0:T(8,128)(2,1)S(1)} %copy-done.22, bf16[2048,768]{1,0:T(8,128)(2,1)} %all-gather.7.cloned.1.call-done.refs_1_, bf16[256,2048]{1,0:T(8,128)(2,1)S(1)} %add_convert_fusion.2.refs_2_, bf16[256,2048]{1,0:T(8,128)(2,1)S(1)} %get-tuple-element.221.refs_3_), custom_call_target="tpu_custom_call" | custom-call | flops 1 | bytes 1 | tf_op jit(solution)/shard_map/pallas_call | solution.py:362
  432.7 5.0 shard_map.292.refs_2_.refs_0_
  439.4 6.0 shard_map.293
  451.1 8.9 %collective-permute-done.43.refs_5_ = bf16[128,2048]{1,0:T(8,128)(2,1)S(1)} collective-permute-done((bf16[128,2048]{1,0:T(8,128)(2,1)S(1)}, bf16[128,2048]{1,0:T(8,128)(2,1)S(1)}, u32[]{:S(2)}, u32[]{:S(2)}) %collective-permute-start.43) | collective-permute-done | bytes 524320 | tf_op jit(solution)/shard_map/ppermute | solution.py:44
  460.2 3.0 copy-done.5
  464.8 11.8 %shard_map.295 = bf16[2048,768]{1,0:T(8,128)(2,1)} custom-call(bf16[768,2048]{1,0:T(8,128)(2,1)} %copy-done.12, bf16[768,2048]{1,0:T(8,128)(2,1)} %collective-permute-done.6.refs_0_.refs_1_, bf16[256,2048]{1,0:T(8,128)(2,1)} %constant_dynamic-update-slice_fusion.3.refs_0_.refs_2_, bf16[256,2048]{1,0:T(8,128)(2,1)} %collective-permute-done.9.refs_0_.refs_3_, ...), custom_call_target="tpu_custom_call" | custom-call | flops 1 | bytes 1 | tf_op jit(solution)/shard_map/pallas_call | solution.py:316
  477.8 4.5 all-to-all-start.4
  488.0 20.4 %collective-permute-done.49.refs_5_ = bf16[256,1024]{1,0:T(8,128)(2,1)S(1)} collective-permute-done((bf16[256,1024]{1,0:T(8,128)(2,1)S(1)}, bf16[256,1024]{1,0:T(8,128)(2,1)S(1)}, u32[]{:S(2)}, u32[]{:S(2)}) %collective-permute-start.49) | collective-permute-done | bytes 524320 | tf_op jit(solution)/shard_map/ppermute | solution.py:44
  508.4 2.9 shard_map.296
  515.9 7.3 %collective-permute-done.45.refs_3_ = bf16[256,2048]{1,0:T(8,128)(2,1)} collective-permute-done((bf16[256,2048]{1,0:T(8,128)(2,1)}, bf16[256,2048]{1,0:T(8,128)(2,1)}, u32[]{:S(2)}, u32[]{:S(2)}) %collective-permute-start.45) | collective-permute-done | bytes 1048608 | tf_op jit(solution)/shard_map/ppermute | solution.py:44
  523.3 7.7 %collective-permute-done.44.refs_2_ = bf16[256,2048]{1,0:T(8,128)(2,1)} collective-permute-done((bf16[256,2048]{1,0:T(8,128)(2,1)}, bf16[256,2048]{1,0:T(8,128)(2,1)}, u32[]{:S(2)}, u32[]{:S(2)}) %collective-permute-start.44) | collective-permute-done | bytes 1048608 | tf_op jit(solution)/shard_map/ppermute | solution.py:44
  532.4 6.7 %shard_map.297 = (f32[256,2048]{1,0:T(8,128)}, f32[8,2048]{1,0:T(8,128)}) custom-call(bf16[768,2048]{1,0:T(8,128)(2,1)} %copy-done.2, bf16[768,2048]{1,0:T(8,128)(2,1)} %copy-done.8, bf16[256,2048]{1,0:T(8,128)(2,1)} %collective-permute-done.44.refs_2_, bf16[256,2048]{1,0:T(8,128)(2,1)} %collective-permute-done.45.refs_3_, bf16[256,2048]{1,0:T(8,128)(2,1)} %bitcast.89, ...), custom_call_target="tpu_custom_call" | custom-call | flops 1 | bytes 1 | tf_op jit(solution)/shard_map/pallas_call | solution.py:528
  539.1 14.3 %collective-permute-done.56 = bf16[512,1024]{1,0:T(8,128)(2,1)} collective-permute-done((bf16[512,1024]{1,0:T(8,128)(2,1)}, bf16[512,1024]{1,0:T(8,128)(2,1)}, u32[]{:S(2)}, u32[]{:S(2)}) %collective-permute-start.56) | collective-permute-done | bytes 1048608 | tf_op jit(solution)/shard_map/ppermute | solution.py:44
  553.4 3.7 add_convert_fusion
  558.2 3.5 all-to-all-start.5
  563.3 8.0 %collective-permute-done.50 = f32[16,1536]{1,0:T(8,128)S(1)} collective-permute-done((f32[16,1536]{1,0:T(8,128)S(1)}, f32[16,1536]{1,0:T(8,128)S(1)}, u32[]{:S(2)}, u32[]{:S(2)}) %collective-permute-start.50) | collective-permute-done | bytes 98336 | tf_op jit(solution)/shard_map/ppermute | solution.py:44
  571.4 12.4 %all-to-all-done.5.refs_1_ = bf16[4,128,768]{2,1,0:T(8,128)(2,1)S(1)} async-done(((bf16[4,128,768]{2,1,0:T(8,128)(2,1)}), bf16[4,128,768]{2,1,0:T(8,128)(2,1)S(1)}, u32[]{:S(2)}, u32[]{:S(2)}) %all-to-all-start.5) | async-done | bytes 786464 | tf_op jit(solution)/shard_map/all_to_all | solution.py:125
  588.9 3.1 collective-permute-done.53
  593.5 3.8 shard_map.301
  597.4 4.5 shard_map.290
  602.5 7.0 %collective-permute-done.54 = f32[16,1536]{1,0:T(8,128)S(1)} collective-permute-done((f32[16,1536]{1,0:T(8,128)S(1)}, f32[16,1536]{1,0:T(8,128)S(1)}, u32[]{:S(2)}, u32[]{:S(2)}) %collective-permute-start.54) | collective-permute-done | bytes 98336 | tf_op jit(solution)/shard_map/ppermute | solution.py:44
  610.7 3.9 shard_map.300
  618.2 3.3 shard_map.298
  (350 shorter events, 140.9 us)
Async XLA Ops:
  7.2 95.5 %all-gather.5.cloned.1.call-start = ((), (), s32[]{:S(2)}) async-start(), calls=%async_computation.10 | async-start | bytes 1310720 | tf_op jit(solution)/shard_map/all_gather | solution.py:117
  16.5 11.0 %collective-permute-start.1 = (bf16[2,1536]{1,0:T(2,128)(2,1)S(1)}, bf16[2,1536]{1,0:T(2,128)(2,1)S(1)}, u32[]{:S(2)}, u32[]{:S(2)}) collective-permute-start(bf16[2,1536]{1,0:T(2,128)(2,1)S(1)} %pad_maximum_fusion.2), channel_id=1, source_target_pairs={{0,4},{2,6},{4,0},{6,2},{1,5},{3,7},{5,1},{7,3},{8,12},{10,14},{12... | collective-permute-start | bytes 18440 | tf_op jit(solution)/shard_map/ppermute | solution.py:44
  20.1 15.2 %all-to-all-start = ((bf16[4,128,768]{1,2,0:T(8,128)(2,1)}), bf16[4,128,768]{1,2,0:T(8,128)(2,1)S(1)}, u32[]{:S(2)}, u32[]{:S(2)}) async-start(bf16[4,128,768]{1,2,0:T(8,128)(2,1)} %bitcast.11), calls=%async_computation | async-start | bytes 1572864 | tf_op jit(solution)/shard_map/all_to_all | solution.py:125
  23.6 83.9 %all-gather.7.cloned.1.call-start = ((), (), s32[]{:S(2)}) async-start(), calls=%async_computation.11 | async-start | bytes 3932160 | tf_op jit(solution)/shard_map/all_gather | solution.py:117
  44.0 38.0 %collective-permute-start.5 = (bf16[256,2048]{1,0:T(8,128)(2,1)}, bf16[256,2048]{1,0:T(8,128)(2,1)S(1)}, u32[]{:S(2)}, u32[]{:S(2)}) collective-permute-start(bf16[256,2048]{1,0:T(8,128)(2,1)} %shard_map.263), channel_id=1, source_target_pairs={{0,1},{1,0},{2,3},{3,2},{4,5},{5,4},{6,7},{7,6},{8,9},{9,8},{10,11... | collective-permute-start | bytes 3145736 | tf_op jit(solution)/shard_map/ppermute | solution.py:44
  45.5 36.5 %collective-permute-start.4 = (bf16[256,2048]{1,0:T(8,128)(2,1)}, bf16[256,2048]{1,0:T(8,128)(2,1)S(1)}, u32[]{:S(2)}, u32[]{:S(2)}) collective-permute-start(bf16[256,2048]{1,0:T(8,128)(2,1)} %shard_map.263), channel_id=1, source_target_pairs={{0,16},{8,24},{16,0},{24,8},{1,17},{9,25},{17,1},{25,9},{2,18},{10... | collective-permute-start | bytes 3145736 | tf_op jit(solution)/shard_map/ppermute | solution.py:44
  45.9 34.9 %all-to-all-start.1 = ((bf16[4,128,1024]{1,2,0:T(8,128)(2,1)}), bf16[4,128,1024]{1,2,0:T(8,128)(2,1)S(1)}, u32[]{:S(2)}, u32[]{:S(2)}) async-start(bf16[4,128,1024]{1,2,0:T(8,128)(2,1)} %bitcast.6), calls=%async_computation.1 | async-start | bytes 2097152 | tf_op jit(solution)/shard_map/all_to_all | solution.py:125
  49.4 176.7 %all-gather.9.cloned.1.call-start = ((), (), s32[]{:S(2)}) async-start(), calls=%async_computation.12 | async-start | bytes 5242880 | tf_op jit(solution)/shard_map/all_gather | solution.py:117
  86.2 19.2 %collective-permute-start.6 = (bf16[768,2048]{1,0:T(8,128)(2,1)S(1)}, bf16[768,2048]{1,0:T(8,128)(2,1)}, u32[]{:S(2)}, u32[]{:S(2)}) collective-permute-start(bf16[768,2048]{1,0:T(8,128)(2,1)S(1)} %constant_dynamic-update-slice_fusion.refs_0_), channel_id=1, source_target_pairs={{0,8},{8,0},{16,24},{24,16},{1,9},{9,1},{17,25},{25,17},{2,10},{10... | collective-permute-start | bytes 9437192 | tf_op jit(solution)/shard_map/ppermute | solution.py:44
  86.4 14.4 %collective-permute-start.7 = (bf16[128,2048]{1,0:T(8,128)(2,1)S(1)}, bf16[128,2048]{1,0:T(8,128)(2,1)S(1)}, u32[]{:S(2)}, u32[]{:S(2)}) collective-permute-start(bf16[128,2048]{1,0:T(8,128)(2,1)S(1)} %slice.167), channel_id=1, source_target_pairs={{0,1},{1,0},{2,3},{3,2},{4,5},{5,4},{6,7},{7,6},{8,9},{9,8},{10,11... | collective-permute-start | bytes 1572872 | tf_op jit(solution)/shard_map/ppermute | solution.py:44
  87.1 14.5 %collective-permute-start.8 = (bf16[128,2048]{1,0:T(8,128)(2,1)S(1)}, bf16[128,2048]{1,0:T(8,128)(2,1)S(1)}, u32[]{:S(2)}, u32[]{:S(2)}) collective-permute-start(bf16[128,2048]{1,0:T(8,128)(2,1)S(1)} %slice.168), channel_id=1, source_target_pairs={{0,16},{8,24},{16,0},{24,8},{1,17},{9,25},{17,1},{25,9},{2,18},{10... | collective-permute-start | bytes 1572872 | tf_op jit(solution)/shard_map/ppermute | solution.py:44
  102.4 180.6 %all-gather.11.cloned.1.call-start = ((), (), s32[]{:S(2)}) async-start(), calls=%async_computation.13 | async-start | bytes 5242880 | tf_op jit(solution)/shard_map/all_gather | solution.py:117
  105.4 25.5 %collective-permute-start.11 = (bf16[512,1024]{1,0:T(8,128)(2,1)}, bf16[512,1024]{1,0:T(8,128)(2,1)}, u32[]{:S(2)}, u32[]{:S(2)}) collective-permute-start(bf16[512,1024]{1,0:T(8,128)(2,1)} %all-gather.5.cloned.1.call-done), channel_id=1, source_target_pairs={{0,1},{1,0},{2,3},{3,2},{4,5},{5,4},{6,7},{7,6},{8,9},{9,8},{10,11... | collective-permute-start | bytes 3145736 | tf_op jit(solution)/shard_map/ppermute | solution.py:44
  106.4 25.2 %collective-permute-start.10 = (bf16[512,1024]{1,0:T(8,128)(2,1)}, bf16[512,1024]{1,0:T(8,128)(2,1)}, u32[]{:S(2)}, u32[]{:S(2)}) collective-permute-start(bf16[512,1024]{1,0:T(8,128)(2,1)} %all-gather.5.cloned.1.call-done), channel_id=1, source_target_pairs={{0,16},{8,24},{16,0},{24,8},{1,17},{9,25},{17,1},{25,9},{2,18},{10... | collective-permute-start | bytes 3145736 | tf_op jit(solution)/shard_map/ppermute | solution.py:44
  133.8 13.6 %collective-permute-start.13 = (bf16[256,1024]{1,0:T(8,128)(2,1)S(1)}, bf16[256,1024]{1,0:T(8,128)(2,1)S(1)}, u32[]{:S(2)}, u32[]{:S(2)}) collective-permute-start(bf16[256,1024]{1,0:T(8,128)(2,1)S(1)} %slice.172), channel_id=1, source_target_pairs={{0,16},{8,24},{16,0},{24,8},{1,17},{9,25},{17,1},{25,9},{2,18},{10... | collective-permute-start | bytes 1572872 | tf_op jit(solution)/shard_map/ppermute | solution.py:44
  134.5 12.9 %collective-permute-start.12 = (bf16[256,1024]{1,0:T(8,128)(2,1)S(1)}, bf16[256,1024]{1,0:T(8,128)(2,1)}, u32[]{:S(2)}, u32[]{:S(2)}) collective-permute-start(bf16[256,1024]{1,0:T(8,128)(2,1)S(1)} %slice.171), channel_id=1, source_target_pairs={{0,1},{1,0},{2,3},{3,2},{4,5},{5,4},{6,7},{7,6},{8,9},{9,8},{10,11... | collective-permute-start | bytes 1572872 | tf_op jit(solution)/shard_map/ppermute | solution.py:44
  150.3 21.9 %collective-permute-start.14 = (bf16[1536,1024]{1,0:T(8,128)(2,1)S(1)}, bf16[1536,1024]{1,0:T(8,128)(2,1)S(1)}, u32[]{:S(2)}, u32[]{:S(2)}) collective-permute-start(bf16[1536,1024]{1,0:T(8,128)(2,1)S(1)} %constant_dynamic-update-slice_fusion.5.refs_2_.refs_8_), channel_id=1, source_target_pairs={{0,8},{8,0},{16,24},{24,16},{1,9},{9,1},{17,25},{25,17},{2,10},{10... | collective-permute-start | bytes 9437192 | tf_op jit(solution)/shard_map/ppermute | solution.py:44
  151.9 20.2 %collective-permute-start.15 = (bf16[512,1024]{1,0:T(8,128)(2,1)S(1)}, bf16[512,1024]{1,0:T(8,128)(2,1)S(1)}, u32[]{:S(2)}, u32[]{:S(2)}) collective-permute-start(bf16[512,1024]{1,0:T(8,128)(2,1)S(1)} %constant_dynamic-update-slice_fusion.8.refs_4_.refs_10_), channel_id=1, source_target_pairs={{0,8},{8,0},{16,24},{24,16},{1,9},{9,1},{17,25},{25,17},{2,10},{10... | collective-permute-start | bytes 3145736 | tf_op jit(solution)/shard_map/ppermute | solution.py:44
  170.5 26.3 %collective-permute-start.19 = (bf16[256,2048]{1,0:T(8,128)(2,1)}, bf16[256,2048]{1,0:T(8,128)(2,1)}, u32[]{:S(2)}, u32[]{:S(2)}) collective-permute-start(bf16[256,2048]{1,0:T(8,128)(2,1)} %bitcast.32.refs_6_), channel_id=1, source_target_pairs={{0,1},{1,0},{2,3},{3,2},{4,5},{5,4},{6,7},{7,6},{8,9},{9,8},{10,11... | collective-permute-start | bytes 3145736 | tf_op jit(solution)/shard_map/ppermute | solution.py:44
  171.6 26.4 %collective-permute-start.18 = (bf16[256,2048]{1,0:T(8,128)(2,1)}, bf16[256,2048]{1,0:T(8,128)(2,1)}, u32[]{:S(2)}, u32[]{:S(2)}) collective-permute-start(bf16[256,2048]{1,0:T(8,128)(2,1)} %bitcast.32.refs_6_), channel_id=1, source_target_pairs={{0,16},{8,24},{16,0},{24,8},{1,17},{9,25},{17,1},{25,9},{2,18},{10... | collective-permute-start | bytes 3145736 | tf_op jit(solution)/shard_map/ppermute | solution.py:44
  183.8 34.7 %collective-permute-start.17 = (bf16[256,2048]{1,0:T(8,128)(2,1)}, bf16[256,2048]{1,0:T(8,128)(2,1)S(1)}, u32[]{:S(2)}, u32[]{:S(2)}) collective-permute-start(bf16[256,2048]{1,0:T(8,128)(2,1)} %get-tuple-element.168), channel_id=1, source_target_pairs={{0,1},{1,0},{2,3},{3,2},{4,5},{5,4},{6,7},{7,6},{8,9},{9,8},{10,11... | collective-permute-start | bytes 3145736 | tf_op jit(solution)/shard_map/ppermute | solution.py:44
  184.7 34.1 %collective-permute-start.16 = (bf16[256,2048]{1,0:T(8,128)(2,1)}, bf16[256,2048]{1,0:T(8,128)(2,1)S(1)}, u32[]{:S(2)}, u32[]{:S(2)}) collective-permute-start(bf16[256,2048]{1,0:T(8,128)(2,1)} %get-tuple-element.168), channel_id=1, source_target_pairs={{0,16},{8,24},{16,0},{24,8},{1,17},{9,25},{17,1},{25,9},{2,18},{10... | collective-permute-start | bytes 3145736 | tf_op jit(solution)/shard_map/ppermute | solution.py:44
  186.2 203.9 %reduce-scatter.5.cloned.1.call-start = ((), (), s32[]{:S(2)}) async-start(), calls=%async_computation.14 | async-start | bytes 5242880 | tf_op jit(solution)/shard_map/reduce_scatter | solution.py:121
  220.5 14.7 %collective-permute-start.21 = (bf16[128,2048]{1,0:T(8,128)(2,1)}, bf16[128,2048]{1,0:T(8,128)(2,1)}, u32[]{:S(2)}, u32[]{:S(2)}) collective-permute-start(bf16[128,2048]{1,0:T(8,128)(2,1)} %slice.178), channel_id=1, source_target_pairs={{0,16},{8,24},{16,0},{24,8},{1,17},{9,25},{17,1},{25,9},{2,18},{10... | collective-permute-start | bytes 1572872 | tf_op jit(solution)/shard_map/ppermute | solution.py:44
  221.2 14.0 %collective-permute-start.20 = (bf16[128,2048]{1,0:T(8,128)(2,1)}, bf16[128,2048]{1,0:T(8,128)(2,1)}, u32[]{:S(2)}, u32[]{:S(2)}) collective-permute-start(bf16[128,2048]{1,0:T(8,128)(2,1)} %slice.177), channel_id=1, source_target_pairs={{0,1},{1,0},{2,3},{3,2},{4,5},{5,4},{6,7},{7,6},{8,9},{9,8},{10,11... | collective-permute-start | bytes 1572872 | tf_op jit(solution)/shard_map/ppermute | solution.py:44
  226.0 29.9 %collective-permute-start.23 = (bf16[768,2048]{1,0:T(8,128)(2,1)}, bf16[768,2048]{1,0:T(8,128)(2,1)}, u32[]{:S(2)}, u32[]{:S(2)}) collective-permute-start(bf16[768,2048]{1,0:T(8,128)(2,1)} %constant_dynamic-update-slice_fusion.10.h_ref.refs_0_), channel_id=1, source_target_pairs={{0,8},{8,0},{16,24},{24,16},{1,9},{9,1},{17,25},{25,17},{2,10},{10... | collective-permute-start | bytes 9437192 | tf_op jit(solution)/shard_map/ppermute | solution.py:44
  242.2 24.2 %collective-permute-start.22 = (bf16[768,2048]{1,0:T(8,128)(2,1)S(1)}, bf16[768,2048]{1,0:T(8,128)(2,1)}, u32[]{:S(2)}, u32[]{:S(2)}) collective-permute-start(bf16[768,2048]{1,0:T(8,128)(2,1)S(1)} %constant_dynamic-update-slice_fusion.15.refs_4_.refs_0_), channel_id=1, source_target_pairs={{0,8},{8,0},{16,24},{24,16},{1,9},{9,1},{17,25},{25,17},{2,10},{10... | collective-permute-start | bytes 9437192 | tf_op jit(solution)/shard_map/ppermute | solution.py:44
  242.7 8.4 %collective-permute-start.24 = (bf16[256,2048]{1,0:T(8,128)(2,1)S(1)}, bf16[256,2048]{1,0:T(8,128)(2,1)S(1)}, u32[]{:S(2)}, u32[]{:S(2)}) collective-permute-start(bf16[256,2048]{1,0:T(8,128)(2,1)S(1)} %constant_dynamic-update-slice_fusion.13.h_ref.refs_2_), channel_id=1, source_target_pairs={{0,8},{8,0},{16,24},{24,16},{1,9},{9,1},{17,25},{25,17},{2,10},{10... | collective-permute-start | bytes 3145736 | tf_op jit(solution)/shard_map/ppermute | solution.py:44
  245.4 19.8 %collective-permute-start.26 = (bf16[128,2048]{1,0:T(8,128)(2,1)S(1)}, bf16[128,2048]{1,0:T(8,128)(2,1)S(1)}, u32[]{:S(2)}, u32[]{:S(2)}) collective-permute-start(bf16[128,2048]{1,0:T(8,128)(2,1)S(1)} %slice.180), channel_id=1, source_target_pairs={{0,16},{8,24},{16,0},{24,8},{1,17},{9,25},{17,1},{25,9},{2,18},{10... | collective-permute-start | bytes 1572872 | tf_op jit(solution)/shard_map/ppermute | solution.py:44
  246.6 18.6 %collective-permute-start.25 = (bf16[128,2048]{1,0:T(8,128)(2,1)S(1)}, bf16[128,2048]{1,0:T(8,128)(2,1)S(1)}, u32[]{:S(2)}, u32[]{:S(2)}) collective-permute-start(bf16[128,2048]{1,0:T(8,128)(2,1)S(1)} %slice.179), channel_id=1, source_target_pairs={{0,1},{1,0},{2,3},{3,2},{4,5},{5,4},{6,7},{7,6},{8,9},{9,8},{10,11... | collective-permute-start | bytes 1572872 | tf_op jit(solution)/shard_map/ppermute | solution.py:44
  282.8 195.0 %reduce-scatter.7.cloned.1.call-start = ((), (), s32[]{:S(2)}) async-start(), calls=%async_computation.15 | async-start | bytes 5242880 | tf_op jit(solution)/shard_map/reduce_scatter | solution.py:121
  307.0 15.3 %collective-permute-start.29 = (bf16[768,2048]{1,0:T(8,128)(2,1)S(1)}, bf16[768,2048]{1,0:T(8,128)(2,1)S(1)}, u32[]{:S(2)}, u32[]{:S(2)}) collective-permute-start(bf16[768,2048]{1,0:T(8,128)(2,1)S(1)} %get-tuple-element.204), channel_id=1, source_target_pairs={{0,8},{8,0},{16,24},{24,16},{1,9},{9,1},{17,25},{25,17},{2,10},{10... | collective-permute-start | bytes 9437192 | tf_op jit(solution)/shard_map/ppermute | solution.py:44
  307.5 14.8 %collective-permute-start.31 = (bf16[128,2048]{1,0:T(8,128)(2,1)S(1)}, bf16[128,2048]{1,0:T(8,128)(2,1)S(1)}, u32[]{:S(2)}, u32[]{:S(2)}) collective-permute-start(bf16[128,2048]{1,0:T(8,128)(2,1)S(1)} %get-tuple-element.253), channel_id=1, source_target_pairs={{0,16},{8,24},{16,0},{24,8},{1,17},{9,25},{17,1},{25,9},{2,18},{10... | collective-permute-start | bytes 1572872 | tf_op jit(solution)/shard_map/ppermute | solution.py:44
  308.5 13.8 %collective-permute-start.30 = (bf16[128,2048]{1,0:T(8,128)(2,1)S(1)}, bf16[128,2048]{1,0:T(8,128)(2,1)S(1)}, u32[]{:S(2)}, u32[]{:S(2)}) collective-permute-start(bf16[128,2048]{1,0:T(8,128)(2,1)S(1)} %get-tuple-element.254), channel_id=1, source_target_pairs={{0,1},{1,0},{2,3},{3,2},{4,5},{5,4},{6,7},{7,6},{8,9},{9,8},{10,11... | collective-permute-start | bytes 1572872 | tf_op jit(solution)/shard_map/ppermute | solution.py:44
  330.4 19.2 %collective-permute-start.34 = (bf16[256,2048]{1,0:T(8,128)(2,1)S(1)}, bf16[256,2048]{1,0:T(8,128)(2,1)}, u32[]{:S(2)}, u32[]{:S(2)}) collective-permute-start(bf16[256,2048]{1,0:T(8,128)(2,1)S(1)} %shard_map.280.refs_3_), channel_id=1, source_target_pairs={{0,8},{8,0},{16,24},{24,16},{1,9},{9,1},{17,25},{25,17},{2,10},{10... | collective-permute-start | bytes 3145736 | tf_op jit(solution)/shard_map/ppermute | solution.py:44
  330.5 25.7 %collective-permute-start.32 = (bf16[256,2048]{1,0:T(8,128)(2,1)S(1)}, bf16[256,2048]{1,0:T(8,128)(2,1)}, u32[]{:S(2)}, u32[]{:S(2)}) collective-permute-start(bf16[256,2048]{1,0:T(8,128)(2,1)S(1)} %get-tuple-element.205), channel_id=1, source_target_pairs={{0,16},{8,24},{16,0},{24,8},{1,17},{9,25},{17,1},{25,9},{2,18},{10... | collective-permute-start | bytes 3145736 | tf_op jit(solution)/shard_map/ppermute | solution.py:44
  331.6 25.5 %collective-permute-start.33 = (bf16[256,2048]{1,0:T(8,128)(2,1)}, bf16[256,2048]{1,0:T(8,128)(2,1)}, u32[]{:S(2)}, u32[]{:S(2)}) collective-permute-start(bf16[256,2048]{1,0:T(8,128)(2,1)} %get-tuple-element.206.refs_2_), channel_id=1, source_target_pairs={{0,1},{1,0},{2,3},{3,2},{4,5},{5,4},{6,7},{7,6},{8,9},{9,8},{10,11... | collective-permute-start | bytes 3145736 | tf_op jit(solution)/shard_map/ppermute | solution.py:44
  369.7 20.4 %all-to-all-start.3 = ((bf16[8,256,256]{2,1,0:T(8,128)(2,1)}), bf16[8,256,256]{2,1,0:T(8,128)(2,1)}, u32[]{:S(2)}, u32[]{:S(2)}) async-start(bf16[8,256,256]{2,1,0:T(8,128)(2,1)} %get-tuple-element.210), calls=%async_computation.3 | async-start | bytes 2097152 | tf_op jit(solution)/shard_map/all_to_all | solution.py:690
  374.1 184.1 %reduce-scatter.9.cloned.1.call-start = ((), (), s32[]{:S(2)}) async-start(), calls=%async_computation.16 | async-start | bytes 3932160 | tf_op jit(solution)/shard_map/reduce_scatter | solution.py:121
  390.1 30.9 %collective-permute-start.35 = (bf16[768,2048]{1,0:T(8,128)(2,1)}, bf16[768,2048]{1,0:T(8,128)(2,1)S(1)}, u32[]{:S(2)}, u32[]{:S(2)}) collective-permute-start(bf16[768,2048]{1,0:T(8,128)(2,1)} %shard_map.284), channel_id=1, source_target_pairs={{0,8},{8,0},{16,24},{24,16},{1,9},{9,1},{17,25},{25,17},{2,10},{10... | collective-permute-start | bytes 9437192 | tf_op jit(solution)/shard_map/ppermute | solution.py:44
  390.4 25.6 %collective-permute-start.36 = (bf16[256,2048]{1,0:T(8,128)(2,1)}, bf16[256,2048]{1,0:T(8,128)(2,1)S(1)}, u32[]{:S(2)}, u32[]{:S(2)}) collective-permute-start(bf16[256,2048]{1,0:T(8,128)(2,1)} %add_convert_fusion.3.refs_12_), channel_id=1, source_target_pairs={{0,16},{8,24},{16,0},{24,8},{1,17},{9,25},{17,1},{25,9},{2,18},{10... | collective-permute-start | bytes 3145736 | tf_op jit(solution)/shard_map/ppermute | solution.py:44
  392.1 25.5 %collective-permute-start.37 = (bf16[256,2048]{1,0:T(8,128)(2,1)}, bf16[256,2048]{1,0:T(8,128)(2,1)}, u32[]{:S(2)}, u32[]{:S(2)}) collective-permute-start(bf16[256,2048]{1,0:T(8,128)(2,1)} %reduce-scatter.5.cloned.1.call-done.refs_1_), channel_id=1, source_target_pairs={{0,1},{1,0},{2,3},{3,2},{4,5},{5,4},{6,7},{7,6},{8,9},{9,8},{10,11... | collective-permute-start | bytes 3145736 | tf_op jit(solution)/shard_map/ppermute | solution.py:44
  413.3 7.2 %collective-permute-start.40 = (bf16[256,2048]{1,0:T(8,128)(2,1)S(1)}, bf16[256,2048]{1,0:T(8,128)(2,1)S(1)}, u32[]{:S(2)}, u32[]{:S(2)}) collective-permute-start(bf16[256,2048]{1,0:T(8,128)(2,1)S(1)} %shard_map.287.refs_2_), channel_id=1, source_target_pairs={{0,8},{8,0},{16,24},{24,16},{1,9},{9,1},{17,25},{25,17},{2,10},{10... | collective-permute-start | bytes 3145736 | tf_op jit(solution)/shard_map/ppermute | solution.py:44
  432.7 27.5 %collective-permute-start.41 = (bf16[768,2048]{1,0:T(8,128)(2,1)}, bf16[768,2048]{1,0:T(8,128)(2,1)S(1)}, u32[]{:S(2)}, u32[]{:S(2)}) collective-permute-start(bf16[768,2048]{1,0:T(8,128)(2,1)} %shard_map.291.refs_2_), channel_id=1, source_target_pairs={{0,8},{8,0},{16,24},{24,16},{1,9},{9,1},{17,25},{25,17},{2,10},{10... | collective-permute-start | bytes 9437192 | tf_op jit(solution)/shard_map/ppermute | solution.py:44
  446.0 13.9 %collective-permute-start.43 = (bf16[128,2048]{1,0:T(8,128)(2,1)S(1)}, bf16[128,2048]{1,0:T(8,128)(2,1)S(1)}, u32[]{:S(2)}, u32[]{:S(2)}) collective-permute-start(bf16[128,2048]{1,0:T(8,128)(2,1)S(1)} %get-tuple-element.251), channel_id=1, source_target_pairs={{0,16},{8,24},{16,0},{24,8},{1,17},{9,25},{17,1},{25,9},{2,18},{10... | collective-permute-start | bytes 1572872 | tf_op jit(solution)/shard_map/ppermute | solution.py:44
  446.6 13.6 %collective-permute-start.42 = (bf16[128,2048]{1,0:T(8,128)(2,1)S(1)}, bf16[128,2048]{1,0:T(8,128)(2,1)S(1)}, u32[]{:S(2)}, u32[]{:S(2)}) collective-permute-start(bf16[128,2048]{1,0:T(8,128)(2,1)S(1)} %get-tuple-element.252), channel_id=1, source_target_pairs={{0,1},{1,0},{2,3},{3,2},{4,5},{5,4},{6,7},{7,6},{8,9},{9,8},{10,11... | collective-permute-start | bytes 1572872 | tf_op jit(solution)/shard_map/ppermute | solution.py:44
  477.6 10.3 %collective-permute-start.46 = (bf16[1536,1024]{1,0:T(8,128)(2,1)}, bf16[1536,1024]{1,0:T(8,128)(2,1)}, u32[]{:S(2)}, u32[]{:S(2)}) collective-permute-start(bf16[1536,1024]{1,0:T(8,128)(2,1)} %get-tuple-element.232), channel_id=1, source_target_pairs={{0,8},{8,0},{16,24},{24,16},{1,9},{9,1},{17,25},{25,17},{2,10},{10... | collective-permute-start | bytes 9437192 | tf_op jit(solution)/shard_map/ppermute | solution.py:44
  477.8 34.5 %all-to-all-start.4 = ((bf16[4,128,1024]{2,1,0:T(8,128)(2,1)}), bf16[4,128,1024]{2,1,0:T(8,128)(2,1)}, u32[]{:S(2)}, u32[]{:S(2)}) async-start(bf16[4,128,1024]{2,1,0:T(8,128)(2,1)} %bitcast.96), calls=%async_computation.6 | async-start | bytes 2097152 | tf_op jit(solution)/shard_map/all_to_all | solution.py:125
  482.3 119.6 %reduce-scatter.11.cloned.1.call-start = ((), (), s32[]{:S(2)}) async-start(), calls=%async_computation.17 | async-start | bytes 1310720 | tf_op jit(solution)/shard_map/reduce_scatter | solution.py:121
  483.9 24.5 %collective-permute-start.49 = (bf16[256,1024]{1,0:T(8,128)(2,1)S(1)}, bf16[256,1024]{1,0:T(8,128)(2,1)S(1)}, u32[]{:S(2)}, u32[]{:S(2)}) collective-permute-start(bf16[256,1024]{1,0:T(8,128)(2,1)S(1)} %get-tuple-element.249), channel_id=1, source_target_pairs={{0,16},{8,24},{16,0},{24,8},{1,17},{9,25},{17,1},{25,9},{2,18},{10... | collective-permute-start | bytes 1572872 | tf_op jit(solution)/shard_map/ppermute | solution.py:44
  485.9 22.5 %collective-permute-start.48 = (bf16[256,1024]{1,0:T(8,128)(2,1)S(1)}, bf16[256,1024]{1,0:T(8,128)(2,1)S(1)}, u32[]{:S(2)}, u32[]{:S(2)}) collective-permute-start(bf16[256,1024]{1,0:T(8,128)(2,1)S(1)} %get-tuple-element.250), channel_id=1, source_target_pairs={{0,1},{1,0},{2,3},{3,2},{4,5},{5,4},{6,7},{7,6},{8,9},{9,8},{10,11... | collective-permute-start | bytes 1572872 | tf_op jit(solution)/shard_map/ppermute | solution.py:44
  487.3 35.9 %collective-permute-start.45 = (bf16[256,2048]{1,0:T(8,128)(2,1)}, bf16[256,2048]{1,0:T(8,128)(2,1)}, u32[]{:S(2)}, u32[]{:S(2)}) collective-permute-start(bf16[256,2048]{1,0:T(8,128)(2,1)} %copy-done.44), channel_id=1, source_target_pairs={{0,1},{1,0},{2,3},{3,2},{4,5},{5,4},{6,7},{7,6},{8,9},{9,8},{10,11... | collective-permute-start | bytes 3145736 | tf_op jit(solution)/shard_map/ppermute | solution.py:44
  487.9 43.1 %collective-permute-start.44 = (bf16[256,2048]{1,0:T(8,128)(2,1)}, bf16[256,2048]{1,0:T(8,128)(2,1)}, u32[]{:S(2)}, u32[]{:S(2)}) collective-permute-start(bf16[256,2048]{1,0:T(8,128)(2,1)} %copy-done.46), channel_id=1, source_target_pairs={{0,16},{8,24},{16,0},{24,8},{1,17},{9,25},{17,1},{25,9},{2,18},{10... | collective-permute-start | bytes 3145736 | tf_op jit(solution)/shard_map/ppermute | solution.py:44
  512.2 41.2 %collective-permute-start.56 = (bf16[512,1024]{1,0:T(8,128)(2,1)}, bf16[512,1024]{1,0:T(8,128)(2,1)}, u32[]{:S(2)}, u32[]{:S(2)}) collective-permute-start(bf16[512,1024]{1,0:T(8,128)(2,1)} %get-tuple-element.247), channel_id=1, source_target_pairs={{0,16},{8,24},{16,0},{24,8},{1,17},{9,25},{17,1},{25,9},{2,18},{10... | collective-permute-start | bytes 3145736 | tf_op jit(solution)/shard_map/ppermute | solution.py:44
  512.3 41.2 %collective-permute-start.57 = (bf16[512,1024]{1,0:T(8,128)(2,1)}, bf16[512,1024]{1,0:T(8,128)(2,1)}, u32[]{:S(2)}, u32[]{:S(2)}) collective-permute-start(bf16[512,1024]{1,0:T(8,128)(2,1)} %copy-done.41), channel_id=1, source_target_pairs={{0,1},{1,0},{2,3},{3,2},{4,5},{5,4},{6,7},{7,6},{8,9},{9,8},{10,11... | collective-permute-start | bytes 3145736 | tf_op jit(solution)/shard_map/ppermute | solution.py:44
  515.3 82.1 %collective-permute-start.39 = (bf16[256,2048]{1,0:T(8,128)(2,1)}, bf16[256,2048]{1,0:T(8,128)(2,1)}, u32[]{:S(2)}, u32[]{:S(2)}) collective-permute-start(bf16[256,2048]{1,0:T(8,128)(2,1)} %copy-done.40), channel_id=1, source_target_pairs={{0,1},{1,0},{2,3},{3,2},{4,5},{5,4},{6,7},{7,6},{8,9},{9,8},{10,11... | collective-permute-start | bytes 3145736 | tf_op jit(solution)/shard_map/ppermute | solution.py:44
  523.3 74.1 %collective-permute-start.38 = (bf16[256,2048]{1,0:T(8,128)(2,1)}, bf16[256,2048]{1,0:T(8,128)(2,1)}, u32[]{:S(2)}, u32[]{:S(2)}) collective-permute-start(bf16[256,2048]{1,0:T(8,128)(2,1)} %copy-done.45), channel_id=1, source_target_pairs={{0,16},{8,24},{16,0},{24,8},{1,17},{9,25},{17,1},{25,9},{2,18},{10... | collective-permute-start | bytes 3145736 | tf_op jit(solution)/shard_map/ppermute | solution.py:44
  531.0 79.7 %collective-permute-start.59 = (bf16[4,128,1024]{2,1,0:T(8,128)(2,1)}, bf16[4,128,1024]{2,1,0:T(8,128)(2,1)}, u32[]{:S(2)}, u32[]{:S(2)}) collective-permute-start(bf16[4,128,1024]{2,1,0:T(8,128)(2,1)} %all-to-all-done.4.refs_1_), channel_id=1, source_target_pairs={{0,1},{1,0},{2,3},{3,2},{4,5},{5,4},{6,7},{7,6},{8,9},{9,8},{10,11... | collective-permute-start | bytes 3145736 | tf_op jit(solution)/shard_map/ppermute | solution.py:44
  558.2 25.6 %all-to-all-start.5 = ((bf16[4,128,768]{2,1,0:T(8,128)(2,1)}), bf16[4,128,768]{2,1,0:T(8,128)(2,1)S(1)}, u32[]{:S(2)}, u32[]{:S(2)}) async-start(bf16[4,128,768]{2,1,0:T(8,128)(2,1)} %bitcast.98), calls=%async_computation.8 | async-start | bytes 1572864 | tf_op jit(solution)/shard_map/all_to_all | solution.py:125
  561.8 9.5 %collective-permute-start.50 = (f32[16,1536]{1,0:T(8,128)S(1)}, f32[16,1536]{1,0:T(8,128)S(1)}, u32[]{:S(2)}, u32[]{:S(2)}) collective-permute-start(f32[16,1536]{1,0:T(8,128)S(1)} %constant_dynamic-update-slice_fusion.20), channel_id=1, source_target_pairs={{0,2},{2,0},{4,6},{6,4},{1,3},{3,1},{5,7},{7,5},{8,10},{10,8},{12,... | collective-permute-start | bytes 294920 | tf_op jit(solution)/shard_map/ppermute | solution.py:44
  571.3 13.9 %collective-permute-start.51 = (f32[16,1536]{1,0:T(8,128)S(1)}, f32[16,1536]{1,0:T(8,128)S(1)}, u32[]{:S(2)}, u32[]{:S(2)}) collective-permute-start(f32[16,1536]{1,0:T(8,128)S(1)} %add.129), channel_id=1, source_target_pairs={{0,4},{2,6},{4,0},{6,2},{1,5},{3,7},{5,1},{7,3},{8,12},{10,14},{12... | collective-permute-start | bytes 294920 | tf_op jit(solution)/shard_map/ppermute | solution.py:44
  583.8 33.6 %collective-permute-start.55 = (bf16[4,128,768]{2,1,0:T(8,128)(2,1)S(1)}, bf16[4,128,768]{2,1,0:T(8,128)(2,1)S(1)}, u32[]{:S(2)}, u32[]{:S(2)}) collective-permute-start(bf16[4,128,768]{2,1,0:T(8,128)(2,1)S(1)} %all-to-all-done.5.refs_1_), channel_id=1, source_target_pairs={{0,1},{1,0},{2,3},{3,2},{4,5},{5,4},{6,7},{7,6},{8,9},{9,8},{10,11... | collective-permute-start | bytes 2359304 | tf_op jit(solution)/shard_map/ppermute | solution.py:44
  592.0 17.5 %collective-permute-start.54 = (f32[16,1536]{1,0:T(8,128)S(1)}, f32[16,1536]{1,0:T(8,128)S(1)}, u32[]{:S(2)}, u32[]{:S(2)}) collective-permute-start(f32[16,1536]{1,0:T(8,128)S(1)} %add.132), channel_id=1, source_target_pairs={{0,1},{1,0},{2,3},{3,2},{4,5},{5,4},{6,7},{7,6},{8,9},{9,8},{10,11... | collective-permute-start | bytes 294920 | tf_op jit(solution)/shard_map/ppermute | solution.py:44
  601.9 12.7 %collective-permute-start.58 = (bf16[1,128,1024]{2,1,0:T(8,128)(2,1)}, bf16[1,128,1024]{2,1,0:T(8,128)(2,1)S(1)}, u32[]{:S(2)}, u32[]{:S(2)}) collective-permute-start(bf16[1,128,1024]{2,1,0:T(8,128)(2,1)} %bitcast.100), channel_id=1, source_target_pairs={{0,1},{1,0},{2,3},{3,2},{4,5},{5,4},{6,7},{7,6},{8,9},{9,8},{10,11... | collective-permute-start | bytes 786440 | tf_op jit(solution)/shard_map/ppermute | solution.py:44
  (73 other events, 505.3 us)
Sparse Core Ops, SparseCore 0:
  14.2 28.1 all-gather.4
  44.5 62.9 all-gather.6
  109.7 79.3 all-gather.8
  190.6 79.2 all-gather.10
  282.9 74.9 reduce-scatter.4
  369.8 75.5 reduce-scatter.6
  477.8 59.6 reduce-scatter.8
  557.3 29.2 reduce-scatter.10
